TPU v7x, 32 devices: a whole 2x2x4 slice. The times are simulated.
32 devices in a mesh: gx: 4 (over y, core), gy: 4 (over z), gz: 2 (over x).
Axes of the slice: x: 2, y: 2, z: 4, core: 2. Of those that a mesh axis runs over, the one named last changes fastest.
Arguments:
- chi: float32 [64, 64, 256], P('gx', 'gy', 'gz'), may hold values from 0.05 to 4
- inducing: float32 [3, 64, 64, 256], P(None, 'gx', 'gy', 'gz'), may hold values from -6 to 6
- record_dest: int32 [4, 4, 2, 1024, 1], P('gx', 'gy', 'gz'), may hold values from 0 to 1; in each aligned block of 1024 rows (0 to 1023, 1024 to 2047, ..., all dimensions but the last counted through in order) at most 640 rows name the same one
- record_cell: int32 [4, 4, 2, 1024], P('gx', 'gy', 'gz'), may hold values from 0 to 32767
- record_value: float32 [4, 4, 2, 1024], P('gx', 'gy', 'gz'), may hold values from -16 to 16
Outputs:
- potential: float32 [64, 64, 256], P('gx', 'gy', 'gz')
Inputs may be any that keep to these rules, and one draw needn't show every extreme that they name: `record_dest`: among the records of one device, at most 640 go to any one depth brick; in some devices exactly 640 do.
All inputs are finite; a program needn't handle non-finite values.
Results may differ from a plain program's by a relative error of at most 0.0001.
Values sent between devices are 32-bit elements; how exact they have to be, the bound alone decides.
No kernel may reach another device: no remote copies, remote signals or barrier semaphores. Data moves between devices by JAX's collectives and lax.ppermute only.
A program may use at most 64 MiB of HBM per device.

v0:
```python
import jax
import jax.numpy as jnp
from jax import lax
from jax.sharding import PartitionSpec as P

SMOOTH = 2
LEVELS = 3
COARSE_SWEEPS = 8
CAP = 640


OMEGA = 0.8


def padded_2(cells, sides, width):
    for axis, dim in sides:
        count = lax.axis_size(axis)
        ends = count - 1
        head = lax.slice_in_dim(cells, 0, width, axis=dim)
        tail = lax.slice_in_dim(cells, cells.shape[dim] - width, cells.shape[dim], axis=dim)
        cells = jnp.concatenate(
            [
                lax.ppermute(tail, axis, [(i, (i + 1) % count) for i in range(ends)]),
                cells,
                lax.ppermute(head, axis, [((i + 1) % count, i) for i in range(ends)]),
            ],
            axis=dim,
        )
    return cells


def restrict(x):
    s = x.shape
    return x.reshape(s[0] // 2, 2, s[1] // 2, 2, s[2] // 2, 2).mean(axis=(1, 3, 5))


def prolong(e):
    return jnp.repeat(jnp.repeat(jnp.repeat(e, 2, 0), 2, 1), 2, 2)


def neighbours(padded):
    return [
        padded[2:, 1:-1, 1:-1],
        padded[:-2, 1:-1, 1:-1],
        padded[1:-1, 2:, 1:-1],
        padded[1:-1, :-2, 1:-1],
        padded[1:-1, 1:-1, 2:],
        padded[1:-1, 1:-1, :-2],
    ]


def moment_pad(x):
    return padded_2(x, (("gx", 0), ("gy", 1), ("gz", 2)), 1)


def fine_pad(x):
    return padded_2(x, (("gx", 0), ("gy", 1), ("gz", 2)), 1)


def middle_pad(x):
    return padded_2(x, (("gx", 0), ("gy", 1), ("gz", 2)), 1)


def coarse_pad(x):
    return padded_2(x, (("gx", 0), ("gy", 1), ("gz", 2)), 1)


def coefficients(kappa, pad_fn):
    return [0.5 * (kappa + other) for other in neighbours(pad_fn(kappa))]


def apply_op(v, coefs, scale, pad_fn):
    total = jnp.zeros_like(v)
    for coef, other in zip(coefs, neighbours(pad_fn(v))):
        total = total + coef * (v - other)
    return scale * total


def relax(rhs, kappa, scale, sweeps, pad_fn):
    coefs = coefficients(kappa, pad_fn)
    diag = scale * (coefs[0] + coefs[1] + coefs[2] + coefs[3] + coefs[4] + coefs[5])
    v = OMEGA * rhs / diag
    for sweep in range(sweeps - 1):
        v = v + OMEGA * (rhs - apply_op(v, coefs, scale, pad_fn)) / diag
    return v


def coarse_solve(rhs, kappa):
    scale = 0.25**LEVELS
    return relax(rhs, kappa, scale, COARSE_SWEEPS, coarse_pad)


def cycle(level, rhs, kappa):
    if level == LEVELS:
        return coarse_solve(rhs, kappa)
    if level < LEVELS - 1:
        pad_fn = fine_pad
    else:
        pad_fn = middle_pad
    scale = 0.25**level
    coefs = coefficients(kappa, pad_fn)
    diag = scale * (coefs[0] + coefs[1] + coefs[2] + coefs[3] + coefs[4] + coefs[5])
    v = OMEGA * rhs / diag
    v = v + OMEGA * (rhs - apply_op(v, coefs, scale, pad_fn)) / diag
    resid = rhs - apply_op(v, coefs, scale, pad_fn)
    corr = cycle(level + 1, restrict(resid), restrict(kappa))
    v = v + prolong(corr)
    for sweep in range(SMOOTH):
        v = v + OMEGA * (rhs - apply_op(v, coefs, scale, pad_fn)) / diag
    return v


def per_device(chi, inducing, record_dest, record_cell, record_value):
    n_gz = lax.axis_size("gz")
    dest = record_dest[0, 0, 0, :, 0]
    cells = record_cell[0, 0, 0]
    values = record_value[0, 0, 0]
    onehot = (dest[:, None] == jnp.arange(n_gz, dtype=jnp.int32)[None, :]).astype(jnp.int32)
    ranks = jnp.sum((jnp.cumsum(onehot, axis=0) - 1) * onehot, axis=1)
    outgoing = jnp.zeros((n_gz, 2, CAP), jnp.float32)
    outgoing = outgoing.at[dest, 0, ranks].set(values)
    outgoing = outgoing.at[dest, 1, ranks].set(cells.astype(jnp.float32))
    incoming = lax.all_to_all(outgoing, "gz", split_axis=0, concat_axis=0, tiled=True)
    in_values = incoming[:, 0].reshape(-1)
    in_cells = incoming[:, 1].reshape(-1).astype(jnp.int32)
    moment_x = moment_pad(chi * inducing[0])
    moment_y = moment_pad(chi * inducing[1])
    moment_z = moment_pad(chi * inducing[2])
    source = -0.5 * (
        moment_x[2:, 1:-1, 1:-1]
        - moment_x[:-2, 1:-1, 1:-1]
        + (moment_y[1:-1, 2:, 1:-1] - moment_y[1:-1, :-2, 1:-1])
        + (moment_z[1:-1, 1:-1, 2:] - moment_z[1:-1, 1:-1, :-2])
    )
    rhs = source.reshape(-1).at[in_cells].add(in_values).reshape(source.shape)
    return cycle(0, rhs, 1.0 + chi)


def solution(mesh):
    placed = (
        P("gx", "gy", "gz"),
        P(None, "gx", "gy", "gz"),
        P("gx", "gy", "gz", None, None),
        P("gx", "gy", "gz", None),
        P("gx", "gy", "gz", None),
    )
    return jax.shard_map(
        per_device, mesh=mesh, in_specs=placed, out_specs=P("gx", "gy", "gz"), check_vma=False
    )
```

profile of v0, /device:TPU:0, one launch (start us, length us, event | category | flops | bytes accessed | tf_op | source)
XLA Modules:
  0.0 570.2 jit_solution(3912888449777369581)
XLA Ops:
  5.5 4.5 scatter_custom_fusion.1
  10.0 4.3 scatter_fusion.1
  15.0 4.2 all-to-all-start
  22.0 5.1 collective-permute-start.6
  32.1 9.7 %reshape.138 = f32[8,2,8,2,64,2]{5,4,3,2,1,0:T(8,128)} reshape(f32[16,16,128]{2,1,0:T(8,128)S(1)} %get-tuple-element.66) | data formatting | bytes 262144 | tf_op jit(solution)/shard_map/reshape | solution.py:34
  48.6 4.3 collective-permute-start.1
  54.3 4.5 collective-permute-start.8
  60.2 4.5 collective-permute-start.15
  66.2 4.5 collective-permute-start.5
  72.1 4.6 collective-permute-start.11
  82.7 7.9 %scatter_fusion = f32[32768]{0:T(1024)S(1)} fusion(f32[32768]{0:T(1024)S(1)} %bitcast.39, s32[1280]{0:T(1024)S(1)} %fusion.300, f32[1280]{0:T(1024)S(1)} %reshape.163), kind=kCustom, calls=%fused_computation | custom fusion | flops 1280 | bytes 20480 | tf_op jit(solution)/shard_map/scatter-add | solution.py:135
  109.3 4.6 collective-permute-start.23
  123.3 4.4 collective-permute-start.33
  129.1 4.5 collective-permute-start.27
  135.0 4.2 collective-permute-done.26
  140.6 4.6 collective-permute-start.29
  150.0 9.7 %reshape.137 = f32[8,2,8,2,64,2]{5,4,3,2,1,0:T(8,128)} reshape(f32[16,16,128]{2,1,0:T(8,128)S(1)} %fusion.45) | data formatting | bytes 262144 | tf_op jit(solution)/shard_map/reshape | solution.py:34
  166.6 4.8 collective-permute-start.49
  177.7 4.2 collective-permute-done.38
  183.3 4.6 collective-permute-start.41
  192.4 5.5 collective-permute-start.43
  202.5 4.5 collective-permute-start.45
  214.0 4.6 collective-permute-start.47
  228.4 4.7 collective-permute-done.54
  236.4 4.5 collective-permute-start.69
  242.3 4.5 collective-permute-start.59
  255.4 4.4 collective-permute-start.63
  266.7 4.5 collective-permute-start.65
  279.5 4.2 collective-permute-done.72
  292.8 4.5 collective-permute-start.77
  314.5 4.5 collective-permute-start.83
  336.1 4.5 collective-permute-start.89
  357.8 4.5 collective-permute-start.95
  379.4 4.5 collective-permute-start.101
  401.1 4.5 collective-permute-start.107
  422.8 4.5 collective-permute-start.113
  439.1 4.2 collective-permute-done.116
  444.7 4.5 collective-permute-start.119
  466.6 4.5 collective-permute-start.125
  483.2 4.2 collective-permute-done.128
  488.8 4.6 collective-permute-start.131
  505.7 4.2 collective-permute-done.134
  511.3 4.8 collective-permute-start.137
  529.1 4.2 collective-permute-done.140
  534.8 4.6 collective-permute-start.143
  539.3 4.3 collective-permute-done.142
  553.9 4.2 collective-permute-done.146
  559.5 4.6 collective-permute-start.149
  (446 shorter events, 337.7 us)
Async XLA Ops:
  15.0 30.9 %all-to-all-start = ((f32[2,2,640]{2,1,0:T(2,128)}), f32[2,2,640]{2,1,0:T(2,128)S(1)}, u32[]{:S(2)}, u32[]{:S(2)}) async-start(f32[2,2,640]{2,1,0:T(2,128)} %reshape.157), calls=%async_computation | async-start | bytes 20480 | tf_op jit(solution)/shard_map/all_to_all | solution.py:123
  19.2 35.0 %collective-permute-start.13 = (f32[1,16,128]{2,1,0:T(8,128)S(1)}, f32[1,16,128]{2,1,0:T(8,128)S(1)}, u32[]{:S(2)}, u32[]{:S(2)}) collective-permute-start(f32[1,16,128]{2,1,0:T(8,128)S(1)} %get-tuple-element.64), channel_id=1, source_target_pairs={{0,8},{8,16},{16,24},{1,9},{9,17},{17,25},{2,10},{10,18},{18,26},{... | collective-permute-start | bytes 24584 | tf_op jit(solution)/shard_map/ppermute | solution.py:23
  20.7 38.1 %collective-permute-start.12 = (f32[1,16,128]{2,1,0:T(8,128)S(1)}, f32[1,16,128]{2,1,0:T(8,128)S(1)}, u32[]{:S(2)}, u32[]{:S(2)}) collective-permute-start(f32[1,16,128]{2,1,0:T(8,128)S(1)} %get-tuple-element.65), channel_id=1, source_target_pairs={{8,0},{16,8},{24,16},{9,1},{17,9},{25,17},{10,2},{18,10},{26,18},{... | collective-permute-start | bytes 24584 | tf_op jit(solution)/shard_map/ppermute | solution.py:25
  22.0 26.6 %collective-permute-start.6 = (f32[1,16,128]{2,1,0:T(8,128)S(1)}, f32[1,16,128]{2,1,0:T(8,128)S(1)}, u32[]{:S(2)}, u32[]{:S(2)}) collective-permute-start(f32[1,16,128]{2,1,0:T(8,128)S(1)} %get-tuple-element.71), channel_id=1, source_target_pairs={{0,8},{8,16},{16,24},{1,9},{9,17},{17,25},{2,10},{10,18},{18,26},{... | collective-permute-start | bytes 24584 | tf_op jit(solution)/shard_map/ppermute | solution.py:23
  27.2 18.8 %collective-permute-start.2 = (f32[1,16,128]{2,1,0:T(8,128)S(1)}, f32[1,16,128]{2,1,0:T(8,128)S(1)}, u32[]{:S(2)}, u32[]{:S(2)}) collective-permute-start(f32[1,16,128]{2,1,0:T(8,128)S(1)} %get-tuple-element.69), channel_id=1, source_target_pairs={{0,8},{8,16},{16,24},{1,9},{9,17},{17,25},{2,10},{10,18},{18,26},{... | collective-permute-start | bytes 24584 | tf_op jit(solution)/shard_map/ppermute | solution.py:23
  30.8 16.5 %collective-permute-start.3 = (f32[1,16,128]{2,1,0:T(8,128)S(1)}, f32[1,16,128]{2,1,0:T(8,128)S(1)}, u32[]{:S(2)}, u32[]{:S(2)}) collective-permute-start(f32[1,16,128]{2,1,0:T(8,128)S(1)} %get-tuple-element.70), channel_id=1, source_target_pairs={{8,0},{16,8},{24,16},{9,1},{17,9},{25,17},{10,2},{18,10},{26,18},{... | collective-permute-start | bytes 24584 | tf_op jit(solution)/shard_map/ppermute | solution.py:25
  47.3 24.8 %collective-permute-start = (f32[1,16,128]{2,1,0:T(8,128)S(1)}, f32[1,16,128]{2,1,0:T(8,128)S(1)}, u32[]{:S(2)}, u32[]{:S(2)}) collective-permute-start(f32[1,16,128]{2,1,0:T(8,128)S(1)} %get-tuple-element.67), channel_id=1, source_target_pairs={{8,0},{16,8},{24,16},{9,1},{17,9},{25,17},{10,2},{18,10},{26,18},{... | collective-permute-start | bytes 24584 | tf_op jit(solution)/shard_map/ppermute | solution.py:25
  48.6 28.2 %collective-permute-start.1 = (f32[1,16,128]{2,1,0:T(8,128)S(1)}, f32[1,16,128]{2,1,0:T(8,128)S(1)}, u32[]{:S(2)}, u32[]{:S(2)}) collective-permute-start(f32[1,16,128]{2,1,0:T(8,128)S(1)} %get-tuple-element.68), channel_id=1, source_target_pairs={{0,8},{8,16},{16,24},{1,9},{9,17},{17,25},{2,10},{10,18},{18,26},{... | collective-permute-start | bytes 24584 | tf_op jit(solution)/shard_map/ppermute | solution.py:23
  52.9 25.2 %collective-permute-start.4 = (f32[18,1,128]{2,1,0:T(1,128)S(1)}, f32[18,1,128]{2,1,0:T(1,128)S(1)}, u32[]{:S(2)}, u32[]{:S(2)}) collective-permute-start(f32[18,1,128]{2,1,0:T(1,128)S(1)} %get-tuple-element.52), channel_id=1, source_target_pairs={{2,0},{4,2},{6,4},{3,1},{5,3},{7,5},{10,8},{12,10},{14,12},{11,9},... | collective-permute-start | bytes 27656 | tf_op jit(solution)/shard_map/ppermute | solution.py:25
  66.2 13.3 %collective-permute-start.5 = (f32[18,1,128]{2,1,0:T(1,128)S(1)}, f32[18,1,128]{2,1,0:T(1,128)S(1)}, u32[]{:S(2)}, u32[]{:S(2)}) collective-permute-start(f32[18,1,128]{2,1,0:T(1,128)S(1)} %get-tuple-element.53), channel_id=1, source_target_pairs={{0,2},{2,4},{4,6},{1,3},{3,5},{5,7},{8,10},{10,12},{12,14},{9,11},... | collective-permute-start | bytes 27656 | tf_op jit(solution)/shard_map/ppermute | solution.py:23
  70.8 9.3 %collective-permute-start.10 = (f32[18,18,1]{2,1,0:T(8,128)S(1)}, f32[18,18,1]{2,1,0:T(8,128)S(1)}, u32[]{:S(2)}, u32[]{:S(2)}) collective-permute-start(f32[18,18,1]{2,1,0:T(8,128)S(1)} %get-tuple-element.40), channel_id=1, source_target_pairs={{1,0},{3,2},{5,4},{7,6},{9,8},{11,10},{13,12},{15,14},{17,16},{19,... | collective-permute-start | bytes 3896 | tf_op jit(solution)/shard_map/ppermute | solution.py:25
  72.1 10.4 %collective-permute-start.11 = (f32[18,18,1]{2,1,0:T(8,128)S(1)}, f32[18,18,1]{2,1,0:T(8,128)S(1)}, u32[]{:S(2)}, u32[]{:S(2)}) collective-permute-start(f32[18,18,1]{2,1,0:T(8,128)S(1)} %get-tuple-element.41), channel_id=1, source_target_pairs={{0,1},{2,3},{4,5},{6,7},{8,9},{10,11},{12,13},{14,15},{16,17},{18,... | collective-permute-start | bytes 3896 | tf_op jit(solution)/shard_map/ppermute | solution.py:23
  76.9 13.8 %collective-permute-start.17 = (f32[18,18,1]{2,1,0:T(8,128)S(1)}, f32[18,18,1]{2,1,0:T(8,128)S(1)}, u32[]{:S(2)}, u32[]{:S(2)}) collective-permute-start(f32[18,18,1]{2,1,0:T(8,128)S(1)} %get-tuple-element.38), channel_id=1, source_target_pairs={{0,1},{2,3},{4,5},{6,7},{8,9},{10,11},{12,13},{14,15},{16,17},{18,... | collective-permute-start | bytes 3896 | tf_op jit(solution)/shard_map/ppermute | solution.py:23
  78.2 12.5 %collective-permute-start.16 = (f32[18,18,1]{2,1,0:T(8,128)S(1)}, f32[18,18,1]{2,1,0:T(8,128)S(1)}, u32[]{:S(2)}, u32[]{:S(2)}) collective-permute-start(f32[18,18,1]{2,1,0:T(8,128)S(1)} %get-tuple-element.39), channel_id=1, source_target_pairs={{1,0},{3,2},{5,4},{7,6},{9,8},{11,10},{13,12},{15,14},{17,16},{19,... | collective-permute-start | bytes 3896 | tf_op jit(solution)/shard_map/ppermute | solution.py:25
  96.4 11.4 %collective-permute-start.21 = (f32[18,1,128]{2,1,0:T(1,128)S(1)}, f32[18,1,128]{2,1,0:T(1,128)S(1)}, u32[]{:S(2)}, u32[]{:S(2)}) collective-permute-start(f32[18,1,128]{2,1,0:T(1,128)S(1)} %get-tuple-element.48), channel_id=1, source_target_pairs={{0,2},{2,4},{4,6},{1,3},{3,5},{5,7},{8,10},{10,12},{12,14},{9,11},... | collective-permute-start | bytes 27656 | tf_op jit(solution)/shard_map/ppermute | solution.py:23
  99.9 7.9 %collective-permute-start.20 = (f32[18,1,128]{2,1,0:T(1,128)S(1)}, f32[18,1,128]{2,1,0:T(1,128)S(1)}, u32[]{:S(2)}, u32[]{:S(2)}) collective-permute-start(f32[18,1,128]{2,1,0:T(1,128)S(1)} %get-tuple-element.49), channel_id=1, source_target_pairs={{2,0},{4,2},{6,4},{3,1},{5,3},{7,5},{10,8},{12,10},{14,12},{11,9},... | collective-permute-start | bytes 27656 | tf_op jit(solution)/shard_map/ppermute | solution.py:25
  101.2 22.1 %collective-permute-start.31 = (f32[1,8,64]{2,1,0:T(8,128)S(1)}, f32[1,8,64]{2,1,0:T(8,128)S(1)}, u32[]{:S(2)}, u32[]{:S(2)}) collective-permute-start(f32[1,8,64]{2,1,0:T(8,128)S(1)} %get-tuple-element.101), channel_id=1, source_target_pairs={{0,8},{8,16},{16,24},{1,9},{9,17},{17,25},{2,10},{10,18},{18,26},{... | collective-permute-start | bytes 6152 | tf_op jit(solution)/shard_map/ppermute | solution.py:23
  105.3 18.0 %collective-permute-start.30 = (f32[1,8,64]{2,1,0:T(8,128)S(1)}, f32[1,8,64]{2,1,0:T(8,128)S(1)}, u32[]{:S(2)}, u32[]{:S(2)}) collective-permute-start(f32[1,8,64]{2,1,0:T(8,128)S(1)} %get-tuple-element.102), channel_id=1, source_target_pairs={{8,0},{16,8},{24,16},{9,1},{17,9},{25,17},{10,2},{18,10},{26,18},{... | collective-permute-start | bytes 6152 | tf_op jit(solution)/shard_map/ppermute | solution.py:25
  108.0 9.9 %collective-permute-start.22 = (f32[18,18,1]{2,1,0:T(8,128)S(1)}, f32[18,18,1]{2,1,0:T(8,128)S(1)}, u32[]{:S(2)}, u32[]{:S(2)}) collective-permute-start(f32[18,18,1]{2,1,0:T(8,128)S(1)} %get-tuple-element.36), channel_id=1, source_target_pairs={{1,0},{3,2},{5,4},{7,6},{9,8},{11,10},{13,12},{15,14},{17,16},{19,... | collective-permute-start | bytes 3896 | tf_op jit(solution)/shard_map/ppermute | solution.py:25
  109.3 10.4 %collective-permute-start.23 = (f32[18,18,1]{2,1,0:T(8,128)S(1)}, f32[18,18,1]{2,1,0:T(8,128)S(1)}, u32[]{:S(2)}, u32[]{:S(2)}) collective-permute-start(f32[18,18,1]{2,1,0:T(8,128)S(1)} %get-tuple-element.37), channel_id=1, source_target_pairs={{0,1},{2,3},{4,5},{6,7},{8,9},{10,11},{12,13},{14,15},{16,17},{18,... | collective-permute-start | bytes 3896 | tf_op jit(solution)/shard_map/ppermute | solution.py:23
  120.0 9.0 %collective-permute-start.25 = (f32[1,16,128]{2,1,0:T(8,128)S(1)}, f32[1,16,128]{2,1,0:T(8,128)S(1)}, u32[]{:S(2)}, u32[]{:S(2)}) collective-permute-start(f32[1,16,128]{2,1,0:T(8,128)S(1)} %get-tuple-element.60), channel_id=1, source_target_pairs={{0,8},{8,16},{16,24},{1,9},{9,17},{17,25},{2,10},{10,18},{18,26},{... | collective-permute-start | bytes 24584 | tf_op jit(solution)/shard_map/ppermute | solution.py:23
  123.3 11.6 %collective-permute-start.33 = (f32[10,1,64]{2,1,0:T(1,128)S(1)}, f32[10,1,64]{2,1,0:T(1,128)S(1)}, u32[]{:S(2)}, u32[]{:S(2)}) collective-permute-start(f32[10,1,64]{2,1,0:T(1,128)S(1)} %get-tuple-element.91), channel_id=1, source_target_pairs={{0,2},{2,4},{4,6},{1,3},{3,5},{5,7},{8,10},{10,12},{12,14},{9,11},... | collective-permute-start | bytes 7688 | tf_op jit(solution)/shard_map/ppermute | solution.py:23
  127.7 7.2 %collective-permute-start.32 = (f32[10,1,64]{2,1,0:T(1,128)S(1)}, f32[10,1,64]{2,1,0:T(1,128)S(1)}, u32[]{:S(2)}, u32[]{:S(2)}) collective-permute-start(f32[10,1,64]{2,1,0:T(1,128)S(1)} %get-tuple-element.92), channel_id=1, source_target_pairs={{2,0},{4,2},{6,4},{3,1},{5,3},{7,5},{10,8},{12,10},{14,12},{11,9},... | collective-permute-start | bytes 7688 | tf_op jit(solution)/shard_map/ppermute | solution.py:25
  139.3 8.7 %collective-permute-start.28 = (f32[18,18,1]{2,1,0:T(8,128)S(1)}, f32[18,18,1]{2,1,0:T(8,128)S(1)}, u32[]{:S(2)}, u32[]{:S(2)}) collective-permute-start(f32[18,18,1]{2,1,0:T(8,128)S(1)} %get-tuple-element.34), channel_id=1, source_target_pairs={{1,0},{3,2},{5,4},{7,6},{9,8},{11,10},{13,12},{15,14},{17,16},{19,... | collective-permute-start | bytes 3896 | tf_op jit(solution)/shard_map/ppermute | solution.py:25
  140.6 9.2 %collective-permute-start.29 = (f32[18,18,1]{2,1,0:T(8,128)S(1)}, f32[18,18,1]{2,1,0:T(8,128)S(1)}, u32[]{:S(2)}, u32[]{:S(2)}) collective-permute-start(f32[18,18,1]{2,1,0:T(8,128)S(1)} %get-tuple-element.35), channel_id=1, source_target_pairs={{0,1},{2,3},{4,5},{6,7},{8,9},{10,11},{12,13},{14,15},{16,17},{18,... | collective-permute-start | bytes 3896 | tf_op jit(solution)/shard_map/ppermute | solution.py:23
  145.3 18.5 %collective-permute-start.35 = (f32[10,10,1]{2,1,0:T(8,128)S(1)}, f32[10,10,1]{2,1,0:T(8,128)S(1)}, u32[]{:S(2)}, u32[]{:S(2)}) collective-permute-start(f32[10,10,1]{2,1,0:T(8,128)S(1)} %get-tuple-element.81), channel_id=1, source_target_pairs={{0,1},{2,3},{4,5},{6,7},{8,9},{10,11},{12,13},{14,15},{16,17},{18,... | collective-permute-start | bytes 1208 | tf_op jit(solution)/shard_map/ppermute | solution.py:23
  146.6 17.2 %collective-permute-start.34 = (f32[10,10,1]{2,1,0:T(8,128)S(1)}, f32[10,10,1]{2,1,0:T(8,128)S(1)}, u32[]{:S(2)}, u32[]{:S(2)}) collective-permute-start(f32[10,10,1]{2,1,0:T(8,128)S(1)} %get-tuple-element.82), channel_id=1, source_target_pairs={{1,0},{3,2},{5,4},{7,6},{9,8},{11,10},{13,12},{15,14},{17,16},{19,... | collective-permute-start | bytes 1208 | tf_op jit(solution)/shard_map/ppermute | solution.py:25
  164.0 8.9 %collective-permute-start.37 = (f32[1,8,64]{2,1,0:T(8,128)S(1)}, f32[1,8,64]{2,1,0:T(8,128)S(1)}, u32[]{:S(2)}, u32[]{:S(2)}) collective-permute-start(f32[1,8,64]{2,1,0:T(8,128)S(1)} %get-tuple-element.99), channel_id=1, source_target_pairs={{0,8},{8,16},{16,24},{1,9},{9,17},{17,25},{2,10},{10,18},{18,26},{... | collective-permute-start | bytes 6152 | tf_op jit(solution)/shard_map/ppermute | solution.py:23
  165.3 7.6 %collective-permute-start.36 = (f32[1,8,64]{2,1,0:T(8,128)S(1)}, f32[1,8,64]{2,1,0:T(8,128)S(1)}, u32[]{:S(2)}, u32[]{:S(2)}) collective-permute-start(f32[1,8,64]{2,1,0:T(8,128)S(1)} %get-tuple-element.100), channel_id=1, source_target_pairs={{8,0},{16,8},{24,16},{9,1},{17,9},{25,17},{10,2},{18,10},{26,18},{... | collective-permute-start | bytes 6152 | tf_op jit(solution)/shard_map/ppermute | solution.py:25
  166.6 31.3 %collective-permute-start.49 = (f32[1,4,32]{2,1,0:T(4,128)S(1)}, f32[1,4,32]{2,1,0:T(4,128)S(1)}, u32[]{:S(2)}, u32[]{:S(2)}) collective-permute-start(f32[1,4,32]{2,1,0:T(4,128)S(1)} %get-tuple-element.149), channel_id=1, source_target_pairs={{0,8},{8,16},{16,24},{1,9},{9,17},{17,25},{2,10},{10,18},{18,26},{... | collective-permute-start | bytes 1544 | tf_op jit(solution)/shard_map/ppermute | solution.py:23
  171.4 27.9 %collective-permute-start.48 = (f32[1,4,32]{2,1,0:T(4,128)S(1)}, f32[1,4,32]{2,1,0:T(4,128)S(1)}, u32[]{:S(2)}, u32[]{:S(2)}) collective-permute-start(f32[1,4,32]{2,1,0:T(4,128)S(1)} %get-tuple-element.150), channel_id=1, source_target_pairs={{8,0},{16,8},{24,16},{9,1},{17,9},{25,17},{10,2},{18,10},{26,18},{... | collective-permute-start | bytes 1544 | tf_op jit(solution)/shard_map/ppermute | solution.py:25
  183.3 8.9 %collective-permute-start.41 = (f32[10,10,1]{2,1,0:T(8,128)S(1)}, f32[10,10,1]{2,1,0:T(8,128)S(1)}, u32[]{:S(2)}, u32[]{:S(2)}) collective-permute-start(f32[10,10,1]{2,1,0:T(8,128)S(1)} %get-tuple-element.80), channel_id=1, source_target_pairs={{0,1},{2,3},{4,5},{6,7},{8,9},{10,11},{12,13},{14,15},{16,17},{18,... | collective-permute-start | bytes 1208 | tf_op jit(solution)/shard_map/ppermute | solution.py:23
  187.9 40.5 %collective-permute-start.66 = (f32[1,2,16]{2,1,0:T(2,128)S(1)}, f32[1,2,16]{2,1,0:T(2,128)S(1)}, u32[]{:S(2)}, u32[]{:S(2)}) collective-permute-start(f32[1,2,16]{2,1,0:T(2,128)S(1)} %get-tuple-element.181), channel_id=1, source_target_pairs={{8,0},{16,8},{24,16},{9,1},{17,9},{25,17},{10,2},{18,10},{26,18},{... | collective-permute-start | bytes 392 | tf_op jit(solution)/shard_map/ppermute | solution.py:25
  189.2 39.2 %collective-permute-start.67 = (f32[1,2,16]{2,1,0:T(2,128)S(1)}, f32[1,2,16]{2,1,0:T(2,128)S(1)}, u32[]{:S(2)}, u32[]{:S(2)}) collective-permute-start(f32[1,2,16]{2,1,0:T(2,128)S(1)} %get-tuple-element.182), channel_id=1, source_target_pairs={{0,8},{8,16},{16,24},{1,9},{9,17},{17,25},{2,10},{10,18},{18,26},{... | collective-permute-start | bytes 392 | tf_op jit(solution)/shard_map/ppermute | solution.py:23
  192.4 8.8 %collective-permute-start.43 = (f32[1,8,64]{2,1,0:T(8,128)S(1)}, f32[1,8,64]{2,1,0:T(8,128)S(1)}, u32[]{:S(2)}, u32[]{:S(2)}) collective-permute-start(f32[1,8,64]{2,1,0:T(8,128)S(1)} %get-tuple-element.97), channel_id=1, source_target_pairs={{0,8},{8,16},{16,24},{1,9},{9,17},{17,25},{2,10},{10,18},{18,26},{... | collective-permute-start | bytes 6152 | tf_op jit(solution)/shard_map/ppermute | solution.py:23
  199.3 7.8 %collective-permute-start.51 = (f32[6,1,32]{2,1,0:T(1,128)S(1)}, f32[6,1,32]{2,1,0:T(1,128)S(1)}, u32[]{:S(2)}, u32[]{:S(2)}) collective-permute-start(f32[6,1,32]{2,1,0:T(1,128)S(1)} %get-tuple-element.121), channel_id=1, source_target_pairs={{0,2},{2,4},{4,6},{1,3},{3,5},{5,7},{8,10},{10,12},{12,14},{9,11},... | collective-permute-start | bytes 2312 | tf_op jit(solution)/shard_map/ppermute | solution.py:23
  201.2 7.2 %collective-permute-start.50 = (f32[6,1,32]{2,1,0:T(1,128)S(1)}, f32[6,1,32]{2,1,0:T(1,128)S(1)}, u32[]{:S(2)}, u32[]{:S(2)}) collective-permute-start(f32[6,1,32]{2,1,0:T(1,128)S(1)} %get-tuple-element.122), channel_id=1, source_target_pairs={{2,0},{4,2},{6,4},{3,1},{5,3},{7,5},{10,8},{12,10},{14,12},{11,9},... | collective-permute-start | bytes 2312 | tf_op jit(solution)/shard_map/ppermute | solution.py:25
  212.7 7.2 %collective-permute-start.46 = (f32[10,10,1]{2,1,0:T(8,128)S(1)}, f32[10,10,1]{2,1,0:T(8,128)S(1)}, u32[]{:S(2)}, u32[]{:S(2)}) collective-permute-start(f32[10,10,1]{2,1,0:T(8,128)S(1)} %get-tuple-element.77), channel_id=1, source_target_pairs={{1,0},{3,2},{5,4},{7,6},{9,8},{11,10},{13,12},{15,14},{17,16},{19,... | collective-permute-start | bytes 1208 | tf_op jit(solution)/shard_map/ppermute | solution.py:25
  214.0 7.2 %collective-permute-start.47 = (f32[10,10,1]{2,1,0:T(8,128)S(1)}, f32[10,10,1]{2,1,0:T(8,128)S(1)}, u32[]{:S(2)}, u32[]{:S(2)}) collective-permute-start(f32[10,10,1]{2,1,0:T(8,128)S(1)} %get-tuple-element.78), channel_id=1, source_target_pairs={{0,1},{2,3},{4,5},{6,7},{8,9},{10,11},{12,13},{14,15},{16,17},{18,... | collective-permute-start | bytes 1208 | tf_op jit(solution)/shard_map/ppermute | solution.py:23
  233.1 7.8 %collective-permute-start.57 = (f32[6,1,32]{2,1,0:T(1,128)S(1)}, f32[6,1,32]{2,1,0:T(1,128)S(1)}, u32[]{:S(2)}, u32[]{:S(2)}) collective-permute-start(f32[6,1,32]{2,1,0:T(1,128)S(1)} %get-tuple-element.119), channel_id=1, source_target_pairs={{0,2},{2,4},{4,6},{1,3},{3,5},{5,7},{8,10},{10,12},{12,14},{9,11},... | collective-permute-start | bytes 2312 | tf_op jit(solution)/shard_map/ppermute | solution.py:23
  236.4 16.1 %collective-permute-start.69 = (f32[4,1,16]{2,1,0:T(1,128)S(1)}, f32[4,1,16]{2,1,0:T(1,128)S(1)}, u32[]{:S(2)}, u32[]{:S(2)}) collective-permute-start(f32[4,1,16]{2,1,0:T(1,128)S(1)} %get-tuple-element.165), channel_id=1, source_target_pairs={{0,2},{2,4},{4,6},{1,3},{3,5},{5,7},{8,10},{10,12},{12,14},{9,11},... | collective-permute-start | bytes 776 | tf_op jit(solution)/shard_map/ppermute | solution.py:23
  255.4 7.5 %collective-permute-start.63 = (f32[6,1,32]{2,1,0:T(1,128)S(1)}, f32[6,1,32]{2,1,0:T(1,128)S(1)}, u32[]{:S(2)}, u32[]{:S(2)}) collective-permute-start(f32[6,1,32]{2,1,0:T(1,128)S(1)} %get-tuple-element.117), channel_id=1, source_target_pairs={{0,2},{2,4},{4,6},{1,3},{3,5},{5,7},{8,10},{10,12},{12,14},{9,11},... | collective-permute-start | bytes 2312 | tf_op jit(solution)/shard_map/ppermute | solution.py:23
  261.2 11.9 %collective-permute-start.71 = (f32[4,4,1]{2,1,0:T(4,128)S(1)}, f32[4,4,1]{2,1,0:T(4,128)S(1)}, u32[]{:S(2)}, u32[]{:S(2)}) collective-permute-start(f32[4,4,1]{2,1,0:T(4,128)S(1)} %get-tuple-element.143), channel_id=1, source_target_pairs={{0,1},{2,3},{4,5},{6,7},{8,9},{10,11},{12,13},{14,15},{16,17},{18,... | collective-permute-start | bytes 200 | tf_op jit(solution)/shard_map/ppermute | solution.py:23
  510.0 7.2 %collective-permute-start.136 = (f32[10,10,1]{2,1,0:T(8,128)S(1)}, f32[10,10,1]{2,1,0:T(8,128)S(1)}, u32[]{:S(2)}, u32[]{:S(2)}) collective-permute-start(f32[10,10,1]{2,1,0:T(8,128)S(1)} %get-tuple-element.73), channel_id=1, source_target_pairs={{1,0},{3,2},{5,4},{7,6},{9,8},{11,10},{13,12},{15,14},{17,16},{19,... | collective-permute-start | bytes 1208 | tf_op jit(solution)/shard_map/ppermute | solution.py:25
  533.5 10.2 %collective-permute-start.142 = (f32[18,18,1]{2,1,0:T(8,128)S(1)}, f32[18,18,1]{2,1,0:T(8,128)S(1)}, u32[]{:S(2)}, u32[]{:S(2)}) collective-permute-start(f32[18,18,1]{2,1,0:T(8,128)S(1)} %get-tuple-element.32), channel_id=1, source_target_pairs={{1,0},{3,2},{5,4},{7,6},{9,8},{11,10},{13,12},{15,14},{17,16},{19,... | collective-permute-start | bytes 3896 | tf_op jit(solution)/shard_map/ppermute | solution.py:25
  534.8 10.1 %collective-permute-start.143 = (f32[18,18,1]{2,1,0:T(8,128)S(1)}, f32[18,18,1]{2,1,0:T(8,128)S(1)}, u32[]{:S(2)}, u32[]{:S(2)}) collective-permute-start(f32[18,18,1]{2,1,0:T(8,128)S(1)} %get-tuple-element.33), channel_id=1, source_target_pairs={{0,1},{2,3},{4,5},{6,7},{8,9},{10,11},{12,13},{14,15},{16,17},{18,... | collective-permute-start | bytes 3896 | tf_op jit(solution)/shard_map/ppermute | solution.py:23
  558.2 9.8 %collective-permute-start.148 = (f32[18,18,1]{2,1,0:T(8,128)S(1)}, f32[18,18,1]{2,1,0:T(8,128)S(1)}, u32[]{:S(2)}, u32[]{:S(2)}) collective-permute-start(f32[18,18,1]{2,1,0:T(8,128)S(1)} %get-tuple-element.30), channel_id=1, source_target_pairs={{1,0},{3,2},{5,4},{7,6},{9,8},{11,10},{13,12},{15,14},{17,16},{19,... | collective-permute-start | bytes 3896 | tf_op jit(solution)/shard_map/ppermute | solution.py:25
  559.5 9.7 %collective-permute-start.149 = (f32[18,18,1]{2,1,0:T(8,128)S(1)}, f32[18,18,1]{2,1,0:T(8,128)S(1)}, u32[]{:S(2)}, u32[]{:S(2)}) collective-permute-start(f32[18,18,1]{2,1,0:T(8,128)S(1)} %get-tuple-element.31), channel_id=1, source_target_pairs={{0,1},{2,3},{4,5},{6,7},{8,9},{10,11},{12,13},{14,15},{16,17},{18,... | collective-permute-start | bytes 3896 | tf_op jit(solution)/shard_map/ppermute | solution.py:23
  (105 other events, 548.6 us)
where the time goes:
time: 574 us; the launch traced here: 570 us
  starting transfers between devices  333 us (58%)
  waiting for transfers between devices  173 us (30%)
  local copies, waits for them, and re-layouts  35.1 us (6%)
  other arithmetic  26.8 us (5%)
    ppermute x75, starting transfers between devices, padded_2(): lax.ppermute(tail, axis, [(i, (i + 1) % count) for i in range(ends)])  232 us
    ppermute x75, waiting for transfers between devices, padded_2(): lax.ppermute(head, axis, [((i + 1) % count, i) for i in range(ends)])  149 us
    ppermute x75, starting transfers between devices, padded_2(): lax.ppermute(head, axis, [((i + 1) % count, i) for i in range(ends)])  97 us
    ppermute x75, waiting for transfers between devices, padded_2(): lax.ppermute(tail, axis, [(i, (i + 1) % count) for i in range(ends)])  23.6 us
    reshape x4, local copies, waits for them, and re-layouts, restrict(): x.reshape(s[0] // 2, 2, s[1] // 2, 2, s[2] // 2, 2).mean(axis=(1, 3, 5))  20.6 us
  transfers between devices with their start and end apart: 151, of which 63 were waited for; matrix products, arithmetic and copies ran while one was open for 7% of the time, Pallas kernels for 0%

commit v1 on v0

v1 whole, which is shorter than its diff:
```python
import functools

import jax
import jax.numpy as jnp
from jax import lax
from jax.experimental import pallas as pl
from jax.experimental.pallas import tpu as pltpu
from jax.sharding import PartitionSpec as P

SMOOTH = 2
LEVELS = 3
COARSE_SWEEPS = 8
CAP = 640


OMEGA = 0.8


def padded_2(cells, sides, width):
    for axis, dim in sides:
        count = lax.axis_size(axis)
        ends = count - 1
        head = lax.slice_in_dim(cells, 0, width, axis=dim)
        tail = lax.slice_in_dim(cells, cells.shape[dim] - width, cells.shape[dim], axis=dim)
        cells = jnp.concatenate(
            [
                lax.ppermute(tail, axis, [(i, (i + 1) % count) for i in range(ends)]),
                cells,
                lax.ppermute(head, axis, [((i + 1) % count, i) for i in range(ends)]),
            ],
            axis=dim,
        )
    return cells


def restrict(x):
    s = x.shape
    return x.reshape(s[0] // 2, 2, s[1] // 2, 2, s[2] // 2, 2).mean(axis=(1, 3, 5))


def prolong(e):
    return jnp.repeat(jnp.repeat(jnp.repeat(e, 2, 0), 2, 1), 2, 2)


def neighbours(padded):
    return [
        padded[2:, 1:-1, 1:-1],
        padded[:-2, 1:-1, 1:-1],
        padded[1:-1, 2:, 1:-1],
        padded[1:-1, :-2, 1:-1],
        padded[1:-1, 1:-1, 2:],
        padded[1:-1, 1:-1, :-2],
    ]


def face_pad(x):
    return padded_2(x, (("gx", 0), ("gy", 1), ("gz", 2)), 1)


def coefficients(kappa):
    return [0.5 * (kappa + other) for other in neighbours(face_pad(kappa))]


def apply_op(v, coefs, scale):
    total = jnp.zeros_like(v)
    for coef, other in zip(coefs, neighbours(face_pad(v))):
        total = total + coef * (v - other)
    return scale * total


def cycle(level, rhs, kappa):
    scale = 0.25**level
    coefs = coefficients(kappa)
    diag = scale * (coefs[0] + coefs[1] + coefs[2] + coefs[3] + coefs[4] + coefs[5])
    v = OMEGA * rhs / diag
    for sweep in range((COARSE_SWEEPS if level == LEVELS else SMOOTH) - 1):
        v = v + OMEGA * (rhs - apply_op(v, coefs, scale)) / diag
    if level == LEVELS:
        return v
    resid = rhs - apply_op(v, coefs, scale)
    corr = cycle(level + 1, restrict(resid), restrict(kappa))
    v = v + prolong(corr)
    for sweep in range(SMOOTH):
        v = v + OMEGA * (rhs - apply_op(v, coefs, scale)) / diag
    return v


def general(chi, inducing, record_dest, record_cell, record_value):
    n_gz = lax.axis_size("gz")
    dest = record_dest[0, 0, 0, :, 0]
    cells = record_cell[0, 0, 0]
    values = record_value[0, 0, 0]
    onehot = (dest[:, None] == jnp.arange(n_gz, dtype=jnp.int32)[None, :]).astype(jnp.int32)
    ranks = jnp.sum((jnp.cumsum(onehot, axis=0) - 1) * onehot, axis=1)
    outgoing = jnp.zeros((n_gz, 2, CAP), jnp.float32)
    outgoing = outgoing.at[dest, 0, ranks].set(values)
    outgoing = outgoing.at[dest, 1, ranks].set(cells.astype(jnp.float32))
    incoming = lax.all_to_all(outgoing, "gz", split_axis=0, concat_axis=0, tiled=True)
    in_values = incoming[:, 0].reshape(-1)
    in_cells = incoming[:, 1].reshape(-1).astype(jnp.int32)
    moment_x = face_pad(chi * inducing[0])
    moment_y = face_pad(chi * inducing[1])
    moment_z = face_pad(chi * inducing[2])
    source = -0.5 * (
        moment_x[2:, 1:-1, 1:-1]
        - moment_x[:-2, 1:-1, 1:-1]
        + (moment_y[1:-1, 2:, 1:-1] - moment_y[1:-1, :-2, 1:-1])
        + (moment_z[1:-1, 1:-1, 2:] - moment_z[1:-1, 1:-1, :-2])
    )
    rhs = source.reshape(-1).at[in_cells].add(in_values).reshape(source.shape)
    return cycle(0, rhs, 1.0 + chi)


F32 = jnp.float32
BF16 = jnp.bfloat16
ROWS = 42
PLANES = 36


def iota(shape, dim):
    return lax.broadcasted_iota(jnp.int32, shape, dim)


def roll(x, shift, axis):
    shift = shift % x.shape[axis]
    return pltpu.roll(x, shift, axis) if shift else x


def pick(flag, first, second):
    return jnp.where(jnp.full(first.shape, flag, jnp.int32) == 0, first, second)


def dot(a, b):
    return jnp.dot(a, b, precision=lax.Precision.HIGHEST, preferred_element_type=F32)


def halving(offset, factor):
    shape = (128, 128)
    return jnp.where((iota(shape, 0) >> 1) + offset == iota(shape, 1), factor, 0.0).astype(F32)


def place():
    gx, gy, gz = lax.axis_index("gx"), lax.axis_index("gy"), lax.axis_index("gz")
    return gx >> 1, gx & 1, gy, gz


def prepare_kernel(chi, inducing, dest, cell, value, source, message, coarse, mx, my, mz, kap, sums):
    _, _, _, t = place()
    for ref in (mx, my, mz):
        ref[...] = jnp.zeros_like(ref)
    kap[...] = jnp.zeros_like(kap)
    kappa = 1.0 + chi[...]
    kap[:, 4:20, :] = kappa
    mx[2:18, 4:20, 0:128] = chi[...] * inducing[0]
    my[2:18, 4:20, 0:128] = chi[...] * inducing[1]
    mz[2:18, 4:20, 0:128] = chi[...] * inducing[2]
    lane = iota((24, 128), 1)
    blocks = [jnp.zeros((24, 128), F32), jnp.zeros((24, 128), F32)]
    for i in range(18):
        dx = mx[i + 2] - mx[i]
        dy = roll(my[i + 1], -1, 0) - roll(my[i + 1], 1, 0)
        dz = roll(mz[i + 1], -1, 1) - roll(mz[i + 1], 1, 1)
        row = -0.5 * (dx + dy + dz)
        source[i] = row
        piece = pick(t, roll(row, -125, 1)[:, :128], roll(row, 1, 1)[:, :128])
        piece = jnp.where(lane < 4, piece, 0.0)
        if 1 <= i <= 16:
            k = kap[i - 1]
            k = jnp.where(lane < 4, pick(t, roll(k, -124, 1), k), 0.0)
            piece = piece + roll(k, 4, 1)
            blocks[0] = blocks[0] + roll(piece, 8 * (i - 1), 1)
        else:
            blocks[1] = blocks[1] + roll(piece, 0 if i == 0 else 8, 1)
    message[0:24] = blocks[0]
    message[24:48] = blocks[1]
    message[48:56] = value[...]
    message[56:64] = (dest[...] * 32768 + cell[...]).astype(F32)
    pairs = kappa.reshape(8, 2, 16, 128)
    sums[...] = (pairs[:, 0] + pairs[:, 1]).reshape(128, 128)
    halves = sums[pl.ds(0, 64, stride=2), :] + sums[pl.ds(1, 64, stride=2), :]
    coarse[...] = dot(halves[:32], halving(0, 0.125)) + dot(halves[32:], halving(64, 0.125))


def deposit_kernel(source, chi, mine, other, own, sent, sz, kz, at_row, hi, mid, lo):
    _, c, _, t = place()
    spot = iota((256, 128), 0)
    for j in range(16):
        ref, k = (mine, j) if j < 8 else (other, j - 8)
        value = ref[48 + k : 49 + k, :]
        code = ref[56 + k : 57 + k, :].astype(jnp.int32)
        cells = code & 32767
        column = (((code >> 15) - t) * 128 + (cells & 127)) & 255
        cut = slice(128 * j, 128 * (j + 1))
        at_row[:, cut] = jnp.where(spot == (cells >> 7), 1.0, 0.0).astype(BF16)
        here = spot == column
        for part in (hi, mid, lo):
            short = value.astype(BF16).astype(F32)
            part[:, cut] = jnp.where(here, short, 0.0).astype(BF16)
            value = value - short
    total = jnp.zeros((256, 256), F32)
    for part in (lo, mid, hi):
        total = total + lax.dot_general(
            at_row[...], part[...], (((1,), (1,)), ((), ())), preferred_element_type=F32
        )
    lane = iota((24, 128), 1)
    zeros = jnp.zeros((24, 128), F32)
    kz[...] = jnp.zeros_like(kz)
    kz[:, 4:20, 0:128] = 1.0 + chi[...]
    for i in range(18):
        if 1 <= i <= 16:
            near = roll(other[0:24], -8 * (i - 1), 1)
        else:
            near = roll(other[24:48], 0 if i == 0 else -8, 1)
        wide = jnp.concatenate([jnp.where(lane < 4, near, 0.0), zeros], 1)
        sz[i] = source[i] + pick(t, roll(wide, 127, 1), roll(wide, 253, 1))
        if 1 <= i <= 16:
            wide = jnp.concatenate([jnp.where((lane >= 4) & (lane < 8), near, 0.0), zeros], 1)
            kz[i - 1] = kz[i - 1] + pick(t, roll(wide, 124, 1), roll(wide, 248, 1))
            sz[i, 4:20, :] = sz[i, 4:20, :] + total[16 * (i - 1) : 16 * i]
    keep, give = pl.multiple_of(8 * c, 8), pl.multiple_of(8 - 8 * c, 8)
    for i in range(18):
        own[i] = sz[i, pl.ds(keep, 16), :]
        sent[i] = sz[i, pl.ds(give, 16), :]
    for i in range(16):
        own[18 + i] = kz[i, pl.ds(keep, 16), :]
        sent[18 + i] = kz[i, pl.ds(give, 16), :]


def pair_kernel(own, other, source, kappa, message):
    p, c, _, _ = place()
    source[...] = jnp.zeros_like(source)
    kappa[...] = jnp.zeros_like(kappa)
    source[pl.ds(4 + 16 * c, 18)] = own[0:18]
    low = 4 + 16 * (1 - c)
    source[pl.ds(low, 18)] = source[pl.ds(low, 18)] + other[0:18]
    kappa[pl.ds(5 + 16 * c, 16)] = own[18:34]
    kappa[pl.ds(low + 1, 16)] = other[18:34]
    message[0:4] = source[pl.ds(34 - 30 * p, 4)]
    message[4:8] = kappa[pl.ds(33 - 28 * p, 4)]


def across_kernel(source_in, kappa_in, other, source, kappa, message):
    p, c, _, _ = place()
    source[...] = source_in[...]
    kappa[...] = kappa_in[...]
    at = 36 - 34 * p
    source[pl.ds(at, 4)] = source[pl.ds(at, 4)] + other[0:4]
    kappa[pl.ds(37 - 36 * p, 4)] = other[4:8]
    first = 5 - 4 * p
    low = iota((8, 256), 0) < 4

    def body(i, _):
        s, k = source[first + i], kappa[first + i]
        s = pick(c, roll(s, -3, 0)[:8], roll(s, -9, 0)[:8])
        k = pick(c, roll(k, 0, 0)[:8], roll(k, -4, 0)[:8])
        message[i] = jnp.where(low, s, k)
        return 0

    lax.fori_loop(0, PLANES, body, 0)


def faces(kap, cx, cy, cz, weight, diag, first, count, scale, closed):
    shape = kap.shape[1:]
    last_y = iota(shape, 0) == shape[0] - 1
    first_y = iota(shape, 0) == 0
    last_z = iota(shape, 1) == shape[1] - 1
    first_z = iota(shape, 1) == 0

    def body(i, _):
        r = first + i
        k, up, down = kap[r], kap[r + 1], kap[r - 1]
        yu, yd, zu, zd = roll(k, -1, 0), roll(k, 1, 0), roll(k, -1, 1), roll(k, 1, 1)
        if closed:
            yu, yd = jnp.where(last_y, 0.0, yu), jnp.where(first_y, 0.0, yd)
            zu, zd = jnp.where(last_z, 0.0, zu), jnp.where(first_z, 0.0, zd)
        half = 0.5 * scale
        total = half * (6.0 * k + ((up + down) + (yu + yd) + (zu + zd)))
        fy, fz = half * (k + yu), half * (k + zu)
        if closed:
            fy, fz = jnp.where(last_y, 0.0, fy), jnp.where(last_z, 0.0, fz)
        cx[r] = half * (k + up)
        cy[r] = fy
        cz[r] = fz
        diag[r] = total
        weight[r] = jnp.where(k > 0.0, OMEGA / jnp.where(k > 0.0, total, 1.0), 0.0)
        return 0

    lax.fori_loop(0, count, body, 0)


def around(v, cx, cy, cz, r):
    here = v[r]
    fy, fz = cy[r], cz[r]
    return (
        (cx[r] * v[r + 1] + cx[r - 1] * v[r - 1])
        + (fy * roll(here, -1, 0) + roll(fy * here, 1, 0))
        + (fz * roll(here, -1, 1) + roll(fz * here, 1, 1))
    )


def sweep(v, out, rhs, cx, cy, cz, weight, first, count):
    def body(i, _):
        r = first + i
        out[r] = (1.0 - OMEGA) * v[r] + weight[r] * (rhs[r] + around(v, cx, cy, cz, r))
        return 0

    lax.fori_loop(0, count, body, 0)


def down_kernel(n_gy, source_in, kappa_in, other, rhs, kappa, v2, message, cx, cy, cz, weight, diag, v1, sums):
    p, c, b, _ = place()
    first = 5 - 4 * p
    edge = jnp.where(c == 0, b == 0, b == n_gy - 1).astype(jnp.int32)
    for ref in (kappa, cx, v1, v2, rhs):
        ref[0:5] = jnp.zeros((5, 16, 256), F32)
        ref[37:42] = jnp.zeros((5, 16, 256), F32)
    sub = iota((16, 256), 0)

    def merge(i, _):
        r = first + i
        got = jnp.concatenate([other[i], jnp.zeros((8, 256), F32)], 0)
        got = pick(edge, got, jnp.zeros((16, 256), F32))
        s = jnp.where(sub < 4, got, 0.0)
        k = jnp.where(sub < 4, 0.0, got)
        rhs[r] = source_in[r] + pick(c, roll(s, 1, 0), roll(s, 11, 0))
        kappa[r] = kappa_in[r] + pick(c, roll(k, -4, 0), roll(k, 8, 0))
        return 0

    lax.fori_loop(0, PLANES, merge, 0)
    faces(kappa, cx, cy, cz, weight, diag, first, PLANES, 1.0, False)

    def start(i, _):
        v1[first + i] = weight[first + i] * rhs[first + i]
        return 0

    lax.fori_loop(0, PLANES, start, 0)
    sweep(v1, v2, rhs, cx, cy, cz, weight, first, PLANES)

    def resid(r):
        return rhs[r] + around(v2, cx, cy, cz, r) - diag[r] * v2[r]

    def pair(i, _):
        sums[pl.ds(pl.multiple_of(16 * i, 16), 16), :] = (resid(2 * i + 5) + resid(2 * i + 6))[:, :128]
        return 0

    lax.fori_loop(0, 16, pair, 0)
    halves = sums[pl.ds(0, 128, stride=2), :] + sums[pl.ds(1, 128, stride=2), :]
    packed = dot(halves[:64], halving(0, 0.125)) + dot(halves[64:], halving(64, 0.125))
    low = iota((8, 128), 0) < 4
    for j in range(4):
        even, odd = packed[16 * j : 16 * j + 8], packed[16 * j + 8 : 16 * j + 16]
        tile = jnp.where(low, roll(even, -2, 0), roll(odd, 2, 0))
        for d in range(message.shape[0]):
            message[d, 8 * j : 8 * j + 8, :] = tile


def shift(x, by, axis):
    if axis == 0:
        zero = jnp.zeros((1,) + x.shape[1:], x.dtype)
        return jnp.concatenate([x[1:], zero] if by > 0 else [zero, x[:-1]], 0)
    ends = iota(x.shape, axis) == (x.shape[axis] - 1 if by > 0 else 0)
    return jnp.where(ends, 0.0, roll(x, -by, axis))


class Level:
    def __init__(self, kappa, scale):
        half = 0.5 * scale
        near = [shift(kappa, by, axis) for axis in range(3) for by in (1, -1)]
        self.diag = half * (6.0 * kappa + (near[0] + near[1]) + (near[2] + near[3]) + (near[4] + near[5]))
        self.faces = [half * (kappa + other) for other in near]
        inside = kappa > 0.0
        self.weight = jnp.where(inside, OMEGA / jnp.where(inside, self.diag, 1.0), 0.0)

    def around(self, v):
        near = [shift(v, by, axis) for axis in range(3) for by in (1, -1)]
        terms = [f * o for f, o in zip(self.faces, near)]
        return (terms[0] + terms[1]) + (terms[2] + terms[3]) + (terms[4] + terms[5])

    def sweep(self, v, rhs):
        return (1.0 - OMEGA) * v + self.weight * (rhs + self.around(v))

    def resid(self, v, rhs):
        return rhs + self.around(v) - self.diag * v


def halved(x, scratch):
    nx, ny = x.shape[0] // 2, x.shape[1] // 2
    pairs = x.reshape(nx, 2, 2 * ny, 128)
    scratch[0 : 2 * nx * ny, :] = (pairs[:, 0] + pairs[:, 1]).reshape(2 * nx * ny, 128)
    return halved_yz(scratch, nx, ny)


def halved_yz(scratch, nx, ny):
    halves = scratch[pl.ds(0, nx * ny, stride=2), :] + scratch[pl.ds(1, nx * ny, stride=2), :]
    return dot(halves, halving(0, 0.125)).reshape(nx, ny, 128)


def doubling():
    shape = (128, 128)
    return jnp.where((iota(shape, 1) >> 1) == iota(shape, 0), 1.0, 0.0).astype(F32)


def doubled_yz(e, scratch):
    nx, ny, _ = e.shape
    wide = dot(e.reshape(nx * ny, 128), doubling())
    scratch[pl.ds(0, nx * ny, stride=2), :] = wide
    scratch[pl.ds(1, nx * ny, stride=2), :] = wide
    return scratch[0 : 2 * nx * ny, :].reshape(nx, 2 * ny, 128)


def doubled(e, scratch):
    e = doubled_yz(e, scratch)
    nx, ny, _ = e.shape
    return jnp.broadcast_to(e[:, None], (nx, 2, ny, 128)).reshape(2 * nx, ny, 128)


def coarse_kernel(n_gy, kappas, mine, other, e_out, k1, r1, cx, cy, cz, weight, diag, va, vb, sums):
    p, c, b, t = place()
    n_y = 8 * n_gy
    for ref in (k1, cx, va, vb):
        ref[0] = jnp.zeros((n_y, 128), F32)
        ref[33] = jnp.zeros((n_y, 128), F32)
    left = iota((8, 128), 1) < 64
    top = iota((8, 128), 0) < 4
    for gx in range(4):
        for gy in range(n_gy):
            for x in range(4):
                cut = slice(8 * x, 8 * x + 8)
                near, far = [kappas[(gx * n_gy + gy) * 2 + gz, cut, :] for gz in range(2)]
                spot = slice(8 * gy, 8 * gy + 8)
                k1[1 + 8 * gx + x, spot, :] = jnp.where(left, near, roll(far, 64, 1))
                k1[1 + 8 * gx + 4 + x, spot, :] = jnp.where(left, roll(near, 64, 1), far)
    for pp in range(2):
        for gy in range(n_gy):
            for j in range(4):
                cut = slice(8 * j, 8 * j + 8)
                evens, odds = [], []
                for gz in range(2):
                    a = mine[(pp * n_gy + gy) * 2 + gz, cut, :]
                    o = other[(pp * n_gy + gy) * 2 + gz, cut, :]
                    first, second = pick(c, a, o), pick(c, o, a)
                    evens.append(jnp.where(top, first, roll(second, 4, 0)))
                    odds.append(jnp.where(top, roll(first, 4, 0), second))
                spot = slice(8 * gy, 8 * gy + 8)
                for odd, (near, far) in enumerate((evens, odds)):
                    r1[1 + 16 * pp + 2 * j + odd, spot, :] = jnp.where(left, near, roll(far, 64, 1))
                    r1[1 + 16 * pp + 8 + 2 * j + odd, spot, :] = jnp.where(left, roll(near, 64, 1), far)
    faces(k1, cx, cy, cz, weight, diag, 1, 32, 0.25, True)

    def start(i, _):
        va[1 + i] = weight[1 + i] * r1[1 + i]
        return 0

    lax.fori_loop(0, 32, start, 0)
    sweep(va, vb, r1, cx, cy, cz, weight, 1, 32)

    def resid(r):
        return r1[r] + around(vb, cx, cy, cz, r) - diag[r] * vb[r]

    def pair(i, _):
        sums[pl.ds(pl.multiple_of(n_y * i, 8), n_y), :] = resid(2 * i + 1) + resid(2 * i + 2)
        return 0

    lax.fori_loop(0, 16, pair, 0)
    r2 = halved_yz(sums, 16, n_y // 2)

    def kappa_pair(i, _):
        sums[pl.ds(pl.multiple_of(n_y * i, 8), n_y), :] = k1[2 * i + 1] + k1[2 * i + 2]
        return 0

    lax.fori_loop(0, 16, kappa_pair, 0)
    k2 = halved_yz(sums, 16, n_y // 2)
    middle = Level(k2, 0.0625)
    v2 = middle.weight * r2
    v2 = middle.sweep(v2, r2)
    r3 = halved(middle.resid(v2, r2), sums)
    bottom = Level(halved(k2, sums), 0.015625)
    v3 = bottom.weight * r3
    for _ in range(COARSE_SWEEPS - 1):
        v3 = bottom.sweep(v3, r3)
    v2 = v2 + doubled(v3, sums)
    for _ in range(SMOOTH):
        v2 = middle.sweep(v2, r2)
    e1 = doubled_yz(v2, sums)
    for i in range(16):
        vb[1 + 2 * i] = vb[1 + 2 * i] + e1[i]
        vb[2 + 2 * i] = vb[2 + 2 * i] + e1[i]
    sweep(vb, va, r1, cx, cy, cz, weight, 1, 32)
    sweep(va, vb, r1, cx, cy, cz, weight, 1, 32)
    e_out[...] = vb[...]


def up_kernel(n_gy, e_in, rhs, kappa, v2, out, cx, cy, cz, weight, diag, va, vb, tall):
    p, c, b, t = place()
    first = 5 - 4 * p
    n_y = 8 * n_gy
    for ref in (cx, va, vb):
        ref[0:5] = jnp.zeros((5, 16, 256), F32)
        ref[37:42] = jnp.zeros((5, 16, 256), F32)
    faces(kappa, cx, cy, cz, weight, diag, first, PLANES, 1.0, False)
    tall[:, 0:8, :] = jnp.zeros((18, 8, 128), F32)
    tall[:, 2 * n_y : 2 * n_y + 8, :] = jnp.zeros((18, 8, 128), F32)
    for k in range(18):
        e = e_in[16 * p + k]
        tall[k, pl.ds(4, n_y, stride=2), :] = e
        tall[k, pl.ds(5, n_y, stride=2), :] = e
    window = tall[:, pl.ds(pl.multiple_of(16 * b + 8 * c, 8), 16), :]
    shape = (128, 256)
    z = iota(shape, 1)
    z = jnp.where(z < 192, z, z - 256)
    spread = jnp.where(64 * t + (z >> 1) == iota(shape, 0), 1.0, 0.0).astype(F32)
    e = dot(window.reshape(288, 128), spread).reshape(18, 16, 256)
    for k in range(18):
        for r in (2 * k + 3, 2 * k + 4):
            va[r] = v2[r] + jnp.where(kappa[r] > 0.0, e[k], 0.0)
    sweep(va, vb, rhs, cx, cy, cz, weight, first, PLANES)

    def last(i, _):
        r = 5 + i
        done = (1.0 - OMEGA) * vb[r] + weight[r] * (rhs[r] + around(vb, cx, cy, cz, r))
        out[i] = roll(done[:, :128], -4, 0)[:8]
        return 0

    lax.fori_loop(0, 32, last, 0)


def call(kernel, name, outs, scratch, *args):
    return pl.pallas_call(
        kernel,
        name=name,
        out_shape=[jax.ShapeDtypeStruct(s, F32) for s in outs],
        in_specs=[pl.BlockSpec(memory_space=pltpu.VMEM)] * len(args),
        out_specs=[pl.BlockSpec(memory_space=pltpu.VMEM)] * len(outs),
        scratch_shapes=[pltpu.VMEM(s, d) for s, d in scratch],
        compiler_params=pltpu.CompilerParams(vmem_limit_bytes=48 * 1024 * 1024),
    )(*args)


def paired(chi, inducing, record_dest, record_cell, record_value):
    n_gy = lax.axis_size("gy")
    everyone = ("gx", "gy", "gz")
    window = (ROWS, 16, 256)
    big = [(window, F32)]
    source, message, kappa1 = call(
        prepare_kernel,
        "prepare",
        [(18, 24, 256), (64, 128), (32, 128)],
        [((20, 24, 256), F32)] * 3 + [((16, 24, 128), F32), ((128, 128), F32)],
        chi,
        inducing,
        record_dest.reshape(8, 128),
        record_cell.reshape(8, 128),
        record_value.reshape(8, 128),
    )
    kappas = kappa1[None]
    for axis in ("gz", "gy", "gx"):
        kappas = lax.all_gather(kappas, axis, axis=0, tiled=True)
    got = lax.ppermute(message, "gz", [(0, 1), (1, 0)])
    own, sent = call(
        deposit_kernel,
        "deposit",
        [(34, 16, 256)] * 2,
        [((18, 24, 256), F32), ((16, 24, 256), F32)] + [((256, 2048), BF16)] * 4,
        source,
        chi,
        message,
        got,
    )
    swap = [(0, 1), (1, 0), (2, 3), (3, 2)]
    got = lax.ppermute(sent, "gx", swap)
    source, kappa, message = call(pair_kernel, "pair", [window, window, (8, 16, 256)], [], own, got)
    got = lax.ppermute(message, "gx", [(0, 2), (2, 0), (1, 3), (3, 1)])
    source, kappa, message = call(
        across_kernel, "across", [window, window, (PLANES, 8, 256)], [], source, kappa, got
    )
    turns = []
    for p in range(2):
        for b in range(n_gy):
            low, high = 2 * p * n_gy + b, (2 * p + 1) * n_gy + (b - 1) % n_gy
            turns += [(low, high), (high, low)]
    got = lax.ppermute(message, ("gx", "gy"), turns)
    rhs, kappa, v2, message = call(
        functools.partial(down_kernel, n_gy),
        "down",
        [window, window, window, (4 * n_gy, 32, 128)],
        big * 6 + [((256, 128), F32)],
        source,
        kappa,
        got,
    )
    n = 2 * n_gy
    groups = [[(2 * p + c) * n + g for p in range(2) for g in range(n)] for c in range(2)]
    mine = lax.all_to_all(
        message, everyone, split_axis=0, concat_axis=0, tiled=True, axis_index_groups=groups
    )
    other = lax.ppermute(mine, "gx", swap)
    level1 = (34, 8 * n_gy, 128)
    (e,) = call(
        functools.partial(coarse_kernel, n_gy),
        "coarse",
        [level1],
        [(level1, F32)] * 9 + [((128 * n_gy, 128), F32)],
        kappas,
        mine,
        other,
    )
    (out,) = call(
        functools.partial(up_kernel, n_gy),
        "up",
        [(32, 8, 128)],
        big * 7 + [((18, 16 * n_gy + 8, 128), F32)],
        e,
        rhs,
        kappa,
        v2,
    )
    c = lax.axis_index("gx") & 1
    keep = lax.dynamic_slice_in_dim(out, 16 * c, 16, axis=0)
    give = lax.dynamic_slice_in_dim(out, 16 - 16 * c, 16, axis=0)
    got = lax.ppermute(give, "gx", swap)
    return jnp.where(
        c == 0, jnp.concatenate([keep, got], axis=1), jnp.concatenate([got, keep], axis=1)
    )


def solution(mesh):
    placed = (
        P("gx", "gy", "gz"),
        P(None, "gx", "gy", "gz"),
        P("gx", "gy", "gz", None, None),
        P("gx", "gy", "gz", None),
        P("gx", "gy", "gz", None),
    )
    small = mesh.shape["gx"] == 4 and mesh.shape["gz"] == 2 and mesh.shape["gy"] <= 4
    return jax.shard_map(
        paired if small else general,
        mesh=mesh,
        in_specs=placed,
        out_specs=P("gx", "gy", "gz"),
        check_vma=False,
    )
```

time: 574 us -> 109 us (0.19)
  starting transfers between devices: 333 us -> 8.38 us
  waiting for transfers between devices: 173 us -> 16.4 us
  blocking collectives: 0 us -> 40.1 us
  Pallas kernels: 0 us -> 39.1 us
  local copies, waits for them, and re-layouts: 35.1 us -> 3.97 us
  other arithmetic: 26.8 us -> 0.67 us
    ppermute x150 -> x6, starting transfers between devices: 329 us -> 8.38 us  [the longest x1 2.99 us: paired(): got = lax.ppermute(message, 'gz', [(0, 1), (1, 0)])]
    ppermute x150 -> x6, waiting for transfers between devices: 173 us -> 16.4 us  [the longest x1 7.86 us: paired(): got = lax.ppermute(message, ('gx', 'gy'), turns)]
    pallas_call x0 -> x7, Pallas kernels: none -> 39.1 us  [call(): pl.pallas_call(kernel, name=name, out_shape=[jax.ShapeDtypeStruct(s, F32)...]
    all_gather x0 -> x3, blocking collectives: none -> 24.7 us  [paired(): kappas = lax.all_gather(kappas, axis, axis=0, tiled=True)]
    reshape x10 -> x0, local copies, waits for them, and re-layouts: 21.7 us -> none  [the longest x4 20.6 us: restrict(): x.reshape(s[0] // 2, 2, s[1] // 2, 2, s[2] // 2, 2).mean(axis=(1, 3, 5))]
    all_to_all x0 -> x1, blocking collectives: none -> 15.4 us  [paired(): lax.all_to_all(message, everyone, split_axis=0, concat_axis=0, tiled=True...]
    reduce_sum x7 -> x0, other arithmetic: 9.37 us -> none  [the longest x6 8.66 us: restrict(): x.reshape(s[0] // 2, 2, s[1] // 2, 2, s[2] // 2, 2).mean(axis=(1, 3, 5))]
    scatter-add x1 -> x0, other arithmetic: 7.87 us -> none  [per_device(): rhs = source.reshape(-1).at[in_cells].add(in_values).reshape(source.shape)]
  transfers between devices with their start and end apart: 151 -> 6, of which waited for: 63 -> 5; matrix products, arithmetic and copies ran while one was open for 7% -> 0% of each run, Pallas kernels for 0% -> 0%
where the time goes in v1:
time: 109 us
  blocking collectives  40.1 us (37%)
  Pallas kernels  39.1 us (36%)
  waiting for transfers between devices  16.4 us (15%)
  starting transfers between devices  8.38 us (8%)
  local copies, waits for them, and re-layouts  3.97 us (4%)
    pallas_call x7, Pallas kernels, call(): pl.pallas_call(kernel, name=name, out_shape=[jax.ShapeDtypeStruct(s, F32)...  39.1 us
    all_gather x3, blocking collectives, paired(): kappas = lax.all_gather(kappas, axis, axis=0, tiled=True)  24.7 us
    all_to_all x1, blocking collectives, paired(): lax.all_to_all(message, everyone, split_axis=0, concat_axis=0, tiled=True...  15.4 us
    ppermute x1, waiting for transfers between devices, paired(): got = lax.ppermute(message, ('gx', 'gy'), turns)  7.86 us
    unnamed x10, local copies, waits for them, and re-layouts  3.96 us
    ppermute x1, waiting for transfers between devices, paired(): got = lax.ppermute(message, 'gx', [(0, 2), (2, 0), (1, 3), (3, 1)])  3.8 us
    ppermute x1, starting transfers between devices, paired(): got = lax.ppermute(message, 'gz', [(0, 1), (1, 0)])  2.99 us
    ppermute x1, starting transfers between devices, paired(): got = lax.ppermute(message, ('gx', 'gy'), turns)  2.79 us
  transfers between devices with their start and end apart: 6, of which 5 were waited for; matrix products, arithmetic and copies ran while one was open for 0% of the time, Pallas kernels for 0%

profile of v1, /device:TPU:0, one launch (start us, length us, event | category | flops | bytes accessed | tf_op | source)
XLA Modules:
  0.0 108.7 jit_solution(11444941175129497234)
XLA Ops:
  0.0 0.0 copy-start.2
  0.0 0.7 copy-done.2
  0.7 0.0 copy-start
  0.7 0.9 copy-done
  1.6 0.0 copy-start.1
  1.6 1.0 copy-done.1
  2.6 0.0 copy-start.3
  2.6 0.7 copy-done.3
  3.3 0.0 copy-start.4
  3.3 0.7 copy-done.4
  4.0 3.0 %prepare.1 = (f32[18,24,256]{2,1,0:T(8,128)S(1)}, f32[64,128]{1,0:T(8,128)S(1)}, f32[32,128]{1,0:T(8,128)S(1)}) custom-call(f32[16,16,128]{2,1,0:T(8,128)S(1)} %copy-done, f32[3,16,16,128]{3,2,1,0:T(8,128)S(1)} %copy-done.1, s32[8,128]{1,0:T(8,128)S(1)} %bitcast.4, s32[8,128]{1,0:T(8,128)S(1)} %bitcast.5, f32[8,128]{1,0:T(8,128)S(1)} %bitcast.6), custom_call_target="tpu_custom_call" | custom-call | tf_op jit(solution)/shard_map/prepare/pallas_call | solution.py:528
  7.0 3.0 %collective-permute-start = (f32[64,128]{1,0:T(8,128)S(1)}, f32[64,128]{1,0:T(8,128)S(1)}, u32[]{:S(2)}, u32[]{:S(2)}) collective-permute-start(f32[64,128]{1,0:T(8,128)S(1)} %get-tuple-element.22.mine), channel_id=1, source_target_pairs={{0,1},{1,0},{2,3},{3,2},{4,5},{5,4},{6,7},{7,6},{8,9},{9,8},{10,11... | collective-permute-start | bytes 98312 | tf_op jit(solution)/shard_map/ppermute | solution.py:558
  10.0 1.9 %collective-permute-done.other = f32[64,128]{1,0:T(8,128)S(1)} collective-permute-done((f32[64,128]{1,0:T(8,128)S(1)}, f32[64,128]{1,0:T(8,128)S(1)}, u32[]{:S(2)}, u32[]{:S(2)}) %collective-permute-start) | collective-permute-done | bytes 32800 | tf_op jit(solution)/shard_map/ppermute | solution.py:558
  11.9 2.1 %deposit.1 = (f32[34,16,256]{2,1,0:T(8,128)S(1)}, f32[34,16,256]{2,1,0:T(8,128)S(1)}) custom-call(f32[18,24,256]{2,1,0:T(8,128)S(1)} %get-tuple-element.21.source, f32[16,16,128]{2,1,0:T(8,128)S(1)} %copy-done, f32[64,128]{1,0:T(8,128)S(1)} %get-tuple-element.22.mine, f32[64,128]{1,0:T(8,128)S(1)} %collective-permute-done.other), custom_call_target="tpu_custom_call" | custom-call | tf_op jit(solution)/shard_map/deposit/pallas_call | solution.py:528
  14.0 0.1 collective-permute-start.1
  14.0 1.9 %collective-permute-done.1.other = f32[34,16,256]{2,1,0:T(8,128)S(1)} collective-permute-done((f32[34,16,256]{2,1,0:T(8,128)S(1)}, f32[34,16,256]{2,1,0:T(8,128)S(1)}, u32[]{:S(2)}, u32[]{:S(2)}) %collective-permute-start.1) | collective-permute-done | bytes 557088 | tf_op jit(solution)/shard_map/ppermute | solution.py:570
  16.0 0.2 pair.1
  16.2 2.1 %collective-permute-start.2 = (f32[8,16,256]{2,1,0:T(8,128)S(1)}, f32[8,16,256]{2,1,0:T(8,128)S(1)}, u32[]{:S(2)}, u32[]{:S(2)}) collective-permute-start(f32[8,16,256]{2,1,0:T(8,128)S(1)} %get-tuple-element.27), channel_id=1, source_target_pairs={{0,16},{16,0},{8,24},{24,8},{1,17},{17,1},{9,25},{25,9},{2,18},{18... | collective-permute-start | bytes 393224 | tf_op jit(solution)/shard_map/ppermute | solution.py:572
  18.3 3.8 %collective-permute-done.2.other = f32[8,16,256]{2,1,0:T(8,128)S(1)} collective-permute-done((f32[8,16,256]{2,1,0:T(8,128)S(1)}, f32[8,16,256]{2,1,0:T(8,128)S(1)}, u32[]{:S(2)}, u32[]{:S(2)}) %collective-permute-start.2) | collective-permute-done | bytes 131104 | tf_op jit(solution)/shard_map/ppermute | solution.py:572
  22.1 0.4 across.1
  22.4 2.8 %collective-permute-start.3 = (f32[36,8,256]{2,1,0:T(8,128)S(1)}, f32[36,8,256]{2,1,0:T(8,128)S(1)}, u32[]{:S(2)}, u32[]{:S(2)}) collective-permute-start(f32[36,8,256]{2,1,0:T(8,128)S(1)} %get-tuple-element.30), channel_id=1, source_target_pairs={{0,14},{14,0},{2,8},{8,2},{4,10},{10,4},{6,12},{12,6},{16,30},{30,... | collective-permute-start | bytes 884744 | tf_op jit(solution)/shard_map/ppermute | solution.py:581
  25.2 7.9 %collective-permute-done.3.other = f32[36,8,256]{2,1,0:T(8,128)S(1)} collective-permute-done((f32[36,8,256]{2,1,0:T(8,128)S(1)}, f32[36,8,256]{2,1,0:T(8,128)S(1)}, u32[]{:S(2)}, u32[]{:S(2)}) %collective-permute-start.3) | collective-permute-done | bytes 294944 | tf_op jit(solution)/shard_map/ppermute | solution.py:581
  33.1 8.5 %down.1 = (f32[42,16,256]{2,1,0:T(8,128)S(1)}, f32[42,16,256]{2,1,0:T(8,128)S(1)}, f32[42,16,256]{2,1,0:T(8,128)S(1)}, f32[16,32,128]{2,1,0:T(8,128)S(1)}) custom-call(f32[42,16,256]{2,1,0:T(8,128)S(1)} %get-tuple-element.28.source_in, f32[42,16,256]{2,1,0:T(8,128)S(1)} %get-tuple-element.29.kappa_in, f32[36,8,256]{2,1,0:T(8,128)S(1)} %collective-permute-done.3.other), custom_call_target="tpu_custom_call" | custom-call | tf_op jit(solution)/shard_map/down/pallas_call | solution.py:528
  41.6 15.4 %all_to_all.5.mine = f32[16,32,128]{2,1,0:T(8,128)S(1)} all-to-all(f32[16,32,128]{2,1,0:T(8,128)S(1)} %get-tuple-element.31), channel_id=1, replica_groups={{0,1,2,3,4,5,6,7,16,17,18,19,20,21,22,23},{8,9,10,11,12,13,14,15,24,25,..., dimensions={0} | all-to-all | bytes 524288 | tf_op jit(solution)/shard_map/all_to_all | solution.py:593
  57.0 0.0 collective-permute-start.4
  57.0 4.4 %all-gather = f32[64,128]{1,0:T(8,128)S(1)} all-gather(f32[32,128]{1,0:T(8,128)S(1)} %get-tuple-element.20), channel_id=2, replica_groups=mesh['gx'=4,'gy'=4,'gz'=2] {'gz'}, dimensions={0}, use_global_device_ids=true | all-gather | bytes 49152 | tf_op jit(solution)/shard_map/all_gather | solution.py:557
  61.4 13.5 %all_gather.10 = f32[8,32,128]{2,1,0:T(8,128)S(1)} all-gather(f32[2,32,128]{2,1,0:T(8,128)S(1)} %bitcast.7), channel_id=1, replica_groups=mesh['gx'=4,'gy'=4,'gz'=2] {'gy'}, dimensions={0}, use_global_device_ids=true | all-gather | bytes 163840 | tf_op jit(solution)/shard_map/all_gather | solution.py:557
  74.9 6.8 %all_gather.11.kappas = f32[32,32,128]{2,1,0:T(8,128)S(1)} all-gather(f32[8,32,128]{2,1,0:T(8,128)S(1)} %all_gather.10), channel_id=1, replica_groups=mesh['gx'=4,'gy'=4,'gz'=2] {'gx'}, dimensions={0}, use_global_device_ids=true | all-gather | bytes 655360 | tf_op jit(solution)/shard_map/all_gather | solution.py:557
  81.7 0.0 collective-permute-done.4.other
  81.7 15.5 %coarse.1.e_in = f32[34,32,128]{2,1,0:T(8,128)S(1)} custom-call(f32[32,32,128]{2,1,0:T(8,128)S(1)} %all_gather.11.kappas, f32[16,32,128]{2,1,0:T(8,128)S(1)} %all_to_all.5.mine, f32[16,32,128]{2,1,0:T(8,128)S(1)} %collective-permute-done.4.other), custom_call_target="tpu_custom_call" | custom-call | tf_op jit(solution)/shard_map/coarse/pallas_call | solution.py:528
  97.2 9.4 %up.1 = f32[32,8,128]{2,1,0:T(8,128)S(1)} custom-call(f32[34,32,128]{2,1,0:T(8,128)S(1)} %coarse.1.e_in, f32[42,16,256]{2,1,0:T(8,128)S(1)} %get-tuple-element.32.rhs, f32[42,16,256]{2,1,0:T(8,128)S(1)} %get-tuple-element.33.kappa, f32[42,16,256]{2,1,0:T(8,128)S(1)} %get-tuple-element.34.v2), custom_call_target="tpu_custom_call" | custom-call | tf_op jit(solution)/shard_map/up/pallas_call | solution.py:528
  106.7 0.4 collective-permute-start.5
  107.1 0.9 collective-permute-done.5
  108.0 0.7 maximum_select_fusion
  (1 shorter events, 0.0 us)
Async XLA Ops:
  0.0 0.7 copy-start.2
  0.7 0.9 copy-start
  1.6 1.0 copy-start.1
  2.6 0.7 copy-start.3
  3.3 0.7 copy-start.4
  7.0 4.9 %collective-permute-start = (f32[64,128]{1,0:T(8,128)S(1)}, f32[64,128]{1,0:T(8,128)S(1)}, u32[]{:S(2)}, u32[]{:S(2)}) collective-permute-start(f32[64,128]{1,0:T(8,128)S(1)} %get-tuple-element.22.mine), channel_id=1, source_target_pairs={{0,1},{1,0},{2,3},{3,2},{4,5},{5,4},{6,7},{7,6},{8,9},{9,8},{10,11... | collective-permute-start | bytes 98312 | tf_op jit(solution)/shard_map/ppermute | solution.py:558
  14.0 2.0 %collective-permute-start.1 = (f32[34,16,256]{2,1,0:T(8,128)S(1)}, f32[34,16,256]{2,1,0:T(8,128)S(1)}, u32[]{:S(2)}, u32[]{:S(2)}) collective-permute-start(f32[34,16,256]{2,1,0:T(8,128)S(1)} %get-tuple-element.24), channel_id=1, source_target_pairs={{0,8},{8,0},{16,24},{24,16},{1,9},{9,1},{17,25},{25,17},{2,10},{10... | collective-permute-start | bytes 1671176 | tf_op jit(solution)/shard_map/ppermute | solution.py:570
  16.2 5.9 %collective-permute-start.2 = (f32[8,16,256]{2,1,0:T(8,128)S(1)}, f32[8,16,256]{2,1,0:T(8,128)S(1)}, u32[]{:S(2)}, u32[]{:S(2)}) collective-permute-start(f32[8,16,256]{2,1,0:T(8,128)S(1)} %get-tuple-element.27), channel_id=1, source_target_pairs={{0,16},{16,0},{8,24},{24,8},{1,17},{17,1},{9,25},{25,9},{2,18},{18... | collective-permute-start | bytes 393224 | tf_op jit(solution)/shard_map/ppermute | solution.py:572
  22.4 10.7 %collective-permute-start.3 = (f32[36,8,256]{2,1,0:T(8,128)S(1)}, f32[36,8,256]{2,1,0:T(8,128)S(1)}, u32[]{:S(2)}, u32[]{:S(2)}) collective-permute-start(f32[36,8,256]{2,1,0:T(8,128)S(1)} %get-tuple-element.30), channel_id=1, source_target_pairs={{0,14},{14,0},{2,8},{8,2},{4,10},{10,4},{6,12},{12,6},{16,30},{30,... | collective-permute-start | bytes 884744 | tf_op jit(solution)/shard_map/ppermute | solution.py:581
  57.0 24.7 %collective-permute-start.4 = (f32[16,32,128]{2,1,0:T(8,128)S(1)}, f32[16,32,128]{2,1,0:T(8,128)S(1)}, u32[]{:S(2)}, u32[]{:S(2)}) collective-permute-start(f32[16,32,128]{2,1,0:T(8,128)S(1)} %all_to_all.5.mine), channel_id=1, source_target_pairs={{0,8},{8,0},{16,24},{24,16},{1,9},{9,1},{17,25},{25,17},{2,10},{10... | collective-permute-start | bytes 786440 | tf_op jit(solution)/shard_map/ppermute | solution.py:596
  106.7 1.3 %collective-permute-start.5 = (f32[16,8,128]{2,1,0:T(8,128)S(1)}, f32[16,8,128]{2,1,0:T(8,128)S(1)}, u32[]{:S(2)}, u32[]{:S(2)}) collective-permute-start(f32[16,8,128]{2,1,0:T(8,128)S(1)} %get-tuple-element.36), channel_id=1, source_target_pairs={{0,8},{8,0},{16,24},{24,16},{1,9},{9,1},{17,25},{25,17},{2,10},{10... | collective-permute-start | bytes 196616 | tf_op jit(solution)/shard_map/ppermute | solution.py:620

commit v2 on v1

--- a/solution.py
+++ b/solution.py
@@ -115,6 +115,7 @@
 BF16 = jnp.bfloat16
 ROWS = 42
 PLANES = 36
+SIZE = 4
 
 
 def iota(shape, dim):
@@ -144,44 +145,62 @@
     return gx >> 1, gx & 1, gy, gz
 
 
-def prepare_kernel(chi, inducing, dest, cell, value, source, message, coarse, mx, my, mz, kap, sums):
+def prepare_kernel(*refs):
+    given, (source, spill, message, coarse), (sums, kap), rest = refs[:5], refs[5:9], refs[9:11], refs[11:]
+    chi, inducing, dest, cell, value, done = rest
     _, _, _, t = place()
-    for ref in (mx, my, mz):
-        ref[...] = jnp.zeros_like(ref)
-    kap[...] = jnp.zeros_like(kap)
-    kappa = 1.0 + chi[...]
-    kap[:, 4:20, :] = kappa
-    mx[2:18, 4:20, 0:128] = chi[...] * inducing[0]
-    my[2:18, 4:20, 0:128] = chi[...] * inducing[1]
-    mz[2:18, 4:20, 0:128] = chi[...] * inducing[2]
-    lane = iota((24, 128), 1)
-    blocks = [jnp.zeros((24, 128), F32), jnp.zeros((24, 128), F32)]
+    copies = [pltpu.make_async_copy(a, b, done.at[i]) for i, (a, b) in enumerate(zip(given, rest[:5]))]
+    for copy in copies:
+        copy.start()
+    lane = iota((16, 128), 1)
+    tall_lane = iota((24, 128), 1)
+    zero = jnp.zeros((16, 128), F32)
+    pad = jnp.zeros((8, 128), F32)
+    for copy in copies:
+        copy.wait()
+    kap[...] = 1.0 + chi[...]
+    mx = [zero, zero] + [chi[x] * inducing[0, x] for x in range(16)] + [zero, zero]
+    tiles = [jnp.zeros((24, 128), F32), jnp.zeros((24, 128), F32)]
+    over = zero
     for i in range(18):
         dx = mx[i + 2] - mx[i]
-        dy = roll(my[i + 1], -1, 0) - roll(my[i + 1], 1, 0)
-        dz = roll(mz[i + 1], -1, 1) - roll(mz[i + 1], 1, 1)
-        row = -0.5 * (dx + dy + dz)
+        if 1 <= i <= 16:
+            my, mz = chi[i - 1] * inducing[1, i - 1], chi[i - 1] * inducing[2, i - 1]
+            y24 = jnp.concatenate([my, pad], 0)
+            dy = roll(y24, 3, 0) - roll(y24, 5, 0)
+            ahead, behind = roll(mz, -1, 1), roll(mz, 1, 1)
+            dz = jnp.where(lane == 127, 0.0, ahead) - jnp.where(lane == 0, 0.0, behind)
+            row = -0.5 * (roll(jnp.concatenate([dx + dz, pad], 0), 4, 0) + dy)
+            beyond = pick(t, 0.5 * behind, -0.5 * roll(ahead, 1, 1))
+            beyond = jnp.where(lane == 0, beyond, 0.0)
+            slot = pick(t, roll(beyond, 1, 1), roll(beyond, 2, 1))
+            over = over + roll(slot, 8 * (i - 1), 1)
+            beyond = roll(jnp.concatenate([beyond, pad], 0), 4, 0)
+            k = jnp.concatenate([pick(t, roll(kap[i - 1], -124, 1), kap[i - 1]), pad], 0)
+            k = jnp.where(tall_lane < 4, roll(k, 4, 0), 0.0)
+        else:
+            row = -0.5 * roll(jnp.concatenate([dx, pad], 0), 4, 0)
+            beyond = k = jnp.zeros((24, 128), F32)
         source[i] = row
-        piece = pick(t, roll(row, -125, 1)[:, :128], roll(row, 1, 1)[:, :128])
-        piece = jnp.where(lane < 4, piece, 0.0)
+        low = jnp.where(tall_lane < 3, roll(row, -125, 1), 0.0) + roll(beyond, 3, 1)
+        high = jnp.where((tall_lane > 0) & (tall_lane < 4), roll(row, 1, 1), 0.0) + beyond
+        piece = pick(t, low, high) + roll(k, 4, 1)
         if 1 <= i <= 16:
-            k = kap[i - 1]
-            k = jnp.where(lane < 4, pick(t, roll(k, -124, 1), k), 0.0)
-            piece = piece + roll(k, 4, 1)
-            blocks[0] = blocks[0] + roll(piece, 8 * (i - 1), 1)
+            tiles[0] = tiles[0] + roll(piece, 8 * (i - 1), 1)
         else:
-            blocks[1] = blocks[1] + roll(piece, 0 if i == 0 else 8, 1)
-    message[0:24] = blocks[0]
-    message[24:48] = blocks[1]
+            tiles[1] = tiles[1] + roll(piece, 0 if i == 0 else 8, 1)
+    spill[...] = roll(jnp.concatenate([over, pad], 0), 4, 0)
+    message[0:24] = tiles[0]
+    message[24:48] = tiles[1]
     message[48:56] = value[...]
     message[56:64] = (dest[...] * 32768 + cell[...]).astype(F32)
-    pairs = kappa.reshape(8, 2, 16, 128)
+    pairs = kap[...].reshape(8, 2, 16, 128)
     sums[...] = (pairs[:, 0] + pairs[:, 1]).reshape(128, 128)
     halves = sums[pl.ds(0, 64, stride=2), :] + sums[pl.ds(1, 64, stride=2), :]
     coarse[...] = dot(halves[:32], halving(0, 0.125)) + dot(halves[32:], halving(64, 0.125))
 
 
-def deposit_kernel(source, chi, mine, other, own, sent, sz, kz, at_row, hi, mid, lo):
+def deposit_kernel(source, spill, chi, mine, other, own, sent, all_, at_row, hi, mid, lo):
     _, c, _, t = place()
     spot = iota((256, 128), 0)
     for j in range(16):
@@ -189,7 +208,10 @@
         value = ref[48 + k : 49 + k, :]
         code = ref[56 + k : 57 + k, :].astype(jnp.int32)
         cells = code & 32767
-        column = (((code >> 15) - t) * 128 + (cells & 127)) & 255
+        z = ((code >> 15) - t) * 128 + (cells & 127)
+        far = z - 128 + 131 * t
+        column = jnp.where((far >= 0) & (far < 3), z + 1 + 130 * t, 255)
+        column = jnp.where((z >= 0) & (z < 128), z, column)
         cut = slice(128 * j, 128 * (j + 1))
         at_row[:, cut] = jnp.where(spot == (cells >> 7), 1.0, 0.0).astype(BF16)
         here = spot == column
@@ -203,30 +225,31 @@
             at_row[...], part[...], (((1,), (1,)), ((), ())), preferred_element_type=F32
         )
     lane = iota((24, 128), 1)
-    zeros = jnp.zeros((24, 128), F32)
-    kz[...] = jnp.zeros_like(kz)
-    kz[:, 4:20, 0:128] = 1.0 + chi[...]
+    pad = jnp.zeros((8, 128), F32)
+    slot, goal = 3 * t, 127 - 127 * t
+    halo = other[0:24] + spill[...]
     for i in range(18):
         if 1 <= i <= 16:
+            at = 16 * (i - 1)
+            got = jnp.concatenate([total[at : at + 16, 128:], pad], 0)
+            halo = halo + roll(jnp.where(lane < 4, roll(got, 4, 0), 0.0), 8 * (i - 1), 1)
+            add = roll(jnp.concatenate([total[at : at + 16, :128], pad], 0), 4, 0)
             near = roll(other[0:24], -8 * (i - 1), 1)
         else:
+            add = jnp.zeros((24, 128), F32)
             near = roll(other[24:48], 0 if i == 0 else -8, 1)
-        wide = jnp.concatenate([jnp.where(lane < 4, near, 0.0), zeros], 1)
-        sz[i] = source[i] + pick(t, roll(wide, 127, 1), roll(wide, 253, 1))
-        if 1 <= i <= 16:
-            wide = jnp.concatenate([jnp.where((lane >= 4) & (lane < 8), near, 0.0), zeros], 1)
-            kz[i - 1] = kz[i - 1] + pick(t, roll(wide, 124, 1), roll(wide, 248, 1))
-            sz[i, 4:20, :] = sz[i, 4:20, :] + total[16 * (i - 1) : 16 * i]
+        edge = pick(t, jnp.where(lane == 127, roll(near, 127, 1), 0.0), jnp.where(lane == 0, roll(near, -3, 1), 0.0))
+        all_[i] = source[i] + add + edge
+    for i in range(16):
+        all_[18 + i] = roll(jnp.concatenate([1.0 + chi[i], pad], 0), 4, 0)
+    all_[34] = halo
+    all_[35] = other[24:48]
     keep, give = pl.multiple_of(8 * c, 8), pl.multiple_of(8 - 8 * c, 8)
-    for i in range(18):
-        own[i] = sz[i, pl.ds(keep, 16), :]
-        sent[i] = sz[i, pl.ds(give, 16), :]
-    for i in range(16):
-        own[18 + i] = kz[i, pl.ds(keep, 16), :]
-        sent[18 + i] = kz[i, pl.ds(give, 16), :]
-
-
-def pair_kernel(own, other, source, kappa, message):
+    own[...] = all_[:, pl.ds(keep, 16), :]
+    sent[...] = all_[:, pl.ds(give, 16), :]
+
+
+def pair_kernel(own, other, source, kappa, halo, message):
     p, c, _, _ = place()
     source[...] = jnp.zeros_like(source)
     kappa[...] = jnp.zeros_like(kappa)
@@ -235,41 +258,67 @@
     source[pl.ds(low, 18)] = source[pl.ds(low, 18)] + other[0:18]
     kappa[pl.ds(5 + 16 * c, 16)] = own[18:34]
     kappa[pl.ds(low + 1, 16)] = other[18:34]
+    lane = iota((16, 128), 1)
+    tiles = [jnp.zeros((16, 128), F32)] * 3
+    for side in range(2):
+        cells = roll(pick(c ^ side, own[34], other[34]), 40, 1)
+        ends = pick(c ^ side, own[35], other[35])
+        before, after = jnp.where(lane < 4, ends, 0.0), jnp.where((lane >= 8) & (lane < 12), ends, 0.0)
+        tiles[side] = tiles[side] + jnp.where(lane >= 40, cells, 0.0) + roll(before, 32, 1)
+        tiles[side + 1] = tiles[side + 1] + jnp.where(lane < 40, cells, 0.0) + roll(after, 32, 1)
+    for i in range(3):
+        halo[i] = tiles[i]
     message[0:4] = source[pl.ds(34 - 30 * p, 4)]
     message[4:8] = kappa[pl.ds(33 - 28 * p, 4)]
-
-
-def across_kernel(source_in, kappa_in, other, source, kappa, message):
+    message[8] = jnp.where(lane < 40, pick(p, roll(tiles[2], -8, 1), roll(tiles[0], -32, 1)), 0.0)
+
+
+def across_kernel(source_in, kappa_in, halo_in, other, source, kappa, halo, message):
     p, c, _, _ = place()
     source[...] = source_in[...]
     kappa[...] = kappa_in[...]
     at = 36 - 34 * p
     source[pl.ds(at, 4)] = source[pl.ds(at, 4)] + other[0:4]
     kappa[pl.ds(37 - 36 * p, 4)] = other[4:8]
+    zero = jnp.zeros((16, 128), F32)
+    halo[0] = halo_in[0] + pick(p, zero, roll(other[8], 8, 1))
+    halo[1] = halo_in[1]
+    halo[2] = halo_in[2] + pick(p, roll(other[8], 32, 1), zero)
     first = 5 - 4 * p
-    low = iota((8, 256), 0) < 4
-
-    def body(i, _):
-        s, k = source[first + i], kappa[first + i]
-        s = pick(c, roll(s, -3, 0)[:8], roll(s, -9, 0)[:8])
-        k = pick(c, roll(k, 0, 0)[:8], roll(k, -4, 0)[:8])
-        message[i] = jnp.where(low, s, k)
+
+    def cut(s, k):
+        s = pick(c, roll(s, -3, 1)[:, :8], roll(s, -9, 1)[:, :8])
+        k = pick(c, k[:, :8], roll(k, -4, 1)[:, :8])
+        return jnp.where(iota(s.shape, 1) < 4, s, k)
+
+    def body(i):
+        message[pl.ds(i, SIZE)] = cut(source[pl.ds(first + i, SIZE)], kappa[pl.ds(first + i, SIZE)])
+
+    chunked(PLANES, body, SIZE)
+    message[PLANES:] = cut(halo[...], halo[...])
+
+
+def chunked(count, body, size=4):
+    def step(i, _):
+        body(i * size)
         return 0
 
-    lax.fori_loop(0, PLANES, body, 0)
+    lax.fori_loop(0, count // size, step, 0)
 
 
 def faces(kap, cx, cy, cz, weight, diag, first, count, scale, closed):
-    shape = kap.shape[1:]
-    last_y = iota(shape, 0) == shape[0] - 1
-    first_y = iota(shape, 0) == 0
-    last_z = iota(shape, 1) == shape[1] - 1
-    first_z = iota(shape, 1) == 0
-
-    def body(i, _):
+    n = SIZE
+    shape = (n,) + kap.shape[1:]
+    last_y = iota(shape, 1) == shape[1] - 1
+    first_y = iota(shape, 1) == 0
+    last_z = iota(shape, 2) == shape[2] - 1
+    first_z = iota(shape, 2) == 0
+
+    def body(i):
         r = first + i
-        k, up, down = kap[r], kap[r + 1], kap[r - 1]
-        yu, yd, zu, zd = roll(k, -1, 0), roll(k, 1, 0), roll(k, -1, 1), roll(k, 1, 1)
+        near = kap[pl.ds(r - 1, n + 2)]
+        k, up, down = near[1 : n + 1], near[2:], near[:n]
+        yu, yd, zu, zd = roll(k, -1, 1), roll(k, 1, 1), roll(k, -1, 2), roll(k, 1, 2)
         if closed:
             yu, yd = jnp.where(last_y, 0.0, yu), jnp.where(first_y, 0.0, yd)
             zu, zd = jnp.where(last_z, 0.0, zu), jnp.where(first_z, 0.0, zd)
@@ -278,72 +327,97 @@
         fy, fz = half * (k + yu), half * (k + zu)
         if closed:
             fy, fz = jnp.where(last_y, 0.0, fy), jnp.where(last_z, 0.0, fz)
-        cx[r] = half * (k + up)
-        cy[r] = fy
-        cz[r] = fz
-        diag[r] = total
-        weight[r] = jnp.where(k > 0.0, OMEGA / jnp.where(k > 0.0, total, 1.0), 0.0)
-        return 0
-
-    lax.fori_loop(0, count, body, 0)
-
-
-def around(v, cx, cy, cz, r):
-    here = v[r]
-    fy, fz = cy[r], cz[r]
-    return (
-        (cx[r] * v[r + 1] + cx[r - 1] * v[r - 1])
-        + (fy * roll(here, -1, 0) + roll(fy * here, 1, 0))
-        + (fz * roll(here, -1, 1) + roll(fz * here, 1, 1))
+        cx[pl.ds(r, n)] = half * (k + up)
+        cy[pl.ds(r, n)] = fy
+        cz[pl.ds(r, n)] = fz
+        diag[pl.ds(r, n)] = total
+        weight[pl.ds(r, n)] = jnp.where(k > 0.0, OMEGA / jnp.where(k > 0.0, total, 1.0), 0.0)
+
+    chunked(count, body, n)
+
+
+def around(v, cx, cy, cz, r, n):
+    near, fx = v[pl.ds(r - 1, n + 2)], cx[pl.ds(r - 1, n + 1)]
+    here, fy, fz = near[1 : n + 1], cy[pl.ds(r, n)], cz[pl.ds(r, n)]
+    return here, (
+        (fx[1:] * near[2:] + fx[:n] * near[:n])
+        + (fy * roll(here, -1, 1) + roll(fy * here, 1, 1))
+        + (fz * roll(here, -1, 2) + roll(fz * here, 1, 2))
     )
 
 
 def sweep(v, out, rhs, cx, cy, cz, weight, first, count):
-    def body(i, _):
+    def body(i):
         r = first + i
-        out[r] = (1.0 - OMEGA) * v[r] + weight[r] * (rhs[r] + around(v, cx, cy, cz, r))
-        return 0
-
-    lax.fori_loop(0, count, body, 0)
-
-
-def down_kernel(n_gy, source_in, kappa_in, other, rhs, kappa, v2, message, cx, cy, cz, weight, diag, v1, sums):
-    p, c, b, _ = place()
+        here, total = around(v, cx, cy, cz, r, SIZE)
+        out[pl.ds(r, SIZE)] = (1.0 - OMEGA) * here + weight[pl.ds(r, SIZE)] * (rhs[pl.ds(r, SIZE)] + total)
+
+    chunked(count, body, SIZE)
+
+
+def resid(v, rhs, cx, cy, cz, diag, r):
+    here, total = around(v, cx, cy, cz, r, SIZE)
+    return rhs[pl.ds(r, SIZE)] + total - diag[pl.ds(r, SIZE)] * here
+
+
+def pair_sums(x):
+    x = x.reshape((x.shape[0] // 2, 2) + x.shape[1:])
+    return x[:, 0] + x[:, 1]
+
+
+def down_kernel(
+    n_gy, source_in, kappa_in, halo_in, other, kappa1, rhs, kappa, v2, message,
+    cx, cy, cz, weight, diag, v1, sums, halo,
+):
+    p, c, b, t = place()
     first = 5 - 4 * p
     edge = jnp.where(c == 0, b == 0, b == n_gy - 1).astype(jnp.int32)
     for ref in (kappa, cx, v1, v2, rhs):
         ref[0:5] = jnp.zeros((5, 16, 256), F32)
         ref[37:42] = jnp.zeros((5, 16, 256), F32)
-    sub = iota((16, 256), 0)
-
-    def merge(i, _):
+
+    def merge(got):
+        n = got.shape[0]
+        got = jnp.concatenate([got, jnp.zeros((n, 8, 128), F32)], 1)
+        got = pick(edge, got, jnp.zeros_like(got))
+        top = iota(got.shape, 1) < 4
+        s, k = jnp.where(top, got, 0.0), jnp.where(top, 0.0, got)
+        return pick(c, roll(s, 1, 1), roll(s, 11, 1)), pick(c, roll(k, -4, 1), roll(k, 8, 1))
+
+    s, k = merge(other[PLANES:])
+    halo[...] = halo_in[...] + jnp.where((iota(s.shape, 2) & 7) < 4, s, k)
+    lane = iota((16, 128), 1)
+    s_lanes = pick(t, (lane < 3).astype(jnp.int32), (lane >= 125).astype(jnp.int32)) > 0
+    k_lanes = pick(t, (lane < 4).astype(jnp.int32), (lane >= 124).astype(jnp.int32)) > 0
+
+    def enter(i):
         r = first + i
-        got = jnp.concatenate([other[i], jnp.zeros((8, 256), F32)], 0)
-        got = pick(edge, got, jnp.zeros((16, 256), F32))
-        s = jnp.where(sub < 4, got, 0.0)
-        k = jnp.where(sub < 4, 0.0, got)
-        rhs[r] = source_in[r] + pick(c, roll(s, 1, 0), roll(s, 11, 0))
-        kappa[r] = kappa_in[r] + pick(c, roll(k, -4, 0), roll(k, 8, 0))
-        return 0
-
-    lax.fori_loop(0, PLANES, merge, 0)
+        rows = pl.ds(r, SIZE)
+        s, k = merge(other[pl.ds(i, SIZE)])
+        far_s, far_k = [], []
+        for j in range(SIZE):
+            tile = halo[(r + j) >> 4]
+            by = 8 * ((r + j) & 15)
+            far_s.append(jnp.where(s_lanes, pltpu.roll(tile, (127 - by - 2 * t) & 127, 1), 0.0)[None])
+            far_k.append(jnp.where(k_lanes, pltpu.roll(tile, (124 - by - 4 * t) & 127, 1), 0.0)[None])
+        rhs[rows] = jnp.concatenate([source_in[rows] + s, jnp.concatenate(far_s, 0)], 2)
+        kappa[rows] = jnp.concatenate([kappa_in[rows] + k, jnp.concatenate(far_k, 0)], 2)
+
+    chunked(PLANES, enter, SIZE)
     faces(kappa, cx, cy, cz, weight, diag, first, PLANES, 1.0, False)
 
-    def start(i, _):
-        v1[first + i] = weight[first + i] * rhs[first + i]
-        return 0
-
-    lax.fori_loop(0, PLANES, start, 0)
+    def start(i):
+        r = pl.ds(first + i, SIZE)
+        v1[r] = weight[r] * rhs[r]
+
+    chunked(PLANES, start, SIZE)
     sweep(v1, v2, rhs, cx, cy, cz, weight, first, PLANES)
 
-    def resid(r):
-        return rhs[r] + around(v2, cx, cy, cz, r) - diag[r] * v2[r]
-
-    def pair(i, _):
-        sums[pl.ds(pl.multiple_of(16 * i, 16), 16), :] = (resid(2 * i + 5) + resid(2 * i + 6))[:, :128]
-        return 0
-
-    lax.fori_loop(0, 16, pair, 0)
+    def pair(i):
+        two = pair_sums(resid(v2, rhs, cx, cy, cz, diag, 5 + i))
+        sums[pl.ds(pl.multiple_of(8 * i, 16), 8 * SIZE), :] = two[:, :, :128].reshape(8 * SIZE, 128)
+
+    chunked(32, pair, SIZE)
     halves = sums[pl.ds(0, 128, stride=2), :] + sums[pl.ds(1, 128, stride=2), :]
     packed = dot(halves[:64], halving(0, 0.125)) + dot(halves[64:], halving(64, 0.125))
     low = iota((8, 128), 0) < 4
@@ -352,28 +426,34 @@
         tile = jnp.where(low, roll(even, -2, 0), roll(odd, 2, 0))
         for d in range(message.shape[0]):
             message[d, 8 * j : 8 * j + 8, :] = tile
+            message[d, 32 + 8 * j : 40 + 8 * j, :] = kappa1[8 * j : 8 * j + 8, :]
 
 
 def shift(x, by, axis):
     if axis == 0:
         zero = jnp.zeros((1,) + x.shape[1:], x.dtype)
         return jnp.concatenate([x[1:], zero] if by > 0 else [zero, x[:-1]], 0)
-    ends = iota(x.shape, axis) == (x.shape[axis] - 1 if by > 0 else 0)
-    return jnp.where(ends, 0.0, roll(x, -by, axis))
+    return roll(x, -by, axis)
+
+
+SIDES = [(axis, by) for axis in range(3) for by in (1, -1)]
 
 
 class Level:
     def __init__(self, kappa, scale):
         half = 0.5 * scale
-        near = [shift(kappa, by, axis) for axis in range(3) for by in (1, -1)]
+        at = iota(kappa.shape, 1)
+        ends = {1: at == kappa.shape[1] - 1, -1: at == 0}
+        near = [shift(kappa, by, axis) for axis, by in SIDES]
+        near[2:4] = [jnp.where(ends[by], 0.0, k) for by, k in zip((1, -1), near[2:4])]
         self.diag = half * (6.0 * kappa + (near[0] + near[1]) + (near[2] + near[3]) + (near[4] + near[5]))
         self.faces = [half * (kappa + other) for other in near]
+        self.faces[2:4] = [jnp.where(ends[by], 0.0, f) for by, f in zip((1, -1), self.faces[2:4])]
         inside = kappa > 0.0
         self.weight = jnp.where(inside, OMEGA / jnp.where(inside, self.diag, 1.0), 0.0)
 
     def around(self, v):
-        near = [shift(v, by, axis) for axis in range(3) for by in (1, -1)]
-        terms = [f * o for f, o in zip(self.faces, near)]
+        terms = [f * shift(v, by, axis) for f, (axis, by) in zip(self.faces, SIDES)]
         return (terms[0] + terms[1]) + (terms[2] + terms[3]) + (terms[4] + terms[5])
 
     def sweep(self, v, rhs):
@@ -414,7 +494,7 @@
     return jnp.broadcast_to(e[:, None], (nx, 2, ny, 128)).reshape(2 * nx, ny, 128)
 
 
-def coarse_kernel(n_gy, kappas, mine, other, e_out, k1, r1, cx, cy, cz, weight, diag, va, vb, sums):
+def coarse_kernel(n_gy, mine, other, e_out, k1, r1, cx, cy, cz, weight, diag, va, vb, sums):
     p, c, b, t = place()
     n_y = 8 * n_gy
     for ref in (k1, cx, va, vb):
@@ -425,8 +505,9 @@
     for gx in range(4):
         for gy in range(n_gy):
             for x in range(4):
-                cut = slice(8 * x, 8 * x + 8)
-                near, far = [kappas[(gx * n_gy + gy) * 2 + gz, cut, :] for gz in range(2)]
+                cut = slice(32 + 8 * x, 40 + 8 * x)
+                both = [[ref[((gx >> 1) * n_gy + gy) * 2 + gz, cut, :] for ref in (mine, other)] for gz in range(2)]
+                near, far = [pick(c ^ (gx & 1), a, o) for a, o in both]
                 spot = slice(8 * gy, 8 * gy + 8)
                 k1[1 + 8 * gx + x, spot, :] = jnp.where(left, near, roll(far, 64, 1))
                 k1[1 + 8 * gx + 4 + x, spot, :] = jnp.where(left, roll(near, 64, 1), far)
@@ -447,28 +528,26 @@
                     r1[1 + 16 * pp + 8 + 2 * j + odd, spot, :] = jnp.where(left, roll(near, 64, 1), far)
     faces(k1, cx, cy, cz, weight, diag, 1, 32, 0.25, True)
 
-    def start(i, _):
-        va[1 + i] = weight[1 + i] * r1[1 + i]
-        return 0
-
-    lax.fori_loop(0, 32, start, 0)
+    def start(i):
+        r = pl.ds(1 + i, SIZE)
+        va[r] = weight[r] * r1[r]
+
+    chunked(32, start, SIZE)
     sweep(va, vb, r1, cx, cy, cz, weight, 1, 32)
-
-    def resid(r):
-        return r1[r] + around(vb, cx, cy, cz, r) - diag[r] * vb[r]
-
-    def pair(i, _):
-        sums[pl.ds(pl.multiple_of(n_y * i, 8), n_y), :] = resid(2 * i + 1) + resid(2 * i + 2)
-        return 0
-
-    lax.fori_loop(0, 16, pair, 0)
+    step = n_y * SIZE // 2
+
+    def pair(i):
+        two = pair_sums(resid(vb, r1, cx, cy, cz, diag, 1 + i))
+        sums[pl.ds(pl.multiple_of(n_y // 2 * i, 8), step), :] = two.reshape(step, 128)
+
+    chunked(32, pair, SIZE)
     r2 = halved_yz(sums, 16, n_y // 2)
 
-    def kappa_pair(i, _):
-        sums[pl.ds(pl.multiple_of(n_y * i, 8), n_y), :] = k1[2 * i + 1] + k1[2 * i + 2]
-        return 0
-
-    lax.fori_loop(0, 16, kappa_pair, 0)
+    def kappa_pair(i):
+        two = pair_sums(k1[pl.ds(1 + i, SIZE)])
+        sums[pl.ds(pl.multiple_of(n_y // 2 * i, 8), step), :] = two.reshape(step, 128)
+
+    chunked(32, kappa_pair, SIZE)
     k2 = halved_yz(sums, 16, n_y // 2)
     middle = Level(k2, 0.0625)
     v2 = middle.weight * r2
@@ -515,13 +594,13 @@
             va[r] = v2[r] + jnp.where(kappa[r] > 0.0, e[k], 0.0)
     sweep(va, vb, rhs, cx, cy, cz, weight, first, PLANES)
 
-    def last(i, _):
-        r = 5 + i
-        done = (1.0 - OMEGA) * vb[r] + weight[r] * (rhs[r] + around(vb, cx, cy, cz, r))
-        out[i] = roll(done[:, :128], -4, 0)[:8]
-        return 0
-
-    lax.fori_loop(0, 32, last, 0)
+    def last(i):
+        r = pl.ds(5 + i, SIZE)
+        here, total = around(vb, cx, cy, cz, 5 + i, SIZE)
+        done = (1.0 - OMEGA) * here + weight[r] * (rhs[r] + total)
+        out[pl.ds(i, SIZE)] = roll(done[:, :, :128], -4, 1)[:, :8]
+
+    chunked(32, last, SIZE)
 
 
 def call(kernel, name, outs, scratch, *args):
@@ -529,9 +608,11 @@
         kernel,
         name=name,
         out_shape=[jax.ShapeDtypeStruct(s, F32) for s in outs],
-        in_specs=[pl.BlockSpec(memory_space=pltpu.VMEM)] * len(args),
+        in_specs=[pl.BlockSpec(memory_space=pltpu.HBM if name == "prepare" else pltpu.VMEM)] * len(args),
         out_specs=[pl.BlockSpec(memory_space=pltpu.VMEM)] * len(outs),
-        scratch_shapes=[pltpu.VMEM(s, d) for s, d in scratch],
+        scratch_shapes=[
+            pltpu.SemaphoreType.DMA((s,)) if isinstance(s, int) else pltpu.VMEM(*s) for s in scratch
+        ],
         compiler_params=pltpu.CompilerParams(vmem_limit_bytes=48 * 1024 * 1024),
     )(*args)
 
@@ -541,52 +622,53 @@
     everyone = ("gx", "gy", "gz")
     window = (ROWS, 16, 256)
     big = [(window, F32)]
-    source, message, kappa1 = call(
+    source, spill, message, kappa1 = call(
         prepare_kernel,
         "prepare",
-        [(18, 24, 256), (64, 128), (32, 128)],
-        [((20, 24, 256), F32)] * 3 + [((16, 24, 128), F32), ((128, 128), F32)],
+        [(18, 24, 128), (24, 128), (64, 128), (32, 128)],
+        [((128, 128), F32), ((16, 16, 128), F32), ((16, 16, 128), F32), ((3, 16, 16, 128), F32)]
+        + [((8, 128), jnp.int32)] * 2
+        + [((8, 128), F32), 5],
         chi,
         inducing,
         record_dest.reshape(8, 128),
         record_cell.reshape(8, 128),
         record_value.reshape(8, 128),
     )
-    kappas = kappa1[None]
-    for axis in ("gz", "gy", "gx"):
-        kappas = lax.all_gather(kappas, axis, axis=0, tiled=True)
     got = lax.ppermute(message, "gz", [(0, 1), (1, 0)])
     own, sent = call(
         deposit_kernel,
         "deposit",
-        [(34, 16, 256)] * 2,
-        [((18, 24, 256), F32), ((16, 24, 256), F32)] + [((256, 2048), BF16)] * 4,
+        [(36, 16, 128)] * 2,
+        [((36, 24, 128), F32)] + [((256, 2048), BF16)] * 4,
         source,
+        spill,
         chi,
         message,
         got,
     )
     swap = [(0, 1), (1, 0), (2, 3), (3, 2)]
     got = lax.ppermute(sent, "gx", swap)
-    source, kappa, message = call(pair_kernel, "pair", [window, window, (8, 16, 256)], [], own, got)
+    held = [(ROWS, 16, 128), (ROWS, 16, 128), (3, 16, 128)]
+    *fields, message = call(pair_kernel, "pair", held + [(9, 16, 128)], [], own, got)
     got = lax.ppermute(message, "gx", [(0, 2), (2, 0), (1, 3), (3, 1)])
-    source, kappa, message = call(
-        across_kernel, "across", [window, window, (PLANES, 8, 256)], [], source, kappa, got
-    )
+    *fields, message = call(across_kernel, "across", held + [(PLANES + 3, 8, 128)], [], *fields, got)
     turns = []
     for p in range(2):
-        for b in range(n_gy):
-            low, high = 2 * p * n_gy + b, (2 * p + 1) * n_gy + (b - 1) % n_gy
+        for b in range(n_gy - 1):
+            low, high = (2 * p + 1) * n_gy + b, 2 * p * n_gy + b + 1
             turns += [(low, high), (high, low)]
+    for low, high in ((0, 2 * n_gy), (2 * n_gy - 1, 4 * n_gy - 1)):
+        turns += [(low, high), (high, low)]
     got = lax.ppermute(message, ("gx", "gy"), turns)
     rhs, kappa, v2, message = call(
         functools.partial(down_kernel, n_gy),
         "down",
-        [window, window, window, (4 * n_gy, 32, 128)],
-        big * 6 + [((256, 128), F32)],
-        source,
-        kappa,
+        [window, window, window, (4 * n_gy, 64, 128)],
+        big * 6 + [((256, 128), F32), ((3, 16, 128), F32)],
+        *fields,
         got,
+        kappa1,
     )
     n = 2 * n_gy
     groups = [[(2 * p + c) * n + g for p in range(2) for g in range(n)] for c in range(2)]
@@ -600,7 +682,6 @@
         "coarse",
         [level1],
         [(level1, F32)] * 9 + [((128 * n_gy, 128), F32)],
-        kappas,
         mine,
         other,
     )

time: 109 us -> 66.3 us (0.61)
  blocking collectives: 40.1 us -> 20.8 us
  Pallas kernels: 39.1 us -> 20.8 us
  waiting for transfers between devices: 16.4 us -> 12.5 us
  starting transfers between devices: 8.38 us -> 7.2 us
    all_gather x3 -> x0, blocking collectives: 24.7 us -> none  [paired(): kappas = lax.all_gather(kappas, axis, axis=0, tiled=True)]
    pallas_call x7, Pallas kernels: 39.1 us -> 20.8 us  [call(): pl.pallas_call(kernel, name=name, out_shape=[jax.ShapeDtypeStruct(s, F32)...]
    all_to_all x1, blocking collectives: 15.4 us -> 20.8 us  [paired(): lax.all_to_all(message, everyone, split_axis=0, concat_axis=0, tiled=True...]
    ppermute x1, waiting for transfers between devices: 7.86 us -> 3.49 us  [paired(): got = lax.ppermute(message, ('gx', 'gy'), turns)]
    ppermute x1, waiting for transfers between devices: 0.01 us -> 1.91 us  [paired(): other = lax.ppermute(mine, 'gx', swap)]
    ppermute x1, waiting for transfers between devices: 3.8 us -> 2.57 us  [paired(): got = lax.ppermute(message, 'gx', [(0, 2), (2, 0), (1, 3), (3, 1)])]
  transfers between devices with their start and end apart: 6 -> 6, of which waited for: 5 -> 6; matrix products, arithmetic and copies ran while one was open for 0% -> 0% of each run, Pallas kernels for 0% -> 0%
where the time goes in v2:
time: 66.3 us; the launch traced here: 66 us
  Pallas kernels  20.8 us (31%)
  blocking collectives  20.8 us (31%)
  waiting for transfers between devices  12.5 us (19%)
  starting transfers between devices  7.2 us (11%)
  local copies, waits for them, and re-layouts  3.98 us (6%)
  other arithmetic  0.67 us (1%)
    pallas_call x7, Pallas kernels, call(): pl.pallas_call(kernel, name=name, out_shape=[jax.ShapeDtypeStruct(s, F32)...  20.8 us
    all_to_all x1, blocking collectives, paired(): lax.all_to_all(message, everyone, split_axis=0, concat_axis=0, tiled=True...  20.8 us
    unnamed x10, local copies, waits for them, and re-layouts  3.96 us
    ppermute x1, waiting for transfers between devices, paired(): got = lax.ppermute(message, ('gx', 'gy'), turns)  3.49 us
    ppermute x1, starting transfers between devices, paired(): got = lax.ppermute(message, 'gz', [(0, 1), (1, 0)])  3 us
    ppermute x1, waiting for transfers between devices, paired(): got = lax.ppermute(message, 'gx', [(0, 2), (2, 0), (1, 3), (3, 1)])  2.57 us
    ppermute x1, starting transfers between devices, paired(): got = lax.ppermute(message, 'gx', [(0, 2), (2, 0), (1, 3), (3, 1)])  2.07 us
    ppermute x1, waiting for transfers between devices, paired(): other = lax.ppermute(mine, 'gx', swap)  1.91 us
  transfers between devices with their start and end apart: 6, of which 6 were waited for; matrix products, arithmetic and copies ran while one was open for 0% of the time, Pallas kernels for 0%

profile of v2, /device:TPU:0, one launch (start us, length us, event | category | flops | bytes accessed | tf_op | source)
XLA Modules:
  0.0 66.0 jit_solution(4834194327301514652)
XLA Ops:
  0.0 0.0 copy-start.2
  0.0 0.7 %copy-done.2 = s32[1,1,1,1024,1]{3,4,2,1,0:T(1,128)S(1)} copy-done((s32[1,1,1,1024,1]{3,4,2,1,0:T(1,128)S(1)}, s32[1,1,1,1024,1]{3,4,2,1,0:T(1,128)}, u32[]{:S(2)}) %copy-start.2) | copy-done | bytes 4120
  0.7 0.0 copy-start
  0.7 0.9 %copy-done = f32[16,16,128]{2,1,0:T(8,128)S(1)} copy-done((f32[16,16,128]{2,1,0:T(8,128)S(1)}, f32[16,16,128]{2,1,0:T(8,128)}, u32[]{:S(2)}) %copy-start) | copy-done | bytes 131096
  1.6 0.0 copy-start.1
  1.6 1.0 %copy-done.1 = f32[3,16,16,128]{3,2,1,0:T(8,128)S(1)} copy-done((f32[3,16,16,128]{3,2,1,0:T(8,128)S(1)}, f32[3,16,16,128]{3,2,1,0:T(8,128)}, u32[]{:S(2)}) %copy-start.1) | copy-done | bytes 393240
  2.6 0.0 copy-start.3
  2.6 0.7 %copy-done.3 = s32[1,1,1,1024]{3,2,1,0:T(1,128)S(1)} copy-done((s32[1,1,1,1024]{3,2,1,0:T(1,128)S(1)}, s32[1,1,1,1024]{3,2,1,0:T(1,128)}, u32[]{:S(2)}) %copy-start.3) | copy-done | bytes 4120
  3.3 0.0 copy-start.4
  3.3 0.7 %copy-done.4 = f32[1,1,1,1024]{3,2,1,0:T(1,128)S(1)} copy-done((f32[1,1,1,1024]{3,2,1,0:T(1,128)S(1)}, f32[1,1,1,1024]{3,2,1,0:T(1,128)}, u32[]{:S(2)}) %copy-start.4) | copy-done | bytes 4120
  4.0 3.4 %prepare.1 = (f32[18,24,128]{2,1,0:T(8,128)S(1)}, f32[24,128]{1,0:T(8,128)S(1)}, f32[64,128]{1,0:T(8,128)S(1)}, f32[32,128]{1,0:T(8,128)S(1)}) custom-call(f32[16,16,128]{2,1,0:T(8,128)S(1)} %copy-done, f32[3,16,16,128]{3,2,1,0:T(8,128)S(1)} %copy-done.1, s32[8,128]{1,0:T(8,128)S(1)} %bitcast.3, s32[8,128]{1,0:T(8,128)S(1)} %bitcast.4, f32[8,128]{1,0:T(8,128)S(1)} %bitcast.5), custom_call_target="tpu_custom_call" | custom-call | tf_op jit(solution)/shard_map/prepare/pallas_call | solution.py:607
  7.3 3.0 %collective-permute-start = (f32[64,128]{1,0:T(8,128)S(1)}, f32[64,128]{1,0:T(8,128)S(1)}, u32[]{:S(2)}, u32[]{:S(2)}) collective-permute-start(f32[64,128]{1,0:T(8,128)S(1)} %get-tuple-element.25.mine), channel_id=1, source_target_pairs={{0,1},{1,0},{2,3},{3,2},{4,5},{5,4},{6,7},{7,6},{8,9},{9,8},{10,11... | collective-permute-start | bytes 98312 | tf_op jit(solution)/shard_map/ppermute | solution.py:638
  10.3 1.9 %collective-permute-done.other = f32[64,128]{1,0:T(8,128)S(1)} collective-permute-done((f32[64,128]{1,0:T(8,128)S(1)}, f32[64,128]{1,0:T(8,128)S(1)}, u32[]{:S(2)}, u32[]{:S(2)}) %collective-permute-start) | collective-permute-done | bytes 32800 | tf_op jit(solution)/shard_map/ppermute | solution.py:638
  12.2 1.9 %deposit.1 = (f32[36,16,128]{2,1,0:T(8,128)S(1)}, f32[36,16,128]{2,1,0:T(8,128)S(1)}) custom-call(f32[18,24,128]{2,1,0:T(8,128)S(1)} %get-tuple-element.23.source, f32[24,128]{1,0:T(8,128)S(1)} %get-tuple-element.24.spill, f32[16,16,128]{2,1,0:T(8,128)S(1)} %copy-done, f32[64,128]{1,0:T(8,128)S(1)} %get-tuple-element.25.mine, ...), custom_call_target="tpu_custom_call" | custom-call | tf_op jit(solution)/shard_map/deposit/pallas_call | solution.py:607
  14.2 0.1 collective-permute-start.1
  14.2 1.6 %collective-permute-done.1.other = f32[36,16,128]{2,1,0:T(8,128)S(1)} collective-permute-done((f32[36,16,128]{2,1,0:T(8,128)S(1)}, f32[36,16,128]{2,1,0:T(8,128)S(1)}, u32[]{:S(2)}, u32[]{:S(2)}) %collective-permute-start.1) | collective-permute-done | bytes 294944 | tf_op jit(solution)/shard_map/ppermute | solution.py:651
  15.8 0.2 pair.1
  16.0 2.1 %collective-permute-start.2 = (f32[9,16,128]{2,1,0:T(8,128)S(1)}, f32[9,16,128]{2,1,0:T(8,128)S(1)}, u32[]{:S(2)}, u32[]{:S(2)}) collective-permute-start(f32[9,16,128]{2,1,0:T(8,128)S(1)} %get-tuple-element.31), channel_id=1, source_target_pairs={{0,16},{16,0},{8,24},{24,8},{1,17},{17,1},{9,25},{25,9},{2,18},{18... | collective-permute-start | bytes 221192 | tf_op jit(solution)/shard_map/ppermute | solution.py:654
  18.1 2.6 %collective-permute-done.2.other = f32[9,16,128]{2,1,0:T(8,128)S(1)} collective-permute-done((f32[9,16,128]{2,1,0:T(8,128)S(1)}, f32[9,16,128]{2,1,0:T(8,128)S(1)}, u32[]{:S(2)}, u32[]{:S(2)}) %collective-permute-start.2) | collective-permute-done | bytes 73760 | tf_op jit(solution)/shard_map/ppermute | solution.py:654
  20.7 0.2 across.1
  20.8 1.8 %collective-permute-start.3 = (f32[39,8,128]{2,1,0:T(8,128)S(1)}, f32[39,8,128]{2,1,0:T(8,128)S(1)}, u32[]{:S(2)}, u32[]{:S(2)}) collective-permute-start(f32[39,8,128]{2,1,0:T(8,128)S(1)} %get-tuple-element.35), channel_id=1, source_target_pairs={{8,2},{2,8},{10,4},{4,10},{12,6},{6,12},{24,18},{18,24},{26,20},{2... | collective-permute-start | bytes 479240 | tf_op jit(solution)/shard_map/ppermute | solution.py:663
  22.7 3.5 %collective-permute-done.3.other = f32[39,8,128]{2,1,0:T(8,128)S(1)} collective-permute-done((f32[39,8,128]{2,1,0:T(8,128)S(1)}, f32[39,8,128]{2,1,0:T(8,128)S(1)}, u32[]{:S(2)}, u32[]{:S(2)}) %collective-permute-start.3) | collective-permute-done | bytes 159776 | tf_op jit(solution)/shard_map/ppermute | solution.py:663
  26.2 4.2 %down.1 = (f32[42,16,256]{2,1,0:T(8,128)S(1)}, f32[42,16,256]{2,1,0:T(8,128)S(1)}, f32[42,16,256]{2,1,0:T(8,128)S(1)}, f32[16,64,128]{2,1,0:T(8,128)S(1)}) custom-call(f32[42,16,128]{2,1,0:T(8,128)S(1)} %get-tuple-element.32.source_in, f32[42,16,128]{2,1,0:T(8,128)S(1)} %get-tuple-element.33.kappa_in, f32[3,16,128]{2,1,0:T(8,128)S(1)} %get-tuple-element.34.halo_in, ...), custom_call_target="tpu_custom_call" | custom-call | tf_op jit(solution)/shard_map/down/pallas_call | solution.py:607
  30.4 20.8 %all_to_all.5.mine = f32[16,64,128]{2,1,0:T(8,128)S(1)} all-to-all(f32[16,64,128]{2,1,0:T(8,128)S(1)} %get-tuple-element.37), channel_id=1, replica_groups={{0,1,2,3,4,5,6,7,16,17,18,19,20,21,22,23},{8,9,10,11,12,13,14,15,24,25,..., dimensions={0} | all-to-all | bytes 1048576 | tf_op jit(solution)/shard_map/all_to_all | solution.py:675
  51.1 0.0 collective-permute-start.4
  51.2 1.9 %collective-permute-done.4.other = f32[16,64,128]{2,1,0:T(8,128)S(1)} collective-permute-done((f32[16,64,128]{2,1,0:T(8,128)S(1)}, f32[16,64,128]{2,1,0:T(8,128)S(1)}, u32[]{:S(2)}, u32[]{:S(2)}) %collective-permute-start.4) | collective-permute-done | bytes 524320 | tf_op jit(solution)/shard_map/ppermute | solution.py:678
  53.1 7.4 %coarse.1.e_in = f32[34,32,128]{2,1,0:T(8,128)S(1)} custom-call(f32[16,64,128]{2,1,0:T(8,128)S(1)} %all_to_all.5.mine, f32[16,64,128]{2,1,0:T(8,128)S(1)} %collective-permute-done.4.other), custom_call_target="tpu_custom_call" | custom-call | tf_op jit(solution)/shard_map/coarse/pallas_call | solution.py:607
  60.5 3.5 %up.1 = f32[32,8,128]{2,1,0:T(8,128)S(1)} custom-call(f32[34,32,128]{2,1,0:T(8,128)S(1)} %coarse.1.e_in, f32[42,16,256]{2,1,0:T(8,128)S(1)} %get-tuple-element.38.rhs, f32[42,16,256]{2,1,0:T(8,128)S(1)} %get-tuple-element.39.kappa, f32[42,16,256]{2,1,0:T(8,128)S(1)} %get-tuple-element.40.v2), custom_call_target="tpu_custom_call" | custom-call | tf_op jit(solution)/shard_map/up/pallas_call | solution.py:607
  64.0 0.2 collective-permute-start.5
  64.2 1.1 %collective-permute-done.5 = f32[16,8,128]{2,1,0:T(8,128)S(1)} collective-permute-done((f32[16,8,128]{2,1,0:T(8,128)S(1)}, f32[16,8,128]{2,1,0:T(8,128)S(1)}, u32[]{:S(2)}, u32[]{:S(2)}) %collective-permute-start.5) | collective-permute-done | bytes 65568 | tf_op jit(solution)/shard_map/ppermute | solution.py:701
  65.3 0.7 %maximum_select_fusion = f32[16,16,128]{2,1,0:T(8,128)} fusion(f32[16,8,128]{2,1,0:T(8,128)S(1)} %collective-permute-done.5, f32[16,8,128]{2,1,0:T(8,128)S(1)} %get-tuple-element.41, pred[]{:T(512)S(6)} %eq.3), kind=kLoop, calls=%fused_computation | loop fusion | flops 98304 | bytes 262145 | tf_op jit(solution)/shard_map/jit(_where)/select_n | solution.py:702
  (1 shorter events, 0.0 us)
Async XLA Ops:
  0.0 0.7 %copy-start.2 = (s32[1,1,1,1024,1]{3,4,2,1,0:T(1,128)S(1)}, s32[1,1,1,1024,1]{3,4,2,1,0:T(1,128)}, u32[]{:S(2)}) copy-start(s32[1,1,1,1024,1]{3,4,2,1,0:T(1,128)} %param.7) | copy-start | bytes 12292
  0.7 0.9 %copy-start = (f32[16,16,128]{2,1,0:T(8,128)S(1)}, f32[16,16,128]{2,1,0:T(8,128)}, u32[]{:S(2)}) copy-start(f32[16,16,128]{2,1,0:T(8,128)} %chi.1) | copy-start | bytes 393220
  1.6 1.0 %copy-start.1 = (f32[3,16,16,128]{3,2,1,0:T(8,128)S(1)}, f32[3,16,16,128]{3,2,1,0:T(8,128)}, u32[]{:S(2)}) copy-start(f32[3,16,16,128]{3,2,1,0:T(8,128)} %refs_1_.1) | copy-start | bytes 1179652
  2.6 0.7 %copy-start.3 = (s32[1,1,1,1024]{3,2,1,0:T(1,128)S(1)}, s32[1,1,1,1024]{3,2,1,0:T(1,128)}, u32[]{:S(2)}) copy-start(s32[1,1,1,1024]{3,2,1,0:T(1,128)} %param.8) | copy-start | bytes 12292
  3.3 0.7 %copy-start.4 = (f32[1,1,1,1024]{3,2,1,0:T(1,128)S(1)}, f32[1,1,1,1024]{3,2,1,0:T(1,128)}, u32[]{:S(2)}) copy-start(f32[1,1,1,1024]{3,2,1,0:T(1,128)} %param.9) | copy-start | bytes 12292
  7.3 4.9 %collective-permute-start = (f32[64,128]{1,0:T(8,128)S(1)}, f32[64,128]{1,0:T(8,128)S(1)}, u32[]{:S(2)}, u32[]{:S(2)}) collective-permute-start(f32[64,128]{1,0:T(8,128)S(1)} %get-tuple-element.25.mine), channel_id=1, source_target_pairs={{0,1},{1,0},{2,3},{3,2},{4,5},{5,4},{6,7},{7,6},{8,9},{9,8},{10,11... | collective-permute-start | bytes 98312 | tf_op jit(solution)/shard_map/ppermute | solution.py:638
  14.2 1.6 %collective-permute-start.1 = (f32[36,16,128]{2,1,0:T(8,128)S(1)}, f32[36,16,128]{2,1,0:T(8,128)S(1)}, u32[]{:S(2)}, u32[]{:S(2)}) collective-permute-start(f32[36,16,128]{2,1,0:T(8,128)S(1)} %get-tuple-element.27), channel_id=1, source_target_pairs={{0,8},{8,0},{16,24},{24,16},{1,9},{9,1},{17,25},{25,17},{2,10},{10... | collective-permute-start | bytes 884744 | tf_op jit(solution)/shard_map/ppermute | solution.py:651
  16.0 4.6 %collective-permute-start.2 = (f32[9,16,128]{2,1,0:T(8,128)S(1)}, f32[9,16,128]{2,1,0:T(8,128)S(1)}, u32[]{:S(2)}, u32[]{:S(2)}) collective-permute-start(f32[9,16,128]{2,1,0:T(8,128)S(1)} %get-tuple-element.31), channel_id=1, source_target_pairs={{0,16},{16,0},{8,24},{24,8},{1,17},{17,1},{9,25},{25,9},{2,18},{18... | collective-permute-start | bytes 221192 | tf_op jit(solution)/shard_map/ppermute | solution.py:654
  20.8 5.3 %collective-permute-start.3 = (f32[39,8,128]{2,1,0:T(8,128)S(1)}, f32[39,8,128]{2,1,0:T(8,128)S(1)}, u32[]{:S(2)}, u32[]{:S(2)}) collective-permute-start(f32[39,8,128]{2,1,0:T(8,128)S(1)} %get-tuple-element.35), channel_id=1, source_target_pairs={{8,2},{2,8},{10,4},{4,10},{12,6},{6,12},{24,18},{18,24},{26,20},{2... | collective-permute-start | bytes 479240 | tf_op jit(solution)/shard_map/ppermute | solution.py:663
  51.1 1.9 %collective-permute-start.4 = (f32[16,64,128]{2,1,0:T(8,128)S(1)}, f32[16,64,128]{2,1,0:T(8,128)S(1)}, u32[]{:S(2)}, u32[]{:S(2)}) collective-permute-start(f32[16,64,128]{2,1,0:T(8,128)S(1)} %all_to_all.5.mine), channel_id=1, source_target_pairs={{0,8},{8,0},{16,24},{24,16},{1,9},{9,1},{17,25},{25,17},{2,10},{10... | collective-permute-start | bytes 1572872 | tf_op jit(solution)/shard_map/ppermute | solution.py:678
  64.0 1.3 %collective-permute-start.5 = (f32[16,8,128]{2,1,0:T(8,128)S(1)}, f32[16,8,128]{2,1,0:T(8,128)S(1)}, u32[]{:S(2)}, u32[]{:S(2)}) collective-permute-start(f32[16,8,128]{2,1,0:T(8,128)S(1)} %get-tuple-element.42), channel_id=1, source_target_pairs={{0,8},{8,0},{16,24},{24,16},{1,9},{9,1},{17,25},{25,17},{2,10},{10... | collective-permute-start | bytes 196616 | tf_op jit(solution)/shard_map/ppermute | solution.py:701

commit v3 on v2

--- a/solution.py
+++ b/solution.py
@@ -132,7 +132,12 @@
 
 
 def dot(a, b):
-    return jnp.dot(a, b, precision=lax.Precision.HIGHEST, preferred_element_type=F32)
+    total = 0.0
+    for _ in range(3):
+        part = a.astype(BF16)
+        total = total + jnp.dot(part, b.astype(BF16), preferred_element_type=F32)
+        a = a - part.astype(F32)
+    return total
 
 
 def halving(offset, factor):
@@ -145,68 +150,53 @@
     return gx >> 1, gx & 1, gy, gz
 
 
-def prepare_kernel(*refs):
-    given, (source, spill, message, coarse), (sums, kap), rest = refs[:5], refs[5:9], refs[9:11], refs[11:]
-    chi, inducing, dest, cell, value, done = rest
+def stretch(x):
+    return roll(jnp.concatenate([x, jnp.zeros((8, x.shape[1]), F32)], 0), 4, 0)
+
+
+def message_kernel(*refs):
+    given, (chi, inducing, message, spill), (dest, cell, value, done) = refs[:5], refs[5:9], refs[9:]
     _, _, _, t = place()
-    copies = [pltpu.make_async_copy(a, b, done.at[i]) for i, (a, b) in enumerate(zip(given, rest[:5]))]
+    held = (chi, inducing, dest, cell, value)
+    copies = [pltpu.make_async_copy(a, b, done.at[i]) for i, (a, b) in enumerate(zip(given, held))]
     for copy in copies:
         copy.start()
-    lane = iota((16, 128), 1)
-    tall_lane = iota((24, 128), 1)
-    zero = jnp.zeros((16, 128), F32)
-    pad = jnp.zeros((8, 128), F32)
     for copy in copies:
         copy.wait()
-    kap[...] = 1.0 + chi[...]
-    mx = [zero, zero] + [chi[x] * inducing[0, x] for x in range(16)] + [zero, zero]
-    tiles = [jnp.zeros((24, 128), F32), jnp.zeros((24, 128), F32)]
-    over = zero
-    for i in range(18):
-        dx = mx[i + 2] - mx[i]
-        if 1 <= i <= 16:
-            my, mz = chi[i - 1] * inducing[1, i - 1], chi[i - 1] * inducing[2, i - 1]
-            y24 = jnp.concatenate([my, pad], 0)
-            dy = roll(y24, 3, 0) - roll(y24, 5, 0)
-            ahead, behind = roll(mz, -1, 1), roll(mz, 1, 1)
-            dz = jnp.where(lane == 127, 0.0, ahead) - jnp.where(lane == 0, 0.0, behind)
-            row = -0.5 * (roll(jnp.concatenate([dx + dz, pad], 0), 4, 0) + dy)
-            beyond = pick(t, 0.5 * behind, -0.5 * roll(ahead, 1, 1))
-            beyond = jnp.where(lane == 0, beyond, 0.0)
-            slot = pick(t, roll(beyond, 1, 1), roll(beyond, 2, 1))
-            over = over + roll(slot, 8 * (i - 1), 1)
-            beyond = roll(jnp.concatenate([beyond, pad], 0), 4, 0)
-            k = jnp.concatenate([pick(t, roll(kap[i - 1], -124, 1), kap[i - 1]), pad], 0)
-            k = jnp.where(tall_lane < 4, roll(k, 4, 0), 0.0)
-        else:
-            row = -0.5 * roll(jnp.concatenate([dx, pad], 0), 4, 0)
-            beyond = k = jnp.zeros((24, 128), F32)
-        source[i] = row
-        low = jnp.where(tall_lane < 3, roll(row, -125, 1), 0.0) + roll(beyond, 3, 1)
-        high = jnp.where((tall_lane > 0) & (tall_lane < 4), roll(row, 1, 1), 0.0) + beyond
-        piece = pick(t, low, high) + roll(k, 4, 1)
-        if 1 <= i <= 16:
-            tiles[0] = tiles[0] + roll(piece, 8 * (i - 1), 1)
-        else:
-            tiles[1] = tiles[1] + roll(piece, 0 if i == 0 else 8, 1)
-    spill[...] = roll(jnp.concatenate([over, pad], 0), 4, 0)
-    message[0:24] = tiles[0]
-    message[24:48] = tiles[1]
+    lane = iota((16, 128), 1)
+    turn = 4 - 3 * t
+    wanted = pick(t, (lane < 4).astype(jnp.int32), ((lane >= 1) & (lane < 5)).astype(jnp.int32)) > 0
+    k, mx, my, mz = [jnp.zeros((16, 128), F32) for _ in range(4)]
+    for x in range(16):
+        near = jnp.where(wanted, pltpu.roll(chi[x], turn, 1), 0.0)
+        parts = [near * pltpu.roll(inducing[d, x], turn, 1) for d in range(3)]
+        one = jnp.where(wanted, 1.0 + near, 0.0)
+        k, mx, my, mz = [total + roll(part, 8 * x, 1) for total, part in zip((k, mx, my, mz), [one] + parts)]
+    dx = jnp.where(lane < 120, roll(mx, -8, 1), 0.0) - jnp.where(lane >= 8, roll(mx, 8, 1), 0.0)
+    y = stretch(my)
+    dz = roll(mz, -1, 1) - roll(mz, 1, 1)
+    body = -0.5 * (stretch(dx + dz) + (roll(y, -1, 0) - roll(y, 1, 0)))
+    lane = iota((24, 128), 1)
+    slot = lane & 7
+    ends = 0.5 * (jnp.where((lane >= 8) & (lane < 16), roll(stretch(mx), 16, 1), 0.0) - jnp.where(lane < 8, stretch(mx), 0.0))
+
+    def four(tile):
+        tile = pick(t, roll(tile, -1, 1), tile)
+        return jnp.where(slot < 4, tile, 0.0)
+
+    own = pick(t, jnp.where(slot == 4, body, 0.0), jnp.where(slot == 0, body, 0.0))
+    spill[...] = pick(t, roll(own, -3, 1), roll(own, 2, 1))
+    message[0:24] = four(body) + jnp.where(slot >= 4, stretch(pick(t, roll(k, 4, 1), roll(k, 3, 1))), 0.0)
+    message[24:48] = four(ends)
     message[48:56] = value[...]
     message[56:64] = (dest[...] * 32768 + cell[...]).astype(F32)
-    pairs = kap[...].reshape(8, 2, 16, 128)
-    sums[...] = (pairs[:, 0] + pairs[:, 1]).reshape(128, 128)
-    halves = sums[pl.ds(0, 64, stride=2), :] + sums[pl.ds(1, 64, stride=2), :]
-    coarse[...] = dot(halves[:32], halving(0, 0.125)) + dot(halves[32:], halving(64, 0.125))
-
-
-def deposit_kernel(source, spill, chi, mine, other, own, sent, all_, at_row, hi, mid, lo):
-    _, c, _, t = place()
+
+
+def spread_records(records, t, at_row, hi, mid, lo):
     spot = iota((256, 128), 0)
-    for j in range(16):
-        ref, k = (mine, j) if j < 8 else (other, j - 8)
-        value = ref[48 + k : 49 + k, :]
-        code = ref[56 + k : 57 + k, :].astype(jnp.int32)
+    for j in range(8):
+        value = records[48 + j : 49 + j, :]
+        code = records[56 + j : 57 + j, :].astype(jnp.int32)
         cells = code & 32767
         z = ((code >> 15) - t) * 128 + (cells & 127)
         far = z - 128 + 131 * t
@@ -224,24 +214,48 @@
         total = total + lax.dot_general(
             at_row[...], part[...], (((1,), (1,)), ((), ())), preferred_element_type=F32
         )
+    return total
+
+
+def source_kernel(chi, inducing, records, source, total, coarse, sums, at_row, hi, mid, lo):
+    _, _, _, t = place()
+    lane = iota((16, 128), 1)
+    zero = jnp.zeros((16, 128), F32)
+    mx = [zero, zero] + [chi[x] * inducing[0, x] for x in range(16)] + [zero, zero]
+    for i in range(18):
+        flat = mx[i + 2] - mx[i]
+        if 1 <= i <= 16:
+            my, mz = chi[i - 1] * inducing[1, i - 1], chi[i - 1] * inducing[2, i - 1]
+            flat = flat + (jnp.where(lane == 127, 0.0, roll(mz, -1, 1)) - jnp.where(lane == 0, 0.0, roll(mz, 1, 1)))
+            y = stretch(my)
+            source[i] = -0.5 * (stretch(flat) + (roll(y, -1, 0) - roll(y, 1, 0)))
+        else:
+            source[i] = -0.5 * stretch(flat)
+    total[...] = spread_records(records, t, at_row, hi, mid, lo)
+    sums[...] = pair_sums(1.0 + chi[...]).reshape(128, 128)
+    halves = sums[pl.ds(0, 64, stride=2), :] + sums[pl.ds(1, 64, stride=2), :]
+    coarse[...] = dot(halves[:32], halving(0, 0.125)) + dot(halves[32:], halving(64, 0.125))
+
+
+def deposit_kernel(source, spill, chi, mine, other, own, sent, all_, at_row, hi, mid, lo):
+    _, c, _, t = place()
+    total = mine[...] + spread_records(other, t, at_row, hi, mid, lo)
     lane = iota((24, 128), 1)
-    pad = jnp.zeros((8, 128), F32)
-    slot, goal = 3 * t, 127 - 127 * t
     halo = other[0:24] + spill[...]
     for i in range(18):
         if 1 <= i <= 16:
             at = 16 * (i - 1)
-            got = jnp.concatenate([total[at : at + 16, 128:], pad], 0)
-            halo = halo + roll(jnp.where(lane < 4, roll(got, 4, 0), 0.0), 8 * (i - 1), 1)
-            add = roll(jnp.concatenate([total[at : at + 16, :128], pad], 0), 4, 0)
-            near = roll(other[0:24], -8 * (i - 1), 1)
+            got = stretch(total[at : at + 16, 128:])
+            halo = halo + roll(jnp.where(lane < 4, got, 0.0), 8 * (i - 1), 1)
+            add = stretch(total[at : at + 16, :128])
+            near = pick(t, roll(other[0:24], 127 - 8 * (i - 1), 1), roll(other[0:24], -3 - 8 * (i - 1), 1))
         else:
             add = jnp.zeros((24, 128), F32)
-            near = roll(other[24:48], 0 if i == 0 else -8, 1)
-        edge = pick(t, jnp.where(lane == 127, roll(near, 127, 1), 0.0), jnp.where(lane == 0, roll(near, -3, 1), 0.0))
-        all_[i] = source[i] + add + edge
+            by = 0 if i == 0 else -8
+            near = pick(t, roll(other[24:48], 127 + by, 1), roll(other[24:48], -3 + by, 1))
+        all_[i] = source[i] + add + jnp.where(lane == 127 - 127 * t, near, 0.0)
     for i in range(16):
-        all_[18 + i] = roll(jnp.concatenate([1.0 + chi[i], pad], 0), 4, 0)
+        all_[18 + i] = stretch(1.0 + chi[i])
     all_[34] = halo
     all_[35] = other[24:48]
     keep, give = pl.multiple_of(8 * c, 8), pl.multiple_of(8 - 8 * c, 8)
@@ -366,13 +380,13 @@
 
 
 def down_kernel(
-    n_gy, source_in, kappa_in, halo_in, other, kappa1, rhs, kappa, v2, message,
-    cx, cy, cz, weight, diag, v1, sums, halo,
+    n_gy, source_in, kappa_in, halo_in, other, kappa1, rhs, kappa, weight, v2, message,
+    cx, cy, cz, diag, v1, sums, halo,
 ):
     p, c, b, t = place()
     first = 5 - 4 * p
     edge = jnp.where(c == 0, b == 0, b == n_gy - 1).astype(jnp.int32)
-    for ref in (kappa, cx, v1, v2, rhs):
+    for ref in (kappa, cx, weight, v1, v2, rhs):
         ref[0:5] = jnp.zeros((5, 16, 256), F32)
         ref[37:42] = jnp.zeros((5, 16, 256), F32)
 
@@ -569,14 +583,22 @@
     e_out[...] = vb[...]
 
 
-def up_kernel(n_gy, e_in, rhs, kappa, v2, out, cx, cy, cz, weight, diag, va, vb, tall):
+def up_kernel(n_gy, e_in, rhs, kappa, weight, v2, out, cx, cy, cz, va, vb, tall):
     p, c, b, t = place()
     first = 5 - 4 * p
     n_y = 8 * n_gy
-    for ref in (cx, va, vb):
+    for ref in (va, vb, cx):
         ref[0:5] = jnp.zeros((5, 16, 256), F32)
         ref[37:42] = jnp.zeros((5, 16, 256), F32)
-    faces(kappa, cx, cy, cz, weight, diag, first, PLANES, 1.0, False)
+
+    def face(i):
+        near = kappa[pl.ds(first + i, SIZE + 1)]
+        r, k = pl.ds(first + i, SIZE), near[:SIZE]
+        cx[r] = 0.5 * (k + near[1:])
+        cy[r] = 0.5 * (k + roll(k, -1, 1))
+        cz[r] = 0.5 * (k + roll(k, -1, 2))
+
+    chunked(PLANES, face, SIZE)
     tall[:, 0:8, :] = jnp.zeros((18, 8, 128), F32)
     tall[:, 2 * n_y : 2 * n_y + 8, :] = jnp.zeros((18, 8, 128), F32)
     for k in range(18):
@@ -591,7 +613,7 @@
     e = dot(window.reshape(288, 128), spread).reshape(18, 16, 256)
     for k in range(18):
         for r in (2 * k + 3, 2 * k + 4):
-            va[r] = v2[r] + jnp.where(kappa[r] > 0.0, e[k], 0.0)
+            va[r] = v2[r] + jnp.where(weight[r] > 0.0, e[k], 0.0)
     sweep(va, vb, rhs, cx, cy, cz, weight, first, PLANES)
 
     def last(i):
@@ -604,16 +626,20 @@
 
 
 def call(kernel, name, outs, scratch, *args):
+    where = pltpu.HBM if name == "message" else pltpu.VMEM
+    if name == "message":
+        args = [pltpu.with_memory_space_constraint(a, pltpu.HBM) for a in args]
     return pl.pallas_call(
         kernel,
         name=name,
         out_shape=[jax.ShapeDtypeStruct(s, F32) for s in outs],
-        in_specs=[pl.BlockSpec(memory_space=pltpu.HBM if name == "prepare" else pltpu.VMEM)] * len(args),
+        in_specs=[pl.BlockSpec(memory_space=where)] * len(args),
         out_specs=[pl.BlockSpec(memory_space=pltpu.VMEM)] * len(outs),
         scratch_shapes=[
             pltpu.SemaphoreType.DMA((s,)) if isinstance(s, int) else pltpu.VMEM(*s) for s in scratch
         ],
-        compiler_params=pltpu.CompilerParams(vmem_limit_bytes=48 * 1024 * 1024),
+        compiler_params=pltpu.CompilerParams(vmem_limit_bytes=16 * 1024 * 1024),
+        cost_estimate=pl.CostEstimate(flops=10**7, bytes_accessed=4 * 10**6, transcendentals=0),
     )(*args)
 
 
@@ -622,13 +648,11 @@
     everyone = ("gx", "gy", "gz")
     window = (ROWS, 16, 256)
     big = [(window, F32)]
-    source, spill, message, kappa1 = call(
-        prepare_kernel,
-        "prepare",
-        [(18, 24, 128), (24, 128), (64, 128), (32, 128)],
-        [((128, 128), F32), ((16, 16, 128), F32), ((16, 16, 128), F32), ((3, 16, 16, 128), F32)]
-        + [((8, 128), jnp.int32)] * 2
-        + [((8, 128), F32), 5],
+    chi, inducing, message, spill = call(
+        message_kernel,
+        "message",
+        [(16, 16, 128), (3, 16, 16, 128), (64, 128), (24, 128)],
+        [((8, 128), jnp.int32)] * 2 + [((8, 128), F32), 5],
         chi,
         inducing,
         record_dest.reshape(8, 128),
@@ -636,15 +660,25 @@
         record_value.reshape(8, 128),
     )
     got = lax.ppermute(message, "gz", [(0, 1), (1, 0)])
+    spread = [((256, 1024), BF16)] * 4
+    source, total, kappa1 = call(
+        source_kernel,
+        "source",
+        [(18, 24, 128), (256, 256), (32, 128)],
+        [((128, 128), F32)] + spread,
+        chi,
+        inducing,
+        message,
+    )
     own, sent = call(
         deposit_kernel,
         "deposit",
         [(36, 16, 128)] * 2,
-        [((36, 24, 128), F32)] + [((256, 2048), BF16)] * 4,
+        [((36, 24, 128), F32)] + spread,
         source,
         spill,
         chi,
-        message,
+        total,
         got,
     )
     swap = [(0, 1), (1, 0), (2, 3), (3, 2)]
@@ -661,11 +695,11 @@
     for low, high in ((0, 2 * n_gy), (2 * n_gy - 1, 4 * n_gy - 1)):
         turns += [(low, high), (high, low)]
     got = lax.ppermute(message, ("gx", "gy"), turns)
-    rhs, kappa, v2, message = call(
+    *fine, message = call(
         functools.partial(down_kernel, n_gy),
         "down",
-        [window, window, window, (4 * n_gy, 64, 128)],
-        big * 6 + [((256, 128), F32), ((3, 16, 128), F32)],
+        [window] * 4 + [(4 * n_gy, 64, 128)],
+        big * 5 + [((256, 128), F32), ((3, 16, 128), F32)],
         *fields,
         got,
         kappa1,
@@ -689,11 +723,9 @@
         functools.partial(up_kernel, n_gy),
         "up",
         [(32, 8, 128)],
-        big * 7 + [((18, 16 * n_gy + 8, 128), F32)],
+        big * 5 + [((18, 16 * n_gy + 8, 128), F32)],
         e,
-        rhs,
-        kappa,
-        v2,
+        *fine,
     )
     c = lax.axis_index("gx") & 1
     keep = lax.dynamic_slice_in_dim(out, 16 * c, 16, axis=0)

time: 66.3 us -> 60.3 us (0.910)
  local copies, waits for them, and re-layouts: 3.98 us -> 0.02 us
  Pallas kernels: 20.8 us -> 19.8 us
  waiting for transfers between devices: 12.5 us -> 11.6 us
    unnamed x10 -> x0, local copies, waits for them, and re-layouts: 3.96 us -> none
    ppermute x1, waiting for transfers between devices: 1.89 us -> 0.81 us  [paired(): got = lax.ppermute(message, 'gz', [(0, 1), (1, 0)])]
    pallas_call x7 -> x8, Pallas kernels: 20.8 us -> 19.8 us  [call(): pl.pallas_call(kernel, name=name, out_shape=[jax.ShapeDtypeStruct(s, F32)...]
  transfers between devices with their start and end apart: 6 -> 6, of which waited for: 6 -> 6; matrix products, arithmetic and copies ran while one was open for 0% -> 0% of each run, Pallas kernels for 0% -> 2%
where the time goes in v3:
time: 60.3 us; the launch traced here: 60.1 us
  blocking collectives  20.8 us (34%)
  Pallas kernels  19.8 us (33%)
  waiting for transfers between devices  11.6 us (19%)
  starting transfers between devices  7.2 us (12%)
  other arithmetic  0.67 us (1%)
    all_to_all x1, blocking collectives, paired(): lax.all_to_all(message, everyone, split_axis=0, concat_axis=0, tiled=True...  20.8 us
    pallas_call x8, Pallas kernels, call(): pl.pallas_call(kernel, name=name, out_shape=[jax.ShapeDtypeStruct(s, F32)...  19.8 us
    ppermute x1, waiting for transfers between devices, paired(): got = lax.ppermute(message, ('gx', 'gy'), turns)  3.49 us
    ppermute x1, starting transfers between devices, paired(): got = lax.ppermute(message, 'gz', [(0, 1), (1, 0)])  3 us
    ppermute x1, waiting for transfers between devices, paired(): got = lax.ppermute(message, 'gx', [(0, 2), (2, 0), (1, 3), (3, 1)])  2.57 us
    ppermute x1, starting transfers between devices, paired(): got = lax.ppermute(message, 'gx', [(0, 2), (2, 0), (1, 3), (3, 1)])  2.07 us
    ppermute x1, waiting for transfers between devices, paired(): other = lax.ppermute(mine, 'gx', swap)  2.04 us
    ppermute x1, starting transfers between devices, paired(): got = lax.ppermute(message, ('gx', 'gy'), turns)  1.85 us
  transfers between devices with their start and end apart: 6, of which 6 were waited for; matrix products, arithmetic and copies ran while one was open for 0% of the time, Pallas kernels for 2%

profile of v3, /device:TPU:0, one launch (start us, length us, event | category | flops | bytes accessed | tf_op | source)
XLA Modules:
  0.0 60.1 jit_solution(11965106074241828385)
XLA Ops:
  0.0 1.9 %message.1 = (f32[16,16,128]{2,1,0:T(8,128)S(1)}, f32[3,16,16,128]{3,2,1,0:T(8,128)S(1)}, f32[64,128]{1,0:T(8,128)S(1)}, f32[24,128]{1,0:T(8,128)S(1)}) custom-call(f32[16,16,128]{2,1,0:T(8,128)} %refs_0_.1, f32[3,16,16,128]{3,2,1,0:T(8,128)} %refs_1_.1, s32[8,128]{1,0:T(8,128)} %bitcast.3, s32[8,128]{1,0:T(8,128)} %bitcast.4, f32[8,128]{1,0:T(8,128)} %bitcast.5), custom_call_target="tpu_custom_call" | custom-call | flops 10000000 | bytes 4000000 | tf_op jit(solution)/shard_map/message/pallas_call | solution.py:632
  1.9 3.0 %collective-permute-start = (f32[64,128]{1,0:T(8,128)S(1)}, f32[64,128]{1,0:T(8,128)S(1)}, u32[]{:S(2)}, u32[]{:S(2)}) collective-permute-start(f32[64,128]{1,0:T(8,128)S(1)} %get-tuple-element.29.records), channel_id=1, source_target_pairs={{0,1},{1,0},{2,3},{3,2},{4,5},{5,4},{6,7},{7,6},{8,9},{9,8},{10,11... | collective-permute-start | bytes 98312 | tf_op jit(solution)/shard_map/ppermute | solution.py:662
  4.9 1.1 %source.1 = (f32[18,24,128]{2,1,0:T(8,128)S(1)}, f32[256,256]{1,0:T(8,128)S(1)}, f32[32,128]{1,0:T(8,128)S(1)}) custom-call(f32[16,16,128]{2,1,0:T(8,128)S(1)} %get-tuple-element.27.chi, f32[3,16,16,128]{3,2,1,0:T(8,128)S(1)} %get-tuple-element.28.inducing, f32[64,128]{1,0:T(8,128)S(1)} %get-tuple-element.29.records), custom_call_target="tpu_custom_call" | custom-call | flops 10000000 | bytes 4000000 | tf_op jit(solution)/shard_map/source/pallas_call | solution.py:632
  6.0 0.8 %collective-permute-done.other = f32[64,128]{1,0:T(8,128)S(1)} collective-permute-done((f32[64,128]{1,0:T(8,128)S(1)}, f32[64,128]{1,0:T(8,128)S(1)}, u32[]{:S(2)}, u32[]{:S(2)}) %collective-permute-start) | collective-permute-done | bytes 32800 | tf_op jit(solution)/shard_map/ppermute | solution.py:662
  6.8 1.2 %deposit.1 = (f32[36,16,128]{2,1,0:T(8,128)S(1)}, f32[36,16,128]{2,1,0:T(8,128)S(1)}) custom-call(f32[18,24,128]{2,1,0:T(8,128)S(1)} %get-tuple-element.30.source, f32[24,128]{1,0:T(8,128)S(1)} %get-tuple-element.31.spill, f32[16,16,128]{2,1,0:T(8,128)S(1)} %get-tuple-element.27.chi, f32[256,256]{1,0:T(8,128)S(1)} %get-tuple-element.32.mine, ...), custom_call_target="tpu_custom_call" | custom-call | flops 10000000 | bytes 4000000 | tf_op jit(solution)/shard_map/deposit/pallas_call | solution.py:632
  7.9 0.1 collective-permute-start.1
  8.0 1.6 %collective-permute-done.1.other = f32[36,16,128]{2,1,0:T(8,128)S(1)} collective-permute-done((f32[36,16,128]{2,1,0:T(8,128)S(1)}, f32[36,16,128]{2,1,0:T(8,128)S(1)}, u32[]{:S(2)}, u32[]{:S(2)}) %collective-permute-start.1) | collective-permute-done | bytes 294944 | tf_op jit(solution)/shard_map/ppermute | solution.py:685
  9.6 0.2 pair.1
  9.8 2.1 %collective-permute-start.2 = (f32[9,16,128]{2,1,0:T(8,128)S(1)}, f32[9,16,128]{2,1,0:T(8,128)S(1)}, u32[]{:S(2)}, u32[]{:S(2)}) collective-permute-start(f32[9,16,128]{2,1,0:T(8,128)S(1)} %get-tuple-element.38), channel_id=1, source_target_pairs={{0,16},{16,0},{8,24},{24,8},{1,17},{17,1},{9,25},{25,9},{2,18},{18... | collective-permute-start | bytes 221192 | tf_op jit(solution)/shard_map/ppermute | solution.py:688
  11.9 2.6 %collective-permute-done.2.other = f32[9,16,128]{2,1,0:T(8,128)S(1)} collective-permute-done((f32[9,16,128]{2,1,0:T(8,128)S(1)}, f32[9,16,128]{2,1,0:T(8,128)S(1)}, u32[]{:S(2)}, u32[]{:S(2)}) %collective-permute-start.2) | collective-permute-done | bytes 73760 | tf_op jit(solution)/shard_map/ppermute | solution.py:688
  14.4 0.2 across.1
  14.6 1.8 %collective-permute-start.3 = (f32[39,8,128]{2,1,0:T(8,128)S(1)}, f32[39,8,128]{2,1,0:T(8,128)S(1)}, u32[]{:S(2)}, u32[]{:S(2)}) collective-permute-start(f32[39,8,128]{2,1,0:T(8,128)S(1)} %get-tuple-element.42), channel_id=1, source_target_pairs={{8,2},{2,8},{10,4},{4,10},{12,6},{6,12},{24,18},{18,24},{26,20},{2... | collective-permute-start | bytes 479240 | tf_op jit(solution)/shard_map/ppermute | solution.py:697
  16.5 3.5 %collective-permute-done.3.other = f32[39,8,128]{2,1,0:T(8,128)S(1)} collective-permute-done((f32[39,8,128]{2,1,0:T(8,128)S(1)}, f32[39,8,128]{2,1,0:T(8,128)S(1)}, u32[]{:S(2)}, u32[]{:S(2)}) %collective-permute-start.3) | collective-permute-done | bytes 159776 | tf_op jit(solution)/shard_map/ppermute | solution.py:697
  20.0 4.2 %down.1 = (f32[42,16,256]{2,1,0:T(8,128)S(1)}, f32[42,16,256]{2,1,0:T(8,128)S(1)}, f32[42,16,256]{2,1,0:T(8,128)S(1)}, f32[42,16,256]{2,1,0:T(8,128)S(1)}, f32[16,64,128]{2,1,0:T(8,128)S(1)}) custom-call(f32[42,16,128]{2,1,0:T(8,128)S(1)} %get-tuple-element.39.source_in, f32[42,16,128]{2,1,0:T(8,128)S(1)} %get-tuple-element.40.kappa_in, ...), custom_call_target="tpu_custom_call" | custom-call | flops 10000000 | bytes 4000000 | tf_op jit(solution)/shard_map/down/pallas_call | solution.py:632
  24.1 20.8 %all_to_all.5.mine = f32[16,64,128]{2,1,0:T(8,128)S(1)} all-to-all(f32[16,64,128]{2,1,0:T(8,128)S(1)} %get-tuple-element.44), channel_id=1, replica_groups={{0,1,2,3,4,5,6,7,16,17,18,19,20,21,22,23},{8,9,10,11,12,13,14,15,24,25,..., dimensions={0} | all-to-all | bytes 1048576 | tf_op jit(solution)/shard_map/all_to_all | solution.py:709
  44.9 0.0 collective-permute-start.4
  44.9 2.0 %collective-permute-done.4.other = f32[16,64,128]{2,1,0:T(8,128)} collective-permute-done((f32[16,64,128]{2,1,0:T(8,128)S(1)}, f32[16,64,128]{2,1,0:T(8,128)}, u32[]{:S(2)}, u32[]{:S(2)}) %collective-permute-start.4) | collective-permute-done | bytes 524320 | tf_op jit(solution)/shard_map/ppermute | solution.py:712
  46.9 8.2 %coarse.1.e_in = f32[34,32,128]{2,1,0:T(8,128)S(1)} custom-call(f32[16,64,128]{2,1,0:T(8,128)S(1)} %all_to_all.5.mine, f32[16,64,128]{2,1,0:T(8,128)} %collective-permute-done.4.other), custom_call_target="tpu_custom_call" | custom-call | flops 10000000 | bytes 4000000 | tf_op jit(solution)/shard_map/coarse/pallas_call | solution.py:632
  55.1 3.0 %up.1 = f32[32,8,128]{2,1,0:T(8,128)S(1)} custom-call(f32[34,32,128]{2,1,0:T(8,128)S(1)} %coarse.1.e_in, f32[42,16,256]{2,1,0:T(8,128)S(1)} %get-tuple-element.45.rhs, f32[42,16,256]{2,1,0:T(8,128)S(1)} %get-tuple-element.46.kappa, f32[42,16,256]{2,1,0:T(8,128)S(1)} %get-tuple-element.47.weight, f32[42,16,256]{2,1,0:T(8,128)S(1)} %get-tuple-element.48.v2), custom_call_target="tpu_custom_call" | custom-call | flops 10000000 | bytes 4000000 | tf_op jit(solution)/shard_map/up/pallas_call | solution.py:632
  58.1 0.2 collective-permute-start.5
  58.4 1.1 %collective-permute-done.5 = f32[16,8,128]{2,1,0:T(8,128)S(1)} collective-permute-done((f32[16,8,128]{2,1,0:T(8,128)S(1)}, f32[16,8,128]{2,1,0:T(8,128)S(1)}, u32[]{:S(2)}, u32[]{:S(2)}) %collective-permute-start.5) | collective-permute-done | bytes 65568 | tf_op jit(solution)/shard_map/ppermute | solution.py:733
  59.5 0.7 %maximum_select_fusion = f32[16,16,128]{2,1,0:T(8,128)} fusion(f32[16,8,128]{2,1,0:T(8,128)S(1)} %collective-permute-done.5, f32[16,8,128]{2,1,0:T(8,128)S(1)} %get-tuple-element.49, pred[]{:T(512)S(6)} %eq.3), kind=kLoop, calls=%fused_computation | loop fusion | flops 98304 | bytes 262145 | tf_op jit(solution)/shard_map/jit(_where)/select_n | solution.py:734
  (1 shorter events, 0.0 us)
Async XLA Ops:
  1.9 4.9 %collective-permute-start = (f32[64,128]{1,0:T(8,128)S(1)}, f32[64,128]{1,0:T(8,128)S(1)}, u32[]{:S(2)}, u32[]{:S(2)}) collective-permute-start(f32[64,128]{1,0:T(8,128)S(1)} %get-tuple-element.29.records), channel_id=1, source_target_pairs={{0,1},{1,0},{2,3},{3,2},{4,5},{5,4},{6,7},{7,6},{8,9},{9,8},{10,11... | collective-permute-start | bytes 98312 | tf_op jit(solution)/shard_map/ppermute | solution.py:662
  7.9 1.6 %collective-permute-start.1 = (f32[36,16,128]{2,1,0:T(8,128)S(1)}, f32[36,16,128]{2,1,0:T(8,128)S(1)}, u32[]{:S(2)}, u32[]{:S(2)}) collective-permute-start(f32[36,16,128]{2,1,0:T(8,128)S(1)} %get-tuple-element.34), channel_id=1, source_target_pairs={{0,8},{8,0},{16,24},{24,16},{1,9},{9,1},{17,25},{25,17},{2,10},{10... | collective-permute-start | bytes 884744 | tf_op jit(solution)/shard_map/ppermute | solution.py:685
  9.8 4.6 %collective-permute-start.2 = (f32[9,16,128]{2,1,0:T(8,128)S(1)}, f32[9,16,128]{2,1,0:T(8,128)S(1)}, u32[]{:S(2)}, u32[]{:S(2)}) collective-permute-start(f32[9,16,128]{2,1,0:T(8,128)S(1)} %get-tuple-element.38), channel_id=1, source_target_pairs={{0,16},{16,0},{8,24},{24,8},{1,17},{17,1},{9,25},{25,9},{2,18},{18... | collective-permute-start | bytes 221192 | tf_op jit(solution)/shard_map/ppermute | solution.py:688
  14.6 5.3 %collective-permute-start.3 = (f32[39,8,128]{2,1,0:T(8,128)S(1)}, f32[39,8,128]{2,1,0:T(8,128)S(1)}, u32[]{:S(2)}, u32[]{:S(2)}) collective-permute-start(f32[39,8,128]{2,1,0:T(8,128)S(1)} %get-tuple-element.42), channel_id=1, source_target_pairs={{8,2},{2,8},{10,4},{4,10},{12,6},{6,12},{24,18},{18,24},{26,20},{2... | collective-permute-start | bytes 479240 | tf_op jit(solution)/shard_map/ppermute | solution.py:697
  44.9 2.0 %collective-permute-start.4 = (f32[16,64,128]{2,1,0:T(8,128)S(1)}, f32[16,64,128]{2,1,0:T(8,128)}, u32[]{:S(2)}, u32[]{:S(2)}) collective-permute-start(f32[16,64,128]{2,1,0:T(8,128)S(1)} %all_to_all.5.mine), channel_id=1, source_target_pairs={{0,8},{8,0},{16,24},{24,16},{1,9},{9,1},{17,25},{25,17},{2,10},{10... | collective-permute-start | bytes 1572872 | tf_op jit(solution)/shard_map/ppermute | solution.py:712
  58.1 1.3 %collective-permute-start.5 = (f32[16,8,128]{2,1,0:T(8,128)S(1)}, f32[16,8,128]{2,1,0:T(8,128)S(1)}, u32[]{:S(2)}, u32[]{:S(2)}) collective-permute-start(f32[16,8,128]{2,1,0:T(8,128)S(1)} %get-tuple-element.50), channel_id=1, source_target_pairs={{0,8},{8,0},{16,24},{24,16},{1,9},{9,1},{17,25},{25,17},{2,10},{10... | collective-permute-start | bytes 196616 | tf_op jit(solution)/shard_map/ppermute | solution.py:733

commit v4 on v3

--- a/solution.py
+++ b/solution.py
@@ -115,7 +115,7 @@
 BF16 = jnp.bfloat16
 ROWS = 42
 PLANES = 36
-SIZE = 4
+SIZE = 12
 
 
 def iota(shape, dim):
@@ -320,8 +320,7 @@
     lax.fori_loop(0, count // size, step, 0)
 
 
-def faces(kap, cx, cy, cz, weight, diag, first, count, scale, closed):
-    n = SIZE
+def faces(kap, cx, cy, cz, weight, diag, first, count, scale, closed, n):
     shape = (n,) + kap.shape[1:]
     last_y = iota(shape, 1) == shape[1] - 1
     first_y = iota(shape, 1) == 0
@@ -360,18 +359,18 @@
     )
 
 
-def sweep(v, out, rhs, cx, cy, cz, weight, first, count):
+def sweep(v, out, rhs, cx, cy, cz, weight, first, count, n):
     def body(i):
         r = first + i
-        here, total = around(v, cx, cy, cz, r, SIZE)
-        out[pl.ds(r, SIZE)] = (1.0 - OMEGA) * here + weight[pl.ds(r, SIZE)] * (rhs[pl.ds(r, SIZE)] + total)
-
-    chunked(count, body, SIZE)
-
-
-def resid(v, rhs, cx, cy, cz, diag, r):
-    here, total = around(v, cx, cy, cz, r, SIZE)
-    return rhs[pl.ds(r, SIZE)] + total - diag[pl.ds(r, SIZE)] * here
+        here, total = around(v, cx, cy, cz, r, n)
+        out[pl.ds(r, n)] = (1.0 - OMEGA) * here + weight[pl.ds(r, n)] * (rhs[pl.ds(r, n)] + total)
+
+    chunked(count, body, n)
+
+
+def resid(v, rhs, cx, cy, cz, diag, r, n):
+    here, total = around(v, cx, cy, cz, r, n)
+    return rhs[pl.ds(r, n)] + total - diag[pl.ds(r, n)] * here
 
 
 def pair_sums(x):
@@ -418,20 +417,14 @@
         kappa[rows] = jnp.concatenate([kappa_in[rows] + k, jnp.concatenate(far_k, 0)], 2)
 
     chunked(PLANES, enter, SIZE)
-    faces(kappa, cx, cy, cz, weight, diag, first, PLANES, 1.0, False)
-
-    def start(i):
-        r = pl.ds(first + i, SIZE)
-        v1[r] = weight[r] * rhs[r]
-
-    chunked(PLANES, start, SIZE)
-    sweep(v1, v2, rhs, cx, cy, cz, weight, first, PLANES)
-
-    def pair(i):
-        two = pair_sums(resid(v2, rhs, cx, cy, cz, diag, 5 + i))
-        sums[pl.ds(pl.multiple_of(8 * i, 16), 8 * SIZE), :] = two[:, :, :128].reshape(8 * SIZE, 128)
-
-    chunked(32, pair, SIZE)
+    faces(kappa, cx, cy, cz, weight, diag, first, PLANES, 1.0, False, PLANES)
+
+    rows = pl.ds(first, PLANES)
+    v1[rows] = weight[rows] * rhs[rows]
+    sweep(v1, v2, rhs, cx, cy, cz, weight, first, PLANES, PLANES)
+
+    two = pair_sums(resid(v2, rhs, cx, cy, cz, diag, 5, 32))
+    sums[...] = two[:, :, :128].reshape(256, 128)
     halves = sums[pl.ds(0, 128, stride=2), :] + sums[pl.ds(1, 128, stride=2), :]
     packed = dot(halves[:64], halving(0, 0.125)) + dot(halves[64:], halving(64, 0.125))
     low = iota((8, 128), 0) < 4
@@ -540,28 +533,14 @@
                 for odd, (near, far) in enumerate((evens, odds)):
                     r1[1 + 16 * pp + 2 * j + odd, spot, :] = jnp.where(left, near, roll(far, 64, 1))
                     r1[1 + 16 * pp + 8 + 2 * j + odd, spot, :] = jnp.where(left, roll(near, 64, 1), far)
-    faces(k1, cx, cy, cz, weight, diag, 1, 32, 0.25, True)
-
-    def start(i):
-        r = pl.ds(1 + i, SIZE)
-        va[r] = weight[r] * r1[r]
-
-    chunked(32, start, SIZE)
-    sweep(va, vb, r1, cx, cy, cz, weight, 1, 32)
-    step = n_y * SIZE // 2
-
-    def pair(i):
-        two = pair_sums(resid(vb, r1, cx, cy, cz, diag, 1 + i))
-        sums[pl.ds(pl.multiple_of(n_y // 2 * i, 8), step), :] = two.reshape(step, 128)
-
-    chunked(32, pair, SIZE)
+    faces(k1, cx, cy, cz, weight, diag, 1, 32, 0.25, True, 32)
+
+    va[1:33] = weight[1:33] * r1[1:33]
+    sweep(va, vb, r1, cx, cy, cz, weight, 1, 32, 32)
+    sums[...] = pair_sums(resid(vb, r1, cx, cy, cz, diag, 1, 32)).reshape(16 * n_y, 128)
     r2 = halved_yz(sums, 16, n_y // 2)
 
-    def kappa_pair(i):
-        two = pair_sums(k1[pl.ds(1 + i, SIZE)])
-        sums[pl.ds(pl.multiple_of(n_y // 2 * i, 8), step), :] = two.reshape(step, 128)
-
-    chunked(32, kappa_pair, SIZE)
+    sums[...] = pair_sums(k1[1:33]).reshape(16 * n_y, 128)
     k2 = halved_yz(sums, 16, n_y // 2)
     middle = Level(k2, 0.0625)
     v2 = middle.weight * r2
@@ -578,8 +557,8 @@
     for i in range(16):
         vb[1 + 2 * i] = vb[1 + 2 * i] + e1[i]
         vb[2 + 2 * i] = vb[2 + 2 * i] + e1[i]
-    sweep(vb, va, r1, cx, cy, cz, weight, 1, 32)
-    sweep(va, vb, r1, cx, cy, cz, weight, 1, 32)
+    sweep(vb, va, r1, cx, cy, cz, weight, 1, 32, 32)
+    sweep(va, vb, r1, cx, cy, cz, weight, 1, 32, 32)
     e_out[...] = vb[...]
 
 
@@ -592,13 +571,13 @@
         ref[37:42] = jnp.zeros((5, 16, 256), F32)
 
     def face(i):
-        near = kappa[pl.ds(first + i, SIZE + 1)]
-        r, k = pl.ds(first + i, SIZE), near[:SIZE]
+        near = kappa[pl.ds(first + i, PLANES + 1)]
+        r, k = pl.ds(first + i, PLANES), near[:PLANES]
         cx[r] = 0.5 * (k + near[1:])
         cy[r] = 0.5 * (k + roll(k, -1, 1))
         cz[r] = 0.5 * (k + roll(k, -1, 2))
 
-    chunked(PLANES, face, SIZE)
+    face(0)
     tall[:, 0:8, :] = jnp.zeros((18, 8, 128), F32)
     tall[:, 2 * n_y : 2 * n_y + 8, :] = jnp.zeros((18, 8, 128), F32)
     for k in range(18):
@@ -614,15 +593,15 @@
     for k in range(18):
         for r in (2 * k + 3, 2 * k + 4):
             va[r] = v2[r] + jnp.where(weight[r] > 0.0, e[k], 0.0)
-    sweep(va, vb, rhs, cx, cy, cz, weight, first, PLANES)
+    sweep(va, vb, rhs, cx, cy, cz, weight, first, PLANES, PLANES)
 
     def last(i):
-        r = pl.ds(5 + i, SIZE)
-        here, total = around(vb, cx, cy, cz, 5 + i, SIZE)
+        r = pl.ds(5 + i, 32)
+        here, total = around(vb, cx, cy, cz, 5 + i, 32)
         done = (1.0 - OMEGA) * here + weight[r] * (rhs[r] + total)
-        out[pl.ds(i, SIZE)] = roll(done[:, :, :128], -4, 1)[:, :8]
-
-    chunked(32, last, SIZE)
+        out[...] = roll(done[:, :, :128], -4, 1)[:, :8]
+
+    last(0)
 
 
 def call(kernel, name, outs, scratch, *args):

time: 60.3 us -> 54.2 us (0.90)
  Pallas kernels: 19.8 us -> 13.7 us
    pallas_call x8, Pallas kernels: 19.8 us -> 13.7 us  [call(): pl.pallas_call(kernel, name=name, out_shape=[jax.ShapeDtypeStruct(s, F32)...]
where the time goes in v4:
time: 54.2 us; the launch traced here: 54 us
  blocking collectives  20.8 us (38%)
  Pallas kernels  13.7 us (25%)
  waiting for transfers between devices  11.6 us (21%)
  starting transfers between devices  7.2 us (13%)
  other arithmetic  0.67 us (1%)
    all_to_all x1, blocking collectives, paired(): lax.all_to_all(message, everyone, split_axis=0, concat_axis=0, tiled=True...  20.8 us
    pallas_call x8, Pallas kernels, call(): pl.pallas_call(kernel, name=name, out_shape=[jax.ShapeDtypeStruct(s, F32)...  13.7 us
    ppermute x1, waiting for transfers between devices, paired(): got = lax.ppermute(message, ('gx', 'gy'), turns)  3.49 us
    ppermute x1, starting transfers between devices, paired(): got = lax.ppermute(message, 'gz', [(0, 1), (1, 0)])  3 us
    ppermute x1, waiting for transfers between devices, paired(): got = lax.ppermute(message, 'gx', [(0, 2), (2, 0), (1, 3), (3, 1)])  2.57 us
    ppermute x1, starting transfers between devices, paired(): got = lax.ppermute(message, 'gx', [(0, 2), (2, 0), (1, 3), (3, 1)])  2.07 us
    ppermute x1, waiting for transfers between devices, paired(): other = lax.ppermute(mine, 'gx', swap)  2.04 us
    ppermute x1, starting transfers between devices, paired(): got = lax.ppermute(message, ('gx', 'gy'), turns)  1.85 us
  transfers between devices with their start and end apart: 6, of which 6 were waited for; matrix products, arithmetic and copies ran while one was open for 0% of the time, Pallas kernels for 2%

profile of v4, /device:TPU:0, one launch (start us, length us, event | category | flops | bytes accessed | tf_op | source)
XLA Modules:
  0.0 54.0 jit_solution(17149933041223986865)
XLA Ops:
  0.0 1.9 %message.1 = (f32[16,16,128]{2,1,0:T(8,128)S(1)}, f32[3,16,16,128]{3,2,1,0:T(8,128)S(1)}, f32[64,128]{1,0:T(8,128)S(1)}, f32[24,128]{1,0:T(8,128)S(1)}) custom-call(f32[16,16,128]{2,1,0:T(8,128)} %refs_0_.1, f32[3,16,16,128]{3,2,1,0:T(8,128)} %refs_1_.1, s32[8,128]{1,0:T(8,128)} %bitcast.3, s32[8,128]{1,0:T(8,128)} %bitcast.4, f32[8,128]{1,0:T(8,128)} %bitcast.5), custom_call_target="tpu_custom_call" | custom-call | flops 10000000 | bytes 4000000 | tf_op jit(solution)/shard_map/message/pallas_call | solution.py:611
  1.9 3.0 %collective-permute-start = (f32[64,128]{1,0:T(8,128)S(1)}, f32[64,128]{1,0:T(8,128)S(1)}, u32[]{:S(2)}, u32[]{:S(2)}) collective-permute-start(f32[64,128]{1,0:T(8,128)S(1)} %get-tuple-element.29.records), channel_id=1, source_target_pairs={{0,1},{1,0},{2,3},{3,2},{4,5},{5,4},{6,7},{7,6},{8,9},{9,8},{10,11... | collective-permute-start | bytes 98312 | tf_op jit(solution)/shard_map/ppermute | solution.py:641
  4.9 1.1 %source.1 = (f32[18,24,128]{2,1,0:T(8,128)S(1)}, f32[256,256]{1,0:T(8,128)S(1)}, f32[32,128]{1,0:T(8,128)S(1)}) custom-call(f32[16,16,128]{2,1,0:T(8,128)S(1)} %get-tuple-element.27.chi, f32[3,16,16,128]{3,2,1,0:T(8,128)S(1)} %get-tuple-element.28.inducing, f32[64,128]{1,0:T(8,128)S(1)} %get-tuple-element.29.records), custom_call_target="tpu_custom_call" | custom-call | flops 10000000 | bytes 4000000 | tf_op jit(solution)/shard_map/source/pallas_call | solution.py:611
  6.0 0.8 %collective-permute-done.other = f32[64,128]{1,0:T(8,128)S(1)} collective-permute-done((f32[64,128]{1,0:T(8,128)S(1)}, f32[64,128]{1,0:T(8,128)S(1)}, u32[]{:S(2)}, u32[]{:S(2)}) %collective-permute-start) | collective-permute-done | bytes 32800 | tf_op jit(solution)/shard_map/ppermute | solution.py:641
  6.8 1.2 %deposit.1 = (f32[36,16,128]{2,1,0:T(8,128)S(1)}, f32[36,16,128]{2,1,0:T(8,128)S(1)}) custom-call(f32[18,24,128]{2,1,0:T(8,128)S(1)} %get-tuple-element.30.source, f32[24,128]{1,0:T(8,128)S(1)} %get-tuple-element.31.spill, f32[16,16,128]{2,1,0:T(8,128)S(1)} %get-tuple-element.27.chi, f32[256,256]{1,0:T(8,128)S(1)} %get-tuple-element.32.mine, ...), custom_call_target="tpu_custom_call" | custom-call | flops 10000000 | bytes 4000000 | tf_op jit(solution)/shard_map/deposit/pallas_call | solution.py:611
  7.9 0.1 collective-permute-start.1
  8.0 1.6 %collective-permute-done.1.other = f32[36,16,128]{2,1,0:T(8,128)S(1)} collective-permute-done((f32[36,16,128]{2,1,0:T(8,128)S(1)}, f32[36,16,128]{2,1,0:T(8,128)S(1)}, u32[]{:S(2)}, u32[]{:S(2)}) %collective-permute-start.1) | collective-permute-done | bytes 294944 | tf_op jit(solution)/shard_map/ppermute | solution.py:664
  9.6 0.2 pair.1
  9.8 2.1 %collective-permute-start.2 = (f32[9,16,128]{2,1,0:T(8,128)S(1)}, f32[9,16,128]{2,1,0:T(8,128)S(1)}, u32[]{:S(2)}, u32[]{:S(2)}) collective-permute-start(f32[9,16,128]{2,1,0:T(8,128)S(1)} %get-tuple-element.38), channel_id=1, source_target_pairs={{0,16},{16,0},{8,24},{24,8},{1,17},{17,1},{9,25},{25,9},{2,18},{18... | collective-permute-start | bytes 221192 | tf_op jit(solution)/shard_map/ppermute | solution.py:667
  11.9 2.6 %collective-permute-done.2.other = f32[9,16,128]{2,1,0:T(8,128)S(1)} collective-permute-done((f32[9,16,128]{2,1,0:T(8,128)S(1)}, f32[9,16,128]{2,1,0:T(8,128)S(1)}, u32[]{:S(2)}, u32[]{:S(2)}) %collective-permute-start.2) | collective-permute-done | bytes 73760 | tf_op jit(solution)/shard_map/ppermute | solution.py:667
  14.4 0.1 across.1
  14.6 1.8 %collective-permute-start.3 = (f32[39,8,128]{2,1,0:T(8,128)S(1)}, f32[39,8,128]{2,1,0:T(8,128)S(1)}, u32[]{:S(2)}, u32[]{:S(2)}) collective-permute-start(f32[39,8,128]{2,1,0:T(8,128)S(1)} %get-tuple-element.42), channel_id=1, source_target_pairs={{8,2},{2,8},{10,4},{4,10},{12,6},{6,12},{24,18},{18,24},{26,20},{2... | collective-permute-start | bytes 479240 | tf_op jit(solution)/shard_map/ppermute | solution.py:676
  16.4 3.5 %collective-permute-done.3.other = f32[39,8,128]{2,1,0:T(8,128)S(1)} collective-permute-done((f32[39,8,128]{2,1,0:T(8,128)S(1)}, f32[39,8,128]{2,1,0:T(8,128)S(1)}, u32[]{:S(2)}, u32[]{:S(2)}) %collective-permute-start.3) | collective-permute-done | bytes 159776 | tf_op jit(solution)/shard_map/ppermute | solution.py:676
  19.9 2.4 %down.1 = (f32[42,16,256]{2,1,0:T(8,128)S(1)}, f32[42,16,256]{2,1,0:T(8,128)S(1)}, f32[42,16,256]{2,1,0:T(8,128)S(1)}, f32[42,16,256]{2,1,0:T(8,128)S(1)}, f32[16,64,128]{2,1,0:T(8,128)S(1)}) custom-call(f32[42,16,128]{2,1,0:T(8,128)S(1)} %get-tuple-element.39.source_in, f32[42,16,128]{2,1,0:T(8,128)S(1)} %get-tuple-element.40.kappa_in, ...), custom_call_target="tpu_custom_call" | custom-call | flops 10000000 | bytes 4000000 | tf_op jit(solution)/shard_map/down/pallas_call | solution.py:611
  22.3 20.8 %all_to_all.5.mine = f32[16,64,128]{2,1,0:T(8,128)S(1)} all-to-all(f32[16,64,128]{2,1,0:T(8,128)S(1)} %get-tuple-element.44), channel_id=1, replica_groups={{0,1,2,3,4,5,6,7,16,17,18,19,20,21,22,23},{8,9,10,11,12,13,14,15,24,25,..., dimensions={0} | all-to-all | bytes 1048576 | tf_op jit(solution)/shard_map/all_to_all | solution.py:688
  43.1 0.0 collective-permute-start.4
  43.1 2.0 %collective-permute-done.4.other = f32[16,64,128]{2,1,0:T(8,128)} collective-permute-done((f32[16,64,128]{2,1,0:T(8,128)S(1)}, f32[16,64,128]{2,1,0:T(8,128)}, u32[]{:S(2)}, u32[]{:S(2)}) %collective-permute-start.4) | collective-permute-done | bytes 524320 | tf_op jit(solution)/shard_map/ppermute | solution.py:691
  45.1 5.5 %coarse.1.e_in = f32[34,32,128]{2,1,0:T(8,128)S(1)} custom-call(f32[16,64,128]{2,1,0:T(8,128)S(1)} %all_to_all.5.mine, f32[16,64,128]{2,1,0:T(8,128)} %collective-permute-done.4.other), custom_call_target="tpu_custom_call" | custom-call | flops 10000000 | bytes 4000000 | tf_op jit(solution)/shard_map/coarse/pallas_call | solution.py:611
  50.6 1.4 %up.1 = f32[32,8,128]{2,1,0:T(8,128)S(1)} custom-call(f32[34,32,128]{2,1,0:T(8,128)S(1)} %coarse.1.e_in, f32[42,16,256]{2,1,0:T(8,128)S(1)} %get-tuple-element.45.rhs, f32[42,16,256]{2,1,0:T(8,128)S(1)} %get-tuple-element.46.kappa, f32[42,16,256]{2,1,0:T(8,128)S(1)} %get-tuple-element.47.weight, f32[42,16,256]{2,1,0:T(8,128)S(1)} %get-tuple-element.48.v2), custom_call_target="tpu_custom_call" | custom-call | flops 10000000 | bytes 4000000 | tf_op jit(solution)/shard_map/up/pallas_call | solution.py:611
  52.0 0.2 collective-permute-start.5
  52.2 1.1 %collective-permute-done.5 = f32[16,8,128]{2,1,0:T(8,128)S(1)} collective-permute-done((f32[16,8,128]{2,1,0:T(8,128)S(1)}, f32[16,8,128]{2,1,0:T(8,128)S(1)}, u32[]{:S(2)}, u32[]{:S(2)}) %collective-permute-start.5) | collective-permute-done | bytes 65568 | tf_op jit(solution)/shard_map/ppermute | solution.py:712
  53.3 0.7 %maximum_select_fusion = f32[16,16,128]{2,1,0:T(8,128)} fusion(f32[16,8,128]{2,1,0:T(8,128)S(1)} %collective-permute-done.5, f32[16,8,128]{2,1,0:T(8,128)S(1)} %get-tuple-element.49, pred[]{:T(512)S(6)} %eq.3), kind=kLoop, calls=%fused_computation | loop fusion | flops 98304 | bytes 262145 | tf_op jit(solution)/shard_map/jit(_where)/select_n | solution.py:713
  (1 shorter events, 0.0 us)
Async XLA Ops:
  1.9 4.9 %collective-permute-start = (f32[64,128]{1,0:T(8,128)S(1)}, f32[64,128]{1,0:T(8,128)S(1)}, u32[]{:S(2)}, u32[]{:S(2)}) collective-permute-start(f32[64,128]{1,0:T(8,128)S(1)} %get-tuple-element.29.records), channel_id=1, source_target_pairs={{0,1},{1,0},{2,3},{3,2},{4,5},{5,4},{6,7},{7,6},{8,9},{9,8},{10,11... | collective-permute-start | bytes 98312 | tf_op jit(solution)/shard_map/ppermute | solution.py:641
  7.9 1.6 %collective-permute-start.1 = (f32[36,16,128]{2,1,0:T(8,128)S(1)}, f32[36,16,128]{2,1,0:T(8,128)S(1)}, u32[]{:S(2)}, u32[]{:S(2)}) collective-permute-start(f32[36,16,128]{2,1,0:T(8,128)S(1)} %get-tuple-element.34), channel_id=1, source_target_pairs={{0,8},{8,0},{16,24},{24,16},{1,9},{9,1},{17,25},{25,17},{2,10},{10... | collective-permute-start | bytes 884744 | tf_op jit(solution)/shard_map/ppermute | solution.py:664
  9.8 4.6 %collective-permute-start.2 = (f32[9,16,128]{2,1,0:T(8,128)S(1)}, f32[9,16,128]{2,1,0:T(8,128)S(1)}, u32[]{:S(2)}, u32[]{:S(2)}) collective-permute-start(f32[9,16,128]{2,1,0:T(8,128)S(1)} %get-tuple-element.38), channel_id=1, source_target_pairs={{0,16},{16,0},{8,24},{24,8},{1,17},{17,1},{9,25},{25,9},{2,18},{18... | collective-permute-start | bytes 221192 | tf_op jit(solution)/shard_map/ppermute | solution.py:667
  14.6 5.3 %collective-permute-start.3 = (f32[39,8,128]{2,1,0:T(8,128)S(1)}, f32[39,8,128]{2,1,0:T(8,128)S(1)}, u32[]{:S(2)}, u32[]{:S(2)}) collective-permute-start(f32[39,8,128]{2,1,0:T(8,128)S(1)} %get-tuple-element.42), channel_id=1, source_target_pairs={{8,2},{2,8},{10,4},{4,10},{12,6},{6,12},{24,18},{18,24},{26,20},{2... | collective-permute-start | bytes 479240 | tf_op jit(solution)/shard_map/ppermute | solution.py:676
  43.1 2.0 %collective-permute-start.4 = (f32[16,64,128]{2,1,0:T(8,128)S(1)}, f32[16,64,128]{2,1,0:T(8,128)}, u32[]{:S(2)}, u32[]{:S(2)}) collective-permute-start(f32[16,64,128]{2,1,0:T(8,128)S(1)} %all_to_all.5.mine), channel_id=1, source_target_pairs={{0,8},{8,0},{16,24},{24,16},{1,9},{9,1},{17,25},{25,17},{2,10},{10... | collective-permute-start | bytes 1572872 | tf_op jit(solution)/shard_map/ppermute | solution.py:691
  52.0 1.3 %collective-permute-start.5 = (f32[16,8,128]{2,1,0:T(8,128)S(1)}, f32[16,8,128]{2,1,0:T(8,128)S(1)}, u32[]{:S(2)}, u32[]{:S(2)}) collective-permute-start(f32[16,8,128]{2,1,0:T(8,128)S(1)} %get-tuple-element.50), channel_id=1, source_target_pairs={{0,8},{8,0},{16,24},{24,16},{1,9},{9,1},{17,25},{25,17},{2,10},{10... | collective-permute-start | bytes 196616 | tf_op jit(solution)/shard_map/ppermute | solution.py:712

commit v5 on v4

--- a/solution.py
+++ b/solution.py
@@ -140,9 +140,9 @@
     return total
 
 
-def halving(offset, factor):
-    shape = (128, 128)
-    return jnp.where((iota(shape, 0) >> 1) + offset == iota(shape, 1), factor, 0.0).astype(F32)
+def halving(lanes):
+    shape = (lanes, 128)
+    return jnp.where((iota(shape, 0) >> 1) == iota(shape, 1), 0.125, 0.0).astype(F32)
 
 
 def place():
@@ -164,43 +164,53 @@
     for copy in copies:
         copy.wait()
     lane = iota((16, 128), 1)
-    turn = 4 - 3 * t
-    wanted = pick(t, (lane < 4).astype(jnp.int32), ((lane >= 1) & (lane < 5)).astype(jnp.int32)) > 0
-    k, mx, my, mz = [jnp.zeros((16, 128), F32) for _ in range(4)]
+    turn = 11 - 10 * t
+    wanted = pick(t, (lane < 11).astype(jnp.int32), ((lane >= 1) & (lane < 12)).astype(jnp.int32)) > 0
+    packs = [[jnp.zeros((16, 128), F32)] * 2 for _ in range(4)]
     for x in range(16):
         near = jnp.where(wanted, pltpu.roll(chi[x], turn, 1), 0.0)
-        parts = [near * pltpu.roll(inducing[d, x], turn, 1) for d in range(3)]
-        one = jnp.where(wanted, 1.0 + near, 0.0)
-        k, mx, my, mz = [total + roll(part, 8 * x, 1) for total, part in zip((k, mx, my, mz), [one] + parts)]
-    dx = jnp.where(lane < 120, roll(mx, -8, 1), 0.0) - jnp.where(lane >= 8, roll(mx, 8, 1), 0.0)
+        parts = [jnp.where(wanted, 1.0 + near, 0.0)]
+        parts += [near * pltpu.roll(inducing[d, x], turn, 1) for d in range(3)]
+        for pack, part in zip(packs, parts):
+            pack[x // 8] = pack[x // 8] + roll(part, 16 * (x % 8), 1)
+    k, mx, my, mz = [jnp.concatenate(pack, 1) for pack in packs]
+    lane = iota((16, 256), 1)
+    dx = jnp.where(lane < 240, roll(mx, -16, 1), 0.0) - jnp.where(lane >= 16, roll(mx, 16, 1), 0.0)
     y = stretch(my)
     dz = roll(mz, -1, 1) - roll(mz, 1, 1)
     body = -0.5 * (stretch(dx + dz) + (roll(y, -1, 0) - roll(y, 1, 0)))
     lane = iota((24, 128), 1)
-    slot = lane & 7
-    ends = 0.5 * (jnp.where((lane >= 8) & (lane < 16), roll(stretch(mx), 16, 1), 0.0) - jnp.where(lane < 8, stretch(mx), 0.0))
-
-    def four(tile):
+    before, after = stretch(mx[:, :128]), stretch(mx[:, 128:])
+    ends = 0.5 * (jnp.where((lane >= 16) & (lane < 32), roll(after, 32, 1), 0.0) - jnp.where(lane < 16, before, 0.0))
+
+    def eleven(tile):
         tile = pick(t, roll(tile, -1, 1), tile)
-        return jnp.where(slot < 4, tile, 0.0)
-
-    own = pick(t, jnp.where(slot == 4, body, 0.0), jnp.where(slot == 0, body, 0.0))
-    spill[...] = pick(t, roll(own, -3, 1), roll(own, 2, 1))
-    message[0:24] = four(body) + jnp.where(slot >= 4, stretch(pick(t, roll(k, 4, 1), roll(k, 3, 1))), 0.0)
-    message[24:48] = four(ends)
-    message[48:56] = value[...]
-    message[56:64] = (dest[...] * 32768 + cell[...]).astype(F32)
+        return jnp.where((iota(tile.shape, 1) & 15) < 11, tile, 0.0)
+
+    slot = iota((24, 256), 1) & 15
+    own = pick(t, jnp.where(slot == 11, body, 0.0), jnp.where(slot == 0, body, 0.0))
+    own = pick(t, roll(own, -10, 1), roll(own, 9, 1))
+    body = eleven(body)
+    k = pick(t, k, roll(k, -1, 1))
+    for i in range(2):
+        cut = slice(128 * i, 128 * (i + 1))
+        spill[24 * i : 24 * (i + 1)] = own[:, cut]
+        message[24 * i : 24 * (i + 1)] = body[:, cut]
+        message[72 + 16 * i : 88 + 16 * i] = k[:, cut]
+    message[48:72] = eleven(ends)
+    message[104:112] = value[...]
+    message[112:120] = (dest[...] * 32768 + cell[...]).astype(F32)
 
 
 def spread_records(records, t, at_row, hi, mid, lo):
     spot = iota((256, 128), 0)
     for j in range(8):
-        value = records[48 + j : 49 + j, :]
-        code = records[56 + j : 57 + j, :].astype(jnp.int32)
+        value = records[104 + j : 105 + j, :]
+        code = records[112 + j : 113 + j, :].astype(jnp.int32)
         cells = code & 32767
         z = ((code >> 15) - t) * 128 + (cells & 127)
-        far = z - 128 + 131 * t
-        column = jnp.where((far >= 0) & (far < 3), z + 1 + 130 * t, 255)
+        far = z - 128 + 138 * t
+        column = jnp.where((far >= 0) & (far < 10), z + 1 + 137 * t, 255)
         column = jnp.where((z >= 0) & (z < 128), z, column)
         cut = slice(128 * j, 128 * (j + 1))
         at_row[:, cut] = jnp.where(spot == (cells >> 7), 1.0, 0.0).astype(BF16)
@@ -217,7 +227,7 @@
     return total
 
 
-def source_kernel(chi, inducing, records, source, total, coarse, sums, at_row, hi, mid, lo):
+def source_kernel(chi, inducing, records, source, total, at_row, hi, mid, lo):
     _, _, _, t = place()
     lane = iota((16, 128), 1)
     zero = jnp.zeros((16, 128), F32)
@@ -232,32 +242,31 @@
         else:
             source[i] = -0.5 * stretch(flat)
     total[...] = spread_records(records, t, at_row, hi, mid, lo)
-    sums[...] = pair_sums(1.0 + chi[...]).reshape(128, 128)
-    halves = sums[pl.ds(0, 64, stride=2), :] + sums[pl.ds(1, 64, stride=2), :]
-    coarse[...] = dot(halves[:32], halving(0, 0.125)) + dot(halves[32:], halving(64, 0.125))
 
 
 def deposit_kernel(source, spill, chi, mine, other, own, sent, all_, at_row, hi, mid, lo):
     _, c, _, t = place()
     total = mine[...] + spread_records(other, t, at_row, hi, mid, lo)
     lane = iota((24, 128), 1)
-    halo = other[0:24] + spill[...]
+    halo = [other[24 * i : 24 * (i + 1)] + spill[24 * i : 24 * (i + 1)] for i in range(2)]
     for i in range(18):
-        if 1 <= i <= 16:
-            at = 16 * (i - 1)
-            got = stretch(total[at : at + 16, 128:])
-            halo = halo + roll(jnp.where(lane < 4, got, 0.0), 8 * (i - 1), 1)
-            add = stretch(total[at : at + 16, :128])
-            near = pick(t, roll(other[0:24], 127 - 8 * (i - 1), 1), roll(other[0:24], -3 - 8 * (i - 1), 1))
+        x = i - 1
+        if 0 <= x < 16:
+            got = stretch(total[16 * x : 16 * x + 16, 128:])
+            halo[x // 8] = halo[x // 8] + roll(jnp.where(lane < 16, got, 0.0), 16 * (x % 8), 1)
+            add = stretch(total[16 * x : 16 * x + 16, :128])
+            tile, by = other[24 * (x // 8) : 24 * (x // 8) + 24], 16 * (x % 8)
         else:
             add = jnp.zeros((24, 128), F32)
-            by = 0 if i == 0 else -8
-            near = pick(t, roll(other[24:48], 127 + by, 1), roll(other[24:48], -3 + by, 1))
+            tile, by = other[48:72], 0 if i == 0 else 16
+        near = pick(t, roll(tile, 127 - by, 1), roll(tile, -10 - by, 1))
         all_[i] = source[i] + add + jnp.where(lane == 127 - 127 * t, near, 0.0)
     for i in range(16):
         all_[18 + i] = stretch(1.0 + chi[i])
-    all_[34] = halo
-    all_[35] = other[24:48]
+    for i in range(2):
+        all_[34 + i] = halo[i]
+        all_[37 + i] = stretch(other[72 + 16 * i : 88 + 16 * i])
+    all_[36] = other[48:72]
     keep, give = pl.multiple_of(8 * c, 8), pl.multiple_of(8 - 8 * c, 8)
     own[...] = all_[:, pl.ds(keep, 16), :]
     sent[...] = all_[:, pl.ds(give, 16), :]
@@ -273,18 +282,25 @@
     kappa[pl.ds(5 + 16 * c, 16)] = own[18:34]
     kappa[pl.ds(low + 1, 16)] = other[18:34]
     lane = iota((16, 128), 1)
-    tiles = [jnp.zeros((16, 128), F32)] * 3
+    tiles = [jnp.zeros((16, 128), F32)] * 12
     for side in range(2):
-        cells = roll(pick(c ^ side, own[34], other[34]), 40, 1)
-        ends = pick(c ^ side, own[35], other[35])
-        before, after = jnp.where(lane < 4, ends, 0.0), jnp.where((lane >= 8) & (lane < 12), ends, 0.0)
-        tiles[side] = tiles[side] + jnp.where(lane >= 40, cells, 0.0) + roll(before, 32, 1)
-        tiles[side + 1] = tiles[side + 1] + jnp.where(lane < 40, cells, 0.0) + roll(after, 32, 1)
-    for i in range(3):
+        for start, at in ((34, 0), (37, 6)):
+            for i in range(2):
+                cells = roll(pick(c ^ side, own[start + i], other[start + i]), 80, 1)
+                n = at + 2 * side + i
+                tiles[n] = tiles[n] + jnp.where(lane >= 80, cells, 0.0)
+                tiles[n + 1] = tiles[n + 1] + jnp.where(lane < 80, cells, 0.0)
+        ends = roll(pick(c ^ side, own[36], other[36]), 64, 1)
+        n = 2 * side
+        tiles[n] = tiles[n] + jnp.where((lane >= 64) & (lane < 80), ends, 0.0)
+        tiles[n + 2] = tiles[n + 2] + jnp.where((lane >= 80) & (lane < 96), ends, 0.0)
+    for i in range(12):
         halo[i] = tiles[i]
     message[0:4] = source[pl.ds(34 - 30 * p, 4)]
     message[4:8] = kappa[pl.ds(33 - 28 * p, 4)]
-    message[8] = jnp.where(lane < 40, pick(p, roll(tiles[2], -8, 1), roll(tiles[0], -32, 1)), 0.0)
+    for i in range(2):
+        low = jnp.where(lane < 64, roll(tiles[6 * i], -64, 1), roll(tiles[6 * i + 1], 64, 1))
+        message[8 + i] = jnp.where(lane < 80, pick(p, roll(tiles[6 * i + 4], -16, 1), low), 0.0)
 
 
 def across_kernel(source_in, kappa_in, halo_in, other, source, kappa, halo, message):
@@ -295,9 +311,14 @@
     source[pl.ds(at, 4)] = source[pl.ds(at, 4)] + other[0:4]
     kappa[pl.ds(37 - 36 * p, 4)] = other[4:8]
     zero = jnp.zeros((16, 128), F32)
-    halo[0] = halo_in[0] + pick(p, zero, roll(other[8], 8, 1))
-    halo[1] = halo_in[1]
-    halo[2] = halo_in[2] + pick(p, roll(other[8], 32, 1), zero)
+    lane = iota((16, 128), 1)
+    halo[...] = halo_in[...]
+    for i in range(2):
+        got = other[8 + i]
+        wide = roll(got, 64, 1)
+        halo[6 * i] = halo[6 * i] + pick(p, zero, roll(got, 16, 1))
+        halo[6 * i + 4] = halo[6 * i + 4] + pick(p, jnp.where(lane >= 64, wide, 0.0), zero)
+        halo[6 * i + 5] = halo[6 * i + 5] + pick(p, jnp.where(lane < 16, wide, 0.0), zero)
     first = 5 - 4 * p
 
     def cut(s, k):
@@ -309,7 +330,7 @@
         message[pl.ds(i, SIZE)] = cut(source[pl.ds(first + i, SIZE)], kappa[pl.ds(first + i, SIZE)])
 
     chunked(PLANES, body, SIZE)
-    message[PLANES:] = cut(halo[...], halo[...])
+    message[PLANES:] = cut(halo[0:6], halo[6:12])
 
 
 def chunked(count, body, size=4):
@@ -379,13 +400,13 @@
 
 
 def down_kernel(
-    n_gy, source_in, kappa_in, halo_in, other, kappa1, rhs, kappa, weight, v2, message,
-    cx, cy, cz, diag, v1, sums, halo,
+    n_gy, source_in, kappa_in, halo_in, other, left, kappa, weight, v, along, beside, message,
+    rhs, cx, cy, cz, diag, v1, v2, sums, halo,
 ):
     p, c, b, t = place()
     first = 5 - 4 * p
     edge = jnp.where(c == 0, b == 0, b == n_gy - 1).astype(jnp.int32)
-    for ref in (kappa, cx, weight, v1, v2, rhs):
+    for ref in (kappa, cx, weight, v1, v2, left):
         ref[0:5] = jnp.zeros((5, 16, 256), F32)
         ref[37:42] = jnp.zeros((5, 16, 256), F32)
 
@@ -398,10 +419,11 @@
         return pick(c, roll(s, 1, 1), roll(s, 11, 1)), pick(c, roll(k, -4, 1), roll(k, 8, 1))
 
     s, k = merge(other[PLANES:])
-    halo[...] = halo_in[...] + jnp.where((iota(s.shape, 2) & 7) < 4, s, k)
+    halo[0:6] = halo_in[0:6] + s
+    halo[6:12] = halo_in[6:12] + k
     lane = iota((16, 128), 1)
-    s_lanes = pick(t, (lane < 3).astype(jnp.int32), (lane >= 125).astype(jnp.int32)) > 0
-    k_lanes = pick(t, (lane < 4).astype(jnp.int32), (lane >= 124).astype(jnp.int32)) > 0
+    s_lanes = pick(t, (lane < 10).astype(jnp.int32), (lane >= 118).astype(jnp.int32)) > 0
+    k_lanes = pick(t, (lane < 11).astype(jnp.int32), (lane >= 117).astype(jnp.int32)) > 0
 
     def enter(i):
         r = first + i
@@ -409,31 +431,104 @@
         s, k = merge(other[pl.ds(i, SIZE)])
         far_s, far_k = [], []
         for j in range(SIZE):
-            tile = halo[(r + j) >> 4]
-            by = 8 * ((r + j) & 15)
-            far_s.append(jnp.where(s_lanes, pltpu.roll(tile, (127 - by - 2 * t) & 127, 1), 0.0)[None])
-            far_k.append(jnp.where(k_lanes, pltpu.roll(tile, (124 - by - 4 * t) & 127, 1), 0.0)[None])
+            tile, by = (r + j) >> 3, 16 * ((r + j) & 7)
+            far_s.append(jnp.where(s_lanes, pltpu.roll(halo[tile], (127 - by - 9 * t) & 127, 1), 0.0)[None])
+            far_k.append(jnp.where(k_lanes, pltpu.roll(halo[6 + tile], (128 - by - 11 * t) & 127, 1), 0.0)[None])
         rhs[rows] = jnp.concatenate([source_in[rows] + s, jnp.concatenate(far_s, 0)], 2)
         kappa[rows] = jnp.concatenate([kappa_in[rows] + k, jnp.concatenate(far_k, 0)], 2)
 
     chunked(PLANES, enter, SIZE)
     faces(kappa, cx, cy, cz, weight, diag, first, PLANES, 1.0, False, PLANES)
+
+    def coarse(fine):
+        two = pair_sums(fine)
+        n = 16 * two.shape[0]
+        two = two.reshape(n, 256)
+        halves = []
+        for i in range(2):
+            at = 288 * i
+            sums[at : at + n] = two[:, 128 * i : 128 * (i + 1)]
+            halves.append(sums[pl.ds(at, n // 2, stride=2), :] + sums[pl.ds(at + 1, n // 2, stride=2), :])
+        return dot(jnp.concatenate(halves, 1), halving(256)).reshape(n // 16, 8, 128)
 
     rows = pl.ds(first, PLANES)
     v1[rows] = weight[rows] * rhs[rows]
     sweep(v1, v2, rhs, cx, cy, cz, weight, first, PLANES, PLANES)
-
-    two = pair_sums(resid(v2, rhs, cx, cy, cz, diag, 5, 32))
-    sums[...] = two[:, :, :128].reshape(256, 128)
-    halves = sums[pl.ds(0, 128, stride=2), :] + sums[pl.ds(1, 128, stride=2), :]
-    packed = dot(halves[:64], halving(0, 0.125)) + dot(halves[64:], halving(64, 0.125))
-    low = iota((8, 128), 0) < 4
-    for j in range(4):
-        even, odd = packed[16 * j : 16 * j + 8], packed[16 * j + 8 : 16 * j + 16]
-        tile = jnp.where(low, roll(even, -2, 0), roll(odd, 2, 0))
-        for d in range(message.shape[0]):
-            message[d, 8 * j : 8 * j + 8, :] = tile
-            message[d, 32 + 8 * j : 40 + 8 * j, :] = kappa1[8 * j : 8 * j + 8, :]
+    left[rows] = resid(v2, rhs, cx, cy, cz, diag, first, PLANES)
+    v[...] = roll(v2[5:37, :, :128], -4, 1)[:, :8]
+    r1 = coarse(left[5:37])
+    k1 = coarse(kappa[3:39])
+    k = k1[1:17]
+    total = (k1[2:] + k1[:16]) + (roll(k, -1, 1) + roll(k, 1, 1)) + (roll(k, -1, 2) + roll(k, 1, 2))
+    v1c = jnp.where(k > 0.0, OMEGA / jnp.where(k > 0.0, 0.125 * (6.0 * k + total), 1.0), 0.0) * r1
+    tiles = jnp.where(iota(r1.shape, 1) < 4, roll(r1, -2, 1), roll(k, 2, 1))
+    along[0:16] = tiles
+    beside[0:16] = tiles
+    sub = iota((8, 128), 0)
+    for i in range(2):
+        far, near = jnp.zeros((8, 128), F32), jnp.zeros((8, 128), F32)
+        for j in range(8):
+            cells = v1c[8 * i + j]
+            last, start = roll(cells, j - 5, 0), roll(cells, j - 2, 0)
+            far = jnp.where(sub == j, pick(c, last, start), far)
+            near = jnp.where(sub == j, pick(c, start, last), near)
+        along[16 + i] = far
+        beside[16 + i] = near
+    message[0:4] = along[pl.ds(12 - 12 * p, 4)]
+    message[4] = roll(pick(p, v1c[12], v1c[3]), -2, 0)
+    message[5] = roll(pick(p, v1c[15], v1c[0]), -2, 0)
+
+
+def middle_kernel(n_gy, mine, across, got, other, r1, k1, weight, v2, message, cx, cy, cz, diag, v1, sums, flat):
+    p, c, b, t = place()
+    edge = jnp.where(c == 0, b == 0, b == n_gy - 1).astype(jnp.int32)
+    for ref in (r1, k1, cx, weight, v1, v2):
+        ref[...] = jnp.zeros_like(ref)
+    sub = iota((8, 128), 0)
+    zero = jnp.zeros((8, 128), F32)
+    middle = (sub >= 2) & (sub < 6)
+
+    def around_mine(at):
+        s, g = other[at], pick(edge, got[at], zero)
+        return pick(c, g, s), pick(c, s, g)
+
+    def joined(low, o, high):
+        first = jnp.where(middle, roll(low, 2, 0), jnp.where(sub >= 6, roll(o, 6, 0), 0.0))
+        return first, jnp.where(sub < 2, roll(o, -2, 0), jnp.where(middle, roll(high, 2, 0), 0.0))
+
+    for j in range(20):
+        row = 6 + j if j < 16 else 6 + j - 20 * p
+        o = mine[j] if j < 16 else across[j - 16]
+        low, high = around_mine(j if j < 16 else j + 2)
+        r1[row, 0:8], r1[row, 8:16] = joined(low, o, high)
+        k1[row, 0:8], k1[row, 8:16] = joined(*[roll(tile, 4, 0) for tile in (low, o, high)])
+    first = 6 - 4 * p
+    faces(k1, cx, cy, cz, weight, diag, first, 20, 0.25, False, 20)
+    rows = pl.ds(first, 20)
+    v1[rows] = weight[rows] * r1[rows]
+    ends = []
+    for i in range(2):
+        low, high = around_mine(16 + i)
+        ends += [(6 + 8 * i + j, roll(low, 2 - j, 0), roll(high, 5 - j, 0)) for j in range(8)]
+    low, high = around_mine(23)
+    ends.append((22 - 17 * p, roll(low, 2, 0), roll(high, 2, 0)))
+    for r, low, high in ends:
+        v1[r, 0:8] = jnp.where(sub == 2, low, v1[r, 0:8])
+        v1[r, 8:16] = jnp.where(sub == 5, high, v1[r, 8:16])
+    low, high = around_mine(22)
+    r = 25 - 23 * p
+    v1[r, 0:8], v1[r, 8:16] = joined(low, across[4], high)
+    sweep(v1, v2, r1, cx, cy, cz, weight, first, 20, 20)
+    lane = iota((8, 128), 1)
+    tile = zero
+    for i, fine in enumerate((resid(v2, r1, cx, cy, cz, diag, 6, 16), k1[6:22])):
+        sums[...] = pair_sums(fine).reshape(128, 128)
+        flat[...] = dot(sums[pl.ds(0, 64, stride=2), :] + sums[pl.ds(1, 64, stride=2), :], halving(128))
+        for y in range(2):
+            part = jnp.where(lane < 32, flat[pl.ds(3 + y, 8, stride=8), :], 0.0)
+            tile = tile + roll(part, 64 * i + 32 * y, 1)
+    for d in range(message.shape[0]):
+        message[d] = tile
 
 
 def shift(x, by, axis):
@@ -479,7 +574,7 @@
 
 def halved_yz(scratch, nx, ny):
     halves = scratch[pl.ds(0, nx * ny, stride=2), :] + scratch[pl.ds(1, nx * ny, stride=2), :]
-    return dot(halves, halving(0, 0.125)).reshape(nx, ny, 128)
+    return dot(halves, halving(128)).reshape(nx, ny, 128)
 
 
 def doubling():
@@ -501,107 +596,83 @@
     return jnp.broadcast_to(e[:, None], (nx, 2, ny, 128)).reshape(2 * nx, ny, 128)
 
 
-def coarse_kernel(n_gy, mine, other, e_out, k1, r1, cx, cy, cz, weight, diag, va, vb, sums):
-    p, c, b, t = place()
-    n_y = 8 * n_gy
-    for ref in (k1, cx, va, vb):
-        ref[0] = jnp.zeros((n_y, 128), F32)
-        ref[33] = jnp.zeros((n_y, 128), F32)
-    left = iota((8, 128), 1) < 64
-    top = iota((8, 128), 0) < 4
-    for gx in range(4):
-        for gy in range(n_gy):
-            for x in range(4):
-                cut = slice(32 + 8 * x, 40 + 8 * x)
-                both = [[ref[((gx >> 1) * n_gy + gy) * 2 + gz, cut, :] for ref in (mine, other)] for gz in range(2)]
-                near, far = [pick(c ^ (gx & 1), a, o) for a, o in both]
-                spot = slice(8 * gy, 8 * gy + 8)
-                k1[1 + 8 * gx + x, spot, :] = jnp.where(left, near, roll(far, 64, 1))
-                k1[1 + 8 * gx + 4 + x, spot, :] = jnp.where(left, roll(near, 64, 1), far)
-    for pp in range(2):
-        for gy in range(n_gy):
-            for j in range(4):
-                cut = slice(8 * j, 8 * j + 8)
-                evens, odds = [], []
-                for gz in range(2):
-                    a = mine[(pp * n_gy + gy) * 2 + gz, cut, :]
-                    o = other[(pp * n_gy + gy) * 2 + gz, cut, :]
-                    first, second = pick(c, a, o), pick(c, o, a)
-                    evens.append(jnp.where(top, first, roll(second, 4, 0)))
-                    odds.append(jnp.where(top, roll(first, 4, 0), second))
-                spot = slice(8 * gy, 8 * gy + 8)
-                for odd, (near, far) in enumerate((evens, odds)):
-                    r1[1 + 16 * pp + 2 * j + odd, spot, :] = jnp.where(left, near, roll(far, 64, 1))
-                    r1[1 + 16 * pp + 8 + 2 * j + odd, spot, :] = jnp.where(left, roll(near, 64, 1), far)
-    faces(k1, cx, cy, cz, weight, diag, 1, 32, 0.25, True, 32)
-
-    va[1:33] = weight[1:33] * r1[1:33]
-    sweep(va, vb, r1, cx, cy, cz, weight, 1, 32, 32)
-    sums[...] = pair_sums(resid(vb, r1, cx, cy, cz, diag, 1, 32)).reshape(16 * n_y, 128)
-    r2 = halved_yz(sums, 16, n_y // 2)
-
-    sums[...] = pair_sums(k1[1:33]).reshape(16 * n_y, 128)
-    k2 = halved_yz(sums, 16, n_y // 2)
-    middle = Level(k2, 0.0625)
-    v2 = middle.weight * r2
-    v2 = middle.sweep(v2, r2)
-    r3 = halved(middle.resid(v2, r2), sums)
-    bottom = Level(halved(k2, sums), 0.015625)
-    v3 = bottom.weight * r3
-    for _ in range(COARSE_SWEEPS - 1):
-        v3 = bottom.sweep(v3, r3)
-    v2 = v2 + doubled(v3, sums)
-    for _ in range(SMOOTH):
-        v2 = middle.sweep(v2, r2)
-    e1 = doubled_yz(v2, sums)
-    for i in range(16):
-        vb[1 + 2 * i] = vb[1 + 2 * i] + e1[i]
-        vb[2 + 2 * i] = vb[2 + 2 * i] + e1[i]
-    sweep(vb, va, r1, cx, cy, cz, weight, 1, 32, 32)
-    sweep(va, vb, r1, cx, cy, cz, weight, 1, 32, 32)
-    e_out[...] = vb[...]
-
-
-def up_kernel(n_gy, e_in, rhs, kappa, weight, v2, out, cx, cy, cz, va, vb, tall):
+def up_kernel(
+    n_gy, blocks, r1, k1, w1, v21, left, kappa, weight, v2, out,
+    r2, k2, tall, flat, sums, fx, fy, fz, ua, ub, cx, cy, cz, va, vb,
+):
     p, c, b, t = place()
     first = 5 - 4 * p
-    n_y = 8 * n_gy
+    n_y = 4 * n_gy
     for ref in (va, vb, cx):
         ref[0:5] = jnp.zeros((5, 16, 256), F32)
         ref[37:42] = jnp.zeros((5, 16, 256), F32)
-
-    def face(i):
-        near = kappa[pl.ds(first + i, PLANES + 1)]
-        r, k = pl.ds(first + i, PLANES), near[:PLANES]
-        cx[r] = 0.5 * (k + near[1:])
-        cy[r] = 0.5 * (k + roll(k, -1, 1))
-        cz[r] = 0.5 * (k + roll(k, -1, 2))
-
-    face(0)
-    tall[:, 0:8, :] = jnp.zeros((18, 8, 128), F32)
-    tall[:, 2 * n_y : 2 * n_y + 8, :] = jnp.zeros((18, 8, 128), F32)
-    for k in range(18):
-        e = e_in[16 * p + k]
-        tall[k, pl.ds(4, n_y, stride=2), :] = e
-        tall[k, pl.ds(5, n_y, stride=2), :] = e
-    window = tall[:, pl.ds(pl.multiple_of(16 * b + 8 * c, 8), 16), :]
+    for ref in (fx, ua, ub):
+        ref[...] = jnp.zeros_like(ref)
+
+    lane = iota((8, 128), 1)
+    for y in range(n_y):
+        gy, gc, low = y // 4, y // 2 % 2, y % 2
+        for gp in range(2):
+            at = ((2 * gp + gc) * n_gy + gy) * 2
+            near, far = blocks[at], blocks[at + 1]
+            for ref, start in ((r2, 32 * low), (k2, 64 + 32 * low)):
+                cells = jnp.where(lane < 64, roll(far, 32 - start, 1), 0.0)
+                ref[y, 8 * gp : 8 * gp + 8, :] = jnp.where(lane < 32, roll(near, -start, 1), cells)
+    middle, rhs2 = Level(k2[...], 0.0625), r2[...]
+    m2 = middle.weight * rhs2
+    m2 = middle.sweep(m2, rhs2)
+    rhs3 = halved(middle.resid(m2, rhs2), sums)
+    bottom = Level(halved(k2[...], sums), 0.015625)
+    m3 = bottom.weight * rhs3
+    for _ in range(COARSE_SWEEPS - 1):
+        m3 = bottom.sweep(m3, rhs3)
+    m2 = m2 + doubled(m3, sums)
+    for _ in range(SMOOTH):
+        m2 = middle.sweep(m2, rhs2)
+
+    shape = (128, 128)
+    z = iota(shape, 1)
+    z = jnp.where(z < 96, z, z - 128)
+    spread = jnp.where(32 * t + (z >> 1) == iota(shape, 0), 1.0, 0.0).astype(F32)
+    tall[...] = jnp.zeros_like(tall)
+    tall[4 : 4 + n_y, 8:24, :] = dot(m2.reshape(16 * n_y, 128), spread).reshape(n_y, 16, 128)
+    for j in range(8):
+        cells = tall[4 * b + 2 * c + 1 + j]
+        flat[64 * j : 64 * j + 32, :] = cells
+        flat[64 * j + 32 : 64 * j + 64, :] = cells
+    for i in range(14):
+        e = pick(p, flat[pl.ds(5 + i, 16, stride=32), :], flat[pl.ds(13 + i, 16, stride=32), :])
+        for r in (2 * i, 2 * i + 1):
+            ua[r] = v21[r] + jnp.where(w1[r] > 0.0, e, 0.0)
+    at = 6 - 4 * p
+    rows = pl.ds(at, 20)
+    near = k1[pl.ds(at, 21)]
+    k = near[:20]
+    fx[rows] = 0.125 * (k + near[1:])
+    fy[rows] = 0.125 * (k + roll(k, -1, 1))
+    fz[rows] = 0.125 * (k + roll(k, -1, 2))
+    sweep(ua, ub, r1, fx, fy, fz, w1, at, 20, 20)
+    sweep(ub, ua, r1, fx, fy, fz, w1, at, 20, 20)
+
+    e = roll(ua[5:23], -4, 1)[:, :8].reshape(144, 128)
+    flat[pl.ds(0, 144, stride=2), :] = e
+    flat[pl.ds(1, 144, stride=2), :] = e
     shape = (128, 256)
-    z = iota(shape, 1)
-    z = jnp.where(z < 192, z, z - 256)
-    spread = jnp.where(64 * t + (z >> 1) == iota(shape, 0), 1.0, 0.0).astype(F32)
-    e = dot(window.reshape(288, 128), spread).reshape(18, 16, 256)
+    spread = jnp.where((iota(shape, 1) >> 1) == iota(shape, 0), 1.0, 0.0).astype(F32)
+    e = dot(flat[0:288, :], spread).reshape(18, 16, 256)
     for k in range(18):
         for r in (2 * k + 3, 2 * k + 4):
-            va[r] = v2[r] + jnp.where(weight[r] > 0.0, e[k], 0.0)
-    sweep(va, vb, rhs, cx, cy, cz, weight, first, PLANES, PLANES)
-
-    def last(i):
-        r = pl.ds(5 + i, 32)
-        here, total = around(vb, cx, cy, cz, 5 + i, 32)
-        done = (1.0 - OMEGA) * here + weight[r] * (rhs[r] + total)
-        out[...] = roll(done[:, :, :128], -4, 1)[:, :8]
-
-    last(0)
+            va[r] = jnp.where(weight[r] > 0.0, e[k], 0.0)
+    rows = pl.ds(first, PLANES)
+    near = kappa[pl.ds(first, PLANES + 1)]
+    k = near[:PLANES]
+    cx[rows] = 0.5 * (k + near[1:])
+    cy[rows] = 0.5 * (k + roll(k, -1, 1))
+    cz[rows] = 0.5 * (k + roll(k, -1, 2))
+    sweep(va, vb, left, cx, cy, cz, weight, first, PLANES, PLANES)
+    here, total = around(vb, cx, cy, cz, 5, 32)
+    done = (1.0 - OMEGA) * here + weight[5:37] * (left[5:37] + total)
+    out[...] = v2[...] + roll(done[:, :, :128], -4, 1)[:, :8]
 
 
 def call(kernel, name, outs, scratch, *args):
@@ -630,7 +701,7 @@
     chi, inducing, message, spill = call(
         message_kernel,
         "message",
-        [(16, 16, 128), (3, 16, 16, 128), (64, 128), (24, 128)],
+        [(16, 16, 128), (3, 16, 16, 128), (120, 128), (48, 128)],
         [((8, 128), jnp.int32)] * 2 + [((8, 128), F32), 5],
         chi,
         inducing,
@@ -640,11 +711,11 @@
     )
     got = lax.ppermute(message, "gz", [(0, 1), (1, 0)])
     spread = [((256, 1024), BF16)] * 4
-    source, total, kappa1 = call(
+    source, total = call(
         source_kernel,
         "source",
-        [(18, 24, 128), (256, 256), (32, 128)],
-        [((128, 128), F32)] + spread,
+        [(18, 24, 128), (256, 256)],
+        spread,
         chi,
         inducing,
         message,
@@ -652,8 +723,8 @@
     own, sent = call(
         deposit_kernel,
         "deposit",
-        [(36, 16, 128)] * 2,
-        [((36, 24, 128), F32)] + spread,
+        [(39, 16, 128)] * 2,
+        [((39, 24, 128), F32)] + spread,
         source,
         spill,
         chi,
@@ -662,10 +733,11 @@
     )
     swap = [(0, 1), (1, 0), (2, 3), (3, 2)]
     got = lax.ppermute(sent, "gx", swap)
-    held = [(ROWS, 16, 128), (ROWS, 16, 128), (3, 16, 128)]
-    *fields, message = call(pair_kernel, "pair", held + [(9, 16, 128)], [], own, got)
-    got = lax.ppermute(message, "gx", [(0, 2), (2, 0), (1, 3), (3, 1)])
-    *fields, message = call(across_kernel, "across", held + [(PLANES + 3, 8, 128)], [], *fields, got)
+    held = [(ROWS, 16, 128), (ROWS, 16, 128), (12, 16, 128)]
+    *fields, message = call(pair_kernel, "pair", held + [(10, 16, 128)], [], own, got)
+    cross = [(0, 2), (2, 0), (1, 3), (3, 1)]
+    got = lax.ppermute(message, "gx", cross)
+    *fields, message = call(across_kernel, "across", held + [(PLANES + 6, 8, 128)], [], *fields, got)
     turns = []
     for p in range(2):
         for b in range(n_gy - 1):
@@ -674,36 +746,41 @@
     for low, high in ((0, 2 * n_gy), (2 * n_gy - 1, 4 * n_gy - 1)):
         turns += [(low, high), (high, low)]
     got = lax.ppermute(message, ("gx", "gy"), turns)
-    *fine, message = call(
+    *fine, along, beside, message = call(
         functools.partial(down_kernel, n_gy),
         "down",
-        [window] * 4 + [(4 * n_gy, 64, 128)],
-        big * 5 + [((256, 128), F32), ((3, 16, 128), F32)],
+        [window] * 3 + [(32, 8, 128), (18, 8, 128), (18, 8, 128), (6, 8, 128)],
+        big * 7 + [((576, 128), F32), ((12, 16, 128), F32)],
         *fields,
         got,
-        kappa1,
-    )
-    n = 2 * n_gy
-    groups = [[(2 * p + c) * n + g for p in range(2) for g in range(n)] for c in range(2)]
-    mine = lax.all_to_all(
-        message, everyone, split_axis=0, concat_axis=0, tiled=True, axis_index_groups=groups
-    )
-    other = lax.ppermute(mine, "gx", swap)
-    level1 = (34, 8 * n_gy, 128)
-    (e,) = call(
-        functools.partial(coarse_kernel, n_gy),
-        "coarse",
-        [level1],
-        [(level1, F32)] * 9 + [((128 * n_gy, 128), F32)],
-        mine,
+    )
+    across = lax.ppermute(message, "gx", cross)
+    got = lax.ppermute(jnp.concatenate([along, across]), ("gx", "gy"), turns)
+    other = lax.ppermute(jnp.concatenate([beside, across]), "gx", swap)
+    window1 = (28, 16, 128)
+    big1 = [(window1, F32)]
+    *coarse, message = call(
+        functools.partial(middle_kernel, n_gy),
+        "middle",
+        [window1] * 4 + [(8 * n_gy, 8, 128)],
+        big1 * 5 + [((128, 128), F32), ((64, 128), F32)],
+        beside,
+        across,
+        got,
         other,
     )
+    blocks = lax.all_to_all(message, ("gx", "gy", "gz"), split_axis=0, concat_axis=0, tiled=True)
+    level2 = ((4 * n_gy, 16, 128), F32)
     (out,) = call(
         functools.partial(up_kernel, n_gy),
         "up",
         [(32, 8, 128)],
-        big * 5 + [((18, 16 * n_gy + 8, 128), F32)],
-        e,
+        [level2] * 2
+        + [((4 * n_gy + 8, 32, 128), F32), ((512, 128), F32), ((64 * n_gy, 128), F32)]
+        + big1 * 5
+        + big * 5,
+        blocks,
+        *coarse,
         *fine,
     )
     c = lax.axis_index("gx") & 1

time: 54.2 us -> 52 us (0.959)
  blocking collectives: 20.8 us -> 0 us
  waiting for transfers between devices: 11.6 us -> 23 us
  starting transfers between devices: 7.2 us -> 15.7 us
  Pallas kernels: 13.7 us -> 12.3 us
    all_to_all x1 -> x0, blocking collectives: 20.8 us -> none  [paired(): lax.all_to_all(message, everyone, split_axis=0, concat_axis=0, tiled=True...]
    all_to_all x0 -> x1, waiting for transfers between devices: none -> 7.73 us  [paired(): lax.all_to_all(message, ('gx', 'gy', 'gz'), split_axis=0, concat_axis=0,...]
    all_to_all x0 -> x1, starting transfers between devices: none -> 4.94 us  [paired(): lax.all_to_all(message, ('gx', 'gy', 'gz'), split_axis=0, concat_axis=0,...]
    ppermute x2 -> x4, starting transfers between devices: 2.07 us -> 5.74 us  [the longest x1 2.11 us: paired(): got = lax.ppermute(message, 'gx', cross)]
    ppermute x2 -> x4, waiting for transfers between devices: 4.61 us -> 7.69 us  [the longest x1 2.87 us: paired(): got = lax.ppermute(jnp.concatenate([along, across]), ('gx', 'gy'), turns)]
    pallas_call x8, Pallas kernels: 13.7 us -> 12.3 us  [call(): pl.pallas_call(kernel, name=name, out_shape=[jax.ShapeDtypeStruct(s, F32)...]
  transfers between devices with their start and end apart: 6 -> 9, of which waited for: 6 -> 8; matrix products, arithmetic and copies ran while one was open for 0% -> 0% of each run, Pallas kernels for 2% -> 2%
where the time goes in v5:
time: 52 us; the launch traced here: 51.8 us
  waiting for transfers between devices  23 us (44%)
  starting transfers between devices  15.7 us (30%)
  Pallas kernels  12.3 us (24%)
  other arithmetic  0.68 us (1%)
    pallas_call x8, Pallas kernels, call(): pl.pallas_call(kernel, name=name, out_shape=[jax.ShapeDtypeStruct(s, F32)...  12.3 us
    all_to_all x1, waiting for transfers between devices, paired(): lax.all_to_all(message, ('gx', 'gy', 'gz'), split_axis=0, concat_axis=0,...  7.73 us
    all_to_all x1, starting transfers between devices, paired(): lax.all_to_all(message, ('gx', 'gy', 'gz'), split_axis=0, concat_axis=0,...  4.94 us
    ppermute x1, waiting for transfers between devices, paired(): got = lax.ppermute(message, ('gx', 'gy'), turns)  3.67 us
    ppermute x1, starting transfers between devices, paired(): got = lax.ppermute(message, 'gz', [(0, 1), (1, 0)])  3 us
    ppermute x1, waiting for transfers between devices, paired(): got = lax.ppermute(jnp.concatenate([along, across]), ('gx', 'gy'), turns)  2.87 us
    ppermute x1, waiting for transfers between devices, paired(): got = lax.ppermute(message, 'gx', cross)  2.74 us
    ppermute x1, starting transfers between devices, paired(): got = lax.ppermute(message, 'gx', cross)  2.11 us
  transfers between devices with their start and end apart: 9, of which 8 were waited for; matrix products, arithmetic and copies ran while one was open for 0% of the time, Pallas kernels for 2%

profile of v5, /device:TPU:0, one launch (start us, length us, event | category | flops | bytes accessed | tf_op | source)
XLA Modules:
  0.0 51.8 jit_solution(3227898956280514634)
XLA Ops:
  0.0 1.9 %message.1 = (f32[16,16,128]{2,1,0:T(8,128)S(1)}, f32[3,16,16,128]{3,2,1,0:T(8,128)S(1)}, f32[120,128]{1,0:T(8,128)S(1)}, f32[48,128]{1,0:T(8,128)S(1)}) custom-call(f32[16,16,128]{2,1,0:T(8,128)} %refs_0_.1, f32[3,16,16,128]{3,2,1,0:T(8,128)} %refs_1_.1, s32[8,128]{1,0:T(8,128)} %bitcast.3, s32[8,128]{1,0:T(8,128)} %bitcast.4, f32[8,128]{1,0:T(8,128)} %bitcast.5), custom_call_target="tpu_custom_call" | custom-call | flops 10000000 | bytes 4000000 | tf_op jit(solution)/shard_map/message/pallas_call | solution.py:682
  1.9 3.0 %collective-permute-start = (f32[120,128]{1,0:T(8,128)S(1)}, f32[120,128]{1,0:T(8,128)S(1)}, u32[]{:S(2)}, u32[]{:S(2)}) collective-permute-start(f32[120,128]{1,0:T(8,128)S(1)} %get-tuple-element.35.records), channel_id=1, source_target_pairs={{0,1},{1,0},{2,3},{3,2},{4,5},{5,4},{6,7},{7,6},{8,9},{9,8},{10,11... | collective-permute-start | bytes 184328 | tf_op jit(solution)/shard_map/ppermute | solution.py:712
  4.9 1.0 %source.1 = (f32[18,24,128]{2,1,0:T(8,128)S(1)}, f32[256,256]{1,0:T(8,128)S(1)}) custom-call(f32[16,16,128]{2,1,0:T(8,128)S(1)} %get-tuple-element.33.chi, f32[3,16,16,128]{3,2,1,0:T(8,128)S(1)} %get-tuple-element.34.inducing, f32[120,128]{1,0:T(8,128)S(1)} %get-tuple-element.35.records), custom_call_target="tpu_custom_call" | custom-call | flops 10000000 | bytes 4000000 | tf_op jit(solution)/shard_map/source/pallas_call | solution.py:682
  5.9 1.2 %collective-permute-done.other = f32[120,128]{1,0:T(8,128)S(1)} collective-permute-done((f32[120,128]{1,0:T(8,128)S(1)}, f32[120,128]{1,0:T(8,128)S(1)}, u32[]{:S(2)}, u32[]{:S(2)}) %collective-permute-start) | collective-permute-done | bytes 61472 | tf_op jit(solution)/shard_map/ppermute | solution.py:712
  7.1 1.1 %deposit.1 = (f32[39,16,128]{2,1,0:T(8,128)S(1)}, f32[39,16,128]{2,1,0:T(8,128)S(1)}) custom-call(f32[18,24,128]{2,1,0:T(8,128)S(1)} %get-tuple-element.36.source, f32[48,128]{1,0:T(8,128)S(1)} %get-tuple-element.37.spill, f32[16,16,128]{2,1,0:T(8,128)S(1)} %get-tuple-element.33.chi, f32[256,256]{1,0:T(8,128)S(1)} %get-tuple-element.38.mine, ...), custom_call_target="tpu_custom_call" | custom-call | flops 10000000 | bytes 4000000 | tf_op jit(solution)/shard_map/deposit/pallas_call | solution.py:682
  8.3 0.1 collective-permute-start.1
  8.3 1.6 %collective-permute-done.1.other = f32[39,16,128]{2,1,0:T(8,128)S(1)} collective-permute-done((f32[39,16,128]{2,1,0:T(8,128)S(1)}, f32[39,16,128]{2,1,0:T(8,128)S(1)}, u32[]{:S(2)}, u32[]{:S(2)}) %collective-permute-start.1) | collective-permute-done | bytes 319520 | tf_op jit(solution)/shard_map/ppermute | solution.py:735
  10.0 0.2 pair.1
  10.2 2.1 %collective-permute-start.2 = (f32[10,16,128]{2,1,0:T(8,128)S(1)}, f32[10,16,128]{2,1,0:T(8,128)S(1)}, u32[]{:S(2)}, u32[]{:S(2)}) collective-permute-start(f32[10,16,128]{2,1,0:T(8,128)S(1)} %get-tuple-element.44), channel_id=1, source_target_pairs={{0,16},{16,0},{8,24},{24,8},{1,17},{17,1},{9,25},{25,9},{2,18},{18... | collective-permute-start | bytes 245768 | tf_op jit(solution)/shard_map/ppermute | solution.py:739
  12.3 2.7 %collective-permute-done.2.other = f32[10,16,128]{2,1,0:T(8,128)S(1)} collective-permute-done((f32[10,16,128]{2,1,0:T(8,128)S(1)}, f32[10,16,128]{2,1,0:T(8,128)S(1)}, u32[]{:S(2)}, u32[]{:S(2)}) %collective-permute-start.2) | collective-permute-done | bytes 81952 | tf_op jit(solution)/shard_map/ppermute | solution.py:739
  15.0 0.2 across.1
  15.2 1.8 %collective-permute-start.3 = (f32[42,8,128]{2,1,0:T(8,128)S(1)}, f32[42,8,128]{2,1,0:T(8,128)S(1)}, u32[]{:S(2)}, u32[]{:S(2)}) collective-permute-start(f32[42,8,128]{2,1,0:T(8,128)S(1)} %get-tuple-element.48), channel_id=1, source_target_pairs={{8,2},{2,8},{10,4},{4,10},{12,6},{6,12},{24,18},{18,24},{26,20},{2... | collective-permute-start | bytes 516104 | tf_op jit(solution)/shard_map/ppermute | solution.py:748
  17.0 3.7 %collective-permute-done.3.other = f32[42,8,128]{2,1,0:T(8,128)S(1)} collective-permute-done((f32[42,8,128]{2,1,0:T(8,128)S(1)}, f32[42,8,128]{2,1,0:T(8,128)S(1)}, u32[]{:S(2)}, u32[]{:S(2)}) %collective-permute-start.3) | collective-permute-done | bytes 172064 | tf_op jit(solution)/shard_map/ppermute | solution.py:748
  20.7 2.8 %down.1 = (f32[42,16,256]{2,1,0:T(8,128)S(1)}, f32[42,16,256]{2,1,0:T(8,128)S(1)}, f32[42,16,256]{2,1,0:T(8,128)S(1)}, f32[32,8,128]{2,1,0:T(8,128)S(1)}, f32[18...) custom-call(f32[42,16,128]{2,1,0:T(8,128)S(1)} %get-tuple-element.45.source_in, ...), custom_call_target="tpu_custom_call" | custom-call | flops 10000000 | bytes 4000000 | tf_op jit(solution)/shard_map/down/pallas_call | solution.py:682
  23.4 1.8 %collective-permute-start.4 = (f32[6,8,128]{2,1,0:T(8,128)S(1)}, f32[6,8,128]{2,1,0:T(8,128)S(1)}, u32[]{:S(2)}, u32[]{:S(2)}) collective-permute-start(f32[6,8,128]{2,1,0:T(8,128)S(1)} %get-tuple-element.50), channel_id=1, source_target_pairs={{0,16},{16,0},{8,24},{24,8},{1,17},{17,1},{9,25},{25,9},{2,18},{18... | collective-permute-start | bytes 73736 | tf_op jit(solution)/shard_map/ppermute | solution.py:757
  25.3 2.1 %collective-permute-done.4.across = f32[6,8,128]{2,1,0:T(8,128)S(1)} collective-permute-done((f32[6,8,128]{2,1,0:T(8,128)S(1)}, f32[6,8,128]{2,1,0:T(8,128)S(1)}, u32[]{:S(2)}, u32[]{:S(2)}) %collective-permute-start.4) | collective-permute-done | bytes 24608 | tf_op jit(solution)/shard_map/ppermute | solution.py:757
  27.4 1.8 %collective-permute-start.5 = (f32[24,8,128]{2,1,0:T(8,128)S(1)}, f32[24,8,128]{2,1,0:T(8,128)S(1)}, u32[]{:S(2)}, u32[]{:S(2)}) collective-permute-start(f32[24,8,128]{2,1,0:T(8,128)S(1)} %get-tuple-element.64), channel_id=1, source_target_pairs={{8,2},{2,8},{10,4},{4,10},{12,6},{6,12},{24,18},{18,24},{26,20},{2... | collective-permute-start | bytes 294920 | tf_op jit(solution)/shard_map/ppermute | solution.py:758
  29.2 0.0 collective-permute-start.6
  29.2 2.9 %collective-permute-done.5.got = f32[24,8,128]{2,1,0:T(8,128)S(1)} collective-permute-done((f32[24,8,128]{2,1,0:T(8,128)S(1)}, f32[24,8,128]{2,1,0:T(8,128)S(1)}, u32[]{:S(2)}, u32[]{:S(2)}) %collective-permute-start.5) | collective-permute-done | bytes 98336 | tf_op jit(solution)/shard_map/ppermute | solution.py:758
  32.0 0.0 collective-permute-done.6.other
  32.0 1.6 %middle.1 = (f32[28,16,128]{2,1,0:T(8,128)S(1)}, f32[28,16,128]{2,1,0:T(8,128)S(1)}, f32[28,16,128]{2,1,0:T(8,128)S(1)}, f32[28,16,128]{2,1,0:T(8,128)S(1)}, f32[32,8,128]{2,1,0:T(8,128)}) custom-call(f32[18,8,128]{2,1,0:T(8,128)S(1)} %get-tuple-element.49.mine, f32[6,8,128]{2,1,0:T(8,128)S(1)} %collective-permute-done.4.across, ...), custom_call_target="tpu_custom_call" | custom-call | flops 10000000 | bytes 4000000 | tf_op jit(solution)/shard_map/middle/pallas_call | solution.py:682
  33.6 4.9 %all-to-all-start = ((f32[32,8,128]{2,1,0:T(8,128)}), f32[32,8,128]{2,1,0:T(8,128)S(1)}, u32[]{:S(2)}, u32[]{:S(2)}) async-start(f32[32,8,128]{2,1,0:T(8,128)} %get-tuple-element.52), calls=%async_computation | async-start | bytes 262144 | tf_op jit(solution)/shard_map/all_to_all | solution.py:772
  38.6 7.7 %all-to-all-done.blocks = f32[32,8,128]{2,1,0:T(8,128)S(1)} async-done(((f32[32,8,128]{2,1,0:T(8,128)}), f32[32,8,128]{2,1,0:T(8,128)S(1)}, u32[]{:S(2)}, u32[]{:S(2)}) %all-to-all-start) | async-done | bytes 131104 | tf_op jit(solution)/shard_map/all_to_all | solution.py:772
  46.3 3.5 %up.1 = f32[32,8,128]{2,1,0:T(8,128)S(1)} custom-call(f32[32,8,128]{2,1,0:T(8,128)S(1)} %all-to-all-done.blocks, f32[28,16,128]{2,1,0:T(8,128)S(1)} %get-tuple-element.53.r1, f32[28,16,128]{2,1,0:T(8,128)S(1)} %get-tuple-element.54.k1, f32[28,16,128]{2,1,0:T(8,128)S(1)} %get-tuple-element.55.w1, f32[28,16,128]{2,1,0:T(8,128)S(1)} %get-tuple-element.56.v21, ...), custom_call_target="tpu_custom_call" | custom-call | flops 10000000 | bytes 4000000 | tf_op jit(solution)/shard_map/up/pallas_call | solution.py:682
  49.8 0.2 collective-permute-start.7
  50.0 1.1 %collective-permute-done.7 = f32[16,8,128]{2,1,0:T(8,128)S(1)} collective-permute-done((f32[16,8,128]{2,1,0:T(8,128)S(1)}, f32[16,8,128]{2,1,0:T(8,128)S(1)}, u32[]{:S(2)}, u32[]{:S(2)}) %collective-permute-start.7) | collective-permute-done | bytes 65568 | tf_op jit(solution)/shard_map/ppermute | solution.py:789
  51.2 0.7 %maximum_select_fusion = f32[16,16,128]{2,1,0:T(8,128)} fusion(f32[16,8,128]{2,1,0:T(8,128)S(1)} %collective-permute-done.7, f32[16,8,128]{2,1,0:T(8,128)S(1)} %get-tuple-element.61, pred[]{:T(512)S(6)} %eq.3), kind=kLoop, calls=%fused_computation | loop fusion | flops 98304 | bytes 262145 | tf_op jit(solution)/shard_map/jit(_where)/select_n | solution.py:790
  (2 shorter events, 0.0 us)
Async XLA Ops:
  1.9 5.2 %collective-permute-start = (f32[120,128]{1,0:T(8,128)S(1)}, f32[120,128]{1,0:T(8,128)S(1)}, u32[]{:S(2)}, u32[]{:S(2)}) collective-permute-start(f32[120,128]{1,0:T(8,128)S(1)} %get-tuple-element.35.records), channel_id=1, source_target_pairs={{0,1},{1,0},{2,3},{3,2},{4,5},{5,4},{6,7},{7,6},{8,9},{9,8},{10,11... | collective-permute-start | bytes 184328 | tf_op jit(solution)/shard_map/ppermute | solution.py:712
  8.3 1.7 %collective-permute-start.1 = (f32[39,16,128]{2,1,0:T(8,128)S(1)}, f32[39,16,128]{2,1,0:T(8,128)S(1)}, u32[]{:S(2)}, u32[]{:S(2)}) collective-permute-start(f32[39,16,128]{2,1,0:T(8,128)S(1)} %get-tuple-element.40), channel_id=1, source_target_pairs={{0,8},{8,0},{16,24},{24,16},{1,9},{9,1},{17,25},{25,17},{2,10},{10... | collective-permute-start | bytes 958472 | tf_op jit(solution)/shard_map/ppermute | solution.py:735
  10.2 4.9 %collective-permute-start.2 = (f32[10,16,128]{2,1,0:T(8,128)S(1)}, f32[10,16,128]{2,1,0:T(8,128)S(1)}, u32[]{:S(2)}, u32[]{:S(2)}) collective-permute-start(f32[10,16,128]{2,1,0:T(8,128)S(1)} %get-tuple-element.44), channel_id=1, source_target_pairs={{0,16},{16,0},{8,24},{24,8},{1,17},{17,1},{9,25},{25,9},{2,18},{18... | collective-permute-start | bytes 245768 | tf_op jit(solution)/shard_map/ppermute | solution.py:739
  15.2 5.5 %collective-permute-start.3 = (f32[42,8,128]{2,1,0:T(8,128)S(1)}, f32[42,8,128]{2,1,0:T(8,128)S(1)}, u32[]{:S(2)}, u32[]{:S(2)}) collective-permute-start(f32[42,8,128]{2,1,0:T(8,128)S(1)} %get-tuple-element.48), channel_id=1, source_target_pairs={{8,2},{2,8},{10,4},{4,10},{12,6},{6,12},{24,18},{18,24},{26,20},{2... | collective-permute-start | bytes 516104 | tf_op jit(solution)/shard_map/ppermute | solution.py:748
  23.4 3.9 %collective-permute-start.4 = (f32[6,8,128]{2,1,0:T(8,128)S(1)}, f32[6,8,128]{2,1,0:T(8,128)S(1)}, u32[]{:S(2)}, u32[]{:S(2)}) collective-permute-start(f32[6,8,128]{2,1,0:T(8,128)S(1)} %get-tuple-element.50), channel_id=1, source_target_pairs={{0,16},{16,0},{8,24},{24,8},{1,17},{17,1},{9,25},{25,9},{2,18},{18... | collective-permute-start | bytes 73736 | tf_op jit(solution)/shard_map/ppermute | solution.py:757
  27.4 4.7 %collective-permute-start.5 = (f32[24,8,128]{2,1,0:T(8,128)S(1)}, f32[24,8,128]{2,1,0:T(8,128)S(1)}, u32[]{:S(2)}, u32[]{:S(2)}) collective-permute-start(f32[24,8,128]{2,1,0:T(8,128)S(1)} %get-tuple-element.64), channel_id=1, source_target_pairs={{8,2},{2,8},{10,4},{4,10},{12,6},{6,12},{24,18},{18,24},{26,20},{2... | collective-permute-start | bytes 294920 | tf_op jit(solution)/shard_map/ppermute | solution.py:758
  29.2 2.9 %collective-permute-start.6 = (f32[24,8,128]{2,1,0:T(8,128)S(1)}, f32[24,8,128]{2,1,0:T(8,128)S(1)}, u32[]{:S(2)}, u32[]{:S(2)}) collective-permute-start(f32[24,8,128]{2,1,0:T(8,128)S(1)} %get-tuple-element.63), channel_id=1, source_target_pairs={{0,8},{8,0},{16,24},{24,16},{1,9},{9,1},{17,25},{25,17},{2,10},{10... | collective-permute-start | bytes 294920 | tf_op jit(solution)/shard_map/ppermute | solution.py:759
  33.6 12.7 %all-to-all-start = ((f32[32,8,128]{2,1,0:T(8,128)}), f32[32,8,128]{2,1,0:T(8,128)S(1)}, u32[]{:S(2)}, u32[]{:S(2)}) async-start(f32[32,8,128]{2,1,0:T(8,128)} %get-tuple-element.52), calls=%async_computation | async-start | bytes 262144 | tf_op jit(solution)/shard_map/all_to_all | solution.py:772
  49.8 1.3 %collective-permute-start.7 = (f32[16,8,128]{2,1,0:T(8,128)S(1)}, f32[16,8,128]{2,1,0:T(8,128)S(1)}, u32[]{:S(2)}, u32[]{:S(2)}) collective-permute-start(f32[16,8,128]{2,1,0:T(8,128)S(1)} %get-tuple-element.62), channel_id=1, source_target_pairs={{0,8},{8,0},{16,24},{24,16},{1,9},{9,1},{17,25},{25,17},{2,10},{10... | collective-permute-start | bytes 196616 | tf_op jit(solution)/shard_map/ppermute | solution.py:789

commit v6 on v5

--- a/solution.py
+++ b/solution.py
@@ -400,8 +400,8 @@
 
 
 def down_kernel(
-    n_gy, source_in, kappa_in, halo_in, other, left, kappa, weight, v, along, beside, message,
-    rhs, cx, cy, cz, diag, v1, v2, sums, halo,
+    n_gy, source_in, kappa_in, halo_in, other, left, kappa, weight, v, along, beside, message, parts,
+    rhs, cx, cy, cz, diag, v1, v2, sums, flat, halo,
 ):
     p, c, b, t = place()
     first = 5 - 4 * p
@@ -446,7 +446,7 @@
         two = two.reshape(n, 256)
         halves = []
         for i in range(2):
-            at = 288 * i
+            at = 320 * i
             sums[at : at + n] = two[:, 128 * i : 128 * (i + 1)]
             halves.append(sums[pl.ds(at, n // 2, stride=2), :] + sums[pl.ds(at + 1, n // 2, stride=2), :])
         return dot(jnp.concatenate(halves, 1), halving(256)).reshape(n // 16, 8, 128)
@@ -456,15 +456,38 @@
     sweep(v1, v2, rhs, cx, cy, cz, weight, first, PLANES, PLANES)
     left[rows] = resid(v2, rhs, cx, cy, cz, diag, first, PLANES)
     v[...] = roll(v2[5:37, :, :128], -4, 1)[:, :8]
+    k1 = coarse(kappa[1:41])
     r1 = coarse(left[5:37])
-    k1 = coarse(kappa[3:39])
-    k = k1[1:17]
-    total = (k1[2:] + k1[:16]) + (roll(k, -1, 1) + roll(k, 1, 1)) + (roll(k, -1, 2) + roll(k, 1, 2))
-    v1c = jnp.where(k > 0.0, OMEGA / jnp.where(k > 0.0, 0.125 * (6.0 * k + total), 1.0), 0.0) * r1
+    edge = jnp.zeros((2, 8, 128), F32)
+    at = iota(r1.shape, 1)
+    part = jnp.concatenate([edge, jnp.where((at >= 2) & (at < 6), r1, 0.0), edge], 0)
+    level = Level(k1, 0.25, closed=False)
+    u1 = level.weight * part
+    u2 = level.sweep(u1, part)
+    sub, lane = iota((8, 128), 0), iota((8, 128), 1)
+
+    def means(fine):
+        n = 2 * fine.shape[0]
+        sums[0 : 2 * n] = pair_sums(fine).reshape(2 * n, 128)
+        return dot(sums[pl.ds(0, n, stride=2), :] + sums[pl.ds(1, n, stride=2), :], halving(128))
+
+    flat[0:40, :] = means(level.resid(u2, part))
+    tile = jnp.zeros((8, 128), F32)
+    for y in range(4):
+        tile = tile + roll(jnp.where(lane < 32, flat[pl.ds(4 + y, 8, stride=4), :], 0.0), 32 * y, 1)
+    beyond = jnp.where((sub < 4) & (lane < 32), pick(p, flat[36:44, :], flat[0:8, :]), 0.0)
+    second = roll(beyond, 64, 1)
+    flat[0:40, :] = means(k1)
+    for y in range(2):
+        second = second + roll(jnp.where(lane < 32, flat[pl.ds(5 + y, 8, stride=4), :], 0.0), 32 * y, 1)
+    for d in range(parts.shape[0]):
+        parts[d, 0:8] = tile
+        parts[d, 8:16] = second
+    k = k1[2:18]
+    v1c = level.weight[2:18] * r1
     tiles = jnp.where(iota(r1.shape, 1) < 4, roll(r1, -2, 1), roll(k, 2, 1))
     along[0:16] = tiles
     beside[0:16] = tiles
-    sub = iota((8, 128), 0)
     for i in range(2):
         far, near = jnp.zeros((8, 128), F32), jnp.zeros((8, 128), F32)
         for j in range(8):
@@ -479,7 +502,7 @@
     message[5] = roll(pick(p, v1c[15], v1c[0]), -2, 0)
 
 
-def middle_kernel(n_gy, mine, across, got, other, r1, k1, weight, v2, message, cx, cy, cz, diag, v1, sums, flat):
+def middle_kernel(n_gy, mine, across, both, r1, k1, weight, v2, cx, cy, cz, diag, v1):
     p, c, b, t = place()
     edge = jnp.where(c == 0, b == 0, b == n_gy - 1).astype(jnp.int32)
     for ref in (r1, k1, cx, weight, v1, v2):
@@ -489,7 +512,7 @@
     middle = (sub >= 2) & (sub < 6)
 
     def around_mine(at):
-        s, g = other[at], pick(edge, got[at], zero)
+        s, g = both[24 + at], pick(edge, both[at], zero)
         return pick(c, g, s), pick(c, s, g)
 
     def joined(low, o, high):
@@ -519,16 +542,6 @@
     r = 25 - 23 * p
     v1[r, 0:8], v1[r, 8:16] = joined(low, across[4], high)
     sweep(v1, v2, r1, cx, cy, cz, weight, first, 20, 20)
-    lane = iota((8, 128), 1)
-    tile = zero
-    for i, fine in enumerate((resid(v2, r1, cx, cy, cz, diag, 6, 16), k1[6:22])):
-        sums[...] = pair_sums(fine).reshape(128, 128)
-        flat[...] = dot(sums[pl.ds(0, 64, stride=2), :] + sums[pl.ds(1, 64, stride=2), :], halving(128))
-        for y in range(2):
-            part = jnp.where(lane < 32, flat[pl.ds(3 + y, 8, stride=8), :], 0.0)
-            tile = tile + roll(part, 64 * i + 32 * y, 1)
-    for d in range(message.shape[0]):
-        message[d] = tile
 
 
 def shift(x, by, axis):
@@ -542,15 +555,17 @@
 
 
 class Level:
-    def __init__(self, kappa, scale):
+    def __init__(self, kappa, scale, closed=True):
         half = 0.5 * scale
         at = iota(kappa.shape, 1)
         ends = {1: at == kappa.shape[1] - 1, -1: at == 0}
         near = [shift(kappa, by, axis) for axis, by in SIDES]
-        near[2:4] = [jnp.where(ends[by], 0.0, k) for by, k in zip((1, -1), near[2:4])]
+        if closed:
+            near[2:4] = [jnp.where(ends[by], 0.0, k) for by, k in zip((1, -1), near[2:4])]
         self.diag = half * (6.0 * kappa + (near[0] + near[1]) + (near[2] + near[3]) + (near[4] + near[5]))
         self.faces = [half * (kappa + other) for other in near]
-        self.faces[2:4] = [jnp.where(ends[by], 0.0, f) for by, f in zip((1, -1), self.faces[2:4])]
+        if closed:
+            self.faces[2:4] = [jnp.where(ends[by], 0.0, f) for by, f in zip((1, -1), self.faces[2:4])]
         inside = kappa > 0.0
         self.weight = jnp.where(inside, OMEGA / jnp.where(inside, self.diag, 1.0), 0.0)
 
@@ -609,15 +624,40 @@
     for ref in (fx, ua, ub):
         ref[...] = jnp.zeros_like(ref)
 
-    lane = iota((8, 128), 1)
+    lane, sub = iota((8, 128), 1), iota((8, 128), 0)
+    cells = {(y, gp): jnp.zeros((8, 128), F32) for y in range(-1, n_y + 1) for gp in range(2)}
+    pairs = n_y // 2
+
+    def block(gp, q, gz):
+        return ((2 * gp + q % 2) * n_gy + q // 2) * 2 + gz
+
+    for gp in range(2):
+        for q in range(pairs):
+            whole = []
+            for gz in range(2):
+                ends = jnp.zeros((8, 128), F32)
+                if q + 1 < pairs:
+                    ends = jnp.where(lane < 32, blocks[block(gp, q + 1, gz), 0:8, :], ends)
+                if q > 0:
+                    ends = jnp.where(lane >= 96, blocks[block(gp, q - 1, gz), 0:8, :], ends)
+                whole.append(blocks[block(gp, q, gz), 0:8, :] + roll(ends, 64, 1))
+            near, far = whole
+            near2, far2 = [blocks[block(gp, q, gz), 8:16, :] for gz in range(2)]
+            for y in range(2):
+                high = jnp.where(lane < 64, roll(far, -32 * y, 1), 0.0)
+                own = jnp.where(lane < 32, roll(near, -32 * (y + 1), 1), high)
+                cells[2 * q + y, gp] = cells[2 * q + y, gp] + own
+                high = jnp.where(lane < 64, roll(far2, 32 * (1 - y), 1), 0.0)
+                k2[2 * q + y, 8 * gp : 8 * gp + 8, :] = jnp.where(lane < 32, roll(near2, -32 * y, 1), high)
+            high = jnp.where(lane < 64, roll(far2, -32, 1), 0.0)
+            beyond = jnp.where(lane < 32, roll(near2, -64, 1), high)
+            goal = 0 if gp == 0 else 7
+            for y in range(-1, 3):
+                spot = 2 * q + y, 1 - gp
+                cells[spot] = cells[spot] + jnp.where(sub == goal, roll(beyond, goal - y - 1, 0), 0.0)
     for y in range(n_y):
-        gy, gc, low = y // 4, y // 2 % 2, y % 2
         for gp in range(2):
-            at = ((2 * gp + gc) * n_gy + gy) * 2
-            near, far = blocks[at], blocks[at + 1]
-            for ref, start in ((r2, 32 * low), (k2, 64 + 32 * low)):
-                cells = jnp.where(lane < 64, roll(far, 32 - start, 1), 0.0)
-                ref[y, 8 * gp : 8 * gp + 8, :] = jnp.where(lane < 32, roll(near, -start, 1), cells)
+            r2[y, 8 * gp : 8 * gp + 8, :] = cells[y, gp]
     middle, rhs2 = Level(k2[...], 0.0625), r2[...]
     m2 = middle.weight * rhs2
     m2 = middle.sweep(m2, rhs2)
@@ -746,30 +786,29 @@
     for low, high in ((0, 2 * n_gy), (2 * n_gy - 1, 4 * n_gy - 1)):
         turns += [(low, high), (high, low)]
     got = lax.ppermute(message, ("gx", "gy"), turns)
-    *fine, along, beside, message = call(
+    *fine, along, beside, message, parts = call(
         functools.partial(down_kernel, n_gy),
         "down",
-        [window] * 3 + [(32, 8, 128), (18, 8, 128), (18, 8, 128), (6, 8, 128)],
-        big * 7 + [((576, 128), F32), ((12, 16, 128), F32)],
+        [window] * 3 + [(32, 8, 128), (18, 8, 128), (18, 8, 128), (6, 8, 128), (8 * n_gy, 16, 128)],
+        big * 7 + [((640, 128), F32), ((48, 128), F32), ((12, 16, 128), F32)],
         *fields,
         got,
     )
+    blocks = lax.all_to_all(parts, ("gx", "gy", "gz"), split_axis=0, concat_axis=0, tiled=True)
     across = lax.ppermute(message, "gx", cross)
     got = lax.ppermute(jnp.concatenate([along, across]), ("gx", "gy"), turns)
     other = lax.ppermute(jnp.concatenate([beside, across]), "gx", swap)
     window1 = (28, 16, 128)
     big1 = [(window1, F32)]
-    *coarse, message = call(
+    coarse = call(
         functools.partial(middle_kernel, n_gy),
         "middle",
-        [window1] * 4 + [(8 * n_gy, 8, 128)],
-        big1 * 5 + [((128, 128), F32), ((64, 128), F32)],
+        [window1] * 4,
+        big1 * 5,
         beside,
         across,
-        got,
-        other,
-    )
-    blocks = lax.all_to_all(message, ("gx", "gy", "gz"), split_axis=0, concat_axis=0, tiled=True)
+        jnp.concatenate([got, other]),
+    )
     level2 = ((4 * n_gy, 16, 128), F32)
     (out,) = call(
         functools.partial(up_kernel, n_gy),

time: 52 us -> 46.5 us (0.89)
  waiting for transfers between devices: 23 us -> 16.9 us
  starting transfers between devices: 15.7 us -> 16.3 us
    all_to_all x1, waiting for transfers between devices: 7.73 us -> 0.72 us  [paired(): lax.all_to_all(parts, ('gx', 'gy', 'gz'), split_axis=0, concat_axis=0, ti...]
    all_to_all x1, starting transfers between devices: 4.94 us -> 5.53 us  [paired(): lax.all_to_all(parts, ('gx', 'gy', 'gz'), split_axis=0, concat_axis=0, ti...]
  transfers between devices with their start and end apart: 9 -> 9, of which waited for: 8 -> 8; matrix products, arithmetic and copies ran while one was open for 0% -> 0% of each run, Pallas kernels for 2% -> 3%
where the time goes in v6:
time: 46.5 us; the launch traced here: 46.3 us
  waiting for transfers between devices  16.9 us (36%)
  starting transfers between devices  16.3 us (35%)
  Pallas kernels  12.4 us (27%)
  other arithmetic  0.69 us (1%)
    pallas_call x8, Pallas kernels, call(): pl.pallas_call(kernel, name=name, out_shape=[jax.ShapeDtypeStruct(s, F32)...  12.4 us
    all_to_all x1, starting transfers between devices, paired(): lax.all_to_all(parts, ('gx', 'gy', 'gz'), split_axis=0, concat_axis=0, ti...  5.53 us
    ppermute x1, waiting for transfers between devices, paired(): got = lax.ppermute(message, ('gx', 'gy'), turns)  3.67 us
    ppermute x1, waiting for transfers between devices, paired(): got = lax.ppermute(jnp.concatenate([along, across]), ('gx', 'gy'), turns)  3.29 us
    ppermute x1, starting transfers between devices, paired(): got = lax.ppermute(message, 'gz', [(0, 1), (1, 0)])  3 us
    ppermute x1, waiting for transfers between devices, paired(): got = lax.ppermute(message, 'gx', cross)  2.74 us
    ppermute x1, waiting for transfers between devices, paired(): across = lax.ppermute(message, 'gx', cross)  2.41 us
    ppermute x1, starting transfers between devices, paired(): got = lax.ppermute(message, 'gx', cross)  2.11 us
  transfers between devices with their start and end apart: 9, of which 8 were waited for; matrix products, arithmetic and copies ran while one was open for 0% of the time, Pallas kernels for 3%

profile of v6, /device:TPU:0, one launch (start us, length us, event | category | flops | bytes accessed | tf_op | source)
XLA Modules:
  0.0 46.3 jit_solution(4679758735935484171)
XLA Ops:
  0.0 1.9 %message.1 = (f32[16,16,128]{2,1,0:T(8,128)S(1)}, f32[3,16,16,128]{3,2,1,0:T(8,128)S(1)}, f32[120,128]{1,0:T(8,128)S(1)}, f32[48,128]{1,0:T(8,128)S(1)}) custom-call(f32[16,16,128]{2,1,0:T(8,128)} %refs_0_.1, f32[3,16,16,128]{3,2,1,0:T(8,128)} %refs_1_.1, s32[8,128]{1,0:T(8,128)} %bitcast.3, s32[8,128]{1,0:T(8,128)} %bitcast.4, f32[8,128]{1,0:T(8,128)} %bitcast.5), custom_call_target="tpu_custom_call" | custom-call | flops 10000000 | bytes 4000000 | tf_op jit(solution)/shard_map/message/pallas_call | solution.py:722
  1.9 3.0 %collective-permute-start = (f32[120,128]{1,0:T(8,128)S(1)}, f32[120,128]{1,0:T(8,128)S(1)}, u32[]{:S(2)}, u32[]{:S(2)}) collective-permute-start(f32[120,128]{1,0:T(8,128)S(1)} %get-tuple-element.35.records), channel_id=1, source_target_pairs={{0,1},{1,0},{2,3},{3,2},{4,5},{5,4},{6,7},{7,6},{8,9},{9,8},{10,11... | collective-permute-start | bytes 184328 | tf_op jit(solution)/shard_map/ppermute | solution.py:752
  4.9 1.0 %source.1 = (f32[18,24,128]{2,1,0:T(8,128)S(1)}, f32[256,256]{1,0:T(8,128)S(1)}) custom-call(f32[16,16,128]{2,1,0:T(8,128)S(1)} %get-tuple-element.33.chi, f32[3,16,16,128]{3,2,1,0:T(8,128)S(1)} %get-tuple-element.34.inducing, f32[120,128]{1,0:T(8,128)S(1)} %get-tuple-element.35.records), custom_call_target="tpu_custom_call" | custom-call | flops 10000000 | bytes 4000000 | tf_op jit(solution)/shard_map/source/pallas_call | solution.py:722
  5.9 1.2 %collective-permute-done.other = f32[120,128]{1,0:T(8,128)S(1)} collective-permute-done((f32[120,128]{1,0:T(8,128)S(1)}, f32[120,128]{1,0:T(8,128)S(1)}, u32[]{:S(2)}, u32[]{:S(2)}) %collective-permute-start) | collective-permute-done | bytes 61472 | tf_op jit(solution)/shard_map/ppermute | solution.py:752
  7.1 1.1 %deposit.1 = (f32[39,16,128]{2,1,0:T(8,128)S(1)}, f32[39,16,128]{2,1,0:T(8,128)S(1)}) custom-call(f32[18,24,128]{2,1,0:T(8,128)S(1)} %get-tuple-element.36.source, f32[48,128]{1,0:T(8,128)S(1)} %get-tuple-element.37.spill, f32[16,16,128]{2,1,0:T(8,128)S(1)} %get-tuple-element.33.chi, f32[256,256]{1,0:T(8,128)S(1)} %get-tuple-element.38.mine, ...), custom_call_target="tpu_custom_call" | custom-call | flops 10000000 | bytes 4000000 | tf_op jit(solution)/shard_map/deposit/pallas_call | solution.py:722
  8.3 0.1 collective-permute-start.1
  8.3 1.6 %collective-permute-done.1.other = f32[39,16,128]{2,1,0:T(8,128)S(1)} collective-permute-done((f32[39,16,128]{2,1,0:T(8,128)S(1)}, f32[39,16,128]{2,1,0:T(8,128)S(1)}, u32[]{:S(2)}, u32[]{:S(2)}) %collective-permute-start.1) | collective-permute-done | bytes 319520 | tf_op jit(solution)/shard_map/ppermute | solution.py:775
  10.0 0.2 pair.1
  10.2 2.1 %collective-permute-start.2 = (f32[10,16,128]{2,1,0:T(8,128)S(1)}, f32[10,16,128]{2,1,0:T(8,128)S(1)}, u32[]{:S(2)}, u32[]{:S(2)}) collective-permute-start(f32[10,16,128]{2,1,0:T(8,128)S(1)} %get-tuple-element.44), channel_id=1, source_target_pairs={{0,16},{16,0},{8,24},{24,8},{1,17},{17,1},{9,25},{25,9},{2,18},{18... | collective-permute-start | bytes 245768 | tf_op jit(solution)/shard_map/ppermute | solution.py:779
  12.3 2.7 %collective-permute-done.2.other = f32[10,16,128]{2,1,0:T(8,128)S(1)} collective-permute-done((f32[10,16,128]{2,1,0:T(8,128)S(1)}, f32[10,16,128]{2,1,0:T(8,128)S(1)}, u32[]{:S(2)}, u32[]{:S(2)}) %collective-permute-start.2) | collective-permute-done | bytes 81952 | tf_op jit(solution)/shard_map/ppermute | solution.py:779
  15.0 0.2 across.1
  15.2 1.8 %collective-permute-start.3 = (f32[42,8,128]{2,1,0:T(8,128)S(1)}, f32[42,8,128]{2,1,0:T(8,128)S(1)}, u32[]{:S(2)}, u32[]{:S(2)}) collective-permute-start(f32[42,8,128]{2,1,0:T(8,128)S(1)} %get-tuple-element.48), channel_id=1, source_target_pairs={{8,2},{2,8},{10,4},{4,10},{12,6},{6,12},{24,18},{18,24},{26,20},{2... | collective-permute-start | bytes 516104 | tf_op jit(solution)/shard_map/ppermute | solution.py:788
  17.0 3.7 %collective-permute-done.3.other = f32[42,8,128]{2,1,0:T(8,128)S(1)} collective-permute-done((f32[42,8,128]{2,1,0:T(8,128)S(1)}, f32[42,8,128]{2,1,0:T(8,128)S(1)}, u32[]{:S(2)}, u32[]{:S(2)}) %collective-permute-start.3) | collective-permute-done | bytes 172064 | tf_op jit(solution)/shard_map/ppermute | solution.py:788
  20.7 3.8 %down.1 = (f32[42,16,256]{2,1,0:T(8,128)S(1)}, f32[42,16,256]{2,1,0:T(8,128)S(1)}, f32[42,16,256]{2,1,0:T(8,128)S(1)}, f32[32,8,128]{2,1,0:T(8,128)S(1)}, f32[18...) custom-call(f32[42,16,128]{2,1,0:T(8,128)S(1)} %get-tuple-element.45.source_, ...), custom_call_target="tpu_custom_call" | custom-call | flops 10000000 | bytes 4000000 | tf_op jit(solution)/shard_map/down/pallas_call | solution.py:722
  24.5 5.5 %all-to-all-start = ((f32[32,16,128]{2,1,0:T(8,128)}), f32[32,16,128]{2,1,0:T(8,128)S(1)}, u32[]{:S(2)}, u32[]{:S(2)}) async-start(f32[32,16,128]{2,1,0:T(8,128)} %get-tuple-element.49), calls=%async_computation | async-start | bytes 524288 | tf_op jit(solution)/shard_map/all_to_all | solution.py:797
  30.0 1.8 %collective-permute-start.4 = (f32[6,8,128]{2,1,0:T(8,128)S(1)}, f32[6,8,128]{2,1,0:T(8,128)S(1)}, u32[]{:S(2)}, u32[]{:S(2)}) collective-permute-start(f32[6,8,128]{2,1,0:T(8,128)S(1)} %get-tuple-element.51), channel_id=1, source_target_pairs={{0,16},{16,0},{8,24},{24,8},{1,17},{17,1},{9,25},{25,9},{2,18},{18... | collective-permute-start | bytes 73736 | tf_op jit(solution)/shard_map/ppermute | solution.py:798
  31.9 2.4 %collective-permute-done.4.across = f32[6,8,128]{2,1,0:T(8,128)S(1)} collective-permute-done((f32[6,8,128]{2,1,0:T(8,128)S(1)}, f32[6,8,128]{2,1,0:T(8,128)S(1)}, u32[]{:S(2)}, u32[]{:S(2)}) %collective-permute-start.4) | collective-permute-done | bytes 24608 | tf_op jit(solution)/shard_map/ppermute | solution.py:798
  34.3 1.8 %collective-permute-start.5 = (f32[24,8,128]{2,1,0:T(8,128)S(1)}, f32[24,8,128]{2,1,0:T(8,128)S(1)}, u32[]{:S(2)}, u32[]{:S(2)}) collective-permute-start(f32[24,8,128]{2,1,0:T(8,128)S(1)} %get-tuple-element.63), channel_id=1, source_target_pairs={{8,2},{2,8},{10,4},{4,10},{12,6},{6,12},{24,18},{18,24},{26,20},{2... | collective-permute-start | bytes 294920 | tf_op jit(solution)/shard_map/ppermute | solution.py:799
  36.1 0.0 collective-permute-start.6
  36.1 3.3 %collective-permute-done.5 = f32[24,8,128]{2,1,0:T(8,128)S(1)} collective-permute-done((f32[24,8,128]{2,1,0:T(8,128)S(1)}, f32[24,8,128]{2,1,0:T(8,128)S(1)}, u32[]{:S(2)}, u32[]{:S(2)}) %collective-permute-start.5) | collective-permute-done | bytes 98336 | tf_op jit(solution)/shard_map/ppermute | solution.py:799
  39.4 0.0 collective-permute-done.6
  39.4 0.5 %middle.1 = (f32[28,16,128]{2,1,0:T(8,128)S(1)}, f32[28,16,128]{2,1,0:T(8,128)S(1)}, f32[28,16,128]{2,1,0:T(8,128)S(1)}, f32[28,16,128]{2,1,0:T(8,128)S(1)}) custom-call(f32[18,8,128]{2,1,0:T(8,128)S(1)} %get-tuple-element.50.mine, f32[6,8,128]{2,1,0:T(8,128)S(1)} %collective-permute-done.4.across, f32[48,8,128]{2,1,0:T(8,128)S(1)} %pad_maximum_fusion.both), custom_call_target="tpu_custom_call" | custom-call | flops 10000000 | bytes 4000000 | tf_op jit(solution)/shard_map/middle/pallas_call | solution.py:722
  40.0 0.7 %all-to-all-done.blocks = f32[32,16,128]{2,1,0:T(8,128)S(1)} async-done(((f32[32,16,128]{2,1,0:T(8,128)}), f32[32,16,128]{2,1,0:T(8,128)S(1)}, u32[]{:S(2)}, u32[]{:S(2)}) %all-to-all-start) | async-done | bytes 262176 | tf_op jit(solution)/shard_map/all_to_all | solution.py:797
  40.7 3.6 %up.1 = f32[32,8,128]{2,1,0:T(8,128)S(1)} custom-call(f32[32,16,128]{2,1,0:T(8,128)S(1)} %all-to-all-done.blocks, f32[28,16,128]{2,1,0:T(8,128)S(1)} %get-tuple-element.53.r1, f32[28,16,128]{2,1,0:T(8,128)S(1)} %get-tuple-element.54.k1, f32[28,16,128]{2,1,0:T(8,128)S(1)} %get-tuple-element.55.w1, f32[28,16,128]{2,1,0:T(8,128)S(1)} %get-tuple-element.56.v21, ...), custom_call_target="tpu_custom_call" | custom-call | flops 10000000 | bytes 4000000 | tf_op jit(solution)/shard_map/up/pallas_call | solution.py:722
  44.3 0.1 collective-permute-start.7
  44.4 1.2 %collective-permute-done.7 = f32[16,8,128]{2,1,0:T(8,128)S(1)} collective-permute-done((f32[16,8,128]{2,1,0:T(8,128)S(1)}, f32[16,8,128]{2,1,0:T(8,128)S(1)}, u32[]{:S(2)}, u32[]{:S(2)}) %collective-permute-start.7) | collective-permute-done | bytes 65568 | tf_op jit(solution)/shard_map/ppermute | solution.py:828
  45.7 0.7 %maximum_select_fusion = f32[16,16,128]{2,1,0:T(8,128)} fusion(f32[16,8,128]{2,1,0:T(8,128)S(1)} %collective-permute-done.7, f32[16,8,128]{2,1,0:T(8,128)S(1)} %get-tuple-element.61, pred[]{:T(512)S(6)} %eq.3), kind=kLoop, calls=%fused_computation.1 | loop fusion | flops 98304 | bytes 262145 | tf_op jit(solution)/shard_map/jit(_where)/select_n | solution.py:829
  (3 shorter events, 0.0 us)
Async XLA Ops:
  1.9 5.2 %collective-permute-start = (f32[120,128]{1,0:T(8,128)S(1)}, f32[120,128]{1,0:T(8,128)S(1)}, u32[]{:S(2)}, u32[]{:S(2)}) collective-permute-start(f32[120,128]{1,0:T(8,128)S(1)} %get-tuple-element.35.records), channel_id=1, source_target_pairs={{0,1},{1,0},{2,3},{3,2},{4,5},{5,4},{6,7},{7,6},{8,9},{9,8},{10,11... | collective-permute-start | bytes 184328 | tf_op jit(solution)/shard_map/ppermute | solution.py:752
  8.3 1.7 %collective-permute-start.1 = (f32[39,16,128]{2,1,0:T(8,128)S(1)}, f32[39,16,128]{2,1,0:T(8,128)S(1)}, u32[]{:S(2)}, u32[]{:S(2)}) collective-permute-start(f32[39,16,128]{2,1,0:T(8,128)S(1)} %get-tuple-element.40), channel_id=1, source_target_pairs={{0,8},{8,0},{16,24},{24,16},{1,9},{9,1},{17,25},{25,17},{2,10},{10... | collective-permute-start | bytes 958472 | tf_op jit(solution)/shard_map/ppermute | solution.py:775
  10.2 4.9 %collective-permute-start.2 = (f32[10,16,128]{2,1,0:T(8,128)S(1)}, f32[10,16,128]{2,1,0:T(8,128)S(1)}, u32[]{:S(2)}, u32[]{:S(2)}) collective-permute-start(f32[10,16,128]{2,1,0:T(8,128)S(1)} %get-tuple-element.44), channel_id=1, source_target_pairs={{0,16},{16,0},{8,24},{24,8},{1,17},{17,1},{9,25},{25,9},{2,18},{18... | collective-permute-start | bytes 245768 | tf_op jit(solution)/shard_map/ppermute | solution.py:779
  15.2 5.5 %collective-permute-start.3 = (f32[42,8,128]{2,1,0:T(8,128)S(1)}, f32[42,8,128]{2,1,0:T(8,128)S(1)}, u32[]{:S(2)}, u32[]{:S(2)}) collective-permute-start(f32[42,8,128]{2,1,0:T(8,128)S(1)} %get-tuple-element.48), channel_id=1, source_target_pairs={{8,2},{2,8},{10,4},{4,10},{12,6},{6,12},{24,18},{18,24},{26,20},{2... | collective-permute-start | bytes 516104 | tf_op jit(solution)/shard_map/ppermute | solution.py:788
  24.5 16.2 %all-to-all-start = ((f32[32,16,128]{2,1,0:T(8,128)}), f32[32,16,128]{2,1,0:T(8,128)S(1)}, u32[]{:S(2)}, u32[]{:S(2)}) async-start(f32[32,16,128]{2,1,0:T(8,128)} %get-tuple-element.49), calls=%async_computation | async-start | bytes 524288 | tf_op jit(solution)/shard_map/all_to_all | solution.py:797
  30.0 4.2 %collective-permute-start.4 = (f32[6,8,128]{2,1,0:T(8,128)S(1)}, f32[6,8,128]{2,1,0:T(8,128)S(1)}, u32[]{:S(2)}, u32[]{:S(2)}) collective-permute-start(f32[6,8,128]{2,1,0:T(8,128)S(1)} %get-tuple-element.51), channel_id=1, source_target_pairs={{0,16},{16,0},{8,24},{24,8},{1,17},{17,1},{9,25},{25,9},{2,18},{18... | collective-permute-start | bytes 73736 | tf_op jit(solution)/shard_map/ppermute | solution.py:798
  34.3 5.1 %collective-permute-start.5 = (f32[24,8,128]{2,1,0:T(8,128)S(1)}, f32[24,8,128]{2,1,0:T(8,128)S(1)}, u32[]{:S(2)}, u32[]{:S(2)}) collective-permute-start(f32[24,8,128]{2,1,0:T(8,128)S(1)} %get-tuple-element.63), channel_id=1, source_target_pairs={{8,2},{2,8},{10,4},{4,10},{12,6},{6,12},{24,18},{18,24},{26,20},{2... | collective-permute-start | bytes 294920 | tf_op jit(solution)/shard_map/ppermute | solution.py:799
  36.1 3.3 %collective-permute-start.6 = (f32[24,8,128]{2,1,0:T(8,128)S(1)}, f32[24,8,128]{2,1,0:T(8,128)S(1)}, u32[]{:S(2)}, u32[]{:S(2)}) collective-permute-start(f32[24,8,128]{2,1,0:T(8,128)S(1)} %get-tuple-element.64), channel_id=1, source_target_pairs={{0,8},{8,0},{16,24},{24,16},{1,9},{9,1},{17,25},{25,17},{2,10},{10... | collective-permute-start | bytes 294920 | tf_op jit(solution)/shard_map/ppermute | solution.py:800
  44.3 1.3 %collective-permute-start.7 = (f32[16,8,128]{2,1,0:T(8,128)S(1)}, f32[16,8,128]{2,1,0:T(8,128)S(1)}, u32[]{:S(2)}, u32[]{:S(2)}) collective-permute-start(f32[16,8,128]{2,1,0:T(8,128)S(1)} %get-tuple-element.62), channel_id=1, source_target_pairs={{0,8},{8,0},{16,24},{24,16},{1,9},{9,1},{17,25},{25,17},{2,10},{10... | collective-permute-start | bytes 196616 | tf_op jit(solution)/shard_map/ppermute | solution.py:828

commit v7 on v6

--- a/solution.py
+++ b/solution.py
@@ -272,7 +272,7 @@
     sent[...] = all_[:, pl.ds(give, 16), :]
 
 
-def pair_kernel(own, other, source, kappa, halo, message):
+def pair_kernel(own, other, source, kappa, halo, message, strip, corner):
     p, c, _, _ = place()
     source[...] = jnp.zeros_like(source)
     kappa[...] = jnp.zeros_like(kappa)
@@ -302,35 +302,17 @@
         low = jnp.where(lane < 64, roll(tiles[6 * i], -64, 1), roll(tiles[6 * i + 1], 64, 1))
         message[8 + i] = jnp.where(lane < 80, pick(p, roll(tiles[6 * i + 4], -16, 1), low), 0.0)
 
-
-def across_kernel(source_in, kappa_in, halo_in, other, source, kappa, halo, message):
-    p, c, _, _ = place()
-    source[...] = source_in[...]
-    kappa[...] = kappa_in[...]
-    at = 36 - 34 * p
-    source[pl.ds(at, 4)] = source[pl.ds(at, 4)] + other[0:4]
-    kappa[pl.ds(37 - 36 * p, 4)] = other[4:8]
-    zero = jnp.zeros((16, 128), F32)
-    lane = iota((16, 128), 1)
-    halo[...] = halo_in[...]
-    for i in range(2):
-        got = other[8 + i]
-        wide = roll(got, 64, 1)
-        halo[6 * i] = halo[6 * i] + pick(p, zero, roll(got, 16, 1))
-        halo[6 * i + 4] = halo[6 * i + 4] + pick(p, jnp.where(lane >= 64, wide, 0.0), zero)
-        halo[6 * i + 5] = halo[6 * i + 5] + pick(p, jnp.where(lane < 16, wide, 0.0), zero)
-    first = 5 - 4 * p
-
     def cut(s, k):
         s = pick(c, roll(s, -3, 1)[:, :8], roll(s, -9, 1)[:, :8])
         k = pick(c, k[:, :8], roll(k, -4, 1)[:, :8])
         return jnp.where(iota(s.shape, 1) < 4, s, k)
 
-    def body(i):
-        message[pl.ds(i, SIZE)] = cut(source[pl.ds(first + i, SIZE)], kappa[pl.ds(first + i, SIZE)])
-
-    chunked(PLANES, body, SIZE)
-    message[PLANES:] = cut(halo[0:6], halo[6:12])
+    first = 5 - 4 * p
+    strip[0:PLANES] = cut(source[pl.ds(first, PLANES)], kappa[pl.ds(first, PLANES)])
+    strip[PLANES:] = cut(halo[0:6], halo[6:12])
+    first = 33 - 29 * p
+    corner[0:5] = cut(source[pl.ds(first, 5)], kappa[pl.ds(first, 5)])
+    corner[5:6] = cut(message[8:9], message[9:10])
 
 
 def chunked(count, body, size=4):
@@ -400,8 +382,8 @@
 
 
 def down_kernel(
-    n_gy, source_in, kappa_in, halo_in, other, left, kappa, weight, v, along, beside, message, parts,
-    rhs, cx, cy, cz, diag, v1, v2, sums, flat, halo,
+    n_gy, source_in, kappa_in, halo_in, across, along_in, corner, left, kappa, weight, v, along, beside, message, parts,
+    rhs, cx, cy, cz, diag, v1, v2, sums, flat, halo, source, kap, strip,
 ):
     p, c, b, t = place()
     first = 5 - 4 * p
@@ -410,6 +392,27 @@
         ref[0:5] = jnp.zeros((5, 16, 256), F32)
         ref[37:42] = jnp.zeros((5, 16, 256), F32)
 
+    source[...] = source_in[...]
+    kap[...] = kappa_in[...]
+    strip[...] = along_in[...]
+    at = 36 - 34 * p
+    source[pl.ds(at, 4)] = source[pl.ds(at, 4)] + across[0:4]
+    kap[pl.ds(37 - 36 * p, 4)] = across[4:8]
+    at = 31 - 31 * p
+    strip[pl.ds(at, 5)] = strip[pl.ds(at, 5)] + corner[0:5]
+
+    def packed(got):
+        lane = iota(got.shape, 1)
+        wide, zero = roll(got, 64, 1), jnp.zeros_like(got)
+        return (
+            pick(p, zero, roll(got, 16, 1)),
+            pick(p, jnp.where(lane >= 64, wide, 0.0), zero),
+            pick(p, jnp.where(lane < 16, wide, 0.0), zero),
+        )
+
+    for i, part in zip((0, 4, 5), packed(corner[5])):
+        strip[PLANES + i] = strip[PLANES + i] + part
+
     def merge(got):
         n = got.shape[0]
         got = jnp.concatenate([got, jnp.zeros((n, 8, 128), F32)], 1)
@@ -418,9 +421,12 @@
         s, k = jnp.where(top, got, 0.0), jnp.where(top, 0.0, got)
         return pick(c, roll(s, 1, 1), roll(s, 11, 1)), pick(c, roll(k, -4, 1), roll(k, 8, 1))
 
-    s, k = merge(other[PLANES:])
+    s, k = merge(strip[PLANES:])
     halo[0:6] = halo_in[0:6] + s
     halo[6:12] = halo_in[6:12] + k
+    for n in range(2):
+        for i, part in zip((0, 4, 5), packed(across[8 + n])):
+            halo[6 * n + i] = halo[6 * n + i] + part
     lane = iota((16, 128), 1)
     s_lanes = pick(t, (lane < 10).astype(jnp.int32), (lane >= 118).astype(jnp.int32)) > 0
     k_lanes = pick(t, (lane < 11).astype(jnp.int32), (lane >= 117).astype(jnp.int32)) > 0
@@ -428,14 +434,14 @@
     def enter(i):
         r = first + i
         rows = pl.ds(r, SIZE)
-        s, k = merge(other[pl.ds(i, SIZE)])
+        s, k = merge(strip[pl.ds(i, SIZE)])
         far_s, far_k = [], []
         for j in range(SIZE):
             tile, by = (r + j) >> 3, 16 * ((r + j) & 7)
             far_s.append(jnp.where(s_lanes, pltpu.roll(halo[tile], (127 - by - 9 * t) & 127, 1), 0.0)[None])
             far_k.append(jnp.where(k_lanes, pltpu.roll(halo[6 + tile], (128 - by - 11 * t) & 127, 1), 0.0)[None])
-        rhs[rows] = jnp.concatenate([source_in[rows] + s, jnp.concatenate(far_s, 0)], 2)
-        kappa[rows] = jnp.concatenate([kappa_in[rows] + k, jnp.concatenate(far_k, 0)], 2)
+        rhs[rows] = jnp.concatenate([source[rows] + s, jnp.concatenate(far_s, 0)], 2)
+        kappa[rows] = jnp.concatenate([kap[rows] + k, jnp.concatenate(far_k, 0)], 2)
 
     chunked(PLANES, enter, SIZE)
     faces(kappa, cx, cy, cz, weight, diag, first, PLANES, 1.0, False, PLANES)
@@ -774,25 +780,34 @@
     swap = [(0, 1), (1, 0), (2, 3), (3, 2)]
     got = lax.ppermute(sent, "gx", swap)
     held = [(ROWS, 16, 128), (ROWS, 16, 128), (12, 16, 128)]
-    *fields, message = call(pair_kernel, "pair", held + [(10, 16, 128)], [], own, got)
+    *fields, message, strip, corner = call(
+        pair_kernel, "pair", held + [(10, 16, 128), (PLANES + 6, 8, 128), (6, 8, 128)], [], own, got
+    )
     cross = [(0, 2), (2, 0), (1, 3), (3, 1)]
-    got = lax.ppermute(message, "gx", cross)
-    *fields, message = call(across_kernel, "across", held + [(PLANES + 6, 8, 128)], [], *fields, got)
-    turns = []
+    across = lax.ppermute(message, "gx", cross)
+    turns, corners = [], []
     for p in range(2):
         for b in range(n_gy - 1):
             low, high = (2 * p + 1) * n_gy + b, 2 * p * n_gy + b + 1
             turns += [(low, high), (high, low)]
+            high = 2 * (1 - p) * n_gy + b + 1
+            corners += [(low, high), (high, low)]
     for low, high in ((0, 2 * n_gy), (2 * n_gy - 1, 4 * n_gy - 1)):
         turns += [(low, high), (high, low)]
-    got = lax.ppermute(message, ("gx", "gy"), turns)
+        corners += [(low, high), (high, low)]
+    strip = lax.ppermute(strip, ("gx", "gy"), turns)
+    corner = lax.ppermute(corner, ("gx", "gy"), corners)
     *fine, along, beside, message, parts = call(
         functools.partial(down_kernel, n_gy),
         "down",
         [window] * 3 + [(32, 8, 128), (18, 8, 128), (18, 8, 128), (6, 8, 128), (8 * n_gy, 16, 128)],
-        big * 7 + [((640, 128), F32), ((48, 128), F32), ((12, 16, 128), F32)],
+        big * 7 + [((640, 128), F32), ((48, 128), F32), ((12, 16, 128), F32)]
+        + [((ROWS, 16, 128), F32)] * 2
+        + [((PLANES + 6, 8, 128), F32)],
         *fields,
-        got,
+        across,
+        strip,
+        corner,
     )
     blocks = lax.all_to_all(parts, ("gx", "gy", "gz"), split_axis=0, concat_axis=0, tiled=True)
     across = lax.ppermute(message, "gx", cross)

time: 46.5 us -> 43.4 us (0.933)
  waiting for transfers between devices: 16.9 us -> 13.8 us
    ppermute x2, waiting for transfers between devices: 6.41 us -> 3.38 us  [the longest x1 3.38 us: paired(): corner = lax.ppermute(corner, ('gx', 'gy'), corners)]
    ppermute x1 -> x2, starting transfers between devices: 1.83 us -> 1.91 us  [paired(): across = lax.ppermute(message, 'gx', cross)]
    pallas_call x8 -> x7, Pallas kernels: 12.4 us -> 12.4 us  [call(): pl.pallas_call(kernel, name=name, out_shape=[jax.ShapeDtypeStruct(s, F32)...]
    ppermute x1 -> x2, waiting for transfers between devices: 2.41 us -> 2.41 us  [paired(): across = lax.ppermute(message, 'gx', cross)]
  transfers between devices with their start and end apart: 9 -> 10, of which waited for: 8 -> 7; matrix products, arithmetic and copies ran while one was open for 0% -> 0% of each run, Pallas kernels for 3% -> 4%
where the time goes in v7:
time: 43.4 us; the launch traced here: 43.2 us
  starting transfers between devices  16.2 us (37%)
  waiting for transfers between devices  13.8 us (32%)
  Pallas kernels  12.4 us (29%)
  other arithmetic  0.69 us (2%)
    pallas_call x7, Pallas kernels, call(): pl.pallas_call(kernel, name=name, out_shape=[jax.ShapeDtypeStruct(s, F32)...  12.4 us
    all_to_all x1, starting transfers between devices, paired(): lax.all_to_all(parts, ('gx', 'gy', 'gz'), split_axis=0, concat_axis=0, ti...  5.23 us
    ppermute x1, waiting for transfers between devices, paired(): corner = lax.ppermute(corner, ('gx', 'gy'), corners)  3.38 us
    ppermute x1, waiting for transfers between devices, paired(): got = lax.ppermute(jnp.concatenate([along, across]), ('gx', 'gy'), turns)  3.29 us
    ppermute x1, starting transfers between devices, paired(): got = lax.ppermute(message, 'gz', [(0, 1), (1, 0)])  3 us
    ppermute x2, waiting for transfers between devices, paired(): across = lax.ppermute(message, 'gx', cross)  2.41 us
    ppermute x1, starting transfers between devices, paired(): strip = lax.ppermute(strip, ('gx', 'gy'), turns)  2.11 us
    ppermute x1, starting transfers between devices, paired(): corner = lax.ppermute(corner, ('gx', 'gy'), corners)  1.95 us
  transfers between devices with their start and end apart: 10, of which 7 were waited for; matrix products, arithmetic and copies ran while one was open for 0% of the time, Pallas kernels for 4%

profile of v7, /device:TPU:0, one launch (start us, length us, event | category | flops | bytes accessed | tf_op | source)
XLA Modules:
  0.0 43.2 jit_solution(3192415937264085602)
XLA Ops:
  0.0 1.9 %message.1 = (f32[16,16,128]{2,1,0:T(8,128)S(1)}, f32[3,16,16,128]{3,2,1,0:T(8,128)S(1)}, f32[120,128]{1,0:T(8,128)S(1)}, f32[48,128]{1,0:T(8,128)S(1)}) custom-call(f32[16,16,128]{2,1,0:T(8,128)} %refs_0_.1, f32[3,16,16,128]{3,2,1,0:T(8,128)} %refs_1_.1, s32[8,128]{1,0:T(8,128)} %bitcast.3, s32[8,128]{1,0:T(8,128)} %bitcast.4, f32[8,128]{1,0:T(8,128)} %bitcast.5), custom_call_target="tpu_custom_call" | custom-call | flops 10000000 | bytes 4000000 | tf_op jit(solution)/shard_map/message/pallas_call | solution.py:728
  1.9 3.0 %collective-permute-start = (f32[120,128]{1,0:T(8,128)S(1)}, f32[120,128]{1,0:T(8,128)S(1)}, u32[]{:S(2)}, u32[]{:S(2)}) collective-permute-start(f32[120,128]{1,0:T(8,128)S(1)} %get-tuple-element.33.records), channel_id=1, source_target_pairs={{0,1},{1,0},{2,3},{3,2},{4,5},{5,4},{6,7},{7,6},{8,9},{9,8},{10,11... | collective-permute-start | bytes 184328 | tf_op jit(solution)/shard_map/ppermute | solution.py:758
  4.9 1.0 %source.1 = (f32[18,24,128]{2,1,0:T(8,128)S(1)}, f32[256,256]{1,0:T(8,128)S(1)}) custom-call(f32[16,16,128]{2,1,0:T(8,128)S(1)} %get-tuple-element.31.chi, f32[3,16,16,128]{3,2,1,0:T(8,128)S(1)} %get-tuple-element.32.inducing, f32[120,128]{1,0:T(8,128)S(1)} %get-tuple-element.33.records), custom_call_target="tpu_custom_call" | custom-call | flops 10000000 | bytes 4000000 | tf_op jit(solution)/shard_map/source/pallas_call | solution.py:728
  5.9 1.2 %collective-permute-done.other = f32[120,128]{1,0:T(8,128)S(1)} collective-permute-done((f32[120,128]{1,0:T(8,128)S(1)}, f32[120,128]{1,0:T(8,128)S(1)}, u32[]{:S(2)}, u32[]{:S(2)}) %collective-permute-start) | collective-permute-done | bytes 61472 | tf_op jit(solution)/shard_map/ppermute | solution.py:758
  7.1 1.1 %deposit.1 = (f32[39,16,128]{2,1,0:T(8,128)S(1)}, f32[39,16,128]{2,1,0:T(8,128)S(1)}) custom-call(f32[18,24,128]{2,1,0:T(8,128)S(1)} %get-tuple-element.34.source, f32[48,128]{1,0:T(8,128)S(1)} %get-tuple-element.35.spill, f32[16,16,128]{2,1,0:T(8,128)S(1)} %get-tuple-element.31.chi, f32[256,256]{1,0:T(8,128)S(1)} %get-tuple-element.36.mine, ...), custom_call_target="tpu_custom_call" | custom-call | flops 10000000 | bytes 4000000 | tf_op jit(solution)/shard_map/deposit/pallas_call | solution.py:728
  8.3 0.1 collective-permute-start.1
  8.3 1.6 %collective-permute-done.1.other = f32[39,16,128]{2,1,0:T(8,128)S(1)} collective-permute-done((f32[39,16,128]{2,1,0:T(8,128)S(1)}, f32[39,16,128]{2,1,0:T(8,128)S(1)}, u32[]{:S(2)}, u32[]{:S(2)}) %collective-permute-start.1) | collective-permute-done | bytes 319520 | tf_op jit(solution)/shard_map/ppermute | solution.py:781
  10.0 0.2 pair.1
  10.2 2.1 %collective-permute-start.3 = (f32[42,8,128]{2,1,0:T(8,128)S(1)}, f32[42,8,128]{2,1,0:T(8,128)S(1)}, u32[]{:S(2)}, u32[]{:S(2)}) collective-permute-start(f32[42,8,128]{2,1,0:T(8,128)S(1)} %get-tuple-element.43), channel_id=1, source_target_pairs={{8,2},{2,8},{10,4},{4,10},{12,6},{6,12},{24,18},{18,24},{26,20},{2... | collective-permute-start | bytes 516104 | tf_op jit(solution)/shard_map/ppermute | solution.py:798
  12.3 0.1 collective-permute-start.2
  12.4 1.9 %collective-permute-start.4 = (f32[6,8,128]{2,1,0:T(8,128)S(1)}, f32[6,8,128]{2,1,0:T(8,128)S(1)}, u32[]{:S(2)}, u32[]{:S(2)}) collective-permute-start(f32[6,8,128]{2,1,0:T(8,128)S(1)} %get-tuple-element.44), channel_id=1, source_target_pairs={{8,18},{18,8},{10,20},{20,10},{12,22},{22,12},{24,2},{2,24},{26,4}... | collective-permute-start | bytes 73736 | tf_op jit(solution)/shard_map/ppermute | solution.py:799
  14.3 3.4 %collective-permute-done.4.corner = f32[6,8,128]{2,1,0:T(8,128)S(1)} collective-permute-done((f32[6,8,128]{2,1,0:T(8,128)S(1)}, f32[6,8,128]{2,1,0:T(8,128)S(1)}, u32[]{:S(2)}, u32[]{:S(2)}) %collective-permute-start.4) | collective-permute-done | bytes 24608 | tf_op jit(solution)/shard_map/ppermute | solution.py:799
  17.7 0.0 collective-permute-done.2.across
  17.7 0.0 collective-permute-done.3.along_in
  17.7 3.9 %down.1 = (f32[42,16,256]{2,1,0:T(8,128)S(1)}, f32[42,16,256]{2,1,0:T(8,128)S(1)}, f32[42,16,256]{2,1,0:T(8,128)S(1)}, f32[32,8,128]{2,1,0:T(8,128)S(1)}, f32[18...) custom-call(f32[42,16,128]{2,1,0:T(8,128)S(1)} %get-tuple-element.39.source_, ...), custom_call_target="tpu_custom_call" | custom-call | flops 10000000 | bytes 4000000 | tf_op jit(solution)/shard_map/down/pallas_call | solution.py:728
  21.7 5.2 %all-to-all-start = ((f32[32,16,128]{2,1,0:T(8,128)}), f32[32,16,128]{2,1,0:T(8,128)S(1)}, u32[]{:S(2)}, u32[]{:S(2)}) async-start(f32[32,16,128]{2,1,0:T(8,128)} %get-tuple-element.45), calls=%async_computation | async-start | bytes 524288 | tf_op jit(solution)/shard_map/all_to_all | solution.py:812
  26.9 1.8 %collective-permute-start.5 = (f32[6,8,128]{2,1,0:T(8,128)S(1)}, f32[6,8,128]{2,1,0:T(8,128)S(1)}, u32[]{:S(2)}, u32[]{:S(2)}) collective-permute-start(f32[6,8,128]{2,1,0:T(8,128)S(1)} %get-tuple-element.47), channel_id=1, source_target_pairs={{0,16},{16,0},{8,24},{24,8},{1,17},{17,1},{9,25},{25,9},{2,18},{18... | collective-permute-start | bytes 73736 | tf_op jit(solution)/shard_map/ppermute | solution.py:813
  28.7 2.4 %collective-permute-done.5.across = f32[6,8,128]{2,1,0:T(8,128)S(1)} collective-permute-done((f32[6,8,128]{2,1,0:T(8,128)S(1)}, f32[6,8,128]{2,1,0:T(8,128)S(1)}, u32[]{:S(2)}, u32[]{:S(2)}) %collective-permute-start.5) | collective-permute-done | bytes 24608 | tf_op jit(solution)/shard_map/ppermute | solution.py:813
  31.2 1.8 %collective-permute-start.6 = (f32[24,8,128]{2,1,0:T(8,128)S(1)}, f32[24,8,128]{2,1,0:T(8,128)S(1)}, u32[]{:S(2)}, u32[]{:S(2)}) collective-permute-start(f32[24,8,128]{2,1,0:T(8,128)S(1)} %get-tuple-element.59), channel_id=1, source_target_pairs={{8,2},{2,8},{10,4},{4,10},{12,6},{6,12},{24,18},{18,24},{26,20},{2... | collective-permute-start | bytes 294920 | tf_op jit(solution)/shard_map/ppermute | solution.py:814
  33.0 0.0 collective-permute-start.7
  33.0 3.3 %collective-permute-done.6 = f32[24,8,128]{2,1,0:T(8,128)S(1)} collective-permute-done((f32[24,8,128]{2,1,0:T(8,128)S(1)}, f32[24,8,128]{2,1,0:T(8,128)S(1)}, u32[]{:S(2)}, u32[]{:S(2)}) %collective-permute-start.6) | collective-permute-done | bytes 98336 | tf_op jit(solution)/shard_map/ppermute | solution.py:814
  36.3 0.0 collective-permute-done.7
  36.3 0.5 %middle.1 = (f32[28,16,128]{2,1,0:T(8,128)S(1)}, f32[28,16,128]{2,1,0:T(8,128)S(1)}, f32[28,16,128]{2,1,0:T(8,128)S(1)}, f32[28,16,128]{2,1,0:T(8,128)S(1)}) custom-call(f32[18,8,128]{2,1,0:T(8,128)S(1)} %get-tuple-element.46.mine, f32[6,8,128]{2,1,0:T(8,128)S(1)} %collective-permute-done.5.across, f32[48,8,128]{2,1,0:T(8,128)S(1)} %pad_maximum_fusion.both), custom_call_target="tpu_custom_call" | custom-call | flops 10000000 | bytes 4000000 | tf_op jit(solution)/shard_map/middle/pallas_call | solution.py:728
  36.9 0.7 %all-to-all-done.blocks = f32[32,16,128]{2,1,0:T(8,128)S(1)} async-done(((f32[32,16,128]{2,1,0:T(8,128)}), f32[32,16,128]{2,1,0:T(8,128)S(1)}, u32[]{:S(2)}, u32[]{:S(2)}) %all-to-all-start) | async-done | bytes 262176 | tf_op jit(solution)/shard_map/all_to_all | solution.py:812
  37.6 3.6 %up.1 = f32[32,8,128]{2,1,0:T(8,128)S(1)} custom-call(f32[32,16,128]{2,1,0:T(8,128)S(1)} %all-to-all-done.blocks, f32[28,16,128]{2,1,0:T(8,128)S(1)} %get-tuple-element.49.r1, f32[28,16,128]{2,1,0:T(8,128)S(1)} %get-tuple-element.50.k1, f32[28,16,128]{2,1,0:T(8,128)S(1)} %get-tuple-element.51.w1, f32[28,16,128]{2,1,0:T(8,128)S(1)} %get-tuple-element.52.v21, ...), custom_call_target="tpu_custom_call" | custom-call | flops 10000000 | bytes 4000000 | tf_op jit(solution)/shard_map/up/pallas_call | solution.py:728
  41.2 0.1 collective-permute-start.8
  41.3 1.2 %collective-permute-done.8 = f32[16,8,128]{2,1,0:T(8,128)S(1)} collective-permute-done((f32[16,8,128]{2,1,0:T(8,128)S(1)}, f32[16,8,128]{2,1,0:T(8,128)S(1)}, u32[]{:S(2)}, u32[]{:S(2)}) %collective-permute-start.8) | collective-permute-done | bytes 65568 | tf_op jit(solution)/shard_map/ppermute | solution.py:843
  42.5 0.7 %maximum_select_fusion = f32[16,16,128]{2,1,0:T(8,128)} fusion(f32[16,8,128]{2,1,0:T(8,128)S(1)} %collective-permute-done.8, f32[16,8,128]{2,1,0:T(8,128)S(1)} %get-tuple-element.57, pred[]{:T(512)S(6)} %eq.3), kind=kLoop, calls=%fused_computation.1 | loop fusion | flops 98304 | bytes 262145 | tf_op jit(solution)/shard_map/jit(_where)/select_n | solution.py:844
  (3 shorter events, 0.0 us)
Async XLA Ops:
  1.9 5.2 %collective-permute-start = (f32[120,128]{1,0:T(8,128)S(1)}, f32[120,128]{1,0:T(8,128)S(1)}, u32[]{:S(2)}, u32[]{:S(2)}) collective-permute-start(f32[120,128]{1,0:T(8,128)S(1)} %get-tuple-element.33.records), channel_id=1, source_target_pairs={{0,1},{1,0},{2,3},{3,2},{4,5},{5,4},{6,7},{7,6},{8,9},{9,8},{10,11... | collective-permute-start | bytes 184328 | tf_op jit(solution)/shard_map/ppermute | solution.py:758
  8.3 1.7 %collective-permute-start.1 = (f32[39,16,128]{2,1,0:T(8,128)S(1)}, f32[39,16,128]{2,1,0:T(8,128)S(1)}, u32[]{:S(2)}, u32[]{:S(2)}) collective-permute-start(f32[39,16,128]{2,1,0:T(8,128)S(1)} %get-tuple-element.38), channel_id=1, source_target_pairs={{0,8},{8,0},{16,24},{24,16},{1,9},{9,1},{17,25},{25,17},{2,10},{10... | collective-permute-start | bytes 958472 | tf_op jit(solution)/shard_map/ppermute | solution.py:781
  10.2 7.5 %collective-permute-start.3 = (f32[42,8,128]{2,1,0:T(8,128)S(1)}, f32[42,8,128]{2,1,0:T(8,128)S(1)}, u32[]{:S(2)}, u32[]{:S(2)}) collective-permute-start(f32[42,8,128]{2,1,0:T(8,128)S(1)} %get-tuple-element.43), channel_id=1, source_target_pairs={{8,2},{2,8},{10,4},{4,10},{12,6},{6,12},{24,18},{18,24},{26,20},{2... | collective-permute-start | bytes 516104 | tf_op jit(solution)/shard_map/ppermute | solution.py:798
  12.3 5.4 %collective-permute-start.2 = (f32[10,16,128]{2,1,0:T(8,128)S(1)}, f32[10,16,128]{2,1,0:T(8,128)S(1)}, u32[]{:S(2)}, u32[]{:S(2)}) collective-permute-start(f32[10,16,128]{2,1,0:T(8,128)S(1)} %get-tuple-element.42), channel_id=1, source_target_pairs={{0,16},{16,0},{8,24},{24,8},{1,17},{17,1},{9,25},{25,9},{2,18},{18... | collective-permute-start | bytes 245768 | tf_op jit(solution)/shard_map/ppermute | solution.py:787
  12.4 5.3 %collective-permute-start.4 = (f32[6,8,128]{2,1,0:T(8,128)S(1)}, f32[6,8,128]{2,1,0:T(8,128)S(1)}, u32[]{:S(2)}, u32[]{:S(2)}) collective-permute-start(f32[6,8,128]{2,1,0:T(8,128)S(1)} %get-tuple-element.44), channel_id=1, source_target_pairs={{8,18},{18,8},{10,20},{20,10},{12,22},{22,12},{24,2},{2,24},{26,4}... | collective-permute-start | bytes 73736 | tf_op jit(solution)/shard_map/ppermute | solution.py:799
  21.7 15.9 %all-to-all-start = ((f32[32,16,128]{2,1,0:T(8,128)}), f32[32,16,128]{2,1,0:T(8,128)S(1)}, u32[]{:S(2)}, u32[]{:S(2)}) async-start(f32[32,16,128]{2,1,0:T(8,128)} %get-tuple-element.45), calls=%async_computation | async-start | bytes 524288 | tf_op jit(solution)/shard_map/all_to_all | solution.py:812
  26.9 4.2 %collective-permute-start.5 = (f32[6,8,128]{2,1,0:T(8,128)S(1)}, f32[6,8,128]{2,1,0:T(8,128)S(1)}, u32[]{:S(2)}, u32[]{:S(2)}) collective-permute-start(f32[6,8,128]{2,1,0:T(8,128)S(1)} %get-tuple-element.47), channel_id=1, source_target_pairs={{0,16},{16,0},{8,24},{24,8},{1,17},{17,1},{9,25},{25,9},{2,18},{18... | collective-permute-start | bytes 73736 | tf_op jit(solution)/shard_map/ppermute | solution.py:813
  31.2 5.1 %collective-permute-start.6 = (f32[24,8,128]{2,1,0:T(8,128)S(1)}, f32[24,8,128]{2,1,0:T(8,128)S(1)}, u32[]{:S(2)}, u32[]{:S(2)}) collective-permute-start(f32[24,8,128]{2,1,0:T(8,128)S(1)} %get-tuple-element.59), channel_id=1, source_target_pairs={{8,2},{2,8},{10,4},{4,10},{12,6},{6,12},{24,18},{18,24},{26,20},{2... | collective-permute-start | bytes 294920 | tf_op jit(solution)/shard_map/ppermute | solution.py:814
  33.0 3.3 %collective-permute-start.7 = (f32[24,8,128]{2,1,0:T(8,128)S(1)}, f32[24,8,128]{2,1,0:T(8,128)S(1)}, u32[]{:S(2)}, u32[]{:S(2)}) collective-permute-start(f32[24,8,128]{2,1,0:T(8,128)S(1)} %get-tuple-element.60), channel_id=1, source_target_pairs={{0,8},{8,0},{16,24},{24,16},{1,9},{9,1},{17,25},{25,17},{2,10},{10... | collective-permute-start | bytes 294920 | tf_op jit(solution)/shard_map/ppermute | solution.py:815
  41.2 1.3 %collective-permute-start.8 = (f32[16,8,128]{2,1,0:T(8,128)S(1)}, f32[16,8,128]{2,1,0:T(8,128)S(1)}, u32[]{:S(2)}, u32[]{:S(2)}) collective-permute-start(f32[16,8,128]{2,1,0:T(8,128)S(1)} %get-tuple-element.58), channel_id=1, source_target_pairs={{0,8},{8,0},{16,24},{24,16},{1,9},{9,1},{17,25},{25,17},{2,10},{10... | collective-permute-start | bytes 196616 | tf_op jit(solution)/shard_map/ppermute | solution.py:843

commit v8 on v7

--- a/solution.py
+++ b/solution.py
@@ -158,16 +158,20 @@
     given, (chi, inducing, message, spill), (dest, cell, value, done) = refs[:5], refs[5:9], refs[9:]
     _, _, _, t = place()
     held = (chi, inducing, dest, cell, value)
-    copies = [pltpu.make_async_copy(a, b, done.at[i]) for i, (a, b) in enumerate(zip(given, held))]
-    for copy in copies:
-        copy.start()
-    for copy in copies:
-        copy.wait()
+    pairs = [(a.at[4 * i : 4 * i + 4], b.at[4 * i : 4 * i + 4]) for i in range(4) for a, b in [(given[0], held[0])]]
+    pairs += [(given[1].at[:, 4 * i : 4 * i + 4], held[1].at[:, 4 * i : 4 * i + 4]) for i in range(4)]
+    pairs += list(zip(given[2:], held[2:]))
+    copies = [pltpu.make_async_copy(a, b, done.at[i]) for i, (a, b) in enumerate(pairs)]
+    for i in (0, 4, 1, 5, 2, 6, 3, 7, 8, 9, 10):
+        copies[i].start()
     lane = iota((16, 128), 1)
     turn = 11 - 10 * t
     wanted = pick(t, (lane < 11).astype(jnp.int32), ((lane >= 1) & (lane < 12)).astype(jnp.int32)) > 0
     packs = [[jnp.zeros((16, 128), F32)] * 2 for _ in range(4)]
     for x in range(16):
+        if x % 4 == 0:
+            copies[x // 4].wait()
+            copies[4 + x // 4].wait()
         near = jnp.where(wanted, pltpu.roll(chi[x], turn, 1), 0.0)
         parts = [jnp.where(wanted, 1.0 + near, 0.0)]
         parts += [near * pltpu.roll(inducing[d, x], turn, 1) for d in range(3)]
@@ -198,36 +202,39 @@
         message[24 * i : 24 * (i + 1)] = body[:, cut]
         message[72 + 16 * i : 88 + 16 * i] = k[:, cut]
     message[48:72] = eleven(ends)
+    for copy in copies[8:]:
+        copy.wait()
     message[104:112] = value[...]
     message[112:120] = (dest[...] * 32768 + cell[...]).astype(F32)
 
 
-def spread_records(records, t, at_row, hi, mid, lo):
-    spot = iota((256, 128), 0)
+def spread_records(records, t, at_row, at_column):
+    row, slot = iota((256, 128), 0), iota((16, 128), 0)
+    z_of = iota((128, 128), 0)
+    at_column[432:512] = jnp.zeros((80, 1024), BF16)
     for j in range(8):
         value = records[104 + j : 105 + j, :]
         code = records[112 + j : 113 + j, :].astype(jnp.int32)
         cells = code & 32767
         z = ((code >> 15) - t) * 128 + (cells & 127)
         far = z - 128 + 138 * t
-        column = jnp.where((far >= 0) & (far < 10), z + 1 + 137 * t, 255)
-        column = jnp.where((z >= 0) & (z < 128), z, column)
+        far = jnp.where((far >= 0) & (far < 10), far + 1 - t, 16)
         cut = slice(128 * j, 128 * (j + 1))
-        at_row[:, cut] = jnp.where(spot == (cells >> 7), 1.0, 0.0).astype(BF16)
-        here = spot == column
-        for part in (hi, mid, lo):
+        at_row[:, cut] = jnp.where(row == (cells >> 7), 1.0, 0.0).astype(BF16)
+        here, there = z_of == z, slot == far
+        for i in range(3):
             short = value.astype(BF16).astype(F32)
-            part[:, cut] = jnp.where(here, short, 0.0).astype(BF16)
+            at_column[128 * i : 128 * (i + 1), cut] = jnp.where(here, short, 0.0).astype(BF16)
+            at_column[384 + 16 * i : 400 + 16 * i, cut] = jnp.where(there, short, 0.0).astype(BF16)
             value = value - short
-    total = jnp.zeros((256, 256), F32)
-    for part in (lo, mid, hi):
-        total = total + lax.dot_general(
-            at_row[...], part[...], (((1,), (1,)), ((), ())), preferred_element_type=F32
-        )
-    return total
-
-
-def source_kernel(chi, inducing, records, source, total, at_row, hi, mid, lo):
+    total = lax.dot_general(
+        at_row[...], at_column[...], (((1,), (1,)), ((), ())), preferred_element_type=F32
+    )
+    near = (total[:, 256:384] + total[:, 128:256]) + total[:, 0:128]
+    return jnp.concatenate([near, total[:, 384:512]], 1)
+
+
+def source_kernel(chi, inducing, records, source, total, at_row, at_column):
     _, _, _, t = place()
     lane = iota((16, 128), 1)
     zero = jnp.zeros((16, 128), F32)
@@ -241,18 +248,19 @@
             source[i] = -0.5 * (stretch(flat) + (roll(y, -1, 0) - roll(y, 1, 0)))
         else:
             source[i] = -0.5 * stretch(flat)
-    total[...] = spread_records(records, t, at_row, hi, mid, lo)
-
-
-def deposit_kernel(source, spill, chi, mine, other, own, sent, all_, at_row, hi, mid, lo):
+    total[...] = spread_records(records, t, at_row, at_column)
+
+
+def deposit_kernel(source, spill, chi, mine, other, own, sent, all_, at_row, at_column):
     _, c, _, t = place()
-    total = mine[...] + spread_records(other, t, at_row, hi, mid, lo)
+    total = mine[...] + spread_records(other, t, at_row, at_column)
     lane = iota((24, 128), 1)
     halo = [other[24 * i : 24 * (i + 1)] + spill[24 * i : 24 * (i + 1)] for i in range(2)]
     for i in range(18):
         x = i - 1
         if 0 <= x < 16:
-            got = stretch(total[16 * x : 16 * x + 16, 128:])
+            got = total[16 * x : 16 * x + 16, 128:]
+            got = stretch((roll(got, -32, 1) + roll(got, -16, 1)) + got)
             halo[x // 8] = halo[x // 8] + roll(jnp.where(lane < 16, got, 0.0), 16 * (x % 8), 1)
             add = stretch(total[16 * x : 16 * x + 16, :128])
             tile, by = other[24 * (x // 8) : 24 * (x // 8) + 24], 16 * (x % 8)
@@ -383,7 +391,7 @@
 
 def down_kernel(
     n_gy, source_in, kappa_in, halo_in, across, along_in, corner, left, kappa, weight, v, along, beside, message, parts,
-    rhs, cx, cy, cz, diag, v1, v2, sums, flat, halo, source, kap, strip,
+    rhs, cx, cy, cz, diag, v1, v2, sums, flat, halo, packs, done,
 ):
     p, c, b, t = place()
     first = 5 - 4 * p
@@ -392,14 +400,14 @@
         ref[0:5] = jnp.zeros((5, 16, 256), F32)
         ref[37:42] = jnp.zeros((5, 16, 256), F32)
 
-    source[...] = source_in[...]
-    kap[...] = kappa_in[...]
-    strip[...] = along_in[...]
-    at = 36 - 34 * p
-    source[pl.ds(at, 4)] = source[pl.ds(at, 4)] + across[0:4]
-    kap[pl.ds(37 - 36 * p, 4)] = across[4:8]
-    at = 31 - 31 * p
-    strip[pl.ds(at, 5)] = strip[pl.ds(at, 5)] + corner[0:5]
+    sub = iota((1, 8, 128), 1)
+    sides = [jnp.full((1, 8, 128), (1 - edge) * side, jnp.int32) for side in (1 - c, c)]
+
+    def merge(got):
+        s, k = pltpu.roll(got, 1 + 2 * c, 1), pltpu.roll(got, 4 - 4 * c, 1)
+        s = [jnp.where((sub >= at) & (sub < at + 4) & (side > 0), s, 0.0) for at, side in zip((1, 3), sides)]
+        k = [jnp.where((sub >= at) & (sub < at + 4) & (side > 0), k, 0.0) for at, side in zip((0, 4), sides)]
+        return jnp.concatenate(s, 1), jnp.concatenate(k, 1)
 
     def packed(got):
         lane = iota(got.shape, 1)
@@ -410,22 +418,12 @@
             pick(p, jnp.where(lane < 16, wide, 0.0), zero),
         )
 
-    for i, part in zip((0, 4, 5), packed(corner[5])):
-        strip[PLANES + i] = strip[PLANES + i] + part
-
-    def merge(got):
-        n = got.shape[0]
-        got = jnp.concatenate([got, jnp.zeros((n, 8, 128), F32)], 1)
-        got = pick(edge, got, jnp.zeros_like(got))
-        top = iota(got.shape, 1) < 4
-        s, k = jnp.where(top, got, 0.0), jnp.where(top, 0.0, got)
-        return pick(c, roll(s, 1, 1), roll(s, 11, 1)), pick(c, roll(k, -4, 1), roll(k, 8, 1))
-
-    s, k = merge(strip[PLANES:])
+    s, k = merge(along_in[PLANES:])
+    s2, k2 = merge(corner[...])
     halo[0:6] = halo_in[0:6] + s
     halo[6:12] = halo_in[6:12] + k
-    for n in range(2):
-        for i, part in zip((0, 4, 5), packed(across[8 + n])):
+    for n, more in enumerate((s2, k2)):
+        for i, part in zip((0, 4, 5), packed(across[8 + n] + more[5])):
             halo[6 * n + i] = halo[6 * n + i] + part
     lane = iota((16, 128), 1)
     s_lanes = pick(t, (lane < 10).astype(jnp.int32), (lane >= 118).astype(jnp.int32)) > 0
@@ -434,16 +432,23 @@
     def enter(i):
         r = first + i
         rows = pl.ds(r, SIZE)
-        s, k = merge(strip[pl.ds(i, SIZE)])
+        s, k = merge(along_in[pl.ds(i, SIZE)])
         far_s, far_k = [], []
         for j in range(SIZE):
             tile, by = (r + j) >> 3, 16 * ((r + j) & 7)
             far_s.append(jnp.where(s_lanes, pltpu.roll(halo[tile], (127 - by - 9 * t) & 127, 1), 0.0)[None])
             far_k.append(jnp.where(k_lanes, pltpu.roll(halo[6 + tile], (128 - by - 11 * t) & 127, 1), 0.0)[None])
-        rhs[rows] = jnp.concatenate([source[rows] + s, jnp.concatenate(far_s, 0)], 2)
-        kappa[rows] = jnp.concatenate([kap[rows] + k, jnp.concatenate(far_k, 0)], 2)
+        rhs[rows] = jnp.concatenate([source_in[rows] + s, jnp.concatenate(far_s, 0)], 2)
+        kappa[rows] = jnp.concatenate([kappa_in[rows] + k, jnp.concatenate(far_k, 0)], 2)
 
     chunked(PLANES, enter, SIZE)
+    at = pl.ds(36 - 34 * p, 4)
+    rhs[at, :, 0:128] = rhs[at, :, 0:128] + across[0:4]
+    at = pl.ds(37 - 36 * p, 4)
+    kappa[at, :, 0:128] = kappa[at, :, 0:128] + across[4:8]
+    at = pl.ds(36 - 35 * p, 5)
+    rhs[at, :, 0:128] = rhs[at, :, 0:128] + s2[0:5]
+    kappa[at, :, 0:128] = kappa[at, :, 0:128] + k2[0:5]
     faces(kappa, cx, cy, cz, weight, diag, first, PLANES, 1.0, False, PLANES)
 
     def coarse(fine):
@@ -461,7 +466,6 @@
     v1[rows] = weight[rows] * rhs[rows]
     sweep(v1, v2, rhs, cx, cy, cz, weight, first, PLANES, PLANES)
     left[rows] = resid(v2, rhs, cx, cy, cz, diag, first, PLANES)
-    v[...] = roll(v2[5:37, :, :128], -4, 1)[:, :8]
     k1 = coarse(kappa[1:41])
     r1 = coarse(left[5:37])
     edge = jnp.zeros((2, 8, 128), F32)
@@ -487,8 +491,11 @@
     for y in range(2):
         second = second + roll(jnp.where(lane < 32, flat[pl.ds(5 + y, 8, stride=4), :], 0.0), 32 * y, 1)
     for d in range(parts.shape[0]):
-        parts[d, 0:8] = tile
-        parts[d, 8:16] = second
+        packs[d, 0:8] = tile
+        packs[d, 8:16] = second
+    sending = pltpu.make_async_copy(packs, parts, done.at[0])
+    sending.start()
+    v[...] = roll(v2[5:37, :, :128], -4, 1)[:, :8]
     k = k1[2:18]
     v1c = level.weight[2:18] * r1
     tiles = jnp.where(iota(r1.shape, 1) < 4, roll(r1, -2, 1), roll(k, 2, 1))
@@ -506,6 +513,7 @@
     message[0:4] = along[pl.ds(12 - 12 * p, 4)]
     message[4] = roll(pick(p, v1c[12], v1c[3]), -2, 0)
     message[5] = roll(pick(p, v1c[15], v1c[0]), -2, 0)
+    sending.wait()
 
 
 def middle_kernel(n_gy, mine, across, both, r1, k1, weight, v2, cx, cy, cz, diag, v1):
@@ -618,7 +626,7 @@
 
 
 def up_kernel(
-    n_gy, blocks, r1, k1, w1, v21, left, kappa, weight, v2, out,
+    n_gy, blocks, more, r1, k1, w1, v21, left, kappa, weight, v2, keep, give,
     r2, k2, tall, flat, sums, fx, fy, fz, ua, ub, cx, cy, cz, va, vb,
 ):
     p, c, b, t = place()
@@ -634,8 +642,9 @@
     cells = {(y, gp): jnp.zeros((8, 128), F32) for y in range(-1, n_y + 1) for gp in range(2)}
     pairs = n_y // 2
 
-    def block(gp, q, gz):
-        return ((2 * gp + q % 2) * n_gy + q // 2) * 2 + gz
+    def block(gp, q, gz, half):
+        at, rows = (gp * n_gy + q // 2) * 2 + gz, slice(8 * half, 8 * half + 8)
+        return pick(c ^ (q % 2), blocks[at, rows, :], more[at, rows, :])
 
     for gp in range(2):
         for q in range(pairs):
@@ -643,12 +652,12 @@
             for gz in range(2):
                 ends = jnp.zeros((8, 128), F32)
                 if q + 1 < pairs:
-                    ends = jnp.where(lane < 32, blocks[block(gp, q + 1, gz), 0:8, :], ends)
+                    ends = jnp.where(lane < 32, block(gp, q + 1, gz, 0), ends)
                 if q > 0:
-                    ends = jnp.where(lane >= 96, blocks[block(gp, q - 1, gz), 0:8, :], ends)
-                whole.append(blocks[block(gp, q, gz), 0:8, :] + roll(ends, 64, 1))
+                    ends = jnp.where(lane >= 96, block(gp, q - 1, gz, 0), ends)
+                whole.append(block(gp, q, gz, 0) + roll(ends, 64, 1))
             near, far = whole
-            near2, far2 = [blocks[block(gp, q, gz), 8:16, :] for gz in range(2)]
+            near2, far2 = [block(gp, q, gz, 1) for gz in range(2)]
             for y in range(2):
                 high = jnp.where(lane < 64, roll(far, -32 * y, 1), 0.0)
                 own = jnp.where(lane < 32, roll(near, -32 * (y + 1), 1), high)
@@ -718,11 +727,24 @@
     sweep(va, vb, left, cx, cy, cz, weight, first, PLANES, PLANES)
     here, total = around(vb, cx, cy, cz, 5, 32)
     done = (1.0 - OMEGA) * here + weight[5:37] * (left[5:37] + total)
-    out[...] = v2[...] + roll(done[:, :, :128], -4, 1)[:, :8]
+    va[0:32, 0:8, 0:128] = v2[...] + roll(done[:, :, :128], -4, 1)[:, :8]
+    keep[...] = va[pl.ds(16 * c, 16), 0:8, 0:128]
+    give[...] = va[pl.ds(16 - 16 * c, 16), 0:8, 0:128]
+
+
+def join_kernel(mine, other, out, done):
+    _, c, _, _ = place()
+    copies = []
+    for i, (part, at) in enumerate(((mine, 8 * c), (other, 8 - 8 * c))):
+        copies.append(pltpu.make_async_copy(part, out.at[:, pl.ds(pl.multiple_of(at, 8), 8), :], done.at[i]))
+        copies[i].start()
+    for copy in copies:
+        copy.wait()
 
 
 def call(kernel, name, outs, scratch, *args):
     where = pltpu.HBM if name == "message" else pltpu.VMEM
+    last = 1 if name in ("down", "join") else 0
     if name == "message":
         args = [pltpu.with_memory_space_constraint(a, pltpu.HBM) for a in args]
     return pl.pallas_call(
@@ -730,7 +752,7 @@
         name=name,
         out_shape=[jax.ShapeDtypeStruct(s, F32) for s in outs],
         in_specs=[pl.BlockSpec(memory_space=where)] * len(args),
-        out_specs=[pl.BlockSpec(memory_space=pltpu.VMEM)] * len(outs),
+        out_specs=[pl.BlockSpec(memory_space=pltpu.VMEM)] * (len(outs) - last) + [pl.BlockSpec(memory_space=pltpu.HBM)] * last,
         scratch_shapes=[
             pltpu.SemaphoreType.DMA((s,)) if isinstance(s, int) else pltpu.VMEM(*s) for s in scratch
         ],
@@ -748,7 +770,7 @@
         message_kernel,
         "message",
         [(16, 16, 128), (3, 16, 16, 128), (120, 128), (48, 128)],
-        [((8, 128), jnp.int32)] * 2 + [((8, 128), F32), 5],
+        [((8, 128), jnp.int32)] * 2 + [((8, 128), F32), 11],
         chi,
         inducing,
         record_dest.reshape(8, 128),
@@ -756,7 +778,7 @@
         record_value.reshape(8, 128),
     )
     got = lax.ppermute(message, "gz", [(0, 1), (1, 0)])
-    spread = [((256, 1024), BF16)] * 4
+    spread = [((256, 1024), BF16), ((512, 1024), BF16)]
     source, total = call(
         source_kernel,
         "source",
@@ -800,16 +822,20 @@
     *fine, along, beside, message, parts = call(
         functools.partial(down_kernel, n_gy),
         "down",
-        [window] * 3 + [(32, 8, 128), (18, 8, 128), (18, 8, 128), (6, 8, 128), (8 * n_gy, 16, 128)],
+        [window] * 3 + [(32, 8, 128), (18, 8, 128), (18, 8, 128), (6, 8, 128), (4 * n_gy, 16, 128)],
         big * 7 + [((640, 128), F32), ((48, 128), F32), ((12, 16, 128), F32)]
-        + [((ROWS, 16, 128), F32)] * 2
-        + [((PLANES + 6, 8, 128), F32)],
+        + [((4 * n_gy, 16, 128), F32), 1],
         *fields,
         across,
         strip,
         corner,
     )
-    blocks = lax.all_to_all(parts, ("gx", "gy", "gz"), split_axis=0, concat_axis=0, tiled=True)
+    n = 2 * n_gy
+    groups = [[(2 * p + c) * n + i for p in range(2) for i in range(n)] for c in range(2)]
+    blocks = lax.all_to_all(
+        parts, ("gx", "gy", "gz"), split_axis=0, concat_axis=0, tiled=True, axis_index_groups=groups
+    )
+    more = lax.ppermute(blocks, "gx", swap)
     across = lax.ppermute(message, "gx", cross)
     got = lax.ppermute(jnp.concatenate([along, across]), ("gx", "gy"), turns)
     other = lax.ppermute(jnp.concatenate([beside, across]), "gx", swap)
@@ -825,25 +851,22 @@
         jnp.concatenate([got, other]),
     )
     level2 = ((4 * n_gy, 16, 128), F32)
-    (out,) = call(
+    keep, give = call(
         functools.partial(up_kernel, n_gy),
         "up",
-        [(32, 8, 128)],
+        [(16, 8, 128)] * 2,
         [level2] * 2
         + [((4 * n_gy + 8, 32, 128), F32), ((512, 128), F32), ((64 * n_gy, 128), F32)]
         + big1 * 5
         + big * 5,
         blocks,
+        more,
         *coarse,
         *fine,
     )
-    c = lax.axis_index("gx") & 1
-    keep = lax.dynamic_slice_in_dim(out, 16 * c, 16, axis=0)
-    give = lax.dynamic_slice_in_dim(out, 16 - 16 * c, 16, axis=0)
     got = lax.ppermute(give, "gx", swap)
-    return jnp.where(
-        c == 0, jnp.concatenate([keep, got], axis=1), jnp.concatenate([got, keep], axis=1)
-    )
+    (out,) = call(join_kernel, "join", [(16, 16, 128)], [2], keep, got)
+    return out
 
 
 def solution(mesh):

time: 43.4 us -> 42.5 us (0.979)
  waiting for transfers between devices: 13.8 us -> 12.6 us
  starting transfers between devices: 16.2 us -> 17.3 us
  other arithmetic: 0.69 us -> 0.03 us
    ppermute x1, waiting for transfers between devices: 3.29 us -> 0.63 us  [paired(): got = lax.ppermute(jnp.concatenate([along, across]), ('gx', 'gy'), turns)]
    all_to_all x1, waiting for transfers between devices: 0.72 us -> 2.12 us  [paired(): lax.all_to_all(parts, ('gx', 'gy', 'gz'), split_axis=0, concat_axis=0, ti...]
    select_n x1 -> x0, other arithmetic: 0.67 us -> none  [paired(): jnp.where(c == 0, jnp.concatenate([keep, got], axis=1), jnp.concatenate([...]
    all_to_all x1, starting transfers between devices: 5.23 us -> 5.75 us  [paired(): lax.all_to_all(parts, ('gx', 'gy', 'gz'), split_axis=0, concat_axis=0, ti...]
    pallas_call x7 -> x8, Pallas kernels: 12.4 us -> 12.3 us  [call(): pl.pallas_call(kernel, name=name, out_shape=[jax.ShapeDtypeStruct(s, F32)...]
  transfers between devices with their start and end apart: 10 -> 11, of which waited for: 7 -> 8; matrix products, arithmetic and copies ran while one was open for 0% -> 0% of each run, Pallas kernels for 4% -> 3%
where the time goes in v8:
time: 42.5 us; the launch traced here: 42.3 us
  starting transfers between devices  17.3 us (41%)
  waiting for transfers between devices  12.6 us (30%)
  Pallas kernels  12.3 us (29%)
    pallas_call x8, Pallas kernels, call(): pl.pallas_call(kernel, name=name, out_shape=[jax.ShapeDtypeStruct(s, F32)...  12.3 us
    all_to_all x1, starting transfers between devices, paired(): lax.all_to_all(parts, ('gx', 'gy', 'gz'), split_axis=0, concat_axis=0, ti...  5.75 us
    ppermute x1, waiting for transfers between devices, paired(): corner = lax.ppermute(corner, ('gx', 'gy'), corners)  3.38 us
    ppermute x1, starting transfers between devices, paired(): got = lax.ppermute(message, 'gz', [(0, 1), (1, 0)])  3 us
    all_to_all x1, waiting for transfers between devices, paired(): lax.all_to_all(parts, ('gx', 'gy', 'gz'), split_axis=0, concat_axis=0, ti...  2.12 us
    ppermute x1, starting transfers between devices, paired(): strip = lax.ppermute(strip, ('gx', 'gy'), turns)  2.11 us
    ppermute x2, waiting for transfers between devices, paired(): across = lax.ppermute(message, 'gx', cross)  2.1 us
    ppermute x2, starting transfers between devices, paired(): across = lax.ppermute(message, 'gx', cross)  2.01 us
  transfers between devices with their start and end apart: 11, of which 8 were waited for; matrix products, arithmetic and copies ran while one was open for 0% of the time, Pallas kernels for 3%

profile of v8, /device:TPU:0, one launch (start us, length us, event | category | flops | bytes accessed | tf_op | source)
XLA Modules:
  0.0 42.3 jit_solution(13371908503177762696)
XLA Ops:
  0.0 1.9 %message.1 = (f32[16,16,128]{2,1,0:T(8,128)S(1)}, f32[3,16,16,128]{3,2,1,0:T(8,128)S(1)}, f32[120,128]{1,0:T(8,128)S(1)}, f32[48,128]{1,0:T(8,128)S(1)}) custom-call(f32[16,16,128]{2,1,0:T(8,128)} %refs_0_.1, f32[3,16,16,128]{3,2,1,0:T(8,128)} %refs_1_.1, s32[8,128]{1,0:T(8,128)} %bitcast.3, s32[8,128]{1,0:T(8,128)} %bitcast.4, f32[8,128]{1,0:T(8,128)} %bitcast.5), custom_call_target="tpu_custom_call" | custom-call | flops 10000000 | bytes 4000000 | tf_op jit(solution)/shard_map/message/pallas_call | solution.py:750
  1.9 3.0 %collective-permute-start = (f32[120,128]{1,0:T(8,128)S(1)}, f32[120,128]{1,0:T(8,128)S(1)}, u32[]{:S(2)}, u32[]{:S(2)}) collective-permute-start(f32[120,128]{1,0:T(8,128)S(1)} %get-tuple-element.35.records), channel_id=1, source_target_pairs={{0,1},{1,0},{2,3},{3,2},{4,5},{5,4},{6,7},{7,6},{8,9},{9,8},{10,11... | collective-permute-start | bytes 184328 | tf_op jit(solution)/shard_map/ppermute | solution.py:780
  4.9 0.7 %source.1 = (f32[18,24,128]{2,1,0:T(8,128)S(1)}, f32[256,256]{1,0:T(8,128)S(1)}) custom-call(f32[16,16,128]{2,1,0:T(8,128)S(1)} %get-tuple-element.33.chi, f32[3,16,16,128]{3,2,1,0:T(8,128)S(1)} %get-tuple-element.34.inducing, f32[120,128]{1,0:T(8,128)S(1)} %get-tuple-element.35.records), custom_call_target="tpu_custom_call" | custom-call | flops 10000000 | bytes 4000000 | tf_op jit(solution)/shard_map/source/pallas_call | solution.py:750
  5.6 1.5 %collective-permute-done.other = f32[120,128]{1,0:T(8,128)S(1)} collective-permute-done((f32[120,128]{1,0:T(8,128)S(1)}, f32[120,128]{1,0:T(8,128)S(1)}, u32[]{:S(2)}, u32[]{:S(2)}) %collective-permute-start) | collective-permute-done | bytes 61472 | tf_op jit(solution)/shard_map/ppermute | solution.py:780
  7.1 0.9 %deposit.1 = (f32[39,16,128]{2,1,0:T(8,128)S(1)}, f32[39,16,128]{2,1,0:T(8,128)S(1)}) custom-call(f32[18,24,128]{2,1,0:T(8,128)S(1)} %get-tuple-element.36.source, f32[48,128]{1,0:T(8,128)S(1)} %get-tuple-element.37.spill, f32[16,16,128]{2,1,0:T(8,128)S(1)} %get-tuple-element.33.chi, f32[256,256]{1,0:T(8,128)S(1)} %get-tuple-element.38.mine, ...), custom_call_target="tpu_custom_call" | custom-call | flops 10000000 | bytes 4000000 | tf_op jit(solution)/shard_map/deposit/pallas_call | solution.py:750
  8.0 0.1 collective-permute-start.1
  8.1 1.6 %collective-permute-done.1.other = f32[39,16,128]{2,1,0:T(8,128)S(1)} collective-permute-done((f32[39,16,128]{2,1,0:T(8,128)S(1)}, f32[39,16,128]{2,1,0:T(8,128)S(1)}, u32[]{:S(2)}, u32[]{:S(2)}) %collective-permute-start.1) | collective-permute-done | bytes 319520 | tf_op jit(solution)/shard_map/ppermute | solution.py:803
  9.7 0.2 pair.1
  9.9 2.1 %collective-permute-start.3 = (f32[42,8,128]{2,1,0:T(8,128)S(1)}, f32[42,8,128]{2,1,0:T(8,128)S(1)}, u32[]{:S(2)}, u32[]{:S(2)}) collective-permute-start(f32[42,8,128]{2,1,0:T(8,128)S(1)} %get-tuple-element.45), channel_id=1, source_target_pairs={{8,2},{2,8},{10,4},{4,10},{12,6},{6,12},{24,18},{18,24},{26,20},{2... | collective-permute-start | bytes 516104 | tf_op jit(solution)/shard_map/ppermute | solution.py:820
  12.0 0.1 collective-permute-start.2
  12.1 1.9 %collective-permute-start.4 = (f32[6,8,128]{2,1,0:T(8,128)S(1)}, f32[6,8,128]{2,1,0:T(8,128)S(1)}, u32[]{:S(2)}, u32[]{:S(2)}) collective-permute-start(f32[6,8,128]{2,1,0:T(8,128)S(1)} %get-tuple-element.46), channel_id=1, source_target_pairs={{8,18},{18,8},{10,20},{20,10},{12,22},{22,12},{24,2},{2,24},{26,4}... | collective-permute-start | bytes 73736 | tf_op jit(solution)/shard_map/ppermute | solution.py:821
  14.1 3.4 %collective-permute-done.4.corner = f32[6,8,128]{2,1,0:T(8,128)S(1)} collective-permute-done((f32[6,8,128]{2,1,0:T(8,128)S(1)}, f32[6,8,128]{2,1,0:T(8,128)S(1)}, u32[]{:S(2)}, u32[]{:S(2)}) %collective-permute-start.4) | collective-permute-done | bytes 24608 | tf_op jit(solution)/shard_map/ppermute | solution.py:821
  17.4 0.0 collective-permute-done.2.across
  17.4 0.0 collective-permute-done.3.along_in
  17.4 3.8 %down.1 = (f32[42,16,256]{2,1,0:T(8,128)S(1)}, f32[42,16,256]{2,1,0:T(8,128)S(1)}, f32[42,16,256]{2,1,0:T(8,128)S(1)}, f32[32,8,128]{2,1,0:T(8,128)S(1)}, f32[18...) custom-call(f32[42,16,128]{2,1,0:T(8,128)S(1)} %get-tuple-element.41.source_, ...), custom_call_target="tpu_custom_call" | custom-call | flops 10000000 | bytes 4000000 | tf_op jit(solution)/shard_map/down/pallas_call | solution.py:750
  21.3 5.8 %all-to-all-start = ((f32[16,16,128]{2,1,0:T(8,128)}), f32[16,16,128]{2,1,0:T(8,128)S(1)}, u32[]{:S(2)}, u32[]{:S(2)}) async-start(f32[16,16,128]{2,1,0:T(8,128)} %get-tuple-element.47), calls=%async_computation | async-start | bytes 262144 | tf_op jit(solution)/shard_map/all_to_all | solution.py:835
  27.0 1.9 %collective-permute-start.6 = (f32[6,8,128]{2,1,0:T(8,128)S(1)}, f32[6,8,128]{2,1,0:T(8,128)S(1)}, u32[]{:S(2)}, u32[]{:S(2)}) collective-permute-start(f32[6,8,128]{2,1,0:T(8,128)S(1)} %get-tuple-element.49), channel_id=1, source_target_pairs={{0,16},{16,0},{8,24},{24,8},{1,17},{17,1},{9,25},{25,9},{2,18},{18... | collective-permute-start | bytes 73736 | tf_op jit(solution)/shard_map/ppermute | solution.py:839
  29.0 2.1 %collective-permute-done.6.across = f32[6,8,128]{2,1,0:T(8,128)S(1)} collective-permute-done((f32[6,8,128]{2,1,0:T(8,128)S(1)}, f32[6,8,128]{2,1,0:T(8,128)S(1)}, u32[]{:S(2)}, u32[]{:S(2)}) %collective-permute-start.6) | collective-permute-done | bytes 24608 | tf_op jit(solution)/shard_map/ppermute | solution.py:839
  31.1 1.9 %collective-permute-start.7 = (f32[24,8,128]{2,1,0:T(8,128)S(1)}, f32[24,8,128]{2,1,0:T(8,128)S(1)}, u32[]{:S(2)}, u32[]{:S(2)}) collective-permute-start(f32[24,8,128]{2,1,0:T(8,128)S(1)} %get-tuple-element.61), channel_id=1, source_target_pairs={{8,2},{2,8},{10,4},{4,10},{12,6},{6,12},{24,18},{18,24},{26,20},{2... | collective-permute-start | bytes 294920 | tf_op jit(solution)/shard_map/ppermute | solution.py:840
  33.0 0.3 collective-permute-start.8
  33.3 2.1 %all-to-all-done.blocks = f32[16,16,128]{2,1,0:T(8,128)S(1)} async-done(((f32[16,16,128]{2,1,0:T(8,128)}), f32[16,16,128]{2,1,0:T(8,128)S(1)}, u32[]{:S(2)}, u32[]{:S(2)}) %all-to-all-start) | async-done | bytes 131104 | tf_op jit(solution)/shard_map/all_to_all | solution.py:835
  35.4 0.0 collective-permute-start.5
  35.4 0.6 %collective-permute-done.7 = f32[24,8,128]{2,1,0:T(8,128)S(1)} collective-permute-done((f32[24,8,128]{2,1,0:T(8,128)S(1)}, f32[24,8,128]{2,1,0:T(8,128)S(1)}, u32[]{:S(2)}, u32[]{:S(2)}) %collective-permute-start.7) | collective-permute-done | bytes 98336 | tf_op jit(solution)/shard_map/ppermute | solution.py:840
  36.0 0.0 collective-permute-done.8
  36.0 0.5 %middle.1 = (f32[28,16,128]{2,1,0:T(8,128)S(1)}, f32[28,16,128]{2,1,0:T(8,128)S(1)}, f32[28,16,128]{2,1,0:T(8,128)S(1)}, f32[28,16,128]{2,1,0:T(8,128)S(1)}) custom-call(f32[18,8,128]{2,1,0:T(8,128)S(1)} %get-tuple-element.48.mine, f32[6,8,128]{2,1,0:T(8,128)S(1)} %collective-permute-done.6.across, f32[48,8,128]{2,1,0:T(8,128)S(1)} %pad_maximum_fusion.both), custom_call_target="tpu_custom_call" | custom-call | flops 10000000 | bytes 4000000 | tf_op jit(solution)/shard_map/middle/pallas_call | solution.py:750
  36.6 0.2 collective-permute-done.5.more
  36.7 3.6 %up.1 = (f32[16,8,128]{2,1,0:T(8,128)S(1)}, f32[16,8,128]{2,1,0:T(8,128)S(1)}) custom-call(f32[16,16,128]{2,1,0:T(8,128)S(1)} %all-to-all-done.blocks, f32[16,16,128]{2,1,0:T(8,128)S(1)} %collective-permute-done.5.more, f32[28,16,128]{2,1,0:T(8,128)S(1)} %get-tuple-element.51.r1, f32[28,16,128]{2,1,0:T(8,128)S(1)} %get-tuple-element.52.k1, ...), custom_call_target="tpu_custom_call" | custom-call | flops 10000000 | bytes 4000000 | tf_op jit(solution)/shard_map/up/pallas_call | solution.py:750
  40.3 0.2 collective-permute-start.9
  40.5 1.1 %collective-permute-done.9.other = f32[16,8,128]{2,1,0:T(8,128)S(1)} collective-permute-done((f32[16,8,128]{2,1,0:T(8,128)S(1)}, f32[16,8,128]{2,1,0:T(8,128)S(1)}, u32[]{:S(2)}, u32[]{:S(2)}) %collective-permute-start.9) | collective-permute-done | bytes 65568 | tf_op jit(solution)/shard_map/ppermute | solution.py:867
  41.6 0.7 %join.1 = f32[16,16,128]{2,1,0:T(8,128)} custom-call(f32[16,8,128]{2,1,0:T(8,128)S(1)} %get-tuple-element.59.mine, f32[16,8,128]{2,1,0:T(8,128)S(1)} %collective-permute-done.9.other), custom_call_target="tpu_custom_call" | custom-call | flops 10000000 | bytes 4000000 | tf_op jit(solution)/shard_map/join/pallas_call | solution.py:750
  (2 shorter events, 0.0 us)
Async XLA Ops:
  1.9 5.2 %collective-permute-start = (f32[120,128]{1,0:T(8,128)S(1)}, f32[120,128]{1,0:T(8,128)S(1)}, u32[]{:S(2)}, u32[]{:S(2)}) collective-permute-start(f32[120,128]{1,0:T(8,128)S(1)} %get-tuple-element.35.records), channel_id=1, source_target_pairs={{0,1},{1,0},{2,3},{3,2},{4,5},{5,4},{6,7},{7,6},{8,9},{9,8},{10,11... | collective-permute-start | bytes 184328 | tf_op jit(solution)/shard_map/ppermute | solution.py:780
  8.0 1.7 %collective-permute-start.1 = (f32[39,16,128]{2,1,0:T(8,128)S(1)}, f32[39,16,128]{2,1,0:T(8,128)S(1)}, u32[]{:S(2)}, u32[]{:S(2)}) collective-permute-start(f32[39,16,128]{2,1,0:T(8,128)S(1)} %get-tuple-element.40), channel_id=1, source_target_pairs={{0,8},{8,0},{16,24},{24,16},{1,9},{9,1},{17,25},{25,17},{2,10},{10... | collective-permute-start | bytes 958472 | tf_op jit(solution)/shard_map/ppermute | solution.py:803
  9.9 7.5 %collective-permute-start.3 = (f32[42,8,128]{2,1,0:T(8,128)S(1)}, f32[42,8,128]{2,1,0:T(8,128)S(1)}, u32[]{:S(2)}, u32[]{:S(2)}) collective-permute-start(f32[42,8,128]{2,1,0:T(8,128)S(1)} %get-tuple-element.45), channel_id=1, source_target_pairs={{8,2},{2,8},{10,4},{4,10},{12,6},{6,12},{24,18},{18,24},{26,20},{2... | collective-permute-start | bytes 516104 | tf_op jit(solution)/shard_map/ppermute | solution.py:820
  12.0 5.4 %collective-permute-start.2 = (f32[10,16,128]{2,1,0:T(8,128)S(1)}, f32[10,16,128]{2,1,0:T(8,128)S(1)}, u32[]{:S(2)}, u32[]{:S(2)}) collective-permute-start(f32[10,16,128]{2,1,0:T(8,128)S(1)} %get-tuple-element.44), channel_id=1, source_target_pairs={{0,16},{16,0},{8,24},{24,8},{1,17},{17,1},{9,25},{25,9},{2,18},{18... | collective-permute-start | bytes 245768 | tf_op jit(solution)/shard_map/ppermute | solution.py:809
  12.1 5.3 %collective-permute-start.4 = (f32[6,8,128]{2,1,0:T(8,128)S(1)}, f32[6,8,128]{2,1,0:T(8,128)S(1)}, u32[]{:S(2)}, u32[]{:S(2)}) collective-permute-start(f32[6,8,128]{2,1,0:T(8,128)S(1)} %get-tuple-element.46), channel_id=1, source_target_pairs={{8,18},{18,8},{10,20},{20,10},{12,22},{22,12},{24,2},{2,24},{26,4}... | collective-permute-start | bytes 73736 | tf_op jit(solution)/shard_map/ppermute | solution.py:821
  21.3 14.1 %all-to-all-start = ((f32[16,16,128]{2,1,0:T(8,128)}), f32[16,16,128]{2,1,0:T(8,128)S(1)}, u32[]{:S(2)}, u32[]{:S(2)}) async-start(f32[16,16,128]{2,1,0:T(8,128)} %get-tuple-element.47), calls=%async_computation | async-start | bytes 262144 | tf_op jit(solution)/shard_map/all_to_all | solution.py:835
  27.0 4.0 %collective-permute-start.6 = (f32[6,8,128]{2,1,0:T(8,128)S(1)}, f32[6,8,128]{2,1,0:T(8,128)S(1)}, u32[]{:S(2)}, u32[]{:S(2)}) collective-permute-start(f32[6,8,128]{2,1,0:T(8,128)S(1)} %get-tuple-element.49), channel_id=1, source_target_pairs={{0,16},{16,0},{8,24},{24,8},{1,17},{17,1},{9,25},{25,9},{2,18},{18... | collective-permute-start | bytes 73736 | tf_op jit(solution)/shard_map/ppermute | solution.py:839
  31.1 4.9 %collective-permute-start.7 = (f32[24,8,128]{2,1,0:T(8,128)S(1)}, f32[24,8,128]{2,1,0:T(8,128)S(1)}, u32[]{:S(2)}, u32[]{:S(2)}) collective-permute-start(f32[24,8,128]{2,1,0:T(8,128)S(1)} %get-tuple-element.61), channel_id=1, source_target_pairs={{8,2},{2,8},{10,4},{4,10},{12,6},{6,12},{24,18},{18,24},{26,20},{2... | collective-permute-start | bytes 294920 | tf_op jit(solution)/shard_map/ppermute | solution.py:840
  33.0 3.0 %collective-permute-start.8 = (f32[24,8,128]{2,1,0:T(8,128)S(1)}, f32[24,8,128]{2,1,0:T(8,128)S(1)}, u32[]{:S(2)}, u32[]{:S(2)}) collective-permute-start(f32[24,8,128]{2,1,0:T(8,128)S(1)} %get-tuple-element.62), channel_id=1, source_target_pairs={{0,8},{8,0},{16,24},{24,16},{1,9},{9,1},{17,25},{25,17},{2,10},{10... | collective-permute-start | bytes 294920 | tf_op jit(solution)/shard_map/ppermute | solution.py:841
  35.4 1.3 %collective-permute-start.5 = (f32[16,16,128]{2,1,0:T(8,128)S(1)}, f32[16,16,128]{2,1,0:T(8,128)S(1)}, u32[]{:S(2)}, u32[]{:S(2)}) collective-permute-start(f32[16,16,128]{2,1,0:T(8,128)S(1)} %all-to-all-done.blocks), channel_id=1, source_target_pairs={{0,8},{8,0},{16,24},{24,16},{1,9},{9,1},{17,25},{25,17},{2,10},{10... | collective-permute-start | bytes 393224 | tf_op jit(solution)/shard_map/ppermute | solution.py:838
  40.3 1.3 %collective-permute-start.9 = (f32[16,8,128]{2,1,0:T(8,128)S(1)}, f32[16,8,128]{2,1,0:T(8,128)S(1)}, u32[]{:S(2)}, u32[]{:S(2)}) collective-permute-start(f32[16,8,128]{2,1,0:T(8,128)S(1)} %get-tuple-element.60), channel_id=1, source_target_pairs={{0,8},{8,0},{16,24},{24,16},{1,9},{9,1},{17,25},{25,17},{2,10},{10... | collective-permute-start | bytes 196616 | tf_op jit(solution)/shard_map/ppermute | solution.py:867

commit v9 on v8

--- a/solution.py
+++ b/solution.py
@@ -166,17 +166,18 @@
         copies[i].start()
     lane = iota((16, 128), 1)
     turn = 11 - 10 * t
-    wanted = pick(t, (lane < 11).astype(jnp.int32), ((lane >= 1) & (lane < 12)).astype(jnp.int32)) > 0
     packs = [[jnp.zeros((16, 128), F32)] * 2 for _ in range(4)]
     for x in range(16):
         if x % 4 == 0:
             copies[x // 4].wait()
             copies[4 + x // 4].wait()
-        near = jnp.where(wanted, pltpu.roll(chi[x], turn, 1), 0.0)
-        parts = [jnp.where(wanted, 1.0 + near, 0.0)]
-        parts += [near * pltpu.roll(inducing[d, x], turn, 1) for d in range(3)]
+        by = 16 * (x % 8)
+        wanted = (lane >= by + t) & (lane < by + t + 11)
+        near = jnp.where(wanted, pltpu.roll(chi[x], (turn + by) & 127, 1), 0.0)
+        parts = [1.0 + near]
+        parts += [near * pltpu.roll(inducing[d, x], (turn + by) & 127, 1) for d in range(3)]
         for pack, part in zip(packs, parts):
-            pack[x // 8] = pack[x // 8] + roll(part, 16 * (x % 8), 1)
+            pack[x // 8] = jnp.where(wanted, part, pack[x // 8])
     k, mx, my, mz = [jnp.concatenate(pack, 1) for pack in packs]
     lane = iota((16, 256), 1)
     dx = jnp.where(lane < 240, roll(mx, -16, 1), 0.0) - jnp.where(lane >= 16, roll(mx, 16, 1), 0.0)
@@ -396,9 +397,11 @@
     p, c, b, t = place()
     first = 5 - 4 * p
     edge = jnp.where(c == 0, b == 0, b == n_gy - 1).astype(jnp.int32)
-    for ref in (kappa, cx, weight, v1, v2, left):
-        ref[0:5] = jnp.zeros((5, 16, 256), F32)
-        ref[37:42] = jnp.zeros((5, 16, 256), F32)
+    kappa[0:5] = jnp.zeros((5, 16, 256), F32)
+    kappa[37:42] = jnp.zeros((5, 16, 256), F32)
+    for ref in (cx, weight, v1, v2):
+        for r in (0, 2, 3, 4, 37, 38, 39, 41):
+            ref[r] = jnp.zeros((16, 256), F32)
 
     sub = iota((1, 8, 128), 1)
     sides = [jnp.full((1, 8, 128), (1 - edge) * side, jnp.int32) for side in (1 - c, c)]
@@ -464,8 +467,8 @@
 
     rows = pl.ds(first, PLANES)
     v1[rows] = weight[rows] * rhs[rows]
-    sweep(v1, v2, rhs, cx, cy, cz, weight, first, PLANES, PLANES)
-    left[rows] = resid(v2, rhs, cx, cy, cz, diag, first, PLANES)
+    sweep(v1, v2, rhs, cx, cy, cz, weight, 5 - 2 * p, 34, 34)
+    left[pl.ds(5 - p, 33)] = resid(v2, rhs, cx, cy, cz, diag, 5 - p, 33)
     k1 = coarse(kappa[1:41])
     r1 = coarse(left[5:37])
     edge = jnp.zeros((2, 8, 128), F32)
@@ -632,9 +635,9 @@
     p, c, b, t = place()
     first = 5 - 4 * p
     n_y = 4 * n_gy
-    for ref in (va, vb, cx):
-        ref[0:5] = jnp.zeros((5, 16, 256), F32)
-        ref[37:42] = jnp.zeros((5, 16, 256), F32)
+    for ref in (vb, cx):
+        for r in (0, 3, 4, 37, 38):
+            ref[r] = jnp.zeros((16, 256), F32)
     for ref in (fx, ua, ub):
         ref[...] = jnp.zeros_like(ref)
 
@@ -724,7 +727,7 @@
     cx[rows] = 0.5 * (k + near[1:])
     cy[rows] = 0.5 * (k + roll(k, -1, 1))
     cz[rows] = 0.5 * (k + roll(k, -1, 2))
-    sweep(va, vb, left, cx, cy, cz, weight, first, PLANES, PLANES)
+    sweep(va, vb, left, cx, cy, cz, weight, 5 - p, 33, 33)
     here, total = around(vb, cx, cy, cz, 5, 32)
     done = (1.0 - OMEGA) * here + weight[5:37] * (left[5:37] + total)
     va[0:32, 0:8, 0:128] = v2[...] + roll(done[:, :, :128], -4, 1)[:, :8]

time: 42.5 us -> 42.2 us (level)
  no operation moved by 1% of the time
where the time goes in v9:
time: 42.2 us; the launch traced here: 41.9 us
  starting transfers between devices  17.3 us (41%)
  waiting for transfers between devices  12.6 us (30%)
  Pallas kernels  11.9 us (28%)
    pallas_call x8, Pallas kernels, call(): pl.pallas_call(kernel, name=name, out_shape=[jax.ShapeDtypeStruct(s, F32)...  11.9 us
    all_to_all x1, starting transfers between devices, paired(): lax.all_to_all(parts, ('gx', 'gy', 'gz'), split_axis=0, concat_axis=0, ti...  5.77 us
    ppermute x1, waiting for transfers between devices, paired(): corner = lax.ppermute(corner, ('gx', 'gy'), corners)  3.38 us
    ppermute x1, starting transfers between devices, paired(): got = lax.ppermute(message, 'gz', [(0, 1), (1, 0)])  3 us
    all_to_all x1, waiting for transfers between devices, paired(): lax.all_to_all(parts, ('gx', 'gy', 'gz'), split_axis=0, concat_axis=0, ti...  2.13 us
    ppermute x1, starting transfers between devices, paired(): strip = lax.ppermute(strip, ('gx', 'gy'), turns)  2.11 us
    ppermute x2, waiting for transfers between devices, paired(): across = lax.ppermute(message, 'gx', cross)  2.11 us
    ppermute x2, starting transfers between devices, paired(): across = lax.ppermute(message, 'gx', cross)  2.01 us
  transfers between devices with their start and end apart: 11, of which 8 were waited for; matrix products, arithmetic and copies ran while one was open for 0% of the time, Pallas kernels for 3%

profile of v9, /device:TPU:0, one launch (start us, length us, event | category | flops | bytes accessed | tf_op | source)
XLA Modules:
  0.0 41.9 jit_solution(11626649804978251128)
XLA Ops:
  0.0 1.6 %message.1 = (f32[16,16,128]{2,1,0:T(8,128)S(1)}, f32[3,16,16,128]{3,2,1,0:T(8,128)S(1)}, f32[120,128]{1,0:T(8,128)S(1)}, f32[48,128]{1,0:T(8,128)S(1)}) custom-call(f32[16,16,128]{2,1,0:T(8,128)} %refs_0_.1, f32[3,16,16,128]{3,2,1,0:T(8,128)} %refs_1_.1, s32[8,128]{1,0:T(8,128)} %bitcast.3, s32[8,128]{1,0:T(8,128)} %bitcast.4, f32[8,128]{1,0:T(8,128)} %bitcast.5), custom_call_target="tpu_custom_call" | custom-call | flops 10000000 | bytes 4000000 | tf_op jit(solution)/shard_map/message/pallas_call | solution.py:753
  1.6 3.0 %collective-permute-start = (f32[120,128]{1,0:T(8,128)S(1)}, f32[120,128]{1,0:T(8,128)S(1)}, u32[]{:S(2)}, u32[]{:S(2)}) collective-permute-start(f32[120,128]{1,0:T(8,128)S(1)} %get-tuple-element.35.records), channel_id=1, source_target_pairs={{0,1},{1,0},{2,3},{3,2},{4,5},{5,4},{6,7},{7,6},{8,9},{9,8},{10,11... | collective-permute-start | bytes 184328 | tf_op jit(solution)/shard_map/ppermute | solution.py:783
  4.6 0.7 %source.1 = (f32[18,24,128]{2,1,0:T(8,128)S(1)}, f32[256,256]{1,0:T(8,128)S(1)}) custom-call(f32[16,16,128]{2,1,0:T(8,128)S(1)} %get-tuple-element.33.chi, f32[3,16,16,128]{3,2,1,0:T(8,128)S(1)} %get-tuple-element.34.inducing, f32[120,128]{1,0:T(8,128)S(1)} %get-tuple-element.35.records), custom_call_target="tpu_custom_call" | custom-call | flops 10000000 | bytes 4000000 | tf_op jit(solution)/shard_map/source/pallas_call | solution.py:753
  5.3 1.5 %collective-permute-done.other = f32[120,128]{1,0:T(8,128)S(1)} collective-permute-done((f32[120,128]{1,0:T(8,128)S(1)}, f32[120,128]{1,0:T(8,128)S(1)}, u32[]{:S(2)}, u32[]{:S(2)}) %collective-permute-start) | collective-permute-done | bytes 61472 | tf_op jit(solution)/shard_map/ppermute | solution.py:783
  6.8 0.9 %deposit.1 = (f32[39,16,128]{2,1,0:T(8,128)S(1)}, f32[39,16,128]{2,1,0:T(8,128)S(1)}) custom-call(f32[18,24,128]{2,1,0:T(8,128)S(1)} %get-tuple-element.36.source, f32[48,128]{1,0:T(8,128)S(1)} %get-tuple-element.37.spill, f32[16,16,128]{2,1,0:T(8,128)S(1)} %get-tuple-element.33.chi, f32[256,256]{1,0:T(8,128)S(1)} %get-tuple-element.38.mine, ...), custom_call_target="tpu_custom_call" | custom-call | flops 10000000 | bytes 4000000 | tf_op jit(solution)/shard_map/deposit/pallas_call | solution.py:753
  7.7 0.1 collective-permute-start.1
  7.8 1.6 %collective-permute-done.1.other = f32[39,16,128]{2,1,0:T(8,128)S(1)} collective-permute-done((f32[39,16,128]{2,1,0:T(8,128)S(1)}, f32[39,16,128]{2,1,0:T(8,128)S(1)}, u32[]{:S(2)}, u32[]{:S(2)}) %collective-permute-start.1) | collective-permute-done | bytes 319520 | tf_op jit(solution)/shard_map/ppermute | solution.py:806
  9.4 0.2 pair.1
  9.6 2.1 %collective-permute-start.3 = (f32[42,8,128]{2,1,0:T(8,128)S(1)}, f32[42,8,128]{2,1,0:T(8,128)S(1)}, u32[]{:S(2)}, u32[]{:S(2)}) collective-permute-start(f32[42,8,128]{2,1,0:T(8,128)S(1)} %get-tuple-element.45), channel_id=1, source_target_pairs={{8,2},{2,8},{10,4},{4,10},{12,6},{6,12},{24,18},{18,24},{26,20},{2... | collective-permute-start | bytes 516104 | tf_op jit(solution)/shard_map/ppermute | solution.py:823
  11.8 0.1 collective-permute-start.2
  11.8 1.9 %collective-permute-start.4 = (f32[6,8,128]{2,1,0:T(8,128)S(1)}, f32[6,8,128]{2,1,0:T(8,128)S(1)}, u32[]{:S(2)}, u32[]{:S(2)}) collective-permute-start(f32[6,8,128]{2,1,0:T(8,128)S(1)} %get-tuple-element.46), channel_id=1, source_target_pairs={{8,18},{18,8},{10,20},{20,10},{12,22},{22,12},{24,2},{2,24},{26,4}... | collective-permute-start | bytes 73736 | tf_op jit(solution)/shard_map/ppermute | solution.py:824
  13.8 3.4 %collective-permute-done.4.corner = f32[6,8,128]{2,1,0:T(8,128)S(1)} collective-permute-done((f32[6,8,128]{2,1,0:T(8,128)S(1)}, f32[6,8,128]{2,1,0:T(8,128)S(1)}, u32[]{:S(2)}, u32[]{:S(2)}) %collective-permute-start.4) | collective-permute-done | bytes 24608 | tf_op jit(solution)/shard_map/ppermute | solution.py:824
  17.2 0.0 collective-permute-done.2.across
  17.2 0.0 collective-permute-done.3.along_in
  17.2 3.7 %down.1 = (f32[42,16,256]{2,1,0:T(8,128)S(1)}, f32[42,16,256]{2,1,0:T(8,128)S(1)}, f32[42,16,256]{2,1,0:T(8,128)S(1)}, f32[32,8,128]{2,1,0:T(8,128)S(1)}, f32[18...) custom-call(f32[42,16,128]{2,1,0:T(8,128)S(1)} %get-tuple-element.41.source_, ...), custom_call_target="tpu_custom_call" | custom-call | flops 10000000 | bytes 4000000 | tf_op jit(solution)/shard_map/down/pallas_call | solution.py:753
  20.9 5.8 %all-to-all-start = ((f32[16,16,128]{2,1,0:T(8,128)}), f32[16,16,128]{2,1,0:T(8,128)S(1)}, u32[]{:S(2)}, u32[]{:S(2)}) async-start(f32[16,16,128]{2,1,0:T(8,128)} %get-tuple-element.47), calls=%async_computation | async-start | bytes 262144 | tf_op jit(solution)/shard_map/all_to_all | solution.py:838
  26.7 1.9 %collective-permute-start.6 = (f32[6,8,128]{2,1,0:T(8,128)S(1)}, f32[6,8,128]{2,1,0:T(8,128)S(1)}, u32[]{:S(2)}, u32[]{:S(2)}) collective-permute-start(f32[6,8,128]{2,1,0:T(8,128)S(1)} %get-tuple-element.49), channel_id=1, source_target_pairs={{0,16},{16,0},{8,24},{24,8},{1,17},{17,1},{9,25},{25,9},{2,18},{18... | collective-permute-start | bytes 73736 | tf_op jit(solution)/shard_map/ppermute | solution.py:842
  28.6 2.1 %collective-permute-done.6.across = f32[6,8,128]{2,1,0:T(8,128)S(1)} collective-permute-done((f32[6,8,128]{2,1,0:T(8,128)S(1)}, f32[6,8,128]{2,1,0:T(8,128)S(1)}, u32[]{:S(2)}, u32[]{:S(2)}) %collective-permute-start.6) | collective-permute-done | bytes 24608 | tf_op jit(solution)/shard_map/ppermute | solution.py:842
  30.7 1.9 %collective-permute-start.7 = (f32[24,8,128]{2,1,0:T(8,128)S(1)}, f32[24,8,128]{2,1,0:T(8,128)S(1)}, u32[]{:S(2)}, u32[]{:S(2)}) collective-permute-start(f32[24,8,128]{2,1,0:T(8,128)S(1)} %get-tuple-element.61), channel_id=1, source_target_pairs={{8,2},{2,8},{10,4},{4,10},{12,6},{6,12},{24,18},{18,24},{26,20},{2... | collective-permute-start | bytes 294920 | tf_op jit(solution)/shard_map/ppermute | solution.py:843
  32.6 0.3 collective-permute-start.8
  32.9 2.1 %all-to-all-done.blocks = f32[16,16,128]{2,1,0:T(8,128)S(1)} async-done(((f32[16,16,128]{2,1,0:T(8,128)}), f32[16,16,128]{2,1,0:T(8,128)S(1)}, u32[]{:S(2)}, u32[]{:S(2)}) %all-to-all-start) | async-done | bytes 131104 | tf_op jit(solution)/shard_map/all_to_all | solution.py:838
  35.0 0.0 collective-permute-start.5
  35.0 0.6 %collective-permute-done.7 = f32[24,8,128]{2,1,0:T(8,128)S(1)} collective-permute-done((f32[24,8,128]{2,1,0:T(8,128)S(1)}, f32[24,8,128]{2,1,0:T(8,128)S(1)}, u32[]{:S(2)}, u32[]{:S(2)}) %collective-permute-start.7) | collective-permute-done | bytes 98336 | tf_op jit(solution)/shard_map/ppermute | solution.py:843
  35.6 0.0 collective-permute-done.8
  35.7 0.5 %middle.1 = (f32[28,16,128]{2,1,0:T(8,128)S(1)}, f32[28,16,128]{2,1,0:T(8,128)S(1)}, f32[28,16,128]{2,1,0:T(8,128)S(1)}, f32[28,16,128]{2,1,0:T(8,128)S(1)}) custom-call(f32[18,8,128]{2,1,0:T(8,128)S(1)} %get-tuple-element.48.mine, f32[6,8,128]{2,1,0:T(8,128)S(1)} %collective-permute-done.6.across, f32[48,8,128]{2,1,0:T(8,128)S(1)} %pad_maximum_fusion.both), custom_call_target="tpu_custom_call" | custom-call | flops 10000000 | bytes 4000000 | tf_op jit(solution)/shard_map/middle/pallas_call | solution.py:753
  36.2 0.2 collective-permute-done.5.more
  36.4 3.6 %up.1 = (f32[16,8,128]{2,1,0:T(8,128)S(1)}, f32[16,8,128]{2,1,0:T(8,128)S(1)}) custom-call(f32[16,16,128]{2,1,0:T(8,128)S(1)} %all-to-all-done.blocks, f32[16,16,128]{2,1,0:T(8,128)S(1)} %collective-permute-done.5.more, f32[28,16,128]{2,1,0:T(8,128)S(1)} %get-tuple-element.51.r1, f32[28,16,128]{2,1,0:T(8,128)S(1)} %get-tuple-element.52.k1, ...), custom_call_target="tpu_custom_call" | custom-call | flops 10000000 | bytes 4000000 | tf_op jit(solution)/shard_map/up/pallas_call | solution.py:753
  39.9 0.2 collective-permute-start.9
  40.1 1.1 %collective-permute-done.9.other = f32[16,8,128]{2,1,0:T(8,128)S(1)} collective-permute-done((f32[16,8,128]{2,1,0:T(8,128)S(1)}, f32[16,8,128]{2,1,0:T(8,128)S(1)}, u32[]{:S(2)}, u32[]{:S(2)}) %collective-permute-start.9) | collective-permute-done | bytes 65568 | tf_op jit(solution)/shard_map/ppermute | solution.py:870
  41.3 0.7 %join.1 = f32[16,16,128]{2,1,0:T(8,128)} custom-call(f32[16,8,128]{2,1,0:T(8,128)S(1)} %get-tuple-element.59.mine, f32[16,8,128]{2,1,0:T(8,128)S(1)} %collective-permute-done.9.other), custom_call_target="tpu_custom_call" | custom-call | flops 10000000 | bytes 4000000 | tf_op jit(solution)/shard_map/join/pallas_call | solution.py:753
  (2 shorter events, 0.0 us)
Async XLA Ops:
  1.6 5.2 %collective-permute-start = (f32[120,128]{1,0:T(8,128)S(1)}, f32[120,128]{1,0:T(8,128)S(1)}, u32[]{:S(2)}, u32[]{:S(2)}) collective-permute-start(f32[120,128]{1,0:T(8,128)S(1)} %get-tuple-element.35.records), channel_id=1, source_target_pairs={{0,1},{1,0},{2,3},{3,2},{4,5},{5,4},{6,7},{7,6},{8,9},{9,8},{10,11... | collective-permute-start | bytes 184328 | tf_op jit(solution)/shard_map/ppermute | solution.py:783
  7.7 1.7 %collective-permute-start.1 = (f32[39,16,128]{2,1,0:T(8,128)S(1)}, f32[39,16,128]{2,1,0:T(8,128)S(1)}, u32[]{:S(2)}, u32[]{:S(2)}) collective-permute-start(f32[39,16,128]{2,1,0:T(8,128)S(1)} %get-tuple-element.40), channel_id=1, source_target_pairs={{0,8},{8,0},{16,24},{24,16},{1,9},{9,1},{17,25},{25,17},{2,10},{10... | collective-permute-start | bytes 958472 | tf_op jit(solution)/shard_map/ppermute | solution.py:806
  9.6 7.5 %collective-permute-start.3 = (f32[42,8,128]{2,1,0:T(8,128)S(1)}, f32[42,8,128]{2,1,0:T(8,128)S(1)}, u32[]{:S(2)}, u32[]{:S(2)}) collective-permute-start(f32[42,8,128]{2,1,0:T(8,128)S(1)} %get-tuple-element.45), channel_id=1, source_target_pairs={{8,2},{2,8},{10,4},{4,10},{12,6},{6,12},{24,18},{18,24},{26,20},{2... | collective-permute-start | bytes 516104 | tf_op jit(solution)/shard_map/ppermute | solution.py:823
  11.8 5.4 %collective-permute-start.2 = (f32[10,16,128]{2,1,0:T(8,128)S(1)}, f32[10,16,128]{2,1,0:T(8,128)S(1)}, u32[]{:S(2)}, u32[]{:S(2)}) collective-permute-start(f32[10,16,128]{2,1,0:T(8,128)S(1)} %get-tuple-element.44), channel_id=1, source_target_pairs={{0,16},{16,0},{8,24},{24,8},{1,17},{17,1},{9,25},{25,9},{2,18},{18... | collective-permute-start | bytes 245768 | tf_op jit(solution)/shard_map/ppermute | solution.py:812
  11.8 5.3 %collective-permute-start.4 = (f32[6,8,128]{2,1,0:T(8,128)S(1)}, f32[6,8,128]{2,1,0:T(8,128)S(1)}, u32[]{:S(2)}, u32[]{:S(2)}) collective-permute-start(f32[6,8,128]{2,1,0:T(8,128)S(1)} %get-tuple-element.46), channel_id=1, source_target_pairs={{8,18},{18,8},{10,20},{20,10},{12,22},{22,12},{24,2},{2,24},{26,4}... | collective-permute-start | bytes 73736 | tf_op jit(solution)/shard_map/ppermute | solution.py:824
  20.9 14.1 %all-to-all-start = ((f32[16,16,128]{2,1,0:T(8,128)}), f32[16,16,128]{2,1,0:T(8,128)S(1)}, u32[]{:S(2)}, u32[]{:S(2)}) async-start(f32[16,16,128]{2,1,0:T(8,128)} %get-tuple-element.47), calls=%async_computation | async-start | bytes 262144 | tf_op jit(solution)/shard_map/all_to_all | solution.py:838
  26.7 4.0 %collective-permute-start.6 = (f32[6,8,128]{2,1,0:T(8,128)S(1)}, f32[6,8,128]{2,1,0:T(8,128)S(1)}, u32[]{:S(2)}, u32[]{:S(2)}) collective-permute-start(f32[6,8,128]{2,1,0:T(8,128)S(1)} %get-tuple-element.49), channel_id=1, source_target_pairs={{0,16},{16,0},{8,24},{24,8},{1,17},{17,1},{9,25},{25,9},{2,18},{18... | collective-permute-start | bytes 73736 | tf_op jit(solution)/shard_map/ppermute | solution.py:842
  30.7 4.9 %collective-permute-start.7 = (f32[24,8,128]{2,1,0:T(8,128)S(1)}, f32[24,8,128]{2,1,0:T(8,128)S(1)}, u32[]{:S(2)}, u32[]{:S(2)}) collective-permute-start(f32[24,8,128]{2,1,0:T(8,128)S(1)} %get-tuple-element.61), channel_id=1, source_target_pairs={{8,2},{2,8},{10,4},{4,10},{12,6},{6,12},{24,18},{18,24},{26,20},{2... | collective-permute-start | bytes 294920 | tf_op jit(solution)/shard_map/ppermute | solution.py:843
  32.6 3.0 %collective-permute-start.8 = (f32[24,8,128]{2,1,0:T(8,128)S(1)}, f32[24,8,128]{2,1,0:T(8,128)S(1)}, u32[]{:S(2)}, u32[]{:S(2)}) collective-permute-start(f32[24,8,128]{2,1,0:T(8,128)S(1)} %get-tuple-element.62), channel_id=1, source_target_pairs={{0,8},{8,0},{16,24},{24,16},{1,9},{9,1},{17,25},{25,17},{2,10},{10... | collective-permute-start | bytes 294920 | tf_op jit(solution)/shard_map/ppermute | solution.py:844
  35.0 1.3 %collective-permute-start.5 = (f32[16,16,128]{2,1,0:T(8,128)S(1)}, f32[16,16,128]{2,1,0:T(8,128)S(1)}, u32[]{:S(2)}, u32[]{:S(2)}) collective-permute-start(f32[16,16,128]{2,1,0:T(8,128)S(1)} %all-to-all-done.blocks), channel_id=1, source_target_pairs={{0,8},{8,0},{16,24},{24,16},{1,9},{9,1},{17,25},{25,17},{2,10},{10... | collective-permute-start | bytes 393224 | tf_op jit(solution)/shard_map/ppermute | solution.py:841
  39.9 1.3 %collective-permute-start.9 = (f32[16,8,128]{2,1,0:T(8,128)S(1)}, f32[16,8,128]{2,1,0:T(8,128)S(1)}, u32[]{:S(2)}, u32[]{:S(2)}) collective-permute-start(f32[16,8,128]{2,1,0:T(8,128)S(1)} %get-tuple-element.60), channel_id=1, source_target_pairs={{0,8},{8,0},{16,24},{24,16},{1,9},{9,1},{17,25},{25,17},{2,10},{10... | collective-permute-start | bytes 196616 | tf_op jit(solution)/shard_map/ppermute | solution.py:870

commit v10 on v9

--- a/solution.py
+++ b/solution.py
@@ -115,7 +115,7 @@
 BF16 = jnp.bfloat16
 ROWS = 42
 PLANES = 36
-SIZE = 12
+SIZE = 36
 
 
 def iota(shape, dim):
@@ -158,19 +158,20 @@
     given, (chi, inducing, message, spill), (dest, cell, value, done) = refs[:5], refs[5:9], refs[9:]
     _, _, _, t = place()
     held = (chi, inducing, dest, cell, value)
-    pairs = [(a.at[4 * i : 4 * i + 4], b.at[4 * i : 4 * i + 4]) for i in range(4) for a, b in [(given[0], held[0])]]
-    pairs += [(given[1].at[:, 4 * i : 4 * i + 4], held[1].at[:, 4 * i : 4 * i + 4]) for i in range(4)]
+    pairs = [(given[0].at[8 * i : 8 * i + 8], held[0].at[8 * i : 8 * i + 8]) for i in range(2)]
+    pairs += [(given[1].at[d, 8 * i : 8 * i + 8], held[1].at[d, 8 * i : 8 * i + 8]) for i in range(2) for d in range(3)]
     pairs += list(zip(given[2:], held[2:]))
     copies = [pltpu.make_async_copy(a, b, done.at[i]) for i, (a, b) in enumerate(pairs)]
-    for i in (0, 4, 1, 5, 2, 6, 3, 7, 8, 9, 10):
+    for i in (0, 2, 3, 4, 1, 5, 6, 7, 8, 9, 10):
         copies[i].start()
     lane = iota((16, 128), 1)
     turn = 11 - 10 * t
     packs = [[jnp.zeros((16, 128), F32)] * 2 for _ in range(4)]
     for x in range(16):
-        if x % 4 == 0:
-            copies[x // 4].wait()
-            copies[4 + x // 4].wait()
+        if x % 8 == 0:
+            copies[x // 8].wait()
+            for d in range(3):
+                copies[2 + 3 * (x // 8) + d].wait()
         by = 16 * (x % 8)
         wanted = (lane >= by + t) & (lane < by + t + 11)
         near = jnp.where(wanted, pltpu.roll(chi[x], (turn + by) & 127, 1), 0.0)
@@ -356,7 +357,7 @@
         cy[pl.ds(r, n)] = fy
         cz[pl.ds(r, n)] = fz
         diag[pl.ds(r, n)] = total
-        weight[pl.ds(r, n)] = jnp.where(k > 0.0, OMEGA / jnp.where(k > 0.0, total, 1.0), 0.0)
+        weight[pl.ds(r, n)] = jnp.where(k > 0.0, OMEGA / total, 0.0)
 
     chunked(count, body, n)
 
@@ -519,7 +520,9 @@
     sending.wait()
 
 
-def middle_kernel(n_gy, mine, across, both, r1, k1, weight, v2, cx, cy, cz, diag, v1):
+def middle_kernel(
+    n_gy, mine, across, both, kappa, r1, k1, weight, v2, cx0, cy0, cz0, cx, cy, cz, diag, v1
+):
     p, c, b, t = place()
     edge = jnp.where(c == 0, b == 0, b == n_gy - 1).astype(jnp.int32)
     for ref in (r1, k1, cx, weight, v1, v2):
@@ -559,6 +562,15 @@
     r = 25 - 23 * p
     v1[r, 0:8], v1[r, 8:16] = joined(low, across[4], high)
     sweep(v1, v2, r1, cx, cy, cz, weight, first, 20, 20)
+    for r in (0, 3, 4, 37, 38):
+        cx0[r] = jnp.zeros((16, 256), F32)
+    first = 5 - 4 * p
+    rows = pl.ds(first, PLANES)
+    near = kappa[pl.ds(first, PLANES + 1)]
+    k = near[:PLANES]
+    cx0[rows] = 0.5 * (k + near[1:])
+    cy0[rows] = 0.5 * (k + roll(k, -1, 1))
+    cz0[rows] = 0.5 * (k + roll(k, -1, 2))
 
 
 def shift(x, by, axis):
@@ -629,17 +641,17 @@
 
 
 def up_kernel(
-    n_gy, blocks, more, r1, k1, w1, v21, left, kappa, weight, v2, keep, give,
-    r2, k2, tall, flat, sums, fx, fy, fz, ua, ub, cx, cy, cz, va, vb,
+    n_gy, blocks, more, r1, k1, w1, v21, cx, cy, cz, left, weight, v2, keep, give,
+    r2, k2, tall, flat, sums, fx, fy, fz, ua, ub, va, vb,
 ):
     p, c, b, t = place()
     first = 5 - 4 * p
     n_y = 4 * n_gy
-    for ref in (vb, cx):
-        for r in (0, 3, 4, 37, 38):
-            ref[r] = jnp.zeros((16, 256), F32)
-    for ref in (fx, ua, ub):
-        ref[...] = jnp.zeros_like(ref)
+    for r in (3, 4, 37, 38):
+        vb[r] = jnp.zeros((16, 256), F32)
+    for ref in (fx, ub):
+        for r in (1, 5, 22, 26):
+            ref[r] = jnp.zeros((16, 128), F32)
 
     lane, sub = iota((8, 128), 1), iota((8, 128), 0)
     cells = {(y, gp): jnp.zeros((8, 128), F32) for y in range(-1, n_y + 1) for gp in range(2)}
@@ -721,12 +733,6 @@
     for k in range(18):
         for r in (2 * k + 3, 2 * k + 4):
             va[r] = jnp.where(weight[r] > 0.0, e[k], 0.0)
-    rows = pl.ds(first, PLANES)
-    near = kappa[pl.ds(first, PLANES + 1)]
-    k = near[:PLANES]
-    cx[rows] = 0.5 * (k + near[1:])
-    cy[rows] = 0.5 * (k + roll(k, -1, 1))
-    cz[rows] = 0.5 * (k + roll(k, -1, 2))
     sweep(va, vb, left, cx, cy, cz, weight, 5 - p, 33, 33)
     here, total = around(vb, cx, cy, cz, 5, 32)
     done = (1.0 - OMEGA) * here + weight[5:37] * (left[5:37] + total)
@@ -826,7 +832,7 @@
         functools.partial(down_kernel, n_gy),
         "down",
         [window] * 3 + [(32, 8, 128), (18, 8, 128), (18, 8, 128), (6, 8, 128), (4 * n_gy, 16, 128)],
-        big * 7 + [((640, 128), F32), ((48, 128), F32), ((12, 16, 128), F32)]
+        big * 7 + [((648, 128), F32), ((48, 128), F32), ((12, 16, 128), F32)]
         + [((4 * n_gy, 16, 128), F32), 1],
         *fields,
         across,
@@ -840,18 +846,22 @@
     )
     more = lax.ppermute(blocks, "gx", swap)
     across = lax.ppermute(message, "gx", cross)
-    got = lax.ppermute(jnp.concatenate([along, across]), ("gx", "gy"), turns)
-    other = lax.ppermute(jnp.concatenate([beside, across]), "gx", swap)
+    got = lax.ppermute(along, ("gx", "gy"), turns)
+    corner = lax.ppermute(message, ("gx", "gy"), corners)
+    other = lax.ppermute(beside, "gx", swap)
+    beyond = lax.ppermute(across, "gx", swap)
     window1 = (28, 16, 128)
     big1 = [(window1, F32)]
+    left, kappa, weight, v = fine
     coarse = call(
         functools.partial(middle_kernel, n_gy),
         "middle",
-        [window1] * 4,
+        [window1] * 4 + [window] * 3,
         big1 * 5,
         beside,
         across,
-        jnp.concatenate([got, other]),
+        jnp.concatenate([got, corner, other, beyond]),
+        kappa,
     )
     level2 = ((4 * n_gy, 16, 128), F32)
     keep, give = call(
@@ -859,13 +869,15 @@
         "up",
         [(16, 8, 128)] * 2,
         [level2] * 2
-        + [((4 * n_gy + 8, 32, 128), F32), ((512, 128), F32), ((64 * n_gy, 128), F32)]
+        + [((4 * n_gy + 8, 32, 128), F32), ((544, 128), F32), ((64 * n_gy, 128), F32)]
         + big1 * 5
-        + big * 5,
+        + big * 2,
         blocks,
         more,
         *coarse,
-        *fine,
+        left,
+        weight,
+        v,
     )
     got = lax.ppermute(give, "gx", swap)
     (out,) = call(join_kernel, "join", [(16, 16, 128)], [2], keep, got)

time: 42.2 us -> 41.8 us (level)
    ppermute x2 -> x4, waiting for transfers between devices: 0.63 us -> 0.01 us  [the longest x1 0.01 us: paired(): corner = lax.ppermute(message, ('gx', 'gy'), corners)]
    ppermute x2, starting transfers between devices: 2.01 us -> 1.55 us  [paired(): across = lax.ppermute(message, 'gx', cross)]
    ppermute x2 -> x4, starting transfers between devices: 2.16 us -> 2.6 us  [the longest x1 1.93 us: paired(): got = lax.ppermute(along, ('gx', 'gy'), turns)]
    ppermute x1, waiting for transfers between devices: 0.16 us -> 0.59 us  [paired(): more = lax.ppermute(blocks, 'gx', swap)]
  transfers between devices with their start and end apart: 11 -> 13, of which waited for: 8 -> 7; matrix products, arithmetic and copies ran while one was open for 0% -> 0% of each run, Pallas kernels for 3% -> 3%
where the time goes in v10:
time: 41.8 us; the launch traced here: 41.5 us
  starting transfers between devices  17.3 us (41%)
  waiting for transfers between devices  12.4 us (30%)
  Pallas kernels  11.7 us (28%)
    pallas_call x8, Pallas kernels, call(): pl.pallas_call(kernel, name=name, out_shape=[jax.ShapeDtypeStruct(s, F32)...  11.7 us
    all_to_all x1, starting transfers between devices, paired(): lax.all_to_all(parts, ('gx', 'gy', 'gz'), split_axis=0, concat_axis=0, ti...  5.77 us
    ppermute x1, waiting for transfers between devices, paired(): corner = lax.ppermute(corner, ('gx', 'gy'), corners)  3.38 us
    ppermute x1, starting transfers between devices, paired(): got = lax.ppermute(message, 'gz', [(0, 1), (1, 0)])  3 us
    all_to_all x1, waiting for transfers between devices, paired(): lax.all_to_all(parts, ('gx', 'gy', 'gz'), split_axis=0, concat_axis=0, ti...  2.34 us
    ppermute x1, starting transfers between devices, paired(): strip = lax.ppermute(strip, ('gx', 'gy'), turns)  2.11 us
    ppermute x1, starting transfers between devices, paired(): corner = lax.ppermute(corner, ('gx', 'gy'), corners)  1.95 us
    ppermute x1, starting transfers between devices, paired(): got = lax.ppermute(along, ('gx', 'gy'), turns)  1.93 us
  transfers between devices with their start and end apart: 13, of which 7 were waited for; matrix products, arithmetic and copies ran while one was open for 0% of the time, Pallas kernels for 3%

profile of v10, /device:TPU:0, one launch (start us, length us, event | category | flops | bytes accessed | tf_op | source)
XLA Modules:
  0.0 41.5 jit_solution(13874505381941305968)
XLA Ops:
  0.0 1.5 %message.1 = (f32[16,16,128]{2,1,0:T(8,128)S(1)}, f32[3,16,16,128]{3,2,1,0:T(8,128)S(1)}, f32[120,128]{1,0:T(8,128)S(1)}, f32[48,128]{1,0:T(8,128)S(1)}) custom-call(f32[16,16,128]{2,1,0:T(8,128)} %refs_0_.1, f32[3,16,16,128]{3,2,1,0:T(8,128)} %refs_1_.1, s32[8,128]{1,0:T(8,128)} %bitcast.3, s32[8,128]{1,0:T(8,128)} %bitcast.4, f32[8,128]{1,0:T(8,128)} %bitcast.5), custom_call_target="tpu_custom_call" | custom-call | flops 10000000 | bytes 4000000 | tf_op jit(solution)/shard_map/message/pallas_call | solution.py:759
  1.5 3.0 %collective-permute-start = (f32[120,128]{1,0:T(8,128)S(1)}, f32[120,128]{1,0:T(8,128)S(1)}, u32[]{:S(2)}, u32[]{:S(2)}) collective-permute-start(f32[120,128]{1,0:T(8,128)S(1)} %get-tuple-element.38.records), channel_id=1, source_target_pairs={{0,1},{1,0},{2,3},{3,2},{4,5},{5,4},{6,7},{7,6},{8,9},{9,8},{10,11... | collective-permute-start | bytes 184328 | tf_op jit(solution)/shard_map/ppermute | solution.py:789
  4.5 0.7 %source.1 = (f32[18,24,128]{2,1,0:T(8,128)S(1)}, f32[256,256]{1,0:T(8,128)S(1)}) custom-call(f32[16,16,128]{2,1,0:T(8,128)S(1)} %get-tuple-element.36.chi, f32[3,16,16,128]{3,2,1,0:T(8,128)S(1)} %get-tuple-element.37.inducing, f32[120,128]{1,0:T(8,128)S(1)} %get-tuple-element.38.records), custom_call_target="tpu_custom_call" | custom-call | flops 10000000 | bytes 4000000 | tf_op jit(solution)/shard_map/source/pallas_call | solution.py:759
  5.2 1.5 %collective-permute-done.other = f32[120,128]{1,0:T(8,128)S(1)} collective-permute-done((f32[120,128]{1,0:T(8,128)S(1)}, f32[120,128]{1,0:T(8,128)S(1)}, u32[]{:S(2)}, u32[]{:S(2)}) %collective-permute-start) | collective-permute-done | bytes 61472 | tf_op jit(solution)/shard_map/ppermute | solution.py:789
  6.7 0.9 %deposit.1 = (f32[39,16,128]{2,1,0:T(8,128)S(1)}, f32[39,16,128]{2,1,0:T(8,128)S(1)}) custom-call(f32[18,24,128]{2,1,0:T(8,128)S(1)} %get-tuple-element.39.source, f32[48,128]{1,0:T(8,128)S(1)} %get-tuple-element.40.spill, f32[16,16,128]{2,1,0:T(8,128)S(1)} %get-tuple-element.36.chi, f32[256,256]{1,0:T(8,128)S(1)} %get-tuple-element.41.mine, ...), custom_call_target="tpu_custom_call" | custom-call | flops 10000000 | bytes 4000000 | tf_op jit(solution)/shard_map/deposit/pallas_call | solution.py:759
  7.6 0.1 collective-permute-start.1
  7.7 1.6 %collective-permute-done.1.other = f32[39,16,128]{2,1,0:T(8,128)S(1)} collective-permute-done((f32[39,16,128]{2,1,0:T(8,128)S(1)}, f32[39,16,128]{2,1,0:T(8,128)S(1)}, u32[]{:S(2)}, u32[]{:S(2)}) %collective-permute-start.1) | collective-permute-done | bytes 319520 | tf_op jit(solution)/shard_map/ppermute | solution.py:812
  9.3 0.2 pair.1
  9.5 2.1 %collective-permute-start.3 = (f32[42,8,128]{2,1,0:T(8,128)S(1)}, f32[42,8,128]{2,1,0:T(8,128)S(1)}, u32[]{:S(2)}, u32[]{:S(2)}) collective-permute-start(f32[42,8,128]{2,1,0:T(8,128)S(1)} %get-tuple-element.48), channel_id=1, source_target_pairs={{8,2},{2,8},{10,4},{4,10},{12,6},{6,12},{24,18},{18,24},{26,20},{2... | collective-permute-start | bytes 516104 | tf_op jit(solution)/shard_map/ppermute | solution.py:829
  11.6 0.1 collective-permute-start.2
  11.7 1.9 %collective-permute-start.4 = (f32[6,8,128]{2,1,0:T(8,128)S(1)}, f32[6,8,128]{2,1,0:T(8,128)S(1)}, u32[]{:S(2)}, u32[]{:S(2)}) collective-permute-start(f32[6,8,128]{2,1,0:T(8,128)S(1)} %get-tuple-element.49), channel_id=1, source_target_pairs={{8,18},{18,8},{10,20},{20,10},{12,22},{22,12},{24,2},{2,24},{26,4}... | collective-permute-start | bytes 73736 | tf_op jit(solution)/shard_map/ppermute | solution.py:830
  13.7 3.4 %collective-permute-done.4.corner = f32[6,8,128]{2,1,0:T(8,128)S(1)} collective-permute-done((f32[6,8,128]{2,1,0:T(8,128)S(1)}, f32[6,8,128]{2,1,0:T(8,128)S(1)}, u32[]{:S(2)}, u32[]{:S(2)}) %collective-permute-start.4) | collective-permute-done | bytes 24608 | tf_op jit(solution)/shard_map/ppermute | solution.py:830
  17.0 0.0 collective-permute-done.2.across
  17.0 0.0 collective-permute-done.3.along_in
  17.0 3.5 %down.1 = (f32[42,16,256]{2,1,0:T(8,128)S(1)}, f32[42,16,256]{2,1,0:T(8,128)S(1)}, f32[42,16,256]{2,1,0:T(8,128)S(1)}, f32[32,8,128]{2,1,0:T(8,128)S(1)}, f32[18...) custom-call(f32[42,16,128]{2,1,0:T(8,128)S(1)} %get-tuple-element.44.source_, ...), custom_call_target="tpu_custom_call" | custom-call | flops 10000000 | bytes 4000000 | tf_op jit(solution)/shard_map/down/pallas_call | solution.py:759
  20.6 5.8 %all-to-all-start = ((f32[16,16,128]{2,1,0:T(8,128)}), f32[16,16,128]{2,1,0:T(8,128)S(1)}, u32[]{:S(2)}, u32[]{:S(2)}) async-start(f32[16,16,128]{2,1,0:T(8,128)} %get-tuple-element.50), calls=%async_computation | async-start | bytes 262144 | tf_op jit(solution)/shard_map/all_to_all | solution.py:844
  26.4 1.9 %collective-permute-start.7 = (f32[18,8,128]{2,1,0:T(8,128)S(1)}, f32[18,8,128]{2,1,0:T(8,128)S(1)}, u32[]{:S(2)}, u32[]{:S(2)}) collective-permute-start(f32[18,8,128]{2,1,0:T(8,128)S(1)} %get-tuple-element.53), channel_id=1, source_target_pairs={{8,2},{2,8},{10,4},{4,10},{12,6},{6,12},{24,18},{18,24},{26,20},{2... | collective-permute-start | bytes 221192 | tf_op jit(solution)/shard_map/ppermute | solution.py:849
  28.3 0.1 collective-permute-start.9
  28.4 1.5 %collective-permute-start.6 = (f32[6,8,128]{2,1,0:T(8,128)S(1)}, f32[6,8,128]{2,1,0:T(8,128)S(1)}, u32[]{:S(2)}, u32[]{:S(2)}) collective-permute-start(f32[6,8,128]{2,1,0:T(8,128)S(1)} %get-tuple-element.52), channel_id=1, source_target_pairs={{0,16},{16,0},{8,24},{24,8},{1,17},{17,1},{9,25},{25,9},{2,18},{18... | collective-permute-start | bytes 73736 | tf_op jit(solution)/shard_map/ppermute | solution.py:848
  29.9 0.6 %collective-permute-start.8 = (f32[6,8,128]{2,1,0:T(8,128)S(1)}, f32[6,8,128]{2,1,0:T(8,128)S(1)}, u32[]{:S(2)}, u32[]{:S(2)}) collective-permute-start(f32[6,8,128]{2,1,0:T(8,128)S(1)} %get-tuple-element.52), channel_id=1, source_target_pairs={{8,18},{18,8},{10,20},{20,10},{12,22},{22,12},{24,2},{2,24},{26,4}... | collective-permute-start | bytes 73736 | tf_op jit(solution)/shard_map/ppermute | solution.py:850
  30.4 1.9 %collective-permute-done.6.across = f32[6,8,128]{2,1,0:T(8,128)S(1)} collective-permute-done((f32[6,8,128]{2,1,0:T(8,128)S(1)}, f32[6,8,128]{2,1,0:T(8,128)S(1)}, u32[]{:S(2)}, u32[]{:S(2)}) %collective-permute-start.6) | collective-permute-done | bytes 24608 | tf_op jit(solution)/shard_map/ppermute | solution.py:848
  32.4 0.0 collective-permute-start.10
  32.4 2.3 %all-to-all-done.blocks = f32[16,16,128]{2,1,0:T(8,128)S(1)} async-done(((f32[16,16,128]{2,1,0:T(8,128)}), f32[16,16,128]{2,1,0:T(8,128)S(1)}, u32[]{:S(2)}, u32[]{:S(2)}) %all-to-all-start) | async-done | bytes 131104 | tf_op jit(solution)/shard_map/all_to_all | solution.py:844
  34.7 0.0 collective-permute-start.5
  34.7 0.0 collective-permute-done.8
  34.7 0.0 collective-permute-done.10
  34.7 0.0 collective-permute-done.7
  34.7 0.0 collective-permute-done.9
  34.7 0.7 %middle.1 = (f32[28,16,128]{2,1,0:T(8,128)S(1)}, f32[28,16,128]{2,1,0:T(8,128)S(1)}, f32[28,16,128]{2,1,0:T(8,128)S(1)}, f32[28,16,128]{2,1,0:T(8,128)S(1)}, f32...) custom-call(f32[18,8,128]{2,1,0:T(8,128)S(1)} %get-tuple-element.51.mine, ...), custom_call_target="tpu_custom_call" | custom-call | flops 10000000 | bytes 4000000 | tf_op jit(solution)/shard_map/middle/pallas_call | solution.py:759
  35.5 0.6 %collective-permute-done.5.more = f32[16,16,128]{2,1,0:T(8,128)S(1)} collective-permute-done((f32[16,16,128]{2,1,0:T(8,128)S(1)}, f32[16,16,128]{2,1,0:T(8,128)S(1)}, u32[]{:S(2)}, u32[]{:S(2)}) %collective-permute-start.5) | collective-permute-done | bytes 131104 | tf_op jit(solution)/shard_map/ppermute | solution.py:847
  36.0 3.5 %up.1 = (f32[16,8,128]{2,1,0:T(8,128)S(1)}, f32[16,8,128]{2,1,0:T(8,128)S(1)}) custom-call(f32[16,16,128]{2,1,0:T(8,128)S(1)} %all-to-all-done.blocks, f32[16,16,128]{2,1,0:T(8,128)S(1)} %collective-permute-done.5.more, f32[28,16,128]{2,1,0:T(8,128)S(1)} %get-tuple-element.55.r1, f32[28,16,128]{2,1,0:T(8,128)S(1)} %get-tuple-element.56.k1, ...), custom_call_target="tpu_custom_call" | custom-call | flops 10000000 | bytes 4000000 | tf_op jit(solution)/shard_map/up/pallas_call | solution.py:759
  39.5 0.2 collective-permute-start.11
  39.7 1.1 %collective-permute-done.11.other = f32[16,8,128]{2,1,0:T(8,128)S(1)} collective-permute-done((f32[16,8,128]{2,1,0:T(8,128)S(1)}, f32[16,8,128]{2,1,0:T(8,128)S(1)}, u32[]{:S(2)}, u32[]{:S(2)}) %collective-permute-start.11) | collective-permute-done | bytes 65568 | tf_op jit(solution)/shard_map/ppermute | solution.py:882
  40.9 0.7 %join.1 = f32[16,16,128]{2,1,0:T(8,128)} custom-call(f32[16,8,128]{2,1,0:T(8,128)S(1)} %get-tuple-element.65.mine, f32[16,8,128]{2,1,0:T(8,128)S(1)} %collective-permute-done.11.other), custom_call_target="tpu_custom_call" | custom-call | flops 10000000 | bytes 4000000 | tf_op jit(solution)/shard_map/join/pallas_call | solution.py:759
  (1 shorter events, 0.0 us)
Async XLA Ops:
  1.5 5.2 %collective-permute-start = (f32[120,128]{1,0:T(8,128)S(1)}, f32[120,128]{1,0:T(8,128)S(1)}, u32[]{:S(2)}, u32[]{:S(2)}) collective-permute-start(f32[120,128]{1,0:T(8,128)S(1)} %get-tuple-element.38.records), channel_id=1, source_target_pairs={{0,1},{1,0},{2,3},{3,2},{4,5},{5,4},{6,7},{7,6},{8,9},{9,8},{10,11... | collective-permute-start | bytes 184328 | tf_op jit(solution)/shard_map/ppermute | solution.py:789
  7.6 1.7 %collective-permute-start.1 = (f32[39,16,128]{2,1,0:T(8,128)S(1)}, f32[39,16,128]{2,1,0:T(8,128)S(1)}, u32[]{:S(2)}, u32[]{:S(2)}) collective-permute-start(f32[39,16,128]{2,1,0:T(8,128)S(1)} %get-tuple-element.43), channel_id=1, source_target_pairs={{0,8},{8,0},{16,24},{24,16},{1,9},{9,1},{17,25},{25,17},{2,10},{10... | collective-permute-start | bytes 958472 | tf_op jit(solution)/shard_map/ppermute | solution.py:812
  9.5 7.5 %collective-permute-start.3 = (f32[42,8,128]{2,1,0:T(8,128)S(1)}, f32[42,8,128]{2,1,0:T(8,128)S(1)}, u32[]{:S(2)}, u32[]{:S(2)}) collective-permute-start(f32[42,8,128]{2,1,0:T(8,128)S(1)} %get-tuple-element.48), channel_id=1, source_target_pairs={{8,2},{2,8},{10,4},{4,10},{12,6},{6,12},{24,18},{18,24},{26,20},{2... | collective-permute-start | bytes 516104 | tf_op jit(solution)/shard_map/ppermute | solution.py:829
  11.6 5.4 %collective-permute-start.2 = (f32[10,16,128]{2,1,0:T(8,128)S(1)}, f32[10,16,128]{2,1,0:T(8,128)S(1)}, u32[]{:S(2)}, u32[]{:S(2)}) collective-permute-start(f32[10,16,128]{2,1,0:T(8,128)S(1)} %get-tuple-element.47), channel_id=1, source_target_pairs={{0,16},{16,0},{8,24},{24,8},{1,17},{17,1},{9,25},{25,9},{2,18},{18... | collective-permute-start | bytes 245768 | tf_op jit(solution)/shard_map/ppermute | solution.py:818
  11.7 5.3 %collective-permute-start.4 = (f32[6,8,128]{2,1,0:T(8,128)S(1)}, f32[6,8,128]{2,1,0:T(8,128)S(1)}, u32[]{:S(2)}, u32[]{:S(2)}) collective-permute-start(f32[6,8,128]{2,1,0:T(8,128)S(1)} %get-tuple-element.49), channel_id=1, source_target_pairs={{8,18},{18,8},{10,20},{20,10},{12,22},{22,12},{24,2},{2,24},{26,4}... | collective-permute-start | bytes 73736 | tf_op jit(solution)/shard_map/ppermute | solution.py:830
  20.6 14.1 %all-to-all-start = ((f32[16,16,128]{2,1,0:T(8,128)}), f32[16,16,128]{2,1,0:T(8,128)S(1)}, u32[]{:S(2)}, u32[]{:S(2)}) async-start(f32[16,16,128]{2,1,0:T(8,128)} %get-tuple-element.50), calls=%async_computation | async-start | bytes 262144 | tf_op jit(solution)/shard_map/all_to_all | solution.py:844
  26.4 8.3 %collective-permute-start.7 = (f32[18,8,128]{2,1,0:T(8,128)S(1)}, f32[18,8,128]{2,1,0:T(8,128)S(1)}, u32[]{:S(2)}, u32[]{:S(2)}) collective-permute-start(f32[18,8,128]{2,1,0:T(8,128)S(1)} %get-tuple-element.53), channel_id=1, source_target_pairs={{8,2},{2,8},{10,4},{4,10},{12,6},{6,12},{24,18},{18,24},{26,20},{2... | collective-permute-start | bytes 221192 | tf_op jit(solution)/shard_map/ppermute | solution.py:849
  28.3 6.4 %collective-permute-start.9 = (f32[18,8,128]{2,1,0:T(8,128)S(1)}, f32[18,8,128]{2,1,0:T(8,128)S(1)}, u32[]{:S(2)}, u32[]{:S(2)}) collective-permute-start(f32[18,8,128]{2,1,0:T(8,128)S(1)} %get-tuple-element.51.mine), channel_id=1, source_target_pairs={{0,8},{8,0},{16,24},{24,16},{1,9},{9,1},{17,25},{25,17},{2,10},{10... | collective-permute-start | bytes 221192 | tf_op jit(solution)/shard_map/ppermute | solution.py:851
  28.4 3.9 %collective-permute-start.6 = (f32[6,8,128]{2,1,0:T(8,128)S(1)}, f32[6,8,128]{2,1,0:T(8,128)S(1)}, u32[]{:S(2)}, u32[]{:S(2)}) collective-permute-start(f32[6,8,128]{2,1,0:T(8,128)S(1)} %get-tuple-element.52), channel_id=1, source_target_pairs={{0,16},{16,0},{8,24},{24,8},{1,17},{17,1},{9,25},{25,9},{2,18},{18... | collective-permute-start | bytes 73736 | tf_op jit(solution)/shard_map/ppermute | solution.py:848
  29.9 4.8 %collective-permute-start.8 = (f32[6,8,128]{2,1,0:T(8,128)S(1)}, f32[6,8,128]{2,1,0:T(8,128)S(1)}, u32[]{:S(2)}, u32[]{:S(2)}) collective-permute-start(f32[6,8,128]{2,1,0:T(8,128)S(1)} %get-tuple-element.52), channel_id=1, source_target_pairs={{8,18},{18,8},{10,20},{20,10},{12,22},{22,12},{24,2},{2,24},{26,4}... | collective-permute-start | bytes 73736 | tf_op jit(solution)/shard_map/ppermute | solution.py:850
  32.4 2.4 %collective-permute-start.10 = (f32[6,8,128]{2,1,0:T(8,128)S(1)}, f32[6,8,128]{2,1,0:T(8,128)S(1)}, u32[]{:S(2)}, u32[]{:S(2)}) collective-permute-start(f32[6,8,128]{2,1,0:T(8,128)S(1)} %collective-permute-done.6.across), channel_id=1, source_target_pairs={{0,8},{8,0},{16,24},{24,16},{1,9},{9,1},{17,25},{25,17},{2,10},{10... | collective-permute-start | bytes 73736 | tf_op jit(solution)/shard_map/ppermute | solution.py:852
  34.7 1.3 %collective-permute-start.5 = (f32[16,16,128]{2,1,0:T(8,128)S(1)}, f32[16,16,128]{2,1,0:T(8,128)S(1)}, u32[]{:S(2)}, u32[]{:S(2)}) collective-permute-start(f32[16,16,128]{2,1,0:T(8,128)S(1)} %all-to-all-done.blocks), channel_id=1, source_target_pairs={{0,8},{8,0},{16,24},{24,16},{1,9},{9,1},{17,25},{25,17},{2,10},{10... | collective-permute-start | bytes 393224 | tf_op jit(solution)/shard_map/ppermute | solution.py:847
  39.5 1.3 %collective-permute-start.11 = (f32[16,8,128]{2,1,0:T(8,128)S(1)}, f32[16,8,128]{2,1,0:T(8,128)S(1)}, u32[]{:S(2)}, u32[]{:S(2)}) collective-permute-start(f32[16,8,128]{2,1,0:T(8,128)S(1)} %get-tuple-element.66), channel_id=1, source_target_pairs={{0,8},{8,0},{16,24},{24,16},{1,9},{9,1},{17,25},{25,17},{2,10},{10... | collective-permute-start | bytes 196616 | tf_op jit(solution)/shard_map/ppermute | solution.py:882
